TPU v7x, 512 devices: a whole 4x8x8 slice. The times are simulated.
512 devices in a mesh: gx: 32 (over x, y), gy: 16 (over z, core).
Axes of the slice: x: 4, y: 8, z: 8, core: 2. Of those that a mesh axis runs over, the one named last changes fastest.
Arguments:
- features: bfloat16 [64, 64, 128, 32], P(None, 'gx', 'gy'), may hold values from -6 to 6
- encoder_weight: bfloat16 [27, 64, 64], replicated, may hold values from -0.15625 to 0.15625
- lower_weight: bfloat16 [27, 128, 64], replicated, may hold values from -0.15625 to 0.15625
- lift_weight: bfloat16 [8, 64, 128], replicated, may hold values from -0.5 to 0.5
- decoder_weight: bfloat16 [27, 64, 128], replicated, may hold values from -0.109375 to 0.109375
- cotangent: bfloat16 [64, 64, 128, 32], P(None, 'gx', 'gy'), may hold values from -6 to 6
Outputs:
- decoded: bfloat16 [64, 64, 128, 32], P(None, 'gx', 'gy')
- input_gradient: bfloat16 [64, 64, 128, 32], P(None, 'gx', 'gy')
- encoder_gradient: float32 [27, 64, 64], replicated
- lower_gradient: float32 [27, 128, 64], replicated
- lift_gradient: float32 [8, 64, 128], replicated
- decoder_gradient: float32 [27, 64, 128], replicated
All inputs are finite; a program needn't handle non-finite values.
Results may differ from a plain program's by a relative error of at most 0.014.
Values may be sent and summed in bfloat16 or wider, within the bound.
No kernel may reach another device: no remote copies, remote signals or barrier semaphores. Data moves between devices by JAX's collectives and lax.ppermute only.
A program may use at most 64 MiB of HBM per device.

v0:
```python
import jax
import jax.numpy as jnp
from jax import lax
from jax.sharding import PartitionSpec as P

OFFSETS = tuple(
    (
        (shift_x, shift_y, shift_z)
        for shift_x in range(3)
        for shift_y in range(3)
        for shift_z in range(3)
    )
)


def extended(value, sides, width):
    for axis, dim in sides:
        size, length = (lax.axis_size(axis), value.shape[dim])
        up = [(i, (i + 1) % size) for i in range(size - 1)]
        down = [(j, i) for i, j in up]
        last = lax.slice_in_dim(value, length - width, length, axis=dim)
        initial = lax.slice_in_dim(value, 0, width, axis=dim)
        before = lax.ppermute(last, axis, up)
        after = lax.ppermute(initial, axis, down)
        value = jnp.concatenate([before, value, after], axis=dim)
    return value


def pad_depth(block):
    return jnp.pad(block, ((0, 0), (0, 0), (0, 0), (1, 1)))


def apply_taps(padded, weight, shape):
    size_x, size_y, size_z = shape
    total = jnp.zeros((weight.shape[1], size_x, size_y, size_z), jnp.float32)
    for tap_index, (shift_x, shift_y, shift_z) in enumerate(OFFSETS):
        window = padded[
            :, shift_x : shift_x + size_x, shift_y : shift_y + size_y, shift_z : shift_z + size_z
        ]
        total = total + jnp.einsum(
            "oc,cxyz->oxyz", weight[tap_index], window, preferred_element_type=jnp.float32
        )
    return total


def apply_adjoint(padded, weight, shape):
    size_x, size_y, size_z = shape
    total = jnp.zeros((weight.shape[2], size_x, size_y, size_z), jnp.float32)
    for tap_index, (shift_x, shift_y, shift_z) in enumerate(OFFSETS):
        window = padded[
            :,
            2 - shift_x : 2 - shift_x + size_x,
            2 - shift_y : 2 - shift_y + size_y,
            2 - shift_z : 2 - shift_z + size_z,
        ]
        total = total + jnp.einsum(
            "oc,oxyz->cxyz", weight[tap_index], window, preferred_element_type=jnp.float32
        )
    return total


def tap_gradients(grad_out, padded, shape):
    size_x, size_y, size_z = shape
    result = []
    for shift_x, shift_y, shift_z in OFFSETS:
        window = padded[
            :, shift_x : shift_x + size_x, shift_y : shift_y + size_y, shift_z : shift_z + size_z
        ]
        result.append(
            jnp.einsum("oxyz,cxyz->oc", grad_out, window, preferred_element_type=jnp.float32)
        )
    return jnp.stack(result, 0)


def silu_slope(value):
    sigma = jax.nn.sigmoid(value)
    return sigma * (1.0 + value * (1.0 - sigma))


def average_pool(field):
    chans, size_x, size_y, size_z = field.shape
    blocks = field.astype(jnp.float32).reshape(
        chans, size_x // 2, 2, size_y // 2, 2, size_z // 2, 2
    )
    return jnp.mean(blocks, axis=(2, 4, 6))


def spread_up(field):
    chans, size_x, size_y, size_z = field.shape
    wide = jnp.broadcast_to(
        field[:, :, None, :, None, :, None], (chans, size_x, 2, size_y, 2, size_z, 2)
    )
    return wide.reshape(chans, 2 * size_x, 2 * size_y, 2 * size_z)


def lift_up(lower_act, lift_weight):
    chans, size_x, size_y, size_z = lower_act.shape
    taps = lift_weight.reshape(2, 2, 2, lift_weight.shape[1], lift_weight.shape[2])
    out = jnp.einsum("pqroc,cijk->oipjqkr", taps, lower_act, preferred_element_type=jnp.float32)
    return out.reshape(lift_weight.shape[1], 2 * size_x, 2 * size_y, 2 * size_z)


def split_children(field):
    chans, size_x, size_y, size_z = field.shape
    return field.reshape(chans, size_x // 2, 2, size_y // 2, 2, size_z // 2, 2)


def lift_adjoint(lifted_grad, lift_weight):
    taps = lift_weight.reshape(2, 2, 2, lift_weight.shape[1], lift_weight.shape[2])
    return jnp.einsum(
        "pqroc,oipjqkr->cijk", taps, split_children(lifted_grad), preferred_element_type=jnp.float32
    )


def lift_outer(lifted_grad, lower_act):
    out = jnp.einsum(
        "oipjqkr,cijk->pqroc",
        split_children(lifted_grad),
        lower_act,
        preferred_element_type=jnp.float32,
    )
    return out.reshape(8, out.shape[3], out.shape[4])


def per_device(features, encoder_weight, lower_weight, lift_weight, decoder_weight, cotangent):
    channels, brick_x, brick_y, depth = features.shape
    fine_shape = (brick_x, brick_y, depth)
    coarse_shape = (brick_x // 2, brick_y // 2, depth // 2)
    feat_pad = pad_depth(extended(features, (("gx", 1), ("gy", 2)), 1))
    encoder_pre = apply_taps(feat_pad, encoder_weight, fine_shape)
    encoded = jax.nn.silu(encoder_pre).astype(jnp.bfloat16)
    pooled = average_pool(encoded).astype(jnp.bfloat16)
    pool_pad = pad_depth(extended(pooled, (("gx", 1), ("gy", 2)), 1))
    lower_pre = apply_taps(pool_pad, lower_weight, coarse_shape)
    lower_act = jax.nn.silu(lower_pre).astype(jnp.bfloat16)
    lifted = lift_up(lower_act, lift_weight).astype(jnp.bfloat16)
    joined = jnp.concatenate((encoded, lifted), 0)
    join_pad = pad_depth(extended(joined, (("gx", 1), ("gy", 2)), 1))
    decoded = apply_taps(join_pad, decoder_weight, fine_shape).astype(jnp.bfloat16)
    cot_pad = pad_depth(extended(cotangent, (("gx", 1), ("gy", 2)), 1))
    joined_grad = apply_adjoint(cot_pad, decoder_weight, fine_shape).astype(jnp.bfloat16)
    decoder_gradient = tap_gradients(cotangent, join_pad, fine_shape)
    lifted_grad = joined_grad[channels:]
    lower_grad = (lift_adjoint(lifted_grad, lift_weight) * silu_slope(lower_pre)).astype(
        jnp.bfloat16
    )
    lift_gradient = lift_outer(lifted_grad, lower_act)
    grad_pad = pad_depth(extended(lower_grad, (("gx", 1), ("gy", 2)), 1))
    pooled_grad = apply_adjoint(grad_pad, lower_weight, coarse_shape).astype(jnp.bfloat16)
    lower_gradient = lax.psum(tap_gradients(lower_grad, pool_pad, coarse_shape), ("gx", "gy"))
    summed = (
        joined_grad[:channels].astype(jnp.float32)
        + spread_up(pooled_grad.astype(jnp.float32)) / 8.0
    )
    encoded_grad = (summed * silu_slope(encoder_pre)).astype(jnp.bfloat16)
    enc_pad = pad_depth(extended(encoded_grad, (("gx", 1), ("gy", 2)), 1))
    input_gradient = apply_adjoint(enc_pad, encoder_weight, fine_shape).astype(jnp.bfloat16)
    encoder_gradient = tap_gradients(encoded_grad, feat_pad, fine_shape)
    decoder_gradient, lift_gradient, encoder_gradient = lax.psum(
        (decoder_gradient, lift_gradient, encoder_gradient), ("gx", "gy")
    )
    return (
        decoded,
        input_gradient,
        encoder_gradient,
        lower_gradient,
        lift_gradient,
        decoder_gradient,
    )


def solution(mesh):
    return jax.shard_map(
        per_device,
        mesh=mesh,
        in_specs=(P(None, "gx", "gy", None), P(), P(), P(), P(), P(None, "gx", "gy", None)),
        out_specs=(P(None, "gx", "gy", None), P(None, "gx", "gy", None), P(), P(), P(), P()),
        check_vma=False,
    )
```

profile of v0, /device:TPU:1, one launch (start us, length us, event | category | flops | bytes accessed | tf_op | source)
XLA Modules:
  0.0 450.7 jit_solution(6847098636711289828)
XLA Ops:
  7.2 0.9 fusion.803
  8.2 4.0 collective-permute-start
  12.2 1.4 collective-permute-start.1
  13.7 4.0 collective-permute-start.12
  17.7 1.3 collective-permute-start.13
  19.0 0.9 fusion.600
  20.3 5.4 %collective-permute-start.2 = (bf16[64,4,1,32]{0,3,2,1:T(8,128)(2,1)S(1)}, bf16[64,4,1,32]{0,3,2,1:T(8,128)(2,1)S(1)}, u32[]{:S(2)}, u32[]{:S(2)}) collective-permute-start(bf16[64,4,1,32]{0,3,2,1:T(8,128)(2,1)S(1)} %get-tuple-element.22), channel_id=1, source_target_pairs={{0,1},{1,2},{2,3},{3,4},{4,5},{5,6},{6,7},{7,8},{8,9},{9,10},{10,1... | collective-permute-start | bytes 49160 | tf_op jit(solution)/shard_map/ppermute | solution.py:23
  25.7 2.5 collective-permute-start.3
  28.3 3.2 collective-permute-start.14
  31.5 1.9 collective-permute-start.15
  38.2 0.9 convert_reduce_fusion
  39.2 4.3 collective-permute-start.4
  43.5 1.3 collective-permute-start.5
  49.4 1.9 collective-permute-start.7
  51.3 3.9 collective-permute-start.6
  55.5 0.5 collective-permute-done.6
  60.6 4.6 %collective-permute-start.16 = (bf16[128,1,4,16]{0,3,2,1:T(8,128)(2,1)S(1)}, bf16[128,1,4,16]{0,3,2,1:T(8,128)(2,1)S(1)}, u32[]{:S(2)}, u32[]{:S(2)}) collective-permute-start(bf16[128,1,4,16]{0,3,2,1:T(8,128)(2,1)S(1)} %bitcast.1895), channel_id=1, source_target_pairs={{0,16},{16,32},{32,48},{48,64},{64,80},{80,96},{96,112},{112,128},... | collective-permute-start | bytes 49160 | tf_op jit(solution)/shard_map/ppermute | solution.py:23
  65.1 1.3 collective-permute-start.17
  66.4 1.0 fusion.284
  67.9 5.5 %collective-permute-start.8 = (bf16[128,1,8,32]{0,3,2,1:T(8,128)(2,1)S(1)}, bf16[128,1,8,32]{0,3,2,1:T(8,128)(2,1)S(1)}, u32[]{:S(2)}, u32[]{:S(2)}) collective-permute-start(bf16[128,1,8,32]{0,3,2,1:T(8,128)(2,1)S(1)} %get-tuple-element.20), channel_id=1, source_target_pairs={{0,16},{16,32},{32,48},{48,64},{64,80},{80,96},{96,112},{112,128},... | collective-permute-start | bytes 196616 | tf_op jit(solution)/shard_map/ppermute | solution.py:23
  73.4 1.3 collective-permute-start.9
  79.7 4.4 collective-permute-start.18
  84.1 1.9 collective-permute-start.19
  86.2 2.9 collective-permute-done.19
  92.9 0.5 copy-done.18
  99.1 5.5 %collective-permute-start.20 = (bf16[64,1,8,32]{0,3,2,1:T(8,128)(2,1)S(1)}, bf16[64,1,8,32]{0,3,2,1:T(8,128)(2,1)S(1)}, u32[]{:S(2)}, u32[]{:S(2)}) collective-permute-start(bf16[64,1,8,32]{0,3,2,1:T(8,128)(2,1)S(1)} %get-tuple-element.24), channel_id=1, source_target_pairs={{0,16},{16,32},{32,48},{48,64},{64,80},{80,96},{96,112},{112,128},... | collective-permute-start | bytes 98312 | tf_op jit(solution)/shard_map/ppermute | solution.py:23
  104.6 1.3 collective-permute-start.21
  106.3 4.4 collective-permute-done.21
  110.7 1.9 collective-permute-start.23
  112.7 3.6 collective-permute-start.22
  116.6 2.7 collective-permute-start.10
  119.3 2.1 collective-permute-start.11
  126.0 0.8 fusion.82
  128.9 0.9 convolution_bitcast_fusion.9
  129.7 0.9 convolution_bitcast_fusion.31
  130.6 0.9 convolution_bitcast_fusion.32
  131.5 0.9 convolution_bitcast_fusion.33
  132.4 0.9 convolution_bitcast_fusion.34
  133.2 0.9 convolution_bitcast_fusion.35
  134.1 0.9 convolution_bitcast_fusion.36
  141.3 0.4 copy-done.14
  142.7 0.5 copy-done.8
  144.0 0.8 fusion.80
  144.9 294.0 %all-reduce.9.cloned.1.call-done = (f32[27,64,64]{2,1,0:T(8,128)}, f32[27,128,64]{1,2,0:T(8,128)}, f32[8,64,128]{2,1,0:T(8,128)}, f32[27,64,128]{2,1,0:T(8,128)}) async-done(((f32[27,64,64]{2,1,0:T(8,128)}, f32[27,128,64]{1,2,0:T(8,128)}, f32[8,64,128]{2,1,0:T(8,128)}, f32[27,64,128]{2,1,0:T(8,128)}), (f32[27,64,64]{2,1,0:T(8,128)}, f32[27,128,64]{1,2,0:T(8,128)}, f32[8,64,128]{2,1,0:T(8,128)}, ...) | async-done | bytes 2474000 | tf_op jit(solution)/shard_map/psum | solution.py:159
  438.9 2.3 copy.222
  441.1 0.9 copy.223
  442.2 0.7 copy.224
  442.9 0.9 copy.225
  (324 shorter events, 44.5 us)
Async XLA Ops:
  7.2 52.7 %copy-start = (bf16[8,64,128]{2,1,0:T(8,128)(2,1)S(1)}, bf16[8,64,128]{2,1,0:T(8,128)(2,1)}, u32[]{:S(2)}) copy-start(bf16[8,64,128]{2,1,0:T(8,128)(2,1)} %param.9) | copy-start | bytes 393220
  7.2 6.5 %copy-start.1 = (bf16[64,2,8,32]{0,3,2,1:T(8,128)(2,1)S(1)}, bf16[64,2,8,32]{0,3,2,1:T(8,128)(2,1)}, u32[]{:S(2)}) copy-start(bf16[64,2,8,32]{0,3,2,1:T(8,128)(2,1)} %param.11) | copy-start | bytes 196612
  7.2 431.7 %all-reduce.9.cloned.1.call-start = ((), (), s32[]{:S(2)}) async-start(), calls=%async_computation | async-start | bytes 5832704 | tf_op jit(solution)/shard_map/psum | solution.py:159
  8.2 11.9 %collective-permute-start = (bf16[64,1,8,32]{0,3,2,1:T(8,128)(2,1)S(1)}, bf16[64,1,8,32]{0,3,2,1:T(8,128)(2,1)S(1)}, u32[]{:S(2)}, u32[]{:S(2)}) collective-permute-start(bf16[64,1,8,32]{0,3,2,1:T(8,128)(2,1)S(1)} %get-tuple-element.32), channel_id=1, source_target_pairs={{0,16},{16,32},{32,48},{48,64},{64,80},{80,96},{96,112},{112,128},... | collective-permute-start | bytes 98312 | tf_op jit(solution)/shard_map/ppermute | solution.py:23
  12.2 6.8 %copy-start.2 = (bf16[64,2,8,32]{0,3,2,1:T(8,128)(2,1)S(1)}, bf16[64,2,8,32]{0,3,2,1:T(8,128)(2,1)}, u32[]{:S(2)}) copy-start(bf16[64,2,8,32]{0,3,2,1:T(8,128)(2,1)} %param.6) | copy-start | bytes 196612
  12.2 7.7 %copy-start.3 = (bf16[27,64,128]{2,1,0:T(8,128)(2,1)S(1)}, bf16[27,64,128]{2,1,0:T(8,128)(2,1)}, u32[]{:S(2)}) copy-start(bf16[27,64,128]{2,1,0:T(8,128)(2,1)} %param.10) | copy-start | bytes 1327108
  12.2 8.0 %collective-permute-start.1 = (bf16[64,1,8,32]{0,3,2,1:T(8,128)(2,1)S(1)}, bf16[64,1,8,32]{0,3,2,1:T(8,128)(2,1)S(1)}, u32[]{:S(2)}, u32[]{:S(2)}) collective-permute-start(bf16[64,1,8,32]{0,3,2,1:T(8,128)(2,1)S(1)} %get-tuple-element.31), channel_id=1, source_target_pairs={{16,0},{32,16},{48,32},{64,48},{80,64},{96,80},{112,96},{128,112},... | collective-permute-start | bytes 98312 | tf_op jit(solution)/shard_map/ppermute | solution.py:24
  13.7 14.5 %collective-permute-start.12 = (bf16[64,1,8,32]{0,3,2,1:T(8,128)(2,1)S(1)}, bf16[64,1,8,32]{0,3,2,1:T(8,128)(2,1)S(1)}, u32[]{:S(2)}, u32[]{:S(2)}) collective-permute-start(bf16[64,1,8,32]{0,3,2,1:T(8,128)(2,1)S(1)} %get-tuple-element.27), channel_id=1, source_target_pairs={{0,16},{16,32},{32,48},{48,64},{64,80},{80,96},{96,112},{112,128},... | collective-permute-start | bytes 98312 | tf_op jit(solution)/shard_map/ppermute | solution.py:23
  17.7 10.5 %collective-permute-start.13 = (bf16[64,1,8,32]{0,3,2,1:T(8,128)(2,1)S(1)}, bf16[64,1,8,32]{0,3,2,1:T(8,128)(2,1)S(1)}, u32[]{:S(2)}, u32[]{:S(2)}) collective-permute-start(bf16[64,1,8,32]{0,3,2,1:T(8,128)(2,1)S(1)} %get-tuple-element.26), channel_id=1, source_target_pairs={{16,0},{32,16},{48,32},{64,48},{80,64},{96,80},{112,96},{128,112},... | collective-permute-start | bytes 98312 | tf_op jit(solution)/shard_map/ppermute | solution.py:24
  20.3 13.2 %collective-permute-start.2 = (bf16[64,4,1,32]{0,3,2,1:T(8,128)(2,1)S(1)}, bf16[64,4,1,32]{0,3,2,1:T(8,128)(2,1)S(1)}, u32[]{:S(2)}, u32[]{:S(2)}) collective-permute-start(bf16[64,4,1,32]{0,3,2,1:T(8,128)(2,1)S(1)} %get-tuple-element.22), channel_id=1, source_target_pairs={{0,1},{1,2},{2,3},{3,4},{4,5},{5,6},{6,7},{7,8},{8,9},{9,10},{10,1... | collective-permute-start | bytes 49160 | tf_op jit(solution)/shard_map/ppermute | solution.py:23
  25.7 7.8 %collective-permute-start.3 = (bf16[64,4,1,32]{0,3,2,1:T(8,128)(2,1)S(1)}, bf16[64,4,1,32]{0,3,2,1:T(8,128)(2,1)S(1)}, u32[]{:S(2)}, u32[]{:S(2)}) collective-permute-start(bf16[64,4,1,32]{0,3,2,1:T(8,128)(2,1)S(1)} %get-tuple-element.23), channel_id=1, source_target_pairs={{1,0},{2,1},{3,2},{4,3},{5,4},{6,5},{7,6},{8,7},{9,8},{10,9},{11,1... | collective-permute-start | bytes 49160 | tf_op jit(solution)/shard_map/ppermute | solution.py:24
  28.3 5.3 %copy-start.5 = (bf16[27,64,64]{2,1,0:T(8,128)(2,1)S(1)}, bf16[27,64,64]{2,1,0:T(8,128)(2,1)}, u32[]{:S(2)}) copy-start(bf16[27,64,64]{2,1,0:T(8,128)(2,1)} %param.7) | copy-start | bytes 663556
  28.3 16.5 %collective-permute-start.14 = (bf16[64,4,1,32]{0,3,2,1:T(8,128)(2,1)S(1)}, bf16[64,4,1,32]{0,3,2,1:T(8,128)(2,1)S(1)}, u32[]{:S(2)}, u32[]{:S(2)}) collective-permute-start(bf16[64,4,1,32]{0,3,2,1:T(8,128)(2,1)S(1)} %get-tuple-element.18), channel_id=1, source_target_pairs={{0,1},{1,2},{2,3},{3,4},{4,5},{5,6},{6,7},{7,8},{8,9},{9,10},{10,1... | collective-permute-start | bytes 49160 | tf_op jit(solution)/shard_map/ppermute | solution.py:23
  31.5 13.3 %collective-permute-start.15 = (bf16[64,4,1,32]{0,3,2,1:T(8,128)(2,1)S(1)}, bf16[64,4,1,32]{0,3,2,1:T(8,128)(2,1)S(1)}, u32[]{:S(2)}, u32[]{:S(2)}) collective-permute-start(bf16[64,4,1,32]{0,3,2,1:T(8,128)(2,1)S(1)} %get-tuple-element.19), channel_id=1, source_target_pairs={{1,0},{2,1},{3,2},{4,3},{5,4},{6,5},{7,6},{8,7},{9,8},{10,9},{11,1... | collective-permute-start | bytes 49160 | tf_op jit(solution)/shard_map/ppermute | solution.py:24
  39.2 10.1 %collective-permute-start.4 = (bf16[64,1,4,16]{0,3,2,1:T(8,128)(2,1)S(1)}, bf16[64,1,4,16]{0,3,2,1:T(8,128)(2,1)S(1)}, u32[]{:S(2)}, u32[]{:S(2)}) collective-permute-start(bf16[64,1,4,16]{0,3,2,1:T(8,128)(2,1)S(1)} %fusion.798), channel_id=1, source_target_pairs={{0,16},{16,32},{32,48},{48,64},{64,80},{80,96},{96,112},{112,128},... | collective-permute-start | bytes 24584 | tf_op jit(solution)/shard_map/ppermute | solution.py:23
  43.5 5.8 %collective-permute-start.5 = (bf16[64,1,4,16]{0,3,2,1:T(8,128)(2,1)S(1)}, bf16[64,1,4,16]{0,3,2,1:T(8,128)(2,1)S(1)}, u32[]{:S(2)}, u32[]{:S(2)}) collective-permute-start(bf16[64,1,4,16]{0,3,2,1:T(8,128)(2,1)S(1)} %fusion.798), channel_id=1, source_target_pairs={{16,0},{32,16},{48,32},{64,48},{80,64},{96,80},{112,96},{128,112},... | collective-permute-start | bytes 24584 | tf_op jit(solution)/shard_map/ppermute | solution.py:24
  49.4 6.2 %collective-permute-start.7 = (bf16[64,3,1,16]{0,3,2,1:T(8,128)(2,1)S(1)}, bf16[64,3,1,16]{0,3,2,1:T(8,128)(2,1)S(1)}, u32[]{:S(2)}, u32[]{:S(2)}) collective-permute-start(bf16[64,3,1,16]{0,3,2,1:T(8,128)(2,1)S(1)} %get-tuple-element.46), channel_id=1, source_target_pairs={{1,0},{2,1},{3,2},{4,3},{5,4},{6,5},{7,6},{8,7},{9,8},{10,9},{11,1... | collective-permute-start | bytes 18440 | tf_op jit(solution)/shard_map/ppermute | solution.py:24
  51.3 4.7 %collective-permute-start.6 = (bf16[64,3,1,16]{0,3,2,1:T(8,128)(2,1)S(1)}, bf16[64,3,1,16]{0,3,2,1:T(8,128)(2,1)S(1)}, u32[]{:S(2)}, u32[]{:S(2)}) collective-permute-start(bf16[64,3,1,16]{0,3,2,1:T(8,128)(2,1)S(1)} %get-tuple-element.45), channel_id=1, source_target_pairs={{0,1},{1,2},{2,3},{3,4},{4,5},{5,6},{6,7},{7,8},{8,9},{9,10},{10,1... | collective-permute-start | bytes 18440 | tf_op jit(solution)/shard_map/ppermute | solution.py:23
  55.4 1.0 copy-start.4
  60.6 19.1 %collective-permute-start.16 = (bf16[128,1,4,16]{0,3,2,1:T(8,128)(2,1)S(1)}, bf16[128,1,4,16]{0,3,2,1:T(8,128)(2,1)S(1)}, u32[]{:S(2)}, u32[]{:S(2)}) collective-permute-start(bf16[128,1,4,16]{0,3,2,1:T(8,128)(2,1)S(1)} %bitcast.1895), channel_id=1, source_target_pairs={{0,16},{16,32},{32,48},{48,64},{64,80},{80,96},{96,112},{112,128},... | collective-permute-start | bytes 49160 | tf_op jit(solution)/shard_map/ppermute | solution.py:23
  65.1 14.5 %collective-permute-start.17 = (bf16[128,1,4,16]{0,3,2,1:T(8,128)(2,1)S(1)}, bf16[128,1,4,16]{0,3,2,1:T(8,128)(2,1)S(1)}, u32[]{:S(2)}, u32[]{:S(2)}) collective-permute-start(bf16[128,1,4,16]{0,3,2,1:T(8,128)(2,1)S(1)} %bitcast.1896), channel_id=1, source_target_pairs={{16,0},{32,16},{48,32},{64,48},{80,64},{96,80},{112,96},{128,112},... | collective-permute-start | bytes 49160 | tf_op jit(solution)/shard_map/ppermute | solution.py:24
  67.9 48.6 %collective-permute-start.8 = (bf16[128,1,8,32]{0,3,2,1:T(8,128)(2,1)S(1)}, bf16[128,1,8,32]{0,3,2,1:T(8,128)(2,1)S(1)}, u32[]{:S(2)}, u32[]{:S(2)}) collective-permute-start(bf16[128,1,8,32]{0,3,2,1:T(8,128)(2,1)S(1)} %get-tuple-element.20), channel_id=1, source_target_pairs={{0,16},{16,32},{32,48},{48,64},{64,80},{80,96},{96,112},{112,128},... | collective-permute-start | bytes 196616 | tf_op jit(solution)/shard_map/ppermute | solution.py:23
  73.4 43.1 %collective-permute-start.9 = (bf16[128,1,8,32]{0,3,2,1:T(8,128)(2,1)S(1)}, bf16[128,1,8,32]{0,3,2,1:T(8,128)(2,1)S(1)}, u32[]{:S(2)}, u32[]{:S(2)}) collective-permute-start(bf16[128,1,8,32]{0,3,2,1:T(8,128)(2,1)S(1)} %get-tuple-element.21), channel_id=1, source_target_pairs={{16,0},{32,16},{48,32},{64,48},{80,64},{96,80},{112,96},{128,112},... | collective-permute-start | bytes 196616 | tf_op jit(solution)/shard_map/ppermute | solution.py:24
  79.7 6.6 %collective-permute-start.18 = (bf16[128,3,1,16]{0,3,2,1:T(8,128)(2,1)S(1)}, bf16[128,3,1,16]{0,3,2,1:T(8,128)(2,1)S(1)}, u32[]{:S(2)}, u32[]{:S(2)}) collective-permute-start(bf16[128,3,1,16]{0,3,2,1:T(8,128)(2,1)S(1)} %get-tuple-element.43), channel_id=1, source_target_pairs={{0,1},{1,2},{2,3},{3,4},{4,5},{5,6},{6,7},{7,8},{8,9},{9,10},{10,1... | collective-permute-start | bytes 36872 | tf_op jit(solution)/shard_map/ppermute | solution.py:23
  84.1 5.0 %collective-permute-start.19 = (bf16[128,3,1,16]{0,3,2,1:T(8,128)(2,1)S(1)}, bf16[128,3,1,16]{0,3,2,1:T(8,128)(2,1)S(1)}, u32[]{:S(2)}, u32[]{:S(2)}) collective-permute-start(bf16[128,3,1,16]{0,3,2,1:T(8,128)(2,1)S(1)} %get-tuple-element.44), channel_id=1, source_target_pairs={{1,0},{2,1},{3,2},{4,3},{5,4},{6,5},{7,6},{8,7},{9,8},{10,9},{11,1... | collective-permute-start | bytes 36872 | tf_op jit(solution)/shard_map/ppermute | solution.py:24
  86.2 5.1 %copy-start.13 = (f32[27,128,64]{1,2,0:T(8,128)}, f32[27,128,64]{1,2,0:T(8,128)S(1)}, u32[]{:S(2)}) copy-start(f32[27,128,64]{1,2,0:T(8,128)S(1)} %fusion.105) | copy-start | bytes 2654212
  92.4 1.0 copy-start.18
  99.1 7.2 %collective-permute-start.20 = (bf16[64,1,8,32]{0,3,2,1:T(8,128)(2,1)S(1)}, bf16[64,1,8,32]{0,3,2,1:T(8,128)(2,1)S(1)}, u32[]{:S(2)}, u32[]{:S(2)}) collective-permute-start(bf16[64,1,8,32]{0,3,2,1:T(8,128)(2,1)S(1)} %get-tuple-element.24), channel_id=1, source_target_pairs={{0,16},{16,32},{32,48},{48,64},{64,80},{80,96},{96,112},{112,128},... | collective-permute-start | bytes 98312 | tf_op jit(solution)/shard_map/ppermute | solution.py:23
  104.6 6.1 %collective-permute-start.21 = (bf16[64,1,8,32]{0,3,2,1:T(8,128)(2,1)S(1)}, bf16[64,1,8,32]{0,3,2,1:T(8,128)(2,1)S(1)}, u32[]{:S(2)}, u32[]{:S(2)}) collective-permute-start(bf16[64,1,8,32]{0,3,2,1:T(8,128)(2,1)S(1)} %get-tuple-element.25), channel_id=1, source_target_pairs={{16,0},{32,16},{48,32},{64,48},{80,64},{96,80},{112,96},{128,112},... | collective-permute-start | bytes 98312 | tf_op jit(solution)/shard_map/ppermute | solution.py:24
  106.3 15.3 %copy-start.17 = (f32[27,64,64]{2,1,0:T(8,128)}, f32[27,64,64]{2,1,0:T(8,128)S(1)}, u32[]{:S(2)}) copy-start(f32[27,64,64]{2,1,0:T(8,128)S(1)} %fusion.132) | copy-start | bytes 1327108
  110.7 10.9 %collective-permute-start.23 = (bf16[64,4,1,32]{0,3,2,1:T(8,128)(2,1)S(1)}, bf16[64,4,1,32]{0,3,2,1:T(8,128)(2,1)S(1)}, u32[]{:S(2)}, u32[]{:S(2)}) collective-permute-start(bf16[64,4,1,32]{0,3,2,1:T(8,128)(2,1)S(1)} %get-tuple-element.17), channel_id=1, source_target_pairs={{1,0},{2,1},{3,2},{4,3},{5,4},{6,5},{7,6},{8,7},{9,8},{10,9},{11,1... | collective-permute-start | bytes 49160 | tf_op jit(solution)/shard_map/ppermute | solution.py:24
  112.7 9.0 %collective-permute-start.22 = (bf16[64,4,1,32]{0,3,2,1:T(8,128)(2,1)S(1)}, bf16[64,4,1,32]{0,3,2,1:T(8,128)(2,1)S(1)}, u32[]{:S(2)}, u32[]{:S(2)}) collective-permute-start(bf16[64,4,1,32]{0,3,2,1:T(8,128)(2,1)S(1)} %get-tuple-element.16), channel_id=1, source_target_pairs={{0,1},{1,2},{2,3},{3,4},{4,5},{5,6},{6,7},{7,8},{8,9},{9,10},{10,1... | collective-permute-start | bytes 49160 | tf_op jit(solution)/shard_map/ppermute | solution.py:23
  116.6 10.2 %collective-permute-start.10 = (bf16[128,4,1,32]{0,3,2,1:T(8,128)(2,1)S(1)}, bf16[128,4,1,32]{0,3,2,1:T(8,128)(2,1)S(1)}, u32[]{:S(2)}, u32[]{:S(2)}) collective-permute-start(bf16[128,4,1,32]{0,3,2,1:T(8,128)(2,1)S(1)} %get-tuple-element.14), channel_id=1, source_target_pairs={{0,1},{1,2},{2,3},{3,4},{4,5},{5,6},{6,7},{7,8},{8,9},{9,10},{10,1... | collective-permute-start | bytes 98312 | tf_op jit(solution)/shard_map/ppermute | solution.py:23
  119.3 7.6 %collective-permute-start.11 = (bf16[128,4,1,32]{0,3,2,1:T(8,128)(2,1)S(1)}, bf16[128,4,1,32]{0,3,2,1:T(8,128)(2,1)S(1)}, u32[]{:S(2)}, u32[]{:S(2)}) collective-permute-start(bf16[128,4,1,32]{0,3,2,1:T(8,128)(2,1)S(1)} %get-tuple-element.15), channel_id=1, source_target_pairs={{1,0},{2,1},{3,2},{4,3},{5,4},{6,5},{7,6},{8,7},{9,8},{10,9},{11,1... | collective-permute-start | bytes 98312 | tf_op jit(solution)/shard_map/ppermute | solution.py:24
  140.7 0.9 copy-start.14
  142.3 1.0 copy-start.8
  142.3 1.0 copy-start.9
  142.3 1.1 copy-start.10
  142.3 1.2 copy-start.11
  142.3 1.2 copy-start.12
  142.5 1.2 copy-start.6
  142.5 1.2 copy-start.7
  438.9 2.3 copy-start.16
  441.1 1.1 copy-start.19
  441.1 1.8 copy-start.15
Sparse Core Ops, SparseCore 0:
  142.2 296.6 all-reduce.8
where the time goes:
time: 453 us; the launch traced here: 451 us
  waiting for transfers between devices  302 us (67%)
  starting transfers between devices  71.3 us (16%)
  matrix products  51.9 us (11%)
  between operations  15.5 us (3%)
  local copies, waits for them, and re-layouts  8.66 us (2%)
    psum x1, waiting for transfers between devices, per_device(): lax.psum((decoder_gradient, lift_gradient, encoder_gradient), ('gx', 'gy'))  294 us
    ppermute x12, starting transfers between devices, extended(): before = lax.ppermute(last, axis, up)  51.1 us
    ppermute x12, starting transfers between devices, extended(): after = lax.ppermute(initial, axis, down)  20.2 us
    dot_general x80, matrix products, apply_taps(): jnp.einsum('oc,cxyz->oxyz', weight[tap_index], window, preferred_element_...  19.2 us
    dot_general x81, matrix products, tap_gradients(): jnp.einsum('oxyz,cxyz->oc', grad_out, window, preferred_element_type=jnp....  17.1 us
    dot_general x80, matrix products, apply_adjoint(): jnp.einsum('oc,oxyz->cxyz', weight[tap_index], window, preferred_element_...  13.1 us
  transfers between devices with their start and end apart: 25, of which 4 were waited for; matrix products, arithmetic and copies ran while one was open for 8% of the time, Pallas kernels for 0%

commit v1 on v0

v1 whole, which is shorter than its diff:
```python
import math

import jax
import jax.numpy as jnp
from jax import lax
from jax.experimental import pallas as pl
from jax.experimental.pallas import tpu as pltpu
from jax.sharding import Mesh, PartitionSpec as P

F32, BF16 = jnp.float32, jnp.bfloat16
LINK = BF16
GX, GY = ("gx",), ("gz", "gc")
TAPS9 = tuple((a, b) for a in range(3) for b in range(3))


def shifted(piece, axes, step):
    size = math.prod(lax.axis_size(axis) for axis in axes)
    pairs = [(i, i + step) for i in range(size) if 0 <= i + step < size]
    return lax.ppermute(piece, axes, pairs)


def swapped(low, high, axes):
    return shifted(high, axes, 1), shifted(low, axes, -1)


def partner(piece):
    return lax.ppermute(piece, "gc", [(0, 1), (1, 0)])


def call(kernel, outs, scratch, operands, spaces=(), flops=10**6):
    return pl.pallas_call(
        kernel,
        out_shape=[jax.ShapeDtypeStruct(s, d) for s, d in outs],
        in_specs=[
            pl.BlockSpec(memory_space=dict(spaces).get(i, pltpu.VMEM)) for i in range(len(operands))
        ],
        out_specs=[pl.BlockSpec(memory_space=pltpu.VMEM)] * len(outs),
        scratch_shapes=[s if d is None else pltpu.VMEM(s, d) for s, d in scratch],
        compiler_params=pltpu.CompilerParams(vmem_limit_bytes=40 * 2**20),
        cost_estimate=pl.CostEstimate(flops=flops, bytes_accessed=10**4, transcendentals=0),
    )(*operands)


def nn(a, b):
    return lax.dot_general(a, b, (((1,), (0,)), ((), ())), preferred_element_type=F32)


def nt(a, b):
    return lax.dot_general(a, b, (((1,), (1,)), ((), ())), preferred_element_type=F32)


def tn(a, b):
    return lax.dot_general(a, b, (((0,), (0,)), ((), ())), preferred_element_type=F32)


def nn_weight(ref):
    rows = [jnp.concatenate([ref[3 * ab + c] for c in range(3)], -1) for ab in range(9)]
    return jnp.concatenate(rows, 0)


def nt_weight(ref):
    rows = [jnp.concatenate([ref[3 * ab + c] for ab in range(9)], -1) for c in range(3)]
    return jnp.concatenate(rows, 0)


def stacked(ref, x, nx, ny, adjoint, y=0):
    pieces = []
    for a, b in TAPS9:
        i, j = (x + 2 - a, y + 2 - b) if adjoint else (x + a, y + b)
        piece = ref[i : i + nx, j : j + ny]
        pieces.append(piece.reshape(nx * ny * piece.shape[2], piece.shape[3]))
    return jnp.concatenate(pieces, -1)


def zshift(value, step, depth):
    rows = value.shape[0]
    z = lax.broadcasted_iota(jnp.int32, value.shape, 0) & (depth - 1)
    moved = pltpu.roll(value, step % rows, 0)
    return jnp.where(z == (0 if step > 0 else depth - 1), 0.0, moved)


def combined(parts, depth, adjoint):
    ch = parts.shape[1] // 3
    step = -1 if adjoint else 1
    return (
        zshift(parts[:, :ch], step, depth)
        + parts[:, ch : 2 * ch]
        + zshift(parts[:, 2 * ch :], -step, depth)
    )


def ztaps(value, depth, adjoint):
    step = -1 if adjoint else 1
    return jnp.concatenate(
        [
            zshift(value, step, depth).astype(BF16),
            value.astype(BF16),
            zshift(value, -step, depth).astype(BF16),
        ],
        -1,
    )


def assemble(ext, own, ylo, yhi, xlo, xhi):
    size_x, size_y = own.shape[:2]
    ext[1 : 1 + size_x, 1 : 1 + size_y] = own
    ext[1 : 1 + size_x, 0:1] = ylo
    ext[1 : 1 + size_x, 1 + size_y : 2 + size_y] = yhi
    ext[0:1] = xlo
    ext[1 + size_x : 2 + size_x] = xhi


def fetched(sems, *pairs):
    copies = [pltpu.make_async_copy(a, b, sems.at[k]) for k, (a, b) in enumerate(pairs)]
    for copy in copies:
        copy.start()
    for copy in copies:
        copy.wait()


def stack_kernel(first_ref, enc_ref, low_ref, dec_ref, lift_ref, *refs):
    outs, lift_out, (enc, low, dec, sems) = refs[:6], refs[6], refs[7:]
    fetched(sems, (enc_ref, enc), (low_ref, low), (dec_ref, dec), (lift_ref, lift_out))
    for ref, forward, backward in (
        (enc, nt_weight, nn_weight),
        (low, nn_weight, nt_weight),
        (dec, nt_weight, nn_weight),
    ):
        outs[0][...] = forward(ref)
        outs[1][...] = backward(ref)
        outs = outs[2:]


def pack_x_kernel(f_any, c_any, f_ref, c_ref, lo_ref, hi_ref, lo2_ref, hi2_ref, sems):
    fetched(sems, (f_any, f_ref), (c_any, c_ref))
    paired = [jnp.concatenate([f_ref[x, 0:4], f_ref[x, 4:8]], -1) for x in range(2)]
    for x, out, out2 in ((0, lo_ref, lo2_ref), (1, hi_ref, hi2_ref)):
        out[0:8] = jnp.concatenate([f_ref[x], c_ref[x]], -1)
        out[8:12] = paired[1 - x]
        out2[...] = paired[x]


def pack_y_kernel(f_ref, c_ref, xlo, xhi, xlo2, xhi2, lo_ref, hi_ref):
    for first, out in ((0, lo_ref), (5, hi_ref)):
        at = slice(first, first + 3)
        out[0] = xlo[at]
        for x in range(2):
            out[1 + x] = jnp.concatenate([f_ref[x, at], c_ref[x, at]], -1)
        out[3] = xhi[at]
        for k, far, near in ((4, xlo2[...], xlo[8:12]), (5, xhi[8:12], xhi2[...])):
            pair = [jnp.concatenate([v[..., :64], v[..., 64:]], 0)[at] for v in (far, near)]
            out[k] = jnp.concatenate(pair, -1)


def encode_kernel(
    f_ref, ylo, yhi, xlo, xhi, xlo2, xhi2, inside, w_ref, fx_ref, enc_ref, slope_ref, pool_ref, tmp
):
    fx_ref[3:5, 3:11] = f_ref[...]
    fx_ref[2, 3:11] = xlo[0:8, :, :64]
    fx_ref[5, 3:11] = xhi[0:8, :, :64]
    for x, ref, first in ((1, xlo, 8), (6, xhi, 8), (0, xlo2, 0), (7, xhi2, 0)):
        fx_ref[x, 3:7] = ref[first : first + 4, :, :64]
        fx_ref[x, 7:11] = ref[first : first + 4, :, 64:]
    for y, ref in ((0, ylo), (11, yhi)):
        at = slice(y, y + 3)
        fx_ref[2:6, at] = ref[0:4, :, :, :64]
        for x, k in ((0, 4), (6, 5)):
            fx_ref[x, at] = ref[k, :, :, :64]
            fx_ref[x + 1, at] = ref[k, :, :, 64:]
    weight = w_ref[...]
    for x in range(6):
        pre = combined(nt(stacked(fx_ref, x, 1, 12, False), weight), 32, False)
        sigma = jax.nn.sigmoid(pre)
        enc = (pre * sigma).astype(BF16)
        if x in (2, 3):
            slope = sigma * (1.0 + pre * (1.0 - sigma))
            slope_ref[pl.ds((x - 2) * 256, 256), :] = slope[64:320]
            enc_ref[x - 2] = enc[64:320].reshape(8, 32, 64)
        wide = enc.astype(F32).reshape(6, 2, 32, 64)
        part = wide[:, 0] + wide[:, 1]
        if x % 2 == 0:
            held = part
            continue
        tmp[...] = (held + part).reshape(192, 64)
        pooled = tmp[pl.ds(0, 96, stride=2), :] + tmp[pl.ds(1, 96, stride=2), :]
        pooled = pooled * (0.125 if x == 3 else 0.125 * inside[0 if x == 1 else 1])
        pool_ref[x // 2, 1:5] = pooled[16:80].astype(BF16).reshape(4, 16, 64)
        pool_ref[x // 2, 0] = (pooled[0:16] * inside[2]).astype(BF16)
        pool_ref[x // 2, 5] = (pooled[80:96] * inside[3]).astype(BF16)


def joined_grad_kernel(c_ref, *refs):
    (ylo, yhi, xlo, xhi), (w_ref, lift_ref, enc_ref) = refs[:4], refs[4:7]
    cx_ref, jg_ref, kids_ref, adj_ref, dge_ref, tmp = refs[7:]
    cx_ref[1:3, 1:9] = c_ref[...]
    cx_ref[0, 1:9] = xlo[0:8, :, 64:]
    cx_ref[3, 1:9] = xhi[0:8, :, 64:]
    cx_ref[:, 0] = ylo[0:4, 2, :, 64:]
    cx_ref[:, 9] = yhi[0:4, 0, :, 64:]
    weight = w_ref[...]
    for x in range(2):
        grad = combined(nn(stacked(cx_ref, x, 1, 8, True), weight), 32, True)
        grad = grad.astype(BF16)
        jg_ref[pl.ds(x * 256, 256), :] = grad[:, :64]
        tmp[pl.ds(x * 256, 256), :] = grad.astype(F32)
    kids = []
    for p in range(2):
        for q in range(2):
            for r in range(2):
                rows = [
                    tmp[pl.ds(p * 256 + (2 * j + q) * 32 + r, 16, stride=2), :] for j in range(4)
                ]
                kids.append(jnp.concatenate(rows, 0)[:, 64:])
    kids = jnp.concatenate(kids, -1).astype(BF16)
    kids_ref[...] = kids
    adj_ref[...] = nn(kids, lift_ref[...].reshape(512, 128))
    enc = enc_ref[...].reshape(512, 64).astype(F32)
    dge_ref[...] = tn(stacked(cx_ref, 0, 2, 8, True), ztaps(enc, 32, False))


def lower_kernel(px, core, w_ref, lift_ref, adj_ref, kids_ref, cx_ref, dge_ref, enc_ref, *refs):
    la_ref, lg_ref, lifted_ref, keep_ref, send_ref, lo_ref, hi_ref, tmp, halves = refs
    chunk = keep_ref.shape[1]

    def put(row, block):
        at = pl.ds(row % chunk, block.shape[0])
        halves[row // chunk % 2, row // (2 * chunk), at, :] = block.astype(LINK)

    pk = stacked(px, 0, 1, 4, False)
    pre = combined(nn(pk, w_ref[...]), 16, False)
    sigma = jax.nn.sigmoid(pre)
    la = (pre * sigma).astype(BF16)
    lg = (adj_ref[...] * (sigma * (1.0 + pre * (1.0 - sigma)))).astype(BF16)
    la_ref[...] = la.reshape(1, 4, 16, 128)
    lg_ref[...] = lg.reshape(1, 4, 16, 128)
    for j, y, msg in ((0, 0, lo_ref), (3, 7, hi_ref)):
        rows = slice(16 * j, 16 * j + 16)
        msg[0:16] = la[rows]
        msg[16:32] = lg[rows]
        msg[32:64] = jnp.concatenate([enc_ref[0, y], enc_ref[1, y]], -1)
    fine = nt(la, lift_ref[...].reshape(512, 128)).astype(BF16).astype(F32)
    for p in range(2):
        for q in range(2):
            for r in range(2):
                k = 4 * p + 2 * q + r
                for j in range(4):
                    tmp[pl.ds(p * 256 + (2 * j + q) * 32 + r, 16, stride=2), :] = fine[
                        16 * j : 16 * j + 16, 64 * k : 64 * k + 64
                    ]
    lifted = tmp[...]
    lifted_ref[...] = lifted.astype(BF16).reshape(2, 8, 32, 64)
    dgl = tn(stacked(cx_ref, 0, 2, 8, True), ztaps(lifted, 32, False))
    for ab in range(9):
        for c in range(3):
            cols = slice(64 * c, 64 * c + 64)
            rows = slice(64 * ab, 64 * ab + 64)
            both = jnp.concatenate([dge_ref[rows, cols], dgl[rows, cols]], -1)
            put((3 * ab + c) * 64, both)
    low = tn(pk, ztaps(lg.astype(F32), 16, True))
    for ab in range(9):
        for c in range(3):
            block = low[64 * ab : 64 * ab + 64, 128 * c : 128 * c + 128]
            put(1728 + (3 * ab + c) * 64, block)
    lift = tn(kids_ref[...], la)
    for k in range(8):
        put(3456 + 64 * k, lift[64 * k : 64 * k + 64])
    for row in (3968, 4032):
        put(row, jnp.zeros((64, 128), F32))
    mine = core[0]
    keep_ref[...] = halves[mine]
    send_ref[...] = halves[1 - mine]


def add_kernel(a_ref, b_ref, out_ref):
    out_ref[...] = (a_ref[...].astype(F32) + b_ref[...].astype(F32)).astype(LINK)


def joined_x_kernel(la_ref, lg_ref, enc_ref, ylo_ref, yhi_ref, lo_ref, hi_ref):
    for x, out in ((0, lo_ref), (1, hi_ref)):
        cols = slice(64 * x, 64 * x + 64)
        out[0:16] = ylo_ref[0:16]
        out[16:80] = la_ref[...].reshape(64, 128)
        out[80:96] = yhi_ref[0:16]
        out[96:112] = ylo_ref[16:32]
        out[112:176] = lg_ref[...].reshape(64, 128)
        out[176:192] = yhi_ref[16:32]
        enc = enc_ref[x].reshape(256, 64)
        first = jnp.concatenate([ylo_ref[32:64, cols], enc[:128]], 0)
        second = jnp.concatenate([enc[128:], yhi_ref[32:64, cols]], 0)
        out[192:352] = jnp.concatenate([first, second], -1)


def edge_y_kernel(eg_ref, lo_ref, hi_ref):
    lo_ref[...] = jnp.concatenate([eg_ref[0, 0], eg_ref[1, 0]], -1)
    hi_ref[...] = jnp.concatenate([eg_ref[0, 7], eg_ref[1, 7]], -1)


def edge_x_kernel(eg_ref, ylo_ref, yhi_ref, lo_ref, hi_ref):
    for x, out in ((0, lo_ref), (1, hi_ref)):
        cols = slice(64 * x, 64 * x + 64)
        eg = eg_ref[x].reshape(256, 64)
        first = jnp.concatenate([ylo_ref[:, cols], eg[:128]], 0)
        second = jnp.concatenate([eg[128:], yhi_ref[:, cols]], 0)
        out[...] = jnp.concatenate([first, second], -1)


def column(rows):
    return jnp.stack([rows[:, :64], rows[:, 64:]], 0).reshape(2, 1, 32, 64)


def plane(rows):
    return jnp.concatenate([rows[:, :64], rows[:, 64:]], 0).reshape(1, 10, 32, 64)


def encoder_grad_kernel(lg_ref, *refs):
    (ylo, yhi, xlo, xhi), (w_ref, slope_ref, jg_ref, fx_ref) = refs[:4], refs[4:8]
    eg_ref, grads_ref, lo_ref, hi_ref, lx, tmp = refs[8:]
    sides = [h[16:32].reshape(1, 1, 16, 128) for h in (ylo, yhi)]
    sides += [h[96:192].reshape(1, 6, 16, 128) for h in (xlo, xhi)]
    assemble(lx, lg_ref[...], *sides)
    pg = combined(nt(stacked(lx, 0, 1, 4, True), w_ref[...]), 16, True)
    pg = pg.astype(BF16).astype(F32) * 0.125
    tmp[pl.ds(0, 64, stride=2), :] = pg
    tmp[pl.ds(1, 64, stride=2), :] = pg
    wide = tmp[...].reshape(1, 4, 1, 32, 64)
    wide = jnp.broadcast_to(wide, (2, 4, 2, 32, 64)).reshape(512, 64)
    eg = ((jg_ref[...].astype(F32) + wide) * slope_ref[...]).astype(BF16)
    eg_ref[...] = eg.reshape(2, 8, 32, 64)
    edge_y_kernel(eg_ref, lo_ref, hi_ref)
    grad = tn(ztaps(eg.astype(F32), 32, True), stacked(fx_ref, 2, 2, 8, False, 2))
    for ab in range(9):
        for c in range(3):
            block = grad[64 * c : 64 * c + 64, 64 * ab : 64 * ab + 64]
            block = jnp.concatenate([block[:32], block[32:]], -1)
            grads_ref[pl.ds((3 * ab + c) * 32, 32), :] = block.astype(LINK)
    grads_ref[pl.ds(864, 160), :] = jnp.zeros((160, 128), LINK)


def decode_kernel(enc_ref, lifted_ref, *refs):
    (ylo, yhi, xlo, xhi), (lift_ref, w_ref, out_ref, jx, ty, tx) = refs[:4], refs[4:]
    sides = []
    for q, h in ((1, ylo), (0, yhi)):
        for p in range(2):
            for r in range(2):
                fine = nt(h[0:16], lift_ref[4 * p + 2 * q + r]).astype(BF16).astype(F32)
                ty[pl.ds(32 * p + r, 16, stride=2), :] = fine
        lifted = ty[...].astype(BF16).reshape(2, 1, 32, 64)
        sides.append(jnp.concatenate([column(h[32:64]), lifted], -1))
    for p, h in ((1, xlo), (0, xhi)):
        for q in range(2):
            for r in range(2):
                fine = nt(h[0:96], lift_ref[4 * p + 2 * q + r]).astype(BF16).astype(F32)
                for j in range(6):
                    y = 2 * j + q - 1
                    if 0 <= y < 10:
                        tx[pl.ds(32 * y + r, 16, stride=2), :] = fine[16 * j : 16 * j + 16]
        lifted = tx[...].astype(BF16).reshape(1, 10, 32, 64)
        sides.append(jnp.concatenate([plane(h[192:352]), lifted], -1))
    assemble(jx, jnp.concatenate([enc_ref[...], lifted_ref[...]], -1), *sides)
    weight = w_ref[...]
    for x in range(2):
        out = combined(nt(stacked(jx, x, 1, 8, False), weight), 32, False)
        out_ref[x] = out.astype(BF16).reshape(8, 32, 64)


def input_grad_kernel(eg_ref, ylo, yhi, xlo, xhi, w_ref, out_ref, ex):
    sides = [column(ylo[...]), column(yhi[...]), plane(xlo[...]), plane(xhi[...])]
    assemble(ex, eg_ref[...], *sides)
    weight = w_ref[...]
    for x in range(2):
        out = combined(nn(stacked(ex, x, 1, 8, True), weight), 32, True)
        out_ref[x] = out.astype(BF16).reshape(8, 32, 64)


def sum_x_kernel(grads_ref, enc_ref, out_ref):
    first = 0
    for ref in (grads_ref, enc_ref):
        rows = ref.shape[1]
        total = ref[0].astype(F32)
        for k in range(1, ref.shape[0]):
            total = total + ref[k].astype(F32)
        total = total.astype(LINK)
        for k in range(out_ref.shape[0]):
            out_ref[k, first : first + rows] = total
        first += rows


def sum_z_kernel(parts_ref, out_ref):
    total = parts_ref[0].astype(F32)
    for k in range(1, parts_ref.shape[0]):
        total = total + parts_ref[k].astype(F32)
    total = total.astype(LINK)
    for k in range(out_ref.shape[0]):
        out_ref[k] = total


def widen_kernel(core, own_ref, other_ref, encoder_ref, decoder_ref, lower_ref, lift_ref):
    own, other = own_ref[...].astype(F32), other_ref[...].astype(F32)
    first = core[0] == 0
    both = jnp.stack([jnp.where(first, own, other), jnp.where(first, other, own)], 1)
    chunk = own.shape[1] // 5 * 4
    sums = both[:, :, :chunk].reshape(4096, 128)
    decoder_ref[...] = sums[0:1728].reshape(27, 64, 128)
    lower_ref[...] = sums[1728:3456].reshape(27, 64, 128)
    lift_ref[...] = sums[3456:3968].reshape(8, 64, 128)
    wide = both[:, :, chunk:].reshape(1024, 128)[:864].reshape(27, 32, 128)
    encoder_ref[:, 0:32, :] = wide[..., :64]
    encoder_ref[:, 32:64, :] = wide[..., 64:]


def per_device(features, encoder_weight, lower_weight, lift_weight, decoder_weight, cotangent):
    f = jnp.transpose(features, (1, 2, 3, 0))
    c = jnp.transpose(cotangent, (1, 2, 3, 0))
    lower_t = jnp.transpose(lower_weight, (0, 2, 1))
    brick, coarse = (2, 8, 32, 64), (1, 4, 16, 128)

    size_x, size_z = lax.axis_size("gx"), lax.axis_size("gz")
    at_x, at_y = lax.axis_index("gx"), lax.axis_index(GY)
    inside = jnp.stack([at_x > 0, at_x < size_x - 1, at_y > 0, at_y < 2 * size_z - 1]).astype(F32)
    core = lax.axis_index("gc").reshape(1)

    f, c, lo, hi, lo2, hi2 = call(
        pack_x_kernel,
        [(brick, BF16)] * 2 + [((12, 32, 128), BF16)] * 2 + [((4, 32, 128), BF16)] * 2,
        [(pltpu.SemaphoreType.DMA((2,)), None)],
        [f, c],
        spaces={0: pltpu.HBM, 1: pltpu.HBM},
    )
    x_halo = swapped(lo, hi, GX)
    far_halo = [shifted(hi2, GX, 2), shifted(lo2, GX, -2)]
    edges = call(pack_y_kernel, [((6, 3, 32, 128), BF16)] * 2, [], [f, c, *x_halo, *far_halo])
    y_halo = swapped(*edges, GY)
    enc_fwd, enc_bwd, low_fwd, low_bwd, dec_fwd, dec_bwd, lift = call(
        stack_kernel,
        [
            ((192, 576), BF16),
            ((576, 192), BF16),
            ((576, 384), BF16),
            ((192, 1152), BF16),
            ((192, 1152), BF16),
            ((576, 384), BF16),
            ((8, 64, 128), BF16),
        ],
        [
            ((27, 64, 64), BF16),
            ((27, 64, 128), BF16),
            ((27, 64, 128), BF16),
            (pltpu.SemaphoreType.DMA((4,)), None),
        ],
        [edges[0], encoder_weight, lower_t, decoder_weight, lift_weight],
        spaces={k: pltpu.HBM for k in range(5)},
        flops=2 * 10**9,
    )
    fx, encoded, slope, pooled = call(
        encode_kernel,
        [((8, 14, 32, 64), BF16), (brick, BF16), ((512, 64), F32), ((3, 6, 16, 64), BF16)],
        [((192, 64), F32)],
        [f, *y_halo, *x_halo, *far_halo, inside, enc_fwd],
        spaces={7: pltpu.SMEM},
    )
    cx, jg, kids, adj, dge = call(
        joined_grad_kernel,
        [
            ((4, 10, 32, 64), BF16),
            ((512, 64), BF16),
            ((64, 512), BF16),
            ((64, 128), F32),
            ((576, 192), F32),
        ],
        [((512, 128), F32)],
        [c, *y_halo, *x_halo, dec_bwd, lift, encoded],
    )
    half = (size_x, 2048 // size_x, 128)
    la, lg, lifted, keep, send, *edges = call(
        lower_kernel,
        [(coarse, BF16), (coarse, BF16), (brick, BF16), (half, LINK), (half, LINK)]
        + [((64, 128), BF16)] * 2,
        [((512, 64), F32), ((2,) + half, LINK)],
        [pooled, core, low_fwd, lift, adj, kids, cx, dge, encoded],
        spaces={1: pltpu.SMEM},
    )
    (grads,) = call(add_kernel, [(half, LINK)], [], [keep, partner(send)])
    grads = lax.all_to_all(grads, "gx", 0, 0)
    y_halo = swapped(*edges, GY)
    edges = call(joined_x_kernel, [((352, 128), BF16)] * 2, [], [la, lg, encoded, *y_halo])
    halo = [*y_halo, *swapped(*edges, GX)]
    eg, enc_grads, *edges = call(
        encoder_grad_kernel,
        [(brick, BF16), ((1024, 128), LINK)] + [((32, 128), BF16)] * 2,
        [((3, 6, 16, 128), BF16), ((128, 64), F32)],
        [lg, *halo, low_bwd, slope, jg, fx],
    )
    enc_grads, grads = lax.optimization_barrier((enc_grads, grads))
    enc_grads = lax.all_to_all(enc_grads.reshape(2 * size_x, -1, 128), ("gx", "gc"), 0, 0)
    rows = 2560 // size_x
    (sums,) = call(sum_x_kernel, [((size_z, rows, 128), LINK)], [], [grads, enc_grads])
    sums = lax.all_to_all(sums, "gz", 0, 0)
    (sums,) = call(sum_z_kernel, [((size_x, rows, 128), LINK)], [], [sums])
    sums = lax.all_to_all(sums, "gx", 0, 0)
    encoder_gradient, decoder_gradient, lower_gradient, lift_gradient = call(
        widen_kernel,
        [((27, 64, 64), F32), ((27, 64, 128), F32), ((27, 64, 128), F32), ((8, 64, 128), F32)],
        [],
        [core, sums, partner(sums)],
        spaces={0: pltpu.SMEM},
    )
    y_halo = swapped(*edges, GY)
    edges = call(edge_x_kernel, [((160, 128), BF16)] * 2, [], [eg, *y_halo])
    eg_halo = [*y_halo, *swapped(*edges, GX)]
    (decoded,) = call(
        decode_kernel,
        [(brick, BF16)],
        [((4, 10, 32, 128), BF16), ((64, 64), F32), ((320, 64), F32)],
        [encoded, lifted, *halo, lift, dec_fwd],
    )
    (input_grad,) = call(
        input_grad_kernel,
        [(brick, BF16)],
        [((4, 10, 32, 64), BF16)],
        [eg, *eg_halo, enc_bwd],
    )
    return (
        jnp.transpose(decoded, (3, 0, 1, 2)),
        jnp.transpose(input_grad, (3, 0, 1, 2)),
        encoder_gradient,
        jnp.transpose(lower_gradient, (0, 2, 1)),
        lift_gradient,
        decoder_gradient,
    )


def solution(mesh):
    size_x, size_y = mesh.devices.shape
    chips = Mesh(mesh.devices.reshape(size_x, size_y // 2, 2), ("gx", "gz", "gc"))
    field = P(None, "gx", ("gz", "gc"), None)
    return jax.shard_map(
        per_device,
        mesh=chips,
        in_specs=(field, P(), P(), P(), P(), field),
        out_specs=(field, field, P(), P(), P(), P()),
        check_vma=False,
    )
```

time: 453 us -> 161 us (0.36)
  waiting for transfers between devices: 302 us -> 20.6 us
  blocking collectives: 0 us -> 60.6 us
  matrix products: 51.9 us -> 0 us
  between operations: 15.5 us -> 0.95 us
  Pallas kernels: 0 us -> 13.7 us
  starting transfers between devices: 71.3 us -> 59.5 us
    psum x1 -> x0, waiting for transfers between devices: 294 us -> none  [per_device(): lax.psum((decoder_gradient, lift_gradient, encoder_gradient), ('gx', 'gy'))]
    all_to_all x0 -> x3, blocking collectives: none -> 60.6 us  [the longest x1 22 us: per_device(): lax.all_to_all(enc_grads.reshape(2 * size_x, -1, 128), ('gx', 'gc'), 0, 0)]
    dot_general x244 -> x0, matrix products: 50.8 us -> none  [the longest x80 19.2 us: apply_taps(): jnp.einsum('oc,cxyz->oxyz', weight[tap_index], window, preferred_element_...]
    ppermute x24 -> x16, starting transfers between devices: 71.3 us -> 48.9 us  [the longest x14 39.3 us: shifted(): return lax.ppermute(piece, axes, pairs)]
    pallas_call x0 -> x15, Pallas kernels: none -> 13.7 us  [call(): pl.pallas_call(kernel, out_shape=[jax.ShapeDtypeStruct(s, d) for s, d in...]
    ppermute x24 -> x16, waiting for transfers between devices: 7.8 us -> 20.6 us  [the longest x14 18.7 us: shifted(): return lax.ppermute(piece, axes, pairs)]
    all_to_all x0 -> x1, starting transfers between devices: none -> 10.6 us  [per_device(): grads = lax.all_to_all(grads, 'gx', 0, 0)]
  transfers between devices with their start and end apart: 25 -> 17, of which waited for: 4 -> 9; matrix products, arithmetic and copies ran while one was open for 8% -> 0% of each run, Pallas kernels for 0% -> 3%
where the time goes in v1:
time: 161 us
  blocking collectives  60.6 us (38%)
  starting transfers between devices  59.5 us (37%)
  waiting for transfers between devices  20.6 us (13%)
  Pallas kernels  13.7 us (9%)
  local copies, waits for them, and re-layouts  5.2 us (3%)
    ppermute x14, starting transfers between devices, shifted(): return lax.ppermute(piece, axes, pairs)  39.3 us
    all_to_all x1, blocking collectives, per_device(): lax.all_to_all(enc_grads.reshape(2 * size_x, -1, 128), ('gx', 'gc'), 0, 0)  22 us
    all_to_all x1, blocking collectives, per_device(): sums = lax.all_to_all(sums, 'gx', 0, 0)  20.4 us
    ppermute x14, waiting for transfers between devices, shifted(): return lax.ppermute(piece, axes, pairs)  18.7 us
    all_to_all x1, blocking collectives, per_device(): sums = lax.all_to_all(sums, 'gz', 0, 0)  18.2 us
    pallas_call x15, Pallas kernels, call(): pl.pallas_call(kernel, out_shape=[jax.ShapeDtypeStruct(s, d) for s, d in...  13.7 us
    all_to_all x1, starting transfers between devices, per_device(): grads = lax.all_to_all(grads, 'gx', 0, 0)  10.6 us
    ppermute x2, starting transfers between devices, partner(): return lax.ppermute(piece, 'gc', [(0, 1), (1, 0)])  9.55 us
  transfers between devices with their start and end apart: 17, of which 9 were waited for; matrix products, arithmetic and copies ran while one was open for 0% of the time, Pallas kernels for 3%

profile of v1, /device:TPU:1, one launch (start us, length us, event | category | flops | bytes accessed | tf_op | source)
XLA Modules:
  0.0 160.6 jit_solution(2297094281084136543)
XLA Ops:
  0.6 0.9 copy-done.3
  1.5 0.9 copy-done.4
  2.4 0.4 shard_map.109
  2.9 5.0 %collective-permute-start.2 = (bf16[4,32,128]{2,1,0:T(8,128)(2,1)S(1)}, bf16[4,32,128]{2,1,0:T(8,128)(2,1)S(1)}, u32[]{:S(2)}, u32[]{:S(2)}) collective-permute-start(bf16[4,32,128]{2,1,0:T(8,128)(2,1)S(1)} %get-tuple-element.55), channel_id=1, source_target_pairs={{0,32},{16,48},{32,64},{48,80},{64,96},{80,112},{96,128},{112,144}... | collective-permute-start | bytes 98312 | tf_op jit(solution)/shard_map/ppermute | solution.py:19
  8.0 1.3 collective-permute-start.3
  9.3 3.2 %collective-permute-start = (bf16[12,32,128]{2,1,0:T(8,128)(2,1)S(1)}, bf16[12,32,128]{2,1,0:T(8,128)(2,1)S(1)}, u32[]{:S(2)}, u32[]{:S(2)}) collective-permute-start(bf16[12,32,128]{2,1,0:T(8,128)(2,1)S(1)} %get-tuple-element.53), channel_id=1, source_target_pairs={{0,16},{16,32},{32,48},{48,64},{64,80},{80,96},{96,112},{112,128},... | collective-permute-start | bytes 294920 | tf_op jit(solution)/shard_map/ppermute | solution.py:19
  12.5 1.3 collective-permute-start.1
  13.9 1.2 collective-permute-done.3.xhi2
  15.0 4.5 %collective-permute-done.1.xhi.refs_3_ = bf16[12,32,128]{2,1,0:T(8,128)(2,1)S(1)} collective-permute-done((bf16[12,32,128]{2,1,0:T(8,128)(2,1)S(1)}, bf16[12,32,128]{2,1,0:T(8,128)(2,1)S(1)}, u32[]{:S(2)}, u32[]{:S(2)}) %collective-permute-start.1) | collective-permute-done | bytes 98336 | tf_op jit(solution)/shard_map/ppermute | solution.py:19
  19.5 0.2 shard_map.110
  19.7 6.0 %collective-permute-start.4 = (bf16[6,3,32,128]{3,2,1,0:T(8,128)(2,1)S(1)}, bf16[6,3,32,128]{3,2,1,0:T(8,128)(2,1)S(1)}, u32[]{:S(2)}, u32[]{:S(2)}) collective-permute-start(bf16[6,3,32,128]{3,2,1,0:T(8,128)(2,1)S(1)} %get-tuple-element.57), channel_id=1, source_target_pairs={{0,1},{1,2},{2,3},{3,4},{4,5},{5,6},{6,7},{7,8},{8,9},{9,10},{10,1... | collective-permute-start | bytes 442376 | tf_op jit(solution)/shard_map/ppermute | solution.py:19
  25.7 1.9 %collective-permute-start.5 = (bf16[6,3,32,128]{3,2,1,0:T(8,128)(2,1)S(1)}, bf16[6,3,32,128]{3,2,1,0:T(8,128)(2,1)S(1)}, u32[]{:S(2)}, u32[]{:S(2)}) collective-permute-start(bf16[6,3,32,128]{3,2,1,0:T(8,128)(2,1)S(1)} %get-tuple-element.58.first_ref), channel_id=1, source_target_pairs={{1,0},{2,1},{3,2},{4,3},{5,4},{6,5},{7,6},{8,7},{9,8},{10,9},{11,1... | collective-permute-start | bytes 442376 | tf_op jit(solution)/shard_map/ppermute | solution.py:19
  27.7 1.0 copy-done.8
  28.7 1.0 copy-done.9
  29.7 1.3 shard_map.111
  31.0 1.2 collective-permute-done.5.yhi.refs_1_
  32.2 2.1 %shard_map.112 = (bf16[8,14,32,64]{3,2,1,0:T(8,128)(2,1)S(1)}, bf16[2,8,32,64]{3,2,1,0:T(8,128)(2,1)S(1)}, f32[512,64]{1,0:T(8,128)S(1)}, bf16[3,6,16,64]{3,2,1,0:T(8,128)(2,1)S(1)}) custom-call(bf16[2,8,32,64]{3,2,1,0:T(8,128)(2,1)S(1)} %get-tuple-element.51.f_ref, bf16[6,3,32,128]{3,2,1,0:T(8,128)(2,1)S(1)} %collective-permute-done.4.ylo.refs_0_, ...), custom_call_target="tpu_custom_call" | custom-call | flops 1000000 | bytes 10000 | tf_op jit(solution)/shard_map/pallas_call | solution.py:31
  34.2 1.3 shard_map.113
  35.5 1.4 shard_map.114
  36.9 0.6 copy-done.1
  37.6 1.9 %collective-permute-start.14 = (bf16[32,64,128]{2,1,0:T(8,128)(2,1)S(1)}, bf16[32,64,128]{2,1,0:T(8,128)(2,1)S(1)}, u32[]{:S(2)}, u32[]{:S(2)}) collective-permute-start(bf16[32,64,128]{2,1,0:T(8,128)(2,1)S(1)} %get-tuple-element.89), channel_id=1, source_target_pairs={{0,1},{1,0},{2,3},{3,2},{4,5},{5,4},{6,7},{7,6},{8,9},{9,8},{10,11... | collective-permute-start | bytes 1572872 | tf_op jit(solution)/shard_map/ppermute | solution.py:27
  39.5 1.9 %collective-permute-done.14.b_ref = bf16[32,64,128]{2,1,0:T(8,128)(2,1)S(1)} collective-permute-done((bf16[32,64,128]{2,1,0:T(8,128)(2,1)S(1)}, bf16[32,64,128]{2,1,0:T(8,128)(2,1)S(1)}, u32[]{:S(2)}, u32[]{:S(2)}) %collective-permute-start.14) | collective-permute-done | bytes 524320 | tf_op jit(solution)/shard_map/ppermute | solution.py:27
  41.4 0.9 shard_map.120
  42.3 10.6 %all-to-all-start = ((bf16[32,64,128]{2,1,0:T(8,128)(2,1)}), bf16[32,64,128]{2,1,0:T(8,128)(2,1)S(1)}, u32[]{:S(2)}, u32[]{:S(2)}) async-start(bf16[32,64,128]{2,1,0:T(8,128)(2,1)} %shard_map.120), calls=%async_computation | async-start | bytes 1048576 | tf_op jit(solution)/shard_map/all_to_all | solution.py:483
  52.9 4.4 %collective-permute-start.6 = (bf16[64,128]{1,0:T(8,128)(2,1)S(1)}, bf16[64,128]{1,0:T(8,128)(2,1)S(1)}, u32[]{:S(2)}, u32[]{:S(2)}) collective-permute-start(bf16[64,128]{1,0:T(8,128)(2,1)S(1)} %get-tuple-element.70), channel_id=1, source_target_pairs={{0,1},{1,2},{2,3},{3,4},{4,5},{5,6},{6,7},{7,8},{8,9},{9,10},{10,1... | collective-permute-start | bytes 49160 | tf_op jit(solution)/shard_map/ppermute | solution.py:19
  57.4 1.9 %collective-permute-start.7 = (bf16[64,128]{1,0:T(8,128)(2,1)S(1)}, bf16[64,128]{1,0:T(8,128)(2,1)S(1)}, u32[]{:S(2)}, u32[]{:S(2)}) collective-permute-start(bf16[64,128]{1,0:T(8,128)(2,1)S(1)} %get-tuple-element.71), channel_id=1, source_target_pairs={{1,0},{2,1},{3,2},{4,3},{5,4},{6,5},{7,6},{8,7},{9,8},{10,9},{11,1... | collective-permute-start | bytes 49160 | tf_op jit(solution)/shard_map/ppermute | solution.py:19
  59.3 3.4 %collective-permute-done.7.yhi_ref.refs_1_ = bf16[64,128]{1,0:T(8,128)(2,1)S(1)} collective-permute-done((bf16[64,128]{1,0:T(8,128)(2,1)S(1)}, bf16[64,128]{1,0:T(8,128)(2,1)S(1)}, u32[]{:S(2)}, u32[]{:S(2)}) %collective-permute-start.7) | collective-permute-done | bytes 16416 | tf_op jit(solution)/shard_map/ppermute | solution.py:19
  62.8 0.1 shard_map.115
  62.9 3.4 %collective-permute-start.8 = (bf16[352,128]{1,0:T(8,128)(2,1)S(1)}, bf16[352,128]{1,0:T(8,128)(2,1)S(1)}, u32[]{:S(2)}, u32[]{:S(2)}) collective-permute-start(bf16[352,128]{1,0:T(8,128)(2,1)S(1)} %get-tuple-element.74), channel_id=1, source_target_pairs={{0,16},{16,32},{32,48},{48,64},{64,80},{80,96},{96,112},{112,128},... | collective-permute-start | bytes 270344 | tf_op jit(solution)/shard_map/ppermute | solution.py:19
  66.3 1.3 collective-permute-start.9
  67.6 0.3 collective-permute-done.8.refs_2_
  68.0 3.6 %collective-permute-done.9.refs_3_ = bf16[352,128]{1,0:T(8,128)(2,1)S(1)} collective-permute-done((bf16[352,128]{1,0:T(8,128)(2,1)S(1)}, bf16[352,128]{1,0:T(8,128)(2,1)S(1)}, u32[]{:S(2)}, u32[]{:S(2)}) %collective-permute-start.9) | collective-permute-done | bytes 90144 | tf_op jit(solution)/shard_map/ppermute | solution.py:19
  71.6 1.1 shard_map.117
  72.7 0.7 copy-done
  73.4 22.0 %all_to_all.20.enc_ref = bf16[64,16,128]{2,1,0:T(8,128)(2,1)S(1)} all-to-all(bf16[64,16,128]{2,1,0:T(8,128)(2,1)} %bitcast.12), channel_id=1, replica_groups=mesh['gx'=32,'gz'=8,'gc'=2] {'gx','gc'}, dimensions={0} | all-to-all | bytes 524288 | tf_op jit(solution)/shard_map/all_to_all | solution.py:494
  95.6 18.2 %all_to_all.21.parts_ref = bf16[8,80,128]{2,1,0:T(8,128)(2,1)S(1)} all-to-all(bf16[8,80,128]{2,1,0:T(8,128)(2,1)S(1)} %shard_map.121), channel_id=1, replica_groups=mesh['gx'=32,'gz'=8,'gc'=2] {'gz'}, dimensions={0} | all-to-all | bytes 327680 | tf_op jit(solution)/shard_map/all_to_all | solution.py:497
  113.9 20.4 %all_to_all.22.own_ref = bf16[32,80,128]{2,1,0:T(8,128)(2,1)S(1)} all-to-all(bf16[32,80,128]{2,1,0:T(8,128)(2,1)S(1)} %shard_map.122), channel_id=1, replica_groups=mesh['gx'=32,'gz'=8,'gc'=2] {'gx'}, dimensions={0} | all-to-all | bytes 1310720 | tf_op jit(solution)/shard_map/all_to_all | solution.py:499
  134.2 7.6 %collective-permute-start.15 = (bf16[32,80,128]{2,1,0:T(8,128)(2,1)S(1)}, bf16[32,80,128]{2,1,0:T(8,128)(2,1)S(1)}, u32[]{:S(2)}, u32[]{:S(2)}) collective-permute-start(bf16[32,80,128]{2,1,0:T(8,128)(2,1)S(1)} %all_to_all.22.own_ref), channel_id=1, source_target_pairs={{0,1},{1,0},{2,3},{3,2},{4,5},{5,4},{6,7},{7,6},{8,9},{9,8},{10,11... | collective-permute-start | bytes 1966088 | tf_op jit(solution)/shard_map/ppermute | solution.py:27
  141.9 1.9 %collective-permute-start.10 = (bf16[32,128]{1,0:T(8,128)(2,1)S(1)}, bf16[32,128]{1,0:T(8,128)(2,1)S(1)}, u32[]{:S(2)}, u32[]{:S(2)}) collective-permute-start(bf16[32,128]{1,0:T(8,128)(2,1)S(1)} %get-tuple-element.82), channel_id=1, source_target_pairs={{0,1},{1,2},{2,3},{3,4},{4,5},{5,6},{6,7},{7,8},{8,9},{9,10},{10,1... | collective-permute-start | bytes 24584 | tf_op jit(solution)/shard_map/ppermute | solution.py:19
  143.8 2.4 %collective-permute-start.11 = (bf16[32,128]{1,0:T(8,128)(2,1)S(1)}, bf16[32,128]{1,0:T(8,128)(2,1)S(1)}, u32[]{:S(2)}, u32[]{:S(2)}) collective-permute-start(bf16[32,128]{1,0:T(8,128)(2,1)S(1)} %get-tuple-element.83), channel_id=1, source_target_pairs={{1,0},{2,1},{3,2},{4,3},{5,4},{6,5},{7,6},{8,7},{9,8},{10,9},{11,1... | collective-permute-start | bytes 24584 | tf_op jit(solution)/shard_map/ppermute | solution.py:19
  146.2 2.5 %collective-permute-done.11.yhi_ref.yhi = bf16[32,128]{1,0:T(8,128)(2,1)S(1)} collective-permute-done((bf16[32,128]{1,0:T(8,128)(2,1)S(1)}, bf16[32,128]{1,0:T(8,128)(2,1)S(1)}, u32[]{:S(2)}, u32[]{:S(2)}) %collective-permute-start.11) | collective-permute-done | bytes 8224 | tf_op jit(solution)/shard_map/ppermute | solution.py:19
  148.8 0.1 shard_map.118
  148.9 3.9 %collective-permute-start.12 = (bf16[160,128]{1,0:T(8,128)(2,1)S(1)}, bf16[160,128]{1,0:T(8,128)(2,1)S(1)}, u32[]{:S(2)}, u32[]{:S(2)}) collective-permute-start(bf16[160,128]{1,0:T(8,128)(2,1)S(1)} %get-tuple-element.84), channel_id=1, source_target_pairs={{0,16},{16,32},{32,48},{48,64},{64,80},{80,96},{96,112},{112,128},... | collective-permute-start | bytes 122888 | tf_op jit(solution)/shard_map/ppermute | solution.py:19
  152.8 1.3 collective-permute-start.13
  154.1 1.5 shard_map.116
  155.7 1.9 %collective-permute-done.13.xhi = bf16[160,128]{1,0:T(8,128)(2,1)S(1)} collective-permute-done((bf16[160,128]{1,0:T(8,128)(2,1)S(1)}, bf16[160,128]{1,0:T(8,128)(2,1)S(1)}, u32[]{:S(2)}, u32[]{:S(2)}) %collective-permute-start.13) | collective-permute-done | bytes 40992 | tf_op jit(solution)/shard_map/ppermute | solution.py:19
  157.6 1.3 shard_map.119
  158.9 1.8 %shard_map.123 = (f32[27,64,64]{2,1,0:T(8,128)}, f32[27,64,128]{2,1,0:T(8,128)}, f32[27,64,128]{2,1,0:T(8,128)}, f32[8,64,128]{2,1,0:T(8,128)}) custom-call(s32[1]{0:T(128)} %bitcast.7.core, bf16[32,80,128]{2,1,0:T(8,128)(2,1)S(1)} %all_to_all.22.own_ref, bf16[32,80,128]{2,1,0:T(8,128)(2,1)S(1)} %collective-permute-done.15.other_ref), custom_call_target="tpu_custom_call" | custom-call | flops 1000000 | bytes 10000 | tf_op jit(solution)/shard_map/pallas_call | solution.py:31
  (27 shorter events, 0.3 us)
Async XLA Ops:
  0.6 0.9 copy-start.3
  1.5 0.9 copy-start.4
  2.4 25.2 %copy-start.7 = (bf16[27,64,64]{2,1,0:T(8,128)(2,1)S(1)}, bf16[27,64,64]{2,1,0:T(8,128)(2,1)}, u32[]{:S(2)}) copy-start(bf16[27,64,64]{2,1,0:T(8,128)(2,1)} %enc_ref.1) | copy-start | bytes 663556
  2.9 11.0 %collective-permute-start.2 = (bf16[4,32,128]{2,1,0:T(8,128)(2,1)S(1)}, bf16[4,32,128]{2,1,0:T(8,128)(2,1)S(1)}, u32[]{:S(2)}, u32[]{:S(2)}) collective-permute-start(bf16[4,32,128]{2,1,0:T(8,128)(2,1)S(1)} %get-tuple-element.55), channel_id=1, source_target_pairs={{0,32},{16,48},{32,64},{48,80},{64,96},{80,112},{96,128},{112,144}... | collective-permute-start | bytes 98312 | tf_op jit(solution)/shard_map/ppermute | solution.py:19
  8.0 7.1 %collective-permute-start.3 = (bf16[4,32,128]{2,1,0:T(8,128)(2,1)S(1)}, bf16[4,32,128]{2,1,0:T(8,128)(2,1)S(1)}, u32[]{:S(2)}, u32[]{:S(2)}) collective-permute-start(bf16[4,32,128]{2,1,0:T(8,128)(2,1)S(1)} %get-tuple-element.56), channel_id=1, source_target_pairs={{32,0},{48,16},{64,32},{80,48},{96,64},{112,80},{128,96},{144,112}... | collective-permute-start | bytes 98312 | tf_op jit(solution)/shard_map/ppermute | solution.py:19
  9.3 5.8 %collective-permute-start = (bf16[12,32,128]{2,1,0:T(8,128)(2,1)S(1)}, bf16[12,32,128]{2,1,0:T(8,128)(2,1)S(1)}, u32[]{:S(2)}, u32[]{:S(2)}) collective-permute-start(bf16[12,32,128]{2,1,0:T(8,128)(2,1)S(1)} %get-tuple-element.53), channel_id=1, source_target_pairs={{0,16},{16,32},{32,48},{48,64},{64,80},{80,96},{96,112},{112,128},... | collective-permute-start | bytes 294920 | tf_op jit(solution)/shard_map/ppermute | solution.py:19
  12.5 7.0 %collective-permute-start.1 = (bf16[12,32,128]{2,1,0:T(8,128)(2,1)S(1)}, bf16[12,32,128]{2,1,0:T(8,128)(2,1)S(1)}, u32[]{:S(2)}, u32[]{:S(2)}) collective-permute-start(bf16[12,32,128]{2,1,0:T(8,128)(2,1)S(1)} %get-tuple-element.54), channel_id=1, source_target_pairs={{16,0},{32,16},{48,32},{64,48},{80,64},{96,80},{112,96},{128,112},... | collective-permute-start | bytes 294920 | tf_op jit(solution)/shard_map/ppermute | solution.py:19
  19.5 8.1 %copy-start.10 = (bf16[8,64,128]{2,1,0:T(8,128)(2,1)S(1)}, bf16[8,64,128]{2,1,0:T(8,128)(2,1)}, u32[]{:S(2)}) copy-start(bf16[8,64,128]{2,1,0:T(8,128)(2,1)} %lift_ref.1) | copy-start | bytes 393220
  19.7 11.3 %collective-permute-start.4 = (bf16[6,3,32,128]{3,2,1,0:T(8,128)(2,1)S(1)}, bf16[6,3,32,128]{3,2,1,0:T(8,128)(2,1)S(1)}, u32[]{:S(2)}, u32[]{:S(2)}) collective-permute-start(bf16[6,3,32,128]{3,2,1,0:T(8,128)(2,1)S(1)} %get-tuple-element.57), channel_id=1, source_target_pairs={{0,1},{1,2},{2,3},{3,4},{4,5},{5,6},{6,7},{7,8},{8,9},{9,10},{10,1... | collective-permute-start | bytes 442376 | tf_op jit(solution)/shard_map/ppermute | solution.py:19
  25.7 6.5 %collective-permute-start.5 = (bf16[6,3,32,128]{3,2,1,0:T(8,128)(2,1)S(1)}, bf16[6,3,32,128]{3,2,1,0:T(8,128)(2,1)S(1)}, u32[]{:S(2)}, u32[]{:S(2)}) collective-permute-start(bf16[6,3,32,128]{3,2,1,0:T(8,128)(2,1)S(1)} %get-tuple-element.58.first_ref), channel_id=1, source_target_pairs={{1,0},{2,1},{3,2},{4,3},{5,4},{6,5},{7,6},{8,7},{9,8},{10,9},{11,1... | collective-permute-start | bytes 442376 | tf_op jit(solution)/shard_map/ppermute | solution.py:19
  27.7 1.0 copy-start.8
  28.7 1.0 copy-start.9
  35.5 1.4 copy-start.5
  36.9 0.7 copy-start.1
  37.6 3.8 %collective-permute-start.14 = (bf16[32,64,128]{2,1,0:T(8,128)(2,1)S(1)}, bf16[32,64,128]{2,1,0:T(8,128)(2,1)S(1)}, u32[]{:S(2)}, u32[]{:S(2)}) collective-permute-start(bf16[32,64,128]{2,1,0:T(8,128)(2,1)S(1)} %get-tuple-element.89), channel_id=1, source_target_pairs={{0,1},{1,0},{2,3},{3,2},{4,5},{5,4},{6,7},{7,6},{8,9},{9,8},{10,11... | collective-permute-start | bytes 1572872 | tf_op jit(solution)/shard_map/ppermute | solution.py:27
  42.3 31.1 %all-to-all-start = ((bf16[32,64,128]{2,1,0:T(8,128)(2,1)}), bf16[32,64,128]{2,1,0:T(8,128)(2,1)S(1)}, u32[]{:S(2)}, u32[]{:S(2)}) async-start(bf16[32,64,128]{2,1,0:T(8,128)(2,1)} %shard_map.120), calls=%async_computation | async-start | bytes 1048576 | tf_op jit(solution)/shard_map/all_to_all | solution.py:483
  52.9 18.7 %copy-start.6 = (bf16[512,64]{1,0:T(8,128)(2,1)S(1)}, bf16[512,64]{1,0:T(8,128)(2,1)}, u32[]{:S(2)}) copy-start(bf16[512,64]{1,0:T(8,128)(2,1)} %copy-done.5) | copy-start | bytes 196612
  52.9 6.4 %collective-permute-start.6 = (bf16[64,128]{1,0:T(8,128)(2,1)S(1)}, bf16[64,128]{1,0:T(8,128)(2,1)S(1)}, u32[]{:S(2)}, u32[]{:S(2)}) collective-permute-start(bf16[64,128]{1,0:T(8,128)(2,1)S(1)} %get-tuple-element.70), channel_id=1, source_target_pairs={{0,1},{1,2},{2,3},{3,4},{4,5},{5,6},{6,7},{7,8},{8,9},{9,10},{10,1... | collective-permute-start | bytes 49160 | tf_op jit(solution)/shard_map/ppermute | solution.py:19
  57.4 5.4 %collective-permute-start.7 = (bf16[64,128]{1,0:T(8,128)(2,1)S(1)}, bf16[64,128]{1,0:T(8,128)(2,1)S(1)}, u32[]{:S(2)}, u32[]{:S(2)}) collective-permute-start(bf16[64,128]{1,0:T(8,128)(2,1)S(1)} %get-tuple-element.71), channel_id=1, source_target_pairs={{1,0},{2,1},{3,2},{4,3},{5,4},{6,5},{7,6},{8,7},{9,8},{10,9},{11,1... | collective-permute-start | bytes 49160 | tf_op jit(solution)/shard_map/ppermute | solution.py:19
  62.9 5.1 %collective-permute-start.8 = (bf16[352,128]{1,0:T(8,128)(2,1)S(1)}, bf16[352,128]{1,0:T(8,128)(2,1)S(1)}, u32[]{:S(2)}, u32[]{:S(2)}) collective-permute-start(bf16[352,128]{1,0:T(8,128)(2,1)S(1)} %get-tuple-element.74), channel_id=1, source_target_pairs={{0,16},{16,32},{32,48},{48,64},{64,80},{80,96},{96,112},{112,128},... | collective-permute-start | bytes 270344 | tf_op jit(solution)/shard_map/ppermute | solution.py:19
  66.3 5.3 %collective-permute-start.9 = (bf16[352,128]{1,0:T(8,128)(2,1)S(1)}, bf16[352,128]{1,0:T(8,128)(2,1)S(1)}, u32[]{:S(2)}, u32[]{:S(2)}) collective-permute-start(bf16[352,128]{1,0:T(8,128)(2,1)S(1)} %get-tuple-element.75), channel_id=1, source_target_pairs={{16,0},{32,16},{48,32},{64,48},{80,64},{96,80},{112,96},{128,112},... | collective-permute-start | bytes 270344 | tf_op jit(solution)/shard_map/ppermute | solution.py:19
  72.7 0.7 copy-start
  134.2 19.9 %copy-start.2 = (bf16[2,8,32,64]{3,2,1,0:T(8,128)(2,1)S(1)}, bf16[2,8,32,64]{3,2,1,0:T(8,128)(2,1)}, u32[]{:S(2)}) copy-start(bf16[2,8,32,64]{3,2,1,0:T(8,128)(2,1)} %copy-done.1) | copy-start | bytes 196612
  134.2 24.6 %collective-permute-start.15 = (bf16[32,80,128]{2,1,0:T(8,128)(2,1)S(1)}, bf16[32,80,128]{2,1,0:T(8,128)(2,1)S(1)}, u32[]{:S(2)}, u32[]{:S(2)}) collective-permute-start(bf16[32,80,128]{2,1,0:T(8,128)(2,1)S(1)} %all_to_all.22.own_ref), channel_id=1, source_target_pairs={{0,1},{1,0},{2,3},{3,2},{4,5},{5,4},{6,7},{7,6},{8,9},{9,8},{10,11... | collective-permute-start | bytes 1966088 | tf_op jit(solution)/shard_map/ppermute | solution.py:27
  141.9 4.3 %collective-permute-start.10 = (bf16[32,128]{1,0:T(8,128)(2,1)S(1)}, bf16[32,128]{1,0:T(8,128)(2,1)S(1)}, u32[]{:S(2)}, u32[]{:S(2)}) collective-permute-start(bf16[32,128]{1,0:T(8,128)(2,1)S(1)} %get-tuple-element.82), channel_id=1, source_target_pairs={{0,1},{1,2},{2,3},{3,4},{4,5},{5,6},{6,7},{7,8},{8,9},{9,10},{10,1... | collective-permute-start | bytes 24584 | tf_op jit(solution)/shard_map/ppermute | solution.py:19
  143.8 5.0 %collective-permute-start.11 = (bf16[32,128]{1,0:T(8,128)(2,1)S(1)}, bf16[32,128]{1,0:T(8,128)(2,1)S(1)}, u32[]{:S(2)}, u32[]{:S(2)}) collective-permute-start(bf16[32,128]{1,0:T(8,128)(2,1)S(1)} %get-tuple-element.83), channel_id=1, source_target_pairs={{1,0},{2,1},{3,2},{4,3},{5,4},{6,5},{7,6},{8,7},{9,8},{10,9},{11,1... | collective-permute-start | bytes 24584 | tf_op jit(solution)/shard_map/ppermute | solution.py:19
  148.9 6.8 %collective-permute-start.12 = (bf16[160,128]{1,0:T(8,128)(2,1)S(1)}, bf16[160,128]{1,0:T(8,128)(2,1)S(1)}, u32[]{:S(2)}, u32[]{:S(2)}) collective-permute-start(bf16[160,128]{1,0:T(8,128)(2,1)S(1)} %get-tuple-element.84), channel_id=1, source_target_pairs={{0,16},{16,32},{32,48},{48,64},{64,80},{80,96},{96,112},{112,128},... | collective-permute-start | bytes 122888 | tf_op jit(solution)/shard_map/ppermute | solution.py:19
  152.8 4.7 %collective-permute-start.13 = (bf16[160,128]{1,0:T(8,128)(2,1)S(1)}, bf16[160,128]{1,0:T(8,128)(2,1)S(1)}, u32[]{:S(2)}, u32[]{:S(2)}) collective-permute-start(bf16[160,128]{1,0:T(8,128)(2,1)S(1)} %get-tuple-element.85), channel_id=1, source_target_pairs={{16,0},{32,16},{48,32},{64,48},{80,64},{96,80},{112,96},{128,112},... | collective-permute-start | bytes 122888 | tf_op jit(solution)/shard_map/ppermute | solution.py:19

commit v2 on v1

--- a/solution.py
+++ b/solution.py
@@ -27,7 +27,7 @@
     return lax.ppermute(piece, "gc", [(0, 1), (1, 0)])
 
 
-def call(kernel, outs, scratch, operands, spaces=(), flops=10**6):
+def call(kernel, outs, scratch, operands, spaces=(), flops=10**6, aliases=()):
     return pl.pallas_call(
         kernel,
         out_shape=[jax.ShapeDtypeStruct(s, d) for s, d in outs],
@@ -36,6 +36,7 @@
         ],
         out_specs=[pl.BlockSpec(memory_space=pltpu.VMEM)] * len(outs),
         scratch_shapes=[s if d is None else pltpu.VMEM(s, d) for s, d in scratch],
+        input_output_aliases=dict(aliases),
         compiler_params=pltpu.CompilerParams(vmem_limit_bytes=40 * 2**20),
         cost_estimate=pl.CostEstimate(flops=flops, bytes_accessed=10**4, transcendentals=0),
     )(*operands)
@@ -141,8 +142,8 @@
 
 
 def pack_y_kernel(f_ref, c_ref, xlo, xhi, xlo2, xhi2, lo_ref, hi_ref):
-    for first, out in ((0, lo_ref), (5, hi_ref)):
-        at = slice(first, first + 3)
+    for first, out in ((0, lo_ref), (3, hi_ref)):
+        at = slice(first, first + 5)
         out[0] = xlo[at]
         for x in range(2):
             out[1 + x] = jnp.concatenate([f_ref[x, at], c_ref[x, at]], -1)
@@ -155,101 +156,117 @@
 def encode_kernel(
     f_ref, ylo, yhi, xlo, xhi, xlo2, xhi2, inside, w_ref, fx_ref, enc_ref, slope_ref, pool_ref, tmp
 ):
-    fx_ref[3:5, 3:11] = f_ref[...]
-    fx_ref[2, 3:11] = xlo[0:8, :, :64]
-    fx_ref[5, 3:11] = xhi[0:8, :, :64]
+    fx_ref[3:5, 5:13] = f_ref[...]
+    fx_ref[2, 5:13] = xlo[0:8, :, :64]
+    fx_ref[5, 5:13] = xhi[0:8, :, :64]
     for x, ref, first in ((1, xlo, 8), (6, xhi, 8), (0, xlo2, 0), (7, xhi2, 0)):
-        fx_ref[x, 3:7] = ref[first : first + 4, :, :64]
-        fx_ref[x, 7:11] = ref[first : first + 4, :, 64:]
-    for y, ref in ((0, ylo), (11, yhi)):
-        at = slice(y, y + 3)
+        fx_ref[x, 5:9] = ref[first : first + 4, :, :64]
+        fx_ref[x, 9:13] = ref[first : first + 4, :, 64:]
+    for y, ref in ((0, ylo), (13, yhi)):
+        at = slice(y, y + 5)
         fx_ref[2:6, at] = ref[0:4, :, :, :64]
         for x, k in ((0, 4), (6, 5)):
             fx_ref[x, at] = ref[k, :, :, :64]
             fx_ref[x + 1, at] = ref[k, :, :, 64:]
     weight = w_ref[...]
     for x in range(6):
-        pre = combined(nt(stacked(fx_ref, x, 1, 12, False), weight), 32, False)
+        pre = combined(nt(stacked(fx_ref, x, 1, 16, False), weight), 32, False)
         sigma = jax.nn.sigmoid(pre)
         enc = (pre * sigma).astype(BF16)
         if x in (2, 3):
             slope = sigma * (1.0 + pre * (1.0 - sigma))
-            slope_ref[pl.ds((x - 2) * 256, 256), :] = slope[64:320]
-            enc_ref[x - 2] = enc[64:320].reshape(8, 32, 64)
-        wide = enc.astype(F32).reshape(6, 2, 32, 64)
+            slope_ref[pl.ds((x - 2) * 256, 256), :] = slope[128:384]
+            enc_ref[x - 2, 1:9] = enc[128:384].reshape(8, 32, 64)
+            enc_ref[x - 2, 0] = (enc[96:128].astype(F32) * inside[2]).astype(BF16)
+            enc_ref[x - 2, 9] = (enc[384:416].astype(F32) * inside[3]).astype(BF16)
+        wide = enc.astype(F32).reshape(8, 2, 32, 64)
         part = wide[:, 0] + wide[:, 1]
         if x % 2 == 0:
             held = part
             continue
-        tmp[...] = (held + part).reshape(192, 64)
-        pooled = tmp[pl.ds(0, 96, stride=2), :] + tmp[pl.ds(1, 96, stride=2), :]
+        tmp[...] = (held + part).reshape(256, 64)
+        pooled = tmp[pl.ds(0, 128, stride=2), :] + tmp[pl.ds(1, 128, stride=2), :]
         pooled = pooled * (0.125 if x == 3 else 0.125 * inside[0 if x == 1 else 1])
-        pool_ref[x // 2, 1:5] = pooled[16:80].astype(BF16).reshape(4, 16, 64)
-        pool_ref[x // 2, 0] = (pooled[0:16] * inside[2]).astype(BF16)
-        pool_ref[x // 2, 5] = (pooled[80:96] * inside[3]).astype(BF16)
+        pool_ref[x // 2, 2:6] = pooled[32:96].astype(BF16).reshape(4, 16, 64)
+        pool_ref[x // 2, 0:2] = (pooled[0:32] * inside[2]).astype(BF16).reshape(2, 16, 64)
+        pool_ref[x // 2, 6:8] = (pooled[96:128] * inside[3]).astype(BF16).reshape(2, 16, 64)
 
 
 def joined_grad_kernel(c_ref, *refs):
     (ylo, yhi, xlo, xhi), (w_ref, lift_ref, enc_ref) = refs[:4], refs[4:7]
     cx_ref, jg_ref, kids_ref, adj_ref, dge_ref, tmp = refs[7:]
-    cx_ref[1:3, 1:9] = c_ref[...]
-    cx_ref[0, 1:9] = xlo[0:8, :, 64:]
-    cx_ref[3, 1:9] = xhi[0:8, :, 64:]
-    cx_ref[:, 0] = ylo[0:4, 2, :, 64:]
-    cx_ref[:, 9] = yhi[0:4, 0, :, 64:]
+    cx_ref[1:3, 3:11] = c_ref[...]
+    cx_ref[0, 3:11] = xlo[0:8, :, 64:]
+    cx_ref[3, 3:11] = xhi[0:8, :, 64:]
+    cx_ref[:, 0:3] = ylo[0:4, 2:5, :, 64:]
+    cx_ref[:, 11:14] = yhi[0:4, 0:3, :, 64:]
     weight = w_ref[...]
     for x in range(2):
-        grad = combined(nn(stacked(cx_ref, x, 1, 8, True), weight), 32, True)
+        grad = combined(nn(stacked(cx_ref, x, 1, 12, True), weight), 32, True)
         grad = grad.astype(BF16)
-        jg_ref[pl.ds(x * 256, 256), :] = grad[:, :64]
-        tmp[pl.ds(x * 256, 256), :] = grad.astype(F32)
+        jg_ref[pl.ds(x * 256, 256), :] = grad[64:320, :64]
+        tmp[pl.ds(x * 384, 384), :] = grad.astype(F32)
     kids = []
     for p in range(2):
         for q in range(2):
             for r in range(2):
                 rows = [
-                    tmp[pl.ds(p * 256 + (2 * j + q) * 32 + r, 16, stride=2), :] for j in range(4)
+                    tmp[pl.ds(p * 384 + (2 * j + q) * 32 + r, 16, stride=2), :] for j in range(6)
                 ]
                 kids.append(jnp.concatenate(rows, 0)[:, 64:])
     kids = jnp.concatenate(kids, -1).astype(BF16)
-    kids_ref[...] = kids
+    kids_ref[...] = kids[16:80]
     adj_ref[...] = nn(kids, lift_ref[...].reshape(512, 128))
-    enc = enc_ref[...].reshape(512, 64).astype(F32)
-    dge_ref[...] = tn(stacked(cx_ref, 0, 2, 8, True), ztaps(enc, 32, False))
-
-
-def lower_kernel(px, core, w_ref, lift_ref, adj_ref, kids_ref, cx_ref, dge_ref, enc_ref, *refs):
-    la_ref, lg_ref, lifted_ref, keep_ref, send_ref, lo_ref, hi_ref, tmp, halves = refs
-    chunk = keep_ref.shape[1]
+    enc = enc_ref[:, 1:9].reshape(512, 64).astype(F32)
+    dge_ref[...] = tn(stacked(cx_ref, 0, 2, 8, True, 2), ztaps(enc, 32, False))
+
+
+def halver(halves):
+    chunk = halves.shape[2]
 
     def put(row, block):
         at = pl.ds(row % chunk, block.shape[0])
         halves[row // chunk % 2, row // (2 * chunk), at, :] = block.astype(LINK)
 
-    pk = stacked(px, 0, 1, 4, False)
+    return put
+
+
+def lower_kernel(
+    px, core, inside, w_ref, lift_ref, adj_ref, kids_ref, cx_ref, dge_ref, enc_ref, *refs
+):
+    lg_ref, lifted_ref, keep_ref, send_ref, lo_ref, hi_ref, tmp, halves = refs
+    put = halver(halves)
+
+    def masked(value):
+        first, last = value[0:16] * inside[2], value[80:96] * inside[3]
+        return jnp.concatenate([first, value[16:80], last], 0).astype(BF16)
+
+    pk = stacked(px, 0, 1, 6, False)
     pre = combined(nn(pk, w_ref[...]), 16, False)
     sigma = jax.nn.sigmoid(pre)
-    la = (pre * sigma).astype(BF16)
-    lg = (adj_ref[...] * (sigma * (1.0 + pre * (1.0 - sigma)))).astype(BF16)
-    la_ref[...] = la.reshape(1, 4, 16, 128)
-    lg_ref[...] = lg.reshape(1, 4, 16, 128)
-    for j, y, msg in ((0, 0, lo_ref), (3, 7, hi_ref)):
-        rows = slice(16 * j, 16 * j + 16)
-        msg[0:16] = la[rows]
-        msg[16:32] = lg[rows]
-        msg[32:64] = jnp.concatenate([enc_ref[0, y], enc_ref[1, y]], -1)
+    la = masked(pre * sigma)
+    lg = masked(adj_ref[...] * (sigma * (1.0 + pre * (1.0 - sigma))))
+    lg_ref[...] = lg
+    for x, msg in ((0, lo_ref), (1, hi_ref)):
+        msg[0:96] = la
+        msg[96:192] = lg
+        enc = enc_ref[x].reshape(320, 64)
+        msg[192:352] = jnp.concatenate([enc[:160], enc[160:]], -1)
     fine = nt(la, lift_ref[...].reshape(512, 128)).astype(BF16).astype(F32)
     for p in range(2):
         for q in range(2):
             for r in range(2):
                 k = 4 * p + 2 * q + r
-                for j in range(4):
-                    tmp[pl.ds(p * 256 + (2 * j + q) * 32 + r, 16, stride=2), :] = fine[
-                        16 * j : 16 * j + 16, 64 * k : 64 * k + 64
-                    ]
-    lifted = tmp[...]
-    lifted_ref[...] = lifted.astype(BF16).reshape(2, 8, 32, 64)
-    dgl = tn(stacked(cx_ref, 0, 2, 8, True), ztaps(lifted, 32, False))
+                for j in range(6):
+                    y = 2 * j + q - 1
+                    if 0 <= y < 10:
+                        tmp[pl.ds((p * 10 + y) * 32 + r, 16, stride=2), :] = fine[
+                            16 * j : 16 * j + 16, 64 * k : 64 * k + 64
+                        ]
+    lifted_ref[...] = tmp[...].astype(BF16).reshape(2, 10, 32, 64)
+    lifted = jnp.concatenate([tmp[32:288], tmp[352:608]], 0)
+    la, lg, pk = la[16:80], lg[16:80], pk[16:80]
+    dgl = tn(stacked(cx_ref, 0, 2, 8, True, 2), ztaps(lifted, 32, False))
     for ab in range(9):
         for c in range(3):
             cols = slice(64 * c, 64 * c + 64)
@@ -266,28 +283,13 @@
         put(3456 + 64 * k, lift[64 * k : 64 * k + 64])
     for row in (3968, 4032):
         put(row, jnp.zeros((64, 128), F32))
-    mine = core[0]
-    keep_ref[...] = halves[mine]
-    send_ref[...] = halves[1 - mine]
+    mine, chunk = core[0], halves.shape[2]
+    keep_ref[:, :chunk, :] = halves[mine]
+    send_ref[:, :chunk, :] = halves[1 - mine]
 
 
 def add_kernel(a_ref, b_ref, out_ref):
     out_ref[...] = (a_ref[...].astype(F32) + b_ref[...].astype(F32)).astype(LINK)
-
-
-def joined_x_kernel(la_ref, lg_ref, enc_ref, ylo_ref, yhi_ref, lo_ref, hi_ref):
-    for x, out in ((0, lo_ref), (1, hi_ref)):
-        cols = slice(64 * x, 64 * x + 64)
-        out[0:16] = ylo_ref[0:16]
-        out[16:80] = la_ref[...].reshape(64, 128)
-        out[80:96] = yhi_ref[0:16]
-        out[96:112] = ylo_ref[16:32]
-        out[112:176] = lg_ref[...].reshape(64, 128)
-        out[176:192] = yhi_ref[16:32]
-        enc = enc_ref[x].reshape(256, 64)
-        first = jnp.concatenate([ylo_ref[32:64, cols], enc[:128]], 0)
-        second = jnp.concatenate([enc[128:], yhi_ref[32:64, cols]], 0)
-        out[192:352] = jnp.concatenate([first, second], -1)
 
 
 def edge_y_kernel(eg_ref, lo_ref, hi_ref):
@@ -312,12 +314,12 @@
     return jnp.concatenate([rows[:, :64], rows[:, 64:]], 0).reshape(1, 10, 32, 64)
 
 
-def encoder_grad_kernel(lg_ref, *refs):
-    (ylo, yhi, xlo, xhi), (w_ref, slope_ref, jg_ref, fx_ref) = refs[:4], refs[4:8]
-    eg_ref, grads_ref, lo_ref, hi_ref, lx, tmp = refs[8:]
-    sides = [h[16:32].reshape(1, 1, 16, 128) for h in (ylo, yhi)]
-    sides += [h[96:192].reshape(1, 6, 16, 128) for h in (xlo, xhi)]
-    assemble(lx, lg_ref[...], *sides)
+def encoder_grad_kernel(lg_ref, xlo, xhi, core, w_ref, slope_ref, jg_ref, fx_ref, *refs):
+    eg_ref, keep_ref, send_ref, lo_ref, hi_ref, lx, tmp, halves = refs[2:]
+    put = halver(halves)
+    lx[0] = xlo[96:192].reshape(6, 16, 128)
+    lx[1] = lg_ref[...].reshape(6, 16, 128)
+    lx[2] = xhi[96:192].reshape(6, 16, 128)
     pg = combined(nt(stacked(lx, 0, 1, 4, True), w_ref[...]), 16, True)
     pg = pg.astype(BF16).astype(F32) * 0.125
     tmp[pl.ds(0, 64, stride=2), :] = pg
@@ -327,25 +329,22 @@
     eg = ((jg_ref[...].astype(F32) + wide) * slope_ref[...]).astype(BF16)
     eg_ref[...] = eg.reshape(2, 8, 32, 64)
     edge_y_kernel(eg_ref, lo_ref, hi_ref)
-    grad = tn(ztaps(eg.astype(F32), 32, True), stacked(fx_ref, 2, 2, 8, False, 2))
+    grad = tn(ztaps(eg.astype(F32), 32, True), stacked(fx_ref, 2, 2, 8, False, 4))
     for ab in range(9):
         for c in range(3):
             block = grad[64 * c : 64 * c + 64, 64 * ab : 64 * ab + 64]
             block = jnp.concatenate([block[:32], block[32:]], -1)
-            grads_ref[pl.ds((3 * ab + c) * 32, 32), :] = block.astype(LINK)
-    grads_ref[pl.ds(864, 160), :] = jnp.zeros((160, 128), LINK)
-
-
-def decode_kernel(enc_ref, lifted_ref, *refs):
-    (ylo, yhi, xlo, xhi), (lift_ref, w_ref, out_ref, jx, ty, tx) = refs[:4], refs[4:]
-    sides = []
-    for q, h in ((1, ylo), (0, yhi)):
-        for p in range(2):
-            for r in range(2):
-                fine = nt(h[0:16], lift_ref[4 * p + 2 * q + r]).astype(BF16).astype(F32)
-                ty[pl.ds(32 * p + r, 16, stride=2), :] = fine
-        lifted = ty[...].astype(BF16).reshape(2, 1, 32, 64)
-        sides.append(jnp.concatenate([column(h[32:64]), lifted], -1))
+            put((3 * ab + c) * 32, block[:16])
+            put((3 * ab + c) * 32 + 16, block[16:])
+    for row in range(864, 1024, 16):
+        put(row, jnp.zeros((16, 128), F32))
+    mine, chunk = core[0], keep_ref.shape[1] - halves.shape[2]
+    keep_ref[:, chunk:, :] = halves[mine]
+    send_ref[:, chunk:, :] = halves[1 - mine]
+
+
+def decode_kernel(enc_ref, lifted_ref, xlo, xhi, lift_ref, w_ref, out_ref, jx, tx):
+    jx[1:3] = jnp.concatenate([enc_ref[...], lifted_ref[...]], -1)
     for p, h in ((1, xlo), (0, xhi)):
         for q in range(2):
             for r in range(2):
@@ -355,8 +354,8 @@
                     if 0 <= y < 10:
                         tx[pl.ds(32 * y + r, 16, stride=2), :] = fine[16 * j : 16 * j + 16]
         lifted = tx[...].astype(BF16).reshape(1, 10, 32, 64)
-        sides.append(jnp.concatenate([plane(h[192:352]), lifted], -1))
-    assemble(jx, jnp.concatenate([enc_ref[...], lifted_ref[...]], -1), *sides)
+        x = 0 if p == 1 else 3
+        jx[x : x + 1] = jnp.concatenate([plane(h[192:352]), lifted], -1)
     weight = w_ref[...]
     for x in range(2):
         out = combined(nt(stacked(jx, x, 1, 8, False), weight), 32, False)
@@ -372,20 +371,7 @@
         out_ref[x] = out.astype(BF16).reshape(8, 32, 64)
 
 
-def sum_x_kernel(grads_ref, enc_ref, out_ref):
-    first = 0
-    for ref in (grads_ref, enc_ref):
-        rows = ref.shape[1]
-        total = ref[0].astype(F32)
-        for k in range(1, ref.shape[0]):
-            total = total + ref[k].astype(F32)
-        total = total.astype(LINK)
-        for k in range(out_ref.shape[0]):
-            out_ref[k, first : first + rows] = total
-        first += rows
-
-
-def sum_z_kernel(parts_ref, out_ref):
+def sum_kernel(parts_ref, out_ref):
     total = parts_ref[0].astype(F32)
     for k in range(1, parts_ref.shape[0]):
         total = total + parts_ref[k].astype(F32)
@@ -412,7 +398,7 @@
     f = jnp.transpose(features, (1, 2, 3, 0))
     c = jnp.transpose(cotangent, (1, 2, 3, 0))
     lower_t = jnp.transpose(lower_weight, (0, 2, 1))
-    brick, coarse = (2, 8, 32, 64), (1, 4, 16, 128)
+    brick, tall = (2, 8, 32, 64), (2, 10, 32, 64)
 
     size_x, size_z = lax.axis_size("gx"), lax.axis_size("gz")
     at_x, at_y = lax.axis_index("gx"), lax.axis_index(GY)
@@ -428,7 +414,7 @@
     )
     x_halo = swapped(lo, hi, GX)
     far_halo = [shifted(hi2, GX, 2), shifted(lo2, GX, -2)]
-    edges = call(pack_y_kernel, [((6, 3, 32, 128), BF16)] * 2, [], [f, c, *x_halo, *far_halo])
+    edges = call(pack_y_kernel, [((6, 5, 32, 128), BF16)] * 2, [], [f, c, *x_halo, *far_halo])
     y_halo = swapped(*edges, GY)
     enc_fwd, enc_bwd, low_fwd, low_bwd, dec_fwd, dec_bwd, lift = call(
         stack_kernel,
@@ -453,71 +439,74 @@
     )
     fx, encoded, slope, pooled = call(
         encode_kernel,
-        [((8, 14, 32, 64), BF16), (brick, BF16), ((512, 64), F32), ((3, 6, 16, 64), BF16)],
-        [((192, 64), F32)],
+        [((8, 18, 32, 64), BF16), (tall, BF16), ((512, 64), F32), ((3, 8, 16, 64), BF16)],
+        [((256, 64), F32)],
         [f, *y_halo, *x_halo, *far_halo, inside, enc_fwd],
         spaces={7: pltpu.SMEM},
     )
     cx, jg, kids, adj, dge = call(
         joined_grad_kernel,
         [
-            ((4, 10, 32, 64), BF16),
+            ((4, 14, 32, 64), BF16),
             ((512, 64), BF16),
             ((64, 512), BF16),
-            ((64, 128), F32),
+            ((96, 128), F32),
             ((576, 192), F32),
         ],
-        [((512, 128), F32)],
+        [((768, 128), F32)],
         [c, *y_halo, *x_halo, dec_bwd, lift, encoded],
     )
-    half = (size_x, 2048 // size_x, 128)
-    la, lg, lifted, keep, send, *edges = call(
+    half = (size_x, 2560 // size_x, 128)
+    lg, lifted, keep, send, *edges = call(
         lower_kernel,
-        [(coarse, BF16), (coarse, BF16), (brick, BF16), (half, LINK), (half, LINK)]
-        + [((64, 128), BF16)] * 2,
-        [((512, 64), F32), ((2,) + half, LINK)],
-        [pooled, core, low_fwd, lift, adj, kids, cx, dge, encoded],
-        spaces={1: pltpu.SMEM},
-    )
-    (grads,) = call(add_kernel, [(half, LINK)], [], [keep, partner(send)])
-    grads = lax.all_to_all(grads, "gx", 0, 0)
+        [((96, 128), BF16), (tall, BF16), (half, LINK), (half, LINK)]
+        + [((352, 128), BF16)] * 2,
+        [((640, 64), F32), ((2, size_x, 2048 // size_x, 128), LINK)],
+        [pooled, core, inside, low_fwd, lift, adj, kids, cx, dge, encoded],
+        spaces={1: pltpu.SMEM, 2: pltpu.SMEM},
+    )
+    halo = swapped(*edges, GX)
+    eg, keep, send, *edges = call(
+        encoder_grad_kernel,
+        [(brick, BF16), (half, LINK), (half, LINK)] + [((32, 128), BF16)] * 2,
+        [
+            ((3, 6, 16, 128), BF16),
+            ((128, 64), F32),
+            ((2, size_x, 512 // size_x, 128), LINK),
+        ],
+        [lg, *halo, core, low_bwd, slope, jg, fx, keep, send],
+        spaces={3: pltpu.SMEM},
+        aliases={8: 1, 9: 2},
+    )
+    (sums,) = call(add_kernel, [(half, LINK)], [], [keep, partner(send)])
+    sums = lax.all_to_all(sums, "gx", 0, 0)
+    (sums,) = call(sum_kernel, [((size_z,) + half[1:], LINK)], [], [sums])
+    sums = lax.all_to_all(sums, "gz", 0, 0)
+    (sums,) = call(sum_kernel, [(half, LINK)], [], [sums])
+    sums, edges = lax.optimization_barrier((sums, edges))
+    sums = lax.all_to_all(sums, "gx", 0, 0)
     y_halo = swapped(*edges, GY)
-    edges = call(joined_x_kernel, [((352, 128), BF16)] * 2, [], [la, lg, encoded, *y_halo])
-    halo = [*y_halo, *swapped(*edges, GX)]
-    eg, enc_grads, *edges = call(
-        encoder_grad_kernel,
-        [(brick, BF16), ((1024, 128), LINK)] + [((32, 128), BF16)] * 2,
-        [((3, 6, 16, 128), BF16), ((128, 64), F32)],
-        [lg, *halo, low_bwd, slope, jg, fx],
-    )
-    enc_grads, grads = lax.optimization_barrier((enc_grads, grads))
-    enc_grads = lax.all_to_all(enc_grads.reshape(2 * size_x, -1, 128), ("gx", "gc"), 0, 0)
-    rows = 2560 // size_x
-    (sums,) = call(sum_x_kernel, [((size_z, rows, 128), LINK)], [], [grads, enc_grads])
-    sums = lax.all_to_all(sums, "gz", 0, 0)
-    (sums,) = call(sum_z_kernel, [((size_x, rows, 128), LINK)], [], [sums])
-    sums = lax.all_to_all(sums, "gx", 0, 0)
+    edges = call(edge_x_kernel, [((160, 128), BF16)] * 2, [], [eg, *y_halo])
+    eg_halo = [*y_halo, *swapped(*edges, GX)]
+    (decoded,) = call(
+        decode_kernel,
+        [(brick, BF16)],
+        [((4, 10, 32, 128), BF16), ((320, 64), F32)],
+        [encoded, lifted, *halo, lift, dec_fwd],
+    )
+    (input_grad,) = call(
+        input_grad_kernel,
+        [(brick, BF16)],
+        [((4, 10, 32, 64), BF16)],
+        [eg, *eg_halo, enc_bwd],
+    )
+    sums, decoded, input_grad = lax.optimization_barrier((sums, decoded, input_grad))
     encoder_gradient, decoder_gradient, lower_gradient, lift_gradient = call(
         widen_kernel,
         [((27, 64, 64), F32), ((27, 64, 128), F32), ((27, 64, 128), F32), ((8, 64, 128), F32)],
         [],
         [core, sums, partner(sums)],
         spaces={0: pltpu.SMEM},
-    )
-    y_halo = swapped(*edges, GY)
-    edges = call(edge_x_kernel, [((160, 128), BF16)] * 2, [], [eg, *y_halo])
-    eg_halo = [*y_halo, *swapped(*edges, GX)]
-    (decoded,) = call(
-        decode_kernel,
-        [(brick, BF16)],
-        [((4, 10, 32, 128), BF16), ((64, 64), F32), ((320, 64), F32)],
-        [encoded, lifted, *halo, lift, dec_fwd],
-    )
-    (input_grad,) = call(
-        input_grad_kernel,
-        [(brick, BF16)],
-        [((4, 10, 32, 64), BF16)],
-        [eg, *eg_halo, enc_bwd],
     )
     return (
         jnp.transpose(decoded, (3, 0, 1, 2)),

time: 161 us -> 136 us (0.84)
  blocking collectives: 60.6 us -> 43.5 us
  starting transfers between devices: 59.5 us -> 47.6 us
  waiting for transfers between devices: 20.6 us -> 23 us
    all_to_all x1 -> x0, blocking collectives: 22 us -> none  [per_device(): lax.all_to_all(enc_grads.reshape(2 * size_x, -1, 128), ('gx', 'gc'), 0, 0)]
    ppermute x14 -> x12, starting transfers between devices: 39.3 us -> 34.3 us  [shifted(): return lax.ppermute(piece, axes, pairs)]
    ppermute x2, starting transfers between devices: 9.55 us -> 5.07 us  [partner(): return lax.ppermute(piece, 'gc', [(0, 1), (1, 0)])]
    all_to_all x1, blocking collectives: 20.4 us -> 23.5 us  [per_device(): sums = lax.all_to_all(sums, 'gx', 0, 0)]
    all_to_all x1, starting transfers between devices: 10.6 us -> 8.21 us  [per_device(): sums = lax.all_to_all(sums, 'gx', 0, 0)]
    ppermute x2, waiting for transfers between devices: 1.88 us -> 3.77 us  [partner(): return lax.ppermute(piece, 'gc', [(0, 1), (1, 0)])]
    all_to_all x1, blocking collectives: 18.2 us -> 20 us  [per_device(): sums = lax.all_to_all(sums, 'gz', 0, 0)]
    pallas_call x15 -> x14, Pallas kernels: 13.7 us -> 14.9 us  [call(): pl.pallas_call(kernel, out_shape=[jax.ShapeDtypeStruct(s, d) for s, d in...]
  transfers between devices with their start and end apart: 17 -> 15, of which waited for: 9 -> 8; matrix products, arithmetic and copies ran while one was open for 0% -> 0% of each run, Pallas kernels for 3% -> 3%
where the time goes in v2:
time: 136 us
  starting transfers between devices  47.6 us (35%)
  blocking collectives  43.5 us (32%)
  waiting for transfers between devices  23 us (17%)
  Pallas kernels  14.9 us (11%)
  local copies, waits for them, and re-layouts  5.74 us (4%)
    ppermute x12, starting transfers between devices, shifted(): return lax.ppermute(piece, axes, pairs)  34.3 us
    all_to_all x1, blocking collectives, per_device(): sums = lax.all_to_all(sums, 'gx', 0, 0)  23.5 us
    all_to_all x1, blocking collectives, per_device(): sums = lax.all_to_all(sums, 'gz', 0, 0)  20 us
    ppermute x12, waiting for transfers between devices, shifted(): return lax.ppermute(piece, axes, pairs)  19.2 us
    pallas_call x14, Pallas kernels, call(): pl.pallas_call(kernel, out_shape=[jax.ShapeDtypeStruct(s, d) for s, d in...  14.9 us
    all_to_all x1, starting transfers between devices, per_device(): sums = lax.all_to_all(sums, 'gx', 0, 0)  8.21 us
    unnamed x12, local copies, waits for them, and re-layouts  5.74 us
    ppermute x2, starting transfers between devices, partner(): return lax.ppermute(piece, 'gc', [(0, 1), (1, 0)])  5.07 us
  transfers between devices with their start and end apart: 15, of which 8 were waited for; matrix products, arithmetic and copies ran while one was open for 0% of the time, Pallas kernels for 3%

profile of v2, /device:TPU:1, one launch (start us, length us, event | category | flops | bytes accessed | tf_op | source)
XLA Modules:
  0.0 135.6 jit_solution(1295831181427133438)
XLA Ops:
  0.6 0.9 copy-done
  1.5 0.9 copy-done.1
  2.4 0.4 shard_map.109
  2.9 4.0 %collective-permute-start = (bf16[12,32,128]{2,1,0:T(8,128)(2,1)S(1)}, bf16[12,32,128]{2,1,0:T(8,128)(2,1)S(1)}, u32[]{:S(2)}, u32[]{:S(2)}) collective-permute-start(bf16[12,32,128]{2,1,0:T(8,128)(2,1)S(1)} %get-tuple-element.55), channel_id=1, source_target_pairs={{0,16},{16,32},{32,48},{48,64},{64,80},{80,96},{96,112},{112,128},... | collective-permute-start | bytes 294920 | tf_op jit(solution)/shard_map/ppermute | solution.py:19
  6.9 1.3 collective-permute-start.1
  8.2 5.0 %collective-permute-start.2 = (bf16[4,32,128]{2,1,0:T(8,128)(2,1)S(1)}, bf16[4,32,128]{2,1,0:T(8,128)(2,1)S(1)}, u32[]{:S(2)}, u32[]{:S(2)}) collective-permute-start(bf16[4,32,128]{2,1,0:T(8,128)(2,1)S(1)} %get-tuple-element.57), channel_id=1, source_target_pairs={{0,32},{16,48},{32,64},{48,80},{64,96},{80,112},{96,128},{112,144}... | collective-permute-start | bytes 98312 | tf_op jit(solution)/shard_map/ppermute | solution.py:19
  13.2 1.3 collective-permute-start.3
  14.6 6.6 %collective-permute-done.3.xhi2 = bf16[4,32,128]{2,1,0:T(8,128)(2,1)S(1)} collective-permute-done((bf16[4,32,128]{2,1,0:T(8,128)(2,1)S(1)}, bf16[4,32,128]{2,1,0:T(8,128)(2,1)S(1)}, u32[]{:S(2)}, u32[]{:S(2)}) %collective-permute-start.3) | collective-permute-done | bytes 32800 | tf_op jit(solution)/shard_map/ppermute | solution.py:19
  21.2 0.0 collective-permute-done.xlo.refs_2_
  21.2 0.3 shard_map.110
  21.5 6.3 %collective-permute-start.4 = (bf16[6,5,32,128]{3,2,1,0:T(8,128)(2,1)S(1)}, bf16[6,5,32,128]{3,2,1,0:T(8,128)(2,1)S(1)}, u32[]{:S(2)}, u32[]{:S(2)}) collective-permute-start(bf16[6,5,32,128]{3,2,1,0:T(8,128)(2,1)S(1)} %get-tuple-element.59), channel_id=1, source_target_pairs={{0,1},{1,2},{2,3},{3,4},{4,5},{5,6},{6,7},{7,8},{8,9},{9,10},{10,1... | collective-permute-start | bytes 737288 | tf_op jit(solution)/shard_map/ppermute | solution.py:19
  27.8 1.9 %collective-permute-start.5 = (bf16[6,5,32,128]{3,2,1,0:T(8,128)(2,1)S(1)}, bf16[6,5,32,128]{3,2,1,0:T(8,128)(2,1)S(1)}, u32[]{:S(2)}, u32[]{:S(2)}) collective-permute-start(bf16[6,5,32,128]{3,2,1,0:T(8,128)(2,1)S(1)} %get-tuple-element.60.first_ref), channel_id=1, source_target_pairs={{1,0},{2,1},{3,2},{4,3},{5,4},{6,5},{7,6},{8,7},{9,8},{10,9},{11,1... | collective-permute-start | bytes 737288 | tf_op jit(solution)/shard_map/ppermute | solution.py:19
  29.7 0.1 add_convert_fusion.inside
  29.8 1.0 copy-done.2
  30.8 1.0 copy-done.3
  31.9 1.0 copy-done.4
  32.9 0.9 copy-done.5
  33.8 1.3 shard_map.111
  35.1 0.0 collective-permute-done.4.ylo.refs_0_
  35.1 0.3 collective-permute-done.5.yhi.refs_1_
  35.3 2.4 %shard_map.112 = (bf16[8,18,32,64]{3,2,1,0:T(8,128)(2,1)S(1)}, bf16[2,10,32,64]{3,2,1,0:T(8,128)(2,1)S(1)}, f32[512,64]{1,0:T(8,128)S(1)}, bf16[3,8,16,64]{3,2,1,0:T(8,128)(2,1)S(1)}) custom-call(bf16[2,8,32,64]{3,2,1,0:T(8,128)(2,1)S(1)} %get-tuple-element.53.f_ref, bf16[6,5,32,128]{3,2,1,0:T(8,128)(2,1)S(1)} %collective-permute-done.4.ylo.refs_0_, ...), custom_call_target="tpu_custom_call" | custom-call | flops 1000000 | bytes 10000 | tf_op jit(solution)/shard_map/pallas_call | solution.py:31
  37.8 1.6 %shard_map.113 = (bf16[4,14,32,64]{3,2,1,0:T(8,128)(2,1)S(1)}, bf16[512,64]{1,0:T(8,128)(2,1)S(1)}, bf16[64,512]{1,0:T(8,128)(2,1)S(1)}, f32[96,128]{1,0:T(8,128)S(1)}, f32[576,192]{1,0:T(8,128)S(1)}) custom-call(bf16[2,8,32,64]{3,2,1,0:T(8,128)(2,1)S(1)} %get-tuple-element.54.c_ref, bf16[6,5,32,128]{3,2,1,0:T(8,128)(2,1)S(1)} %collective-permute-done.4.ylo.refs_0_, ...), custom_call_target="tpu_custom_call" | custom-call | flops 1000000 | bytes 10000 | tf_op jit(solution)/shard_map/pallas_call | solution.py:31
  39.4 1.9 %shard_map.114 = (bf16[96,128]{1,0:T(8,128)(2,1)S(1)}, bf16[2,10,32,64]{3,2,1,0:T(8,128)(2,1)S(1)}, bf16[32,80,128]{2,1,0:T(8,128)(2,1)S(1)}, bf16[32,80,128]{2,...) custom-call(bf16[3,8,16,64]{3,2,1,0:T(8,128)(2,1)S(1)} %get-tuple-element.62.px, ...), custom_call_target="tpu_custom_call" | custom-call | flops 1000000 | bytes 10000 | tf_op jit(solution)/shard_map/pallas_call | solution.py:31
  41.3 1.8 %collective-permute-start.6 = (bf16[352,128]{1,0:T(8,128)(2,1)S(1)}, bf16[352,128]{1,0:T(8,128)(2,1)S(1)}, u32[]{:S(2)}, u32[]{:S(2)}) collective-permute-start(bf16[352,128]{1,0:T(8,128)(2,1)S(1)} %get-tuple-element.72), channel_id=1, source_target_pairs={{0,16},{16,32},{32,48},{48,64},{64,80},{80,96},{96,112},{112,128},... | collective-permute-start | bytes 270344 | tf_op jit(solution)/shard_map/ppermute | solution.py:19
  43.2 1.3 collective-permute-start.7
  44.5 0.2 collective-permute-done.6.xlo
  44.7 6.4 %collective-permute-done.7.xhi = bf16[352,128]{1,0:T(8,128)(2,1)S(1)} collective-permute-done((bf16[352,128]{1,0:T(8,128)(2,1)S(1)}, bf16[352,128]{1,0:T(8,128)(2,1)S(1)}, u32[]{:S(2)}, u32[]{:S(2)}) %collective-permute-start.7) | collective-permute-done | bytes 90144 | tf_op jit(solution)/shard_map/ppermute | solution.py:19
  51.2 1.1 shard_map.115
  52.3 1.9 %collective-permute-start.8 = (bf16[32,80,128]{2,1,0:T(8,128)(2,1)S(1)}, bf16[32,80,128]{2,1,0:T(8,128)(2,1)S(1)}, u32[]{:S(2)}, u32[]{:S(2)}) collective-permute-start(bf16[32,80,128]{2,1,0:T(8,128)(2,1)S(1)} %get-tuple-element.81), channel_id=1, source_target_pairs={{0,1},{1,0},{2,3},{3,2},{4,5},{5,4},{6,7},{7,6},{8,9},{9,8},{10,11... | collective-permute-start | bytes 1966088 | tf_op jit(solution)/shard_map/ppermute | solution.py:27
  54.2 2.1 %collective-permute-done.8.b_ref = bf16[32,80,128]{2,1,0:T(8,128)(2,1)S(1)} collective-permute-done((bf16[32,80,128]{2,1,0:T(8,128)(2,1)S(1)}, bf16[32,80,128]{2,1,0:T(8,128)(2,1)S(1)}, u32[]{:S(2)}, u32[]{:S(2)}) %collective-permute-start.8) | collective-permute-done | bytes 655392 | tf_op jit(solution)/shard_map/ppermute | solution.py:27
  56.3 0.2 shard_map.116
  56.4 23.5 %all_to_all.15.parts_ref = bf16[32,80,128]{2,1,0:T(8,128)(2,1)S(1)} all-to-all(bf16[32,80,128]{2,1,0:T(8,128)(2,1)S(1)} %shard_map.116), channel_id=1, replica_groups=mesh['gx'=32,'gz'=8,'gc'=2] {'gx'}, dimensions={0} | all-to-all | bytes 1310720 | tf_op jit(solution)/shard_map/all_to_all | solution.py:482
  79.9 0.1 shard_map.117
  80.0 20.0 %all_to_all.16.parts_ref = bf16[8,80,128]{2,1,0:T(8,128)(2,1)S(1)} all-to-all(bf16[8,80,128]{2,1,0:T(8,128)(2,1)S(1)} %shard_map.117), channel_id=1, replica_groups=mesh['gx'=32,'gz'=8,'gc'=2] {'gz'}, dimensions={0} | all-to-all | bytes 327680 | tf_op jit(solution)/shard_map/all_to_all | solution.py:484
  100.0 0.9 shard_map.118
  100.9 8.2 %all-to-all-start.2 = ((bf16[32,80,128]{2,1,0:T(8,128)(2,1)}), bf16[32,80,128]{2,1,0:T(8,128)(2,1)S(1)}, u32[]{:S(2)}, u32[]{:S(2)}) async-start(bf16[32,80,128]{2,1,0:T(8,128)(2,1)} %shard_map.118), calls=%async_computation.2 | async-start | bytes 1310720 | tf_op jit(solution)/shard_map/all_to_all | solution.py:487
  109.1 4.7 %collective-permute-start.9 = (bf16[32,128]{1,0:T(8,128)(2,1)S(1)}, bf16[32,128]{1,0:T(8,128)(2,1)S(1)}, u32[]{:S(2)}, u32[]{:S(2)}) collective-permute-start(bf16[32,128]{1,0:T(8,128)(2,1)S(1)} %get-tuple-element.88), channel_id=1, source_target_pairs={{0,1},{1,2},{2,3},{3,4},{4,5},{5,6},{6,7},{7,8},{8,9},{9,10},{10,1... | collective-permute-start | bytes 24584 | tf_op jit(solution)/shard_map/ppermute | solution.py:19
  113.8 1.9 %collective-permute-start.10 = (bf16[32,128]{1,0:T(8,128)(2,1)S(1)}, bf16[32,128]{1,0:T(8,128)(2,1)S(1)}, u32[]{:S(2)}, u32[]{:S(2)}) collective-permute-start(bf16[32,128]{1,0:T(8,128)(2,1)S(1)} %get-tuple-element.89), channel_id=1, source_target_pairs={{1,0},{2,1},{3,2},{4,3},{5,4},{6,5},{7,6},{8,7},{9,8},{10,9},{11,1... | collective-permute-start | bytes 24584 | tf_op jit(solution)/shard_map/ppermute | solution.py:19
  115.8 3.3 %collective-permute-done.10.yhi_ref.yhi = bf16[32,128]{1,0:T(8,128)(2,1)S(1)} collective-permute-done((bf16[32,128]{1,0:T(8,128)(2,1)S(1)}, bf16[32,128]{1,0:T(8,128)(2,1)S(1)}, u32[]{:S(2)}, u32[]{:S(2)}) %collective-permute-start.10) | collective-permute-done | bytes 8224 | tf_op jit(solution)/shard_map/ppermute | solution.py:19
  119.1 0.1 shard_map.120
  119.2 3.4 %collective-permute-start.11 = (bf16[160,128]{1,0:T(8,128)(2,1)S(1)}, bf16[160,128]{1,0:T(8,128)(2,1)S(1)}, u32[]{:S(2)}, u32[]{:S(2)}) collective-permute-start(bf16[160,128]{1,0:T(8,128)(2,1)S(1)} %get-tuple-element.90), channel_id=1, source_target_pairs={{0,16},{16,32},{32,48},{48,64},{64,80},{80,96},{96,112},{112,128},... | collective-permute-start | bytes 122888 | tf_op jit(solution)/shard_map/ppermute | solution.py:19
  122.7 1.3 collective-permute-start.12
  124.0 1.5 %shard_map.119 = bf16[2,8,32,64]{3,2,1,0:T(8,128)(2,1)} custom-call(bf16[2,10,32,64]{3,2,1,0:T(8,128)(2,1)S(1)} %get-tuple-element.66.refs_6_.enc_ref, bf16[2,10,32,64]{3,2,1,0:T(8,128)(2,1)S(1)} %get-tuple-element.85.lifted_ref, bf16[352,128]{1,0:T(8,128)(2,1)S(1)} %collective-permute-done.6.xlo, bf16[352,128]{1,0:T(8,128)(2,1)S(1)} %collective-permute-done.7.xhi, ...), custom_call_target="tpu_custom_call" | custom-call | flops 1000000 | bytes 10000 | tf_op jit(solution)/shard_map/pallas_call | solution.py:31
  125.4 2.3 %collective-permute-done.12.xhi = bf16[160,128]{1,0:T(8,128)(2,1)S(1)} collective-permute-done((bf16[160,128]{1,0:T(8,128)(2,1)S(1)}, bf16[160,128]{1,0:T(8,128)(2,1)S(1)}, u32[]{:S(2)}, u32[]{:S(2)}) %collective-permute-start.12) | collective-permute-done | bytes 40992 | tf_op jit(solution)/shard_map/ppermute | solution.py:19
  127.7 1.3 shard_map.121
  129.0 3.1 %collective-permute-start.13 = (bf16[32,80,128]{2,1,0:T(8,128)(2,1)S(1)}, bf16[32,80,128]{2,1,0:T(8,128)(2,1)S(1)}, u32[]{:S(2)}, u32[]{:S(2)}) collective-permute-start(bf16[32,80,128]{2,1,0:T(8,128)(2,1)S(1)} %all-to-all-done.2.own_ref), channel_id=1, source_target_pairs={{0,1},{1,0},{2,3},{3,2},{4,5},{5,4},{6,7},{7,6},{8,9},{9,8},{10,11... | collective-permute-start | bytes 1966088 | tf_op jit(solution)/shard_map/ppermute | solution.py:27
  132.1 1.7 %collective-permute-done.13.other_ref = bf16[32,80,128]{2,1,0:T(8,128)(2,1)S(1)} collective-permute-done((bf16[32,80,128]{2,1,0:T(8,128)(2,1)S(1)}, bf16[32,80,128]{2,1,0:T(8,128)(2,1)S(1)}, u32[]{:S(2)}, u32[]{:S(2)}) %collective-permute-start.13) | collective-permute-done | bytes 655392 | tf_op jit(solution)/shard_map/ppermute | solution.py:27
  133.8 1.8 %shard_map.122 = (f32[27,64,64]{2,1,0:T(8,128)}, f32[27,64,128]{2,1,0:T(8,128)}, f32[27,64,128]{2,1,0:T(8,128)}, f32[8,64,128]{2,1,0:T(8,128)}) custom-call(s32[1]{0:T(128)} %bitcast.7.core, bf16[32,80,128]{2,1,0:T(8,128)(2,1)S(1)} %all-to-all-done.2.own_ref, bf16[32,80,128]{2,1,0:T(8,128)(2,1)S(1)} %collective-permute-done.13.other_ref), custom_call_target="tpu_custom_call" | custom-call | flops 1000000 | bytes 10000 | tf_op jit(solution)/shard_map/pallas_call | solution.py:31
  (11 shorter events, 0.0 us)
Async XLA Ops:
  0.6 0.9 copy-start
  1.5 0.9 copy-start.1
  2.9 18.3 %collective-permute-start = (bf16[12,32,128]{2,1,0:T(8,128)(2,1)S(1)}, bf16[12,32,128]{2,1,0:T(8,128)(2,1)S(1)}, u32[]{:S(2)}, u32[]{:S(2)}) collective-permute-start(bf16[12,32,128]{2,1,0:T(8,128)(2,1)S(1)} %get-tuple-element.55), channel_id=1, source_target_pairs={{0,16},{16,32},{32,48},{48,64},{64,80},{80,96},{96,112},{112,128},... | collective-permute-start | bytes 294920 | tf_op jit(solution)/shard_map/ppermute | solution.py:19
  6.9 14.3 %collective-permute-start.1 = (bf16[12,32,128]{2,1,0:T(8,128)(2,1)S(1)}, bf16[12,32,128]{2,1,0:T(8,128)(2,1)S(1)}, u32[]{:S(2)}, u32[]{:S(2)}) collective-permute-start(bf16[12,32,128]{2,1,0:T(8,128)(2,1)S(1)} %get-tuple-element.56), channel_id=1, source_target_pairs={{16,0},{32,16},{48,32},{64,48},{80,64},{96,80},{112,96},{128,112},... | collective-permute-start | bytes 294920 | tf_op jit(solution)/shard_map/ppermute | solution.py:19
  8.2 6.3 %collective-permute-start.2 = (bf16[4,32,128]{2,1,0:T(8,128)(2,1)S(1)}, bf16[4,32,128]{2,1,0:T(8,128)(2,1)S(1)}, u32[]{:S(2)}, u32[]{:S(2)}) collective-permute-start(bf16[4,32,128]{2,1,0:T(8,128)(2,1)S(1)} %get-tuple-element.57), channel_id=1, source_target_pairs={{0,32},{16,48},{32,64},{48,80},{64,96},{80,112},{96,128},{112,144}... | collective-permute-start | bytes 98312 | tf_op jit(solution)/shard_map/ppermute | solution.py:19
  13.2 8.0 %collective-permute-start.3 = (bf16[4,32,128]{2,1,0:T(8,128)(2,1)S(1)}, bf16[4,32,128]{2,1,0:T(8,128)(2,1)S(1)}, u32[]{:S(2)}, u32[]{:S(2)}) collective-permute-start(bf16[4,32,128]{2,1,0:T(8,128)(2,1)S(1)} %get-tuple-element.58), channel_id=1, source_target_pairs={{32,0},{48,16},{64,32},{80,48},{96,64},{112,80},{128,96},{144,112}... | collective-permute-start | bytes 98312 | tf_op jit(solution)/shard_map/ppermute | solution.py:19
  21.5 13.5 %collective-permute-start.4 = (bf16[6,5,32,128]{3,2,1,0:T(8,128)(2,1)S(1)}, bf16[6,5,32,128]{3,2,1,0:T(8,128)(2,1)S(1)}, u32[]{:S(2)}, u32[]{:S(2)}) collective-permute-start(bf16[6,5,32,128]{3,2,1,0:T(8,128)(2,1)S(1)} %get-tuple-element.59), channel_id=1, source_target_pairs={{0,1},{1,2},{2,3},{3,4},{4,5},{5,6},{6,7},{7,8},{8,9},{9,10},{10,1... | collective-permute-start | bytes 737288 | tf_op jit(solution)/shard_map/ppermute | solution.py:19
  27.8 7.5 %collective-permute-start.5 = (bf16[6,5,32,128]{3,2,1,0:T(8,128)(2,1)S(1)}, bf16[6,5,32,128]{3,2,1,0:T(8,128)(2,1)S(1)}, u32[]{:S(2)}, u32[]{:S(2)}) collective-permute-start(bf16[6,5,32,128]{3,2,1,0:T(8,128)(2,1)S(1)} %get-tuple-element.60.first_ref), channel_id=1, source_target_pairs={{1,0},{2,1},{3,2},{4,3},{5,4},{6,5},{7,6},{8,7},{9,8},{10,9},{11,1... | collective-permute-start | bytes 737288 | tf_op jit(solution)/shard_map/ppermute | solution.py:19
  29.8 1.0 copy-start.2
  30.8 1.0 copy-start.3
  31.9 1.0 copy-start.4
  32.9 0.9 copy-start.5
  41.3 3.4 %collective-permute-start.6 = (bf16[352,128]{1,0:T(8,128)(2,1)S(1)}, bf16[352,128]{1,0:T(8,128)(2,1)S(1)}, u32[]{:S(2)}, u32[]{:S(2)}) collective-permute-start(bf16[352,128]{1,0:T(8,128)(2,1)S(1)} %get-tuple-element.72), channel_id=1, source_target_pairs={{0,16},{16,32},{32,48},{48,64},{64,80},{80,96},{96,112},{112,128},... | collective-permute-start | bytes 270344 | tf_op jit(solution)/shard_map/ppermute | solution.py:19
  43.2 8.0 %collective-permute-start.7 = (bf16[352,128]{1,0:T(8,128)(2,1)S(1)}, bf16[352,128]{1,0:T(8,128)(2,1)S(1)}, u32[]{:S(2)}, u32[]{:S(2)}) collective-permute-start(bf16[352,128]{1,0:T(8,128)(2,1)S(1)} %get-tuple-element.73), channel_id=1, source_target_pairs={{16,0},{32,16},{48,32},{64,48},{80,64},{96,80},{112,96},{128,112},... | collective-permute-start | bytes 270344 | tf_op jit(solution)/shard_map/ppermute | solution.py:19
  52.3 4.0 %collective-permute-start.8 = (bf16[32,80,128]{2,1,0:T(8,128)(2,1)S(1)}, bf16[32,80,128]{2,1,0:T(8,128)(2,1)S(1)}, u32[]{:S(2)}, u32[]{:S(2)}) collective-permute-start(bf16[32,80,128]{2,1,0:T(8,128)(2,1)S(1)} %get-tuple-element.81), channel_id=1, source_target_pairs={{0,1},{1,0},{2,3},{3,2},{4,5},{5,4},{6,7},{7,6},{8,9},{9,8},{10,11... | collective-permute-start | bytes 1966088 | tf_op jit(solution)/shard_map/ppermute | solution.py:27
  100.9 28.1 %all-to-all-start.2 = ((bf16[32,80,128]{2,1,0:T(8,128)(2,1)}), bf16[32,80,128]{2,1,0:T(8,128)(2,1)S(1)}, u32[]{:S(2)}, u32[]{:S(2)}) async-start(bf16[32,80,128]{2,1,0:T(8,128)(2,1)} %shard_map.118), calls=%async_computation.2 | async-start | bytes 1310720 | tf_op jit(solution)/shard_map/all_to_all | solution.py:487
  109.1 6.6 %collective-permute-start.9 = (bf16[32,128]{1,0:T(8,128)(2,1)S(1)}, bf16[32,128]{1,0:T(8,128)(2,1)S(1)}, u32[]{:S(2)}, u32[]{:S(2)}) collective-permute-start(bf16[32,128]{1,0:T(8,128)(2,1)S(1)} %get-tuple-element.88), channel_id=1, source_target_pairs={{0,1},{1,2},{2,3},{3,4},{4,5},{5,6},{6,7},{7,8},{8,9},{9,10},{10,1... | collective-permute-start | bytes 24584 | tf_op jit(solution)/shard_map/ppermute | solution.py:19
  113.8 5.3 %collective-permute-start.10 = (bf16[32,128]{1,0:T(8,128)(2,1)S(1)}, bf16[32,128]{1,0:T(8,128)(2,1)S(1)}, u32[]{:S(2)}, u32[]{:S(2)}) collective-permute-start(bf16[32,128]{1,0:T(8,128)(2,1)S(1)} %get-tuple-element.89), channel_id=1, source_target_pairs={{1,0},{2,1},{3,2},{4,3},{5,4},{6,5},{7,6},{8,7},{9,8},{10,9},{11,1... | collective-permute-start | bytes 24584 | tf_op jit(solution)/shard_map/ppermute | solution.py:19
  119.2 6.2 %collective-permute-start.11 = (bf16[160,128]{1,0:T(8,128)(2,1)S(1)}, bf16[160,128]{1,0:T(8,128)(2,1)S(1)}, u32[]{:S(2)}, u32[]{:S(2)}) collective-permute-start(bf16[160,128]{1,0:T(8,128)(2,1)S(1)} %get-tuple-element.90), channel_id=1, source_target_pairs={{0,16},{16,32},{32,48},{48,64},{64,80},{80,96},{96,112},{112,128},... | collective-permute-start | bytes 122888 | tf_op jit(solution)/shard_map/ppermute | solution.py:19
  122.7 5.0 %collective-permute-start.12 = (bf16[160,128]{1,0:T(8,128)(2,1)S(1)}, bf16[160,128]{1,0:T(8,128)(2,1)S(1)}, u32[]{:S(2)}, u32[]{:S(2)}) collective-permute-start(bf16[160,128]{1,0:T(8,128)(2,1)S(1)} %get-tuple-element.91), channel_id=1, source_target_pairs={{16,0},{32,16},{48,32},{64,48},{80,64},{96,80},{112,96},{128,112},... | collective-permute-start | bytes 122888 | tf_op jit(solution)/shard_map/ppermute | solution.py:19
  129.0 4.9 %collective-permute-start.13 = (bf16[32,80,128]{2,1,0:T(8,128)(2,1)S(1)}, bf16[32,80,128]{2,1,0:T(8,128)(2,1)S(1)}, u32[]{:S(2)}, u32[]{:S(2)}) collective-permute-start(bf16[32,80,128]{2,1,0:T(8,128)(2,1)S(1)} %all-to-all-done.2.own_ref), channel_id=1, source_target_pairs={{0,1},{1,0},{2,3},{3,2},{4,5},{5,4},{6,7},{7,6},{8,9},{9,8},{10,11... | collective-permute-start | bytes 1966088 | tf_op jit(solution)/shard_map/ppermute | solution.py:27

commit v3 on v2

--- a/solution.py
+++ b/solution.py
@@ -119,7 +119,7 @@
         copy.wait()
 
 
-def stack_kernel(first_ref, enc_ref, low_ref, dec_ref, lift_ref, *refs):
+def stack_kernel(first_ref, second_ref, enc_ref, low_ref, dec_ref, lift_ref, *refs):
     outs, lift_out, (enc, low, dec, sems) = refs[:6], refs[6], refs[7:]
     fetched(sems, (enc_ref, enc), (low_ref, low), (dec_ref, dec), (lift_ref, lift_out))
     for ref, forward, backward in (
@@ -141,7 +141,7 @@
         out2[...] = paired[x]
 
 
-def pack_y_kernel(f_ref, c_ref, xlo, xhi, xlo2, xhi2, lo_ref, hi_ref):
+def pack_y_kernel(f_ref, c_ref, xlo, xhi, xlo2, xhi2, after_ref, lo_ref, hi_ref):
     for first, out in ((0, lo_ref), (3, hi_ref)):
         at = slice(first, first + 5)
         out[0] = xlo[at]
@@ -193,8 +193,8 @@
 
 
 def joined_grad_kernel(c_ref, *refs):
-    (ylo, yhi, xlo, xhi), (w_ref, lift_ref, enc_ref) = refs[:4], refs[4:7]
-    cx_ref, jg_ref, kids_ref, adj_ref, dge_ref, tmp = refs[7:]
+    (ylo, yhi, xlo, xhi), (w_ref, lift_ref) = refs[:4], refs[4:6]
+    cx_ref, jg_ref, kids_ref, adj_ref, tmp = refs[6:]
     cx_ref[1:3, 3:11] = c_ref[...]
     cx_ref[0, 3:11] = xlo[0:8, :, 64:]
     cx_ref[3, 3:11] = xhi[0:8, :, 64:]
@@ -217,8 +217,6 @@
     kids = jnp.concatenate(kids, -1).astype(BF16)
     kids_ref[...] = kids[16:80]
     adj_ref[...] = nn(kids, lift_ref[...].reshape(512, 128))
-    enc = enc_ref[:, 1:9].reshape(512, 64).astype(F32)
-    dge_ref[...] = tn(stacked(cx_ref, 0, 2, 8, True, 2), ztaps(enc, 32, False))
 
 
 def halver(halves):
@@ -231,27 +229,21 @@
     return put
 
 
-def lower_kernel(
-    px, core, inside, w_ref, lift_ref, adj_ref, kids_ref, cx_ref, dge_ref, enc_ref, *refs
-):
-    lg_ref, lifted_ref, keep_ref, send_ref, lo_ref, hi_ref, tmp, halves = refs
-    put = halver(halves)
-
+def lower_kernel(px, inside, w_ref, adj_ref, la_ref, lg_ref):
     def masked(value):
         first, last = value[0:16] * inside[2], value[80:96] * inside[3]
         return jnp.concatenate([first, value[16:80], last], 0).astype(BF16)
 
-    pk = stacked(px, 0, 1, 6, False)
-    pre = combined(nn(pk, w_ref[...]), 16, False)
+    pre = combined(nn(stacked(px, 0, 1, 6, False), w_ref[...]), 16, False)
     sigma = jax.nn.sigmoid(pre)
-    la = masked(pre * sigma)
-    lg = masked(adj_ref[...] * (sigma * (1.0 + pre * (1.0 - sigma))))
-    lg_ref[...] = lg
-    for x, msg in ((0, lo_ref), (1, hi_ref)):
-        msg[0:96] = la
-        msg[96:192] = lg
-        enc = enc_ref[x].reshape(320, 64)
-        msg[192:352] = jnp.concatenate([enc[:160], enc[160:]], -1)
+    la_ref[...] = masked(pre * sigma)
+    lg_ref[...] = masked(adj_ref[...] * (sigma * (1.0 + pre * (1.0 - sigma))))
+
+
+def grads_kernel(px, la_ref, lg_ref, core, lift_ref, kids_ref, cx_ref, enc_ref, *refs):
+    lifted_ref, keep_ref, send_ref, tmp, halves = refs
+    put = halver(halves)
+    la, lg = la_ref[...], lg_ref[...]
     fine = nt(la, lift_ref[...].reshape(512, 128)).astype(BF16).astype(F32)
     for p in range(2):
         for q in range(2):
@@ -265,15 +257,15 @@
                         ]
     lifted_ref[...] = tmp[...].astype(BF16).reshape(2, 10, 32, 64)
     lifted = jnp.concatenate([tmp[32:288], tmp[352:608]], 0)
-    la, lg, pk = la[16:80], lg[16:80], pk[16:80]
-    dgl = tn(stacked(cx_ref, 0, 2, 8, True, 2), ztaps(lifted, 32, False))
+    la, lg = la[16:80], lg[16:80]
+    enc = enc_ref[:, 1:9].reshape(512, 64).astype(F32)
+    joined = ztaps(jnp.concatenate([enc, lifted], -1), 32, False)
+    dec = tn(stacked(cx_ref, 0, 2, 8, True, 2), joined)
     for ab in range(9):
         for c in range(3):
-            cols = slice(64 * c, 64 * c + 64)
-            rows = slice(64 * ab, 64 * ab + 64)
-            both = jnp.concatenate([dge_ref[rows, cols], dgl[rows, cols]], -1)
-            put((3 * ab + c) * 64, both)
-    low = tn(pk, ztaps(lg.astype(F32), 16, True))
+            block = dec[64 * ab : 64 * ab + 64, 128 * c : 128 * c + 128]
+            put((3 * ab + c) * 64, block)
+    low = tn(stacked(px, 0, 1, 4, False, 1), ztaps(lg.astype(F32), 16, True))
     for ab in range(9):
         for c in range(3):
             block = low[64 * ab : 64 * ab + 64, 128 * c : 128 * c + 128]
@@ -297,13 +289,16 @@
     hi_ref[...] = jnp.concatenate([eg_ref[0, 7], eg_ref[1, 7]], -1)
 
 
-def edge_x_kernel(eg_ref, ylo_ref, yhi_ref, lo_ref, hi_ref):
+def edge_x_kernel(eg_ref, enc_ref, la_ref, ylo_ref, yhi_ref, lo_ref, hi_ref):
     for x, out in ((0, lo_ref), (1, hi_ref)):
         cols = slice(64 * x, 64 * x + 64)
         eg = eg_ref[x].reshape(256, 64)
         first = jnp.concatenate([ylo_ref[:, cols], eg[:128]], 0)
         second = jnp.concatenate([eg[128:], yhi_ref[:, cols]], 0)
-        out[...] = jnp.concatenate([first, second], -1)
+        out[0:160] = jnp.concatenate([first, second], -1)
+        enc = enc_ref[x].reshape(320, 64)
+        out[160:320] = jnp.concatenate([enc[:160], enc[160:]], -1)
+        out[320:416] = la_ref[...]
 
 
 def column(rows):
@@ -317,9 +312,9 @@
 def encoder_grad_kernel(lg_ref, xlo, xhi, core, w_ref, slope_ref, jg_ref, fx_ref, *refs):
     eg_ref, keep_ref, send_ref, lo_ref, hi_ref, lx, tmp, halves = refs[2:]
     put = halver(halves)
-    lx[0] = xlo[96:192].reshape(6, 16, 128)
+    lx[0] = xlo[...].reshape(6, 16, 128)
     lx[1] = lg_ref[...].reshape(6, 16, 128)
-    lx[2] = xhi[96:192].reshape(6, 16, 128)
+    lx[2] = xhi[...].reshape(6, 16, 128)
     pg = combined(nt(stacked(lx, 0, 1, 4, True), w_ref[...]), 16, True)
     pg = pg.astype(BF16).astype(F32) * 0.125
     tmp[pl.ds(0, 64, stride=2), :] = pg
@@ -348,14 +343,14 @@
     for p, h in ((1, xlo), (0, xhi)):
         for q in range(2):
             for r in range(2):
-                fine = nt(h[0:96], lift_ref[4 * p + 2 * q + r]).astype(BF16).astype(F32)
+                fine = nt(h[320:416], lift_ref[4 * p + 2 * q + r]).astype(BF16).astype(F32)
                 for j in range(6):
                     y = 2 * j + q - 1
                     if 0 <= y < 10:
                         tx[pl.ds(32 * y + r, 16, stride=2), :] = fine[16 * j : 16 * j + 16]
         lifted = tx[...].astype(BF16).reshape(1, 10, 32, 64)
         x = 0 if p == 1 else 3
-        jx[x : x + 1] = jnp.concatenate([plane(h[192:352]), lifted], -1)
+        jx[x : x + 1] = jnp.concatenate([plane(h[160:320]), lifted], -1)
     weight = w_ref[...]
     for x in range(2):
         out = combined(nt(stacked(jx, x, 1, 8, False), weight), 32, False)
@@ -363,7 +358,7 @@
 
 
 def input_grad_kernel(eg_ref, ylo, yhi, xlo, xhi, w_ref, out_ref, ex):
-    sides = [column(ylo[...]), column(yhi[...]), plane(xlo[...]), plane(xhi[...])]
+    sides = [column(ylo[...]), column(yhi[...]), plane(xlo[0:160]), plane(xhi[0:160])]
     assemble(ex, eg_ref[...], *sides)
     weight = w_ref[...]
     for x in range(2):
@@ -414,8 +409,6 @@
     )
     x_halo = swapped(lo, hi, GX)
     far_halo = [shifted(hi2, GX, 2), shifted(lo2, GX, -2)]
-    edges = call(pack_y_kernel, [((6, 5, 32, 128), BF16)] * 2, [], [f, c, *x_halo, *far_halo])
-    y_halo = swapped(*edges, GY)
     enc_fwd, enc_bwd, low_fwd, low_bwd, dec_fwd, dec_bwd, lift = call(
         stack_kernel,
         [
@@ -433,10 +426,18 @@
             ((27, 64, 128), BF16),
             (pltpu.SemaphoreType.DMA((4,)), None),
         ],
-        [edges[0], encoder_weight, lower_t, decoder_weight, lift_weight],
-        spaces={k: pltpu.HBM for k in range(5)},
+        [*x_halo, encoder_weight, lower_t, decoder_weight, lift_weight],
+        spaces={k: pltpu.HBM for k in range(6)},
         flops=2 * 10**9,
     )
+    edges = call(
+        pack_y_kernel,
+        [((6, 5, 32, 128), BF16)] * 2,
+        [],
+        [f, c, *x_halo, *far_halo, enc_fwd],
+        spaces={6: pltpu.HBM},
+    )
+    y_halo = swapped(*edges, GY)
     fx, encoded, slope, pooled = call(
         encode_kernel,
         [((8, 18, 32, 64), BF16), (tall, BF16), ((512, 64), F32), ((3, 8, 16, 64), BF16)],
@@ -444,28 +445,34 @@
         [f, *y_halo, *x_halo, *far_halo, inside, enc_fwd],
         spaces={7: pltpu.SMEM},
     )
-    cx, jg, kids, adj, dge = call(
+    cx, jg, kids, adj = call(
         joined_grad_kernel,
         [
             ((4, 14, 32, 64), BF16),
             ((512, 64), BF16),
             ((64, 512), BF16),
             ((96, 128), F32),
-            ((576, 192), F32),
         ],
         [((768, 128), F32)],
-        [c, *y_halo, *x_halo, dec_bwd, lift, encoded],
+        [c, *y_halo, *x_halo, dec_bwd, lift],
     )
     half = (size_x, 2560 // size_x, 128)
-    lg, lifted, keep, send, *edges = call(
+    la, lg = call(
         lower_kernel,
-        [((96, 128), BF16), (tall, BF16), (half, LINK), (half, LINK)]
-        + [((352, 128), BF16)] * 2,
+        [((96, 128), BF16)] * 2,
+        [],
+        [pooled, inside, low_fwd, adj],
+        spaces={1: pltpu.SMEM},
+    )
+    halo = swapped(lg, lg, GX)
+    lifted, keep, send = call(
+        grads_kernel,
+        [(tall, BF16), (half, LINK), (half, LINK)],
         [((640, 64), F32), ((2, size_x, 2048 // size_x, 128), LINK)],
-        [pooled, core, inside, low_fwd, lift, adj, kids, cx, dge, encoded],
-        spaces={1: pltpu.SMEM, 2: pltpu.SMEM},
-    )
-    halo = swapped(*edges, GX)
+        [pooled, la, lg, core, lift, kids, cx, encoded],
+        spaces={3: pltpu.SMEM},
+        flops=2 * 10**9,
+    )
     eg, keep, send, *edges = call(
         encoder_grad_kernel,
         [(brick, BF16), (half, LINK), (half, LINK)] + [((32, 128), BF16)] * 2,
@@ -479,15 +486,19 @@
         aliases={8: 1, 9: 2},
     )
     (sums,) = call(add_kernel, [(half, LINK)], [], [keep, partner(send)])
-    sums = lax.all_to_all(sums, "gx", 0, 0)
-    (sums,) = call(sum_kernel, [((size_z,) + half[1:], LINK)], [], [sums])
-    sums = lax.all_to_all(sums, "gz", 0, 0)
-    (sums,) = call(sum_kernel, [(half, LINK)], [], [sums])
     sums, edges = lax.optimization_barrier((sums, edges))
     sums = lax.all_to_all(sums, "gx", 0, 0)
     y_halo = swapped(*edges, GY)
-    edges = call(edge_x_kernel, [((160, 128), BF16)] * 2, [], [eg, *y_halo])
-    eg_halo = [*y_halo, *swapped(*edges, GX)]
+    (sums,) = call(sum_kernel, [((size_z,) + half[1:], LINK)], [], [sums])
+    sums, y_halo = lax.optimization_barrier((sums, y_halo))
+    sums = lax.all_to_all(sums, "gz", 0, 0)
+    edges = call(
+        edge_x_kernel, [((416, 128), BF16)] * 2, [], [eg, encoded, la, *y_halo]
+    )
+    halo = swapped(*edges, GX)
+    (sums,) = call(sum_kernel, [(half, LINK)], [], [sums])
+    sums, halo = lax.optimization_barrier((sums, halo))
+    sums = lax.all_to_all(sums, "gx", 0, 0)
     (decoded,) = call(
         decode_kernel,
         [(brick, BF16)],
@@ -498,7 +509,7 @@
         input_grad_kernel,
         [(brick, BF16)],
         [((4, 10, 32, 64), BF16)],
-        [eg, *eg_halo, enc_bwd],
+        [eg, *y_halo, *halo, enc_bwd],
     )
     sums, decoded, input_grad = lax.optimization_barrier((sums, decoded, input_grad))
     encoder_gradient, decoder_gradient, lower_gradient, lift_gradient = call(

time: 136 us -> 140 us (1.029)
  blocking collectives: 43.5 us -> 0 us
  starting transfers between devices: 47.6 us -> 77.1 us
  waiting for transfers between devices: 23 us -> 35.9 us
  Pallas kernels: 14.9 us -> 17.3 us
  local copies, waits for them, and re-layouts: 5.74 us -> 7.26 us
    all_to_all x2 -> x0, blocking collectives: 43.5 us -> none  [the longest x1 23.5 us: per_device(): sums = lax.all_to_all(sums, 'gx', 0, 0)]
    all_to_all x1 -> x2, waiting for transfers between devices: 0.01 us -> 21.5 us  [per_device(): sums = lax.all_to_all(sums, 'gx', 0, 0)]
    all_to_all x0 -> x1, starting transfers between devices: none -> 10.1 us  [per_device(): sums = lax.all_to_all(sums, 'gz', 0, 0)]
    ppermute x12, waiting for transfers between devices: 19.2 us -> 9.21 us  [shifted(): return lax.ppermute(piece, axes, pairs)]
    all_to_all x1 -> x2, starting transfers between devices: 8.21 us -> 18 us  [per_device(): sums = lax.all_to_all(sums, 'gx', 0, 0)]
    ppermute x2, starting transfers between devices: 5.07 us -> 11 us  [partner(): return lax.ppermute(piece, 'gc', [(0, 1), (1, 0)])]
    ppermute x12, starting transfers between devices: 34.3 us -> 38 us  [shifted(): return lax.ppermute(piece, axes, pairs)]
    pallas_call x14 -> x15, Pallas kernels: 14.9 us -> 17.3 us  [call(): pl.pallas_call(kernel, out_shape=[jax.ShapeDtypeStruct(s, d) for s, d in...]
  transfers between devices with their start and end apart: 15 -> 17, of which waited for: 8 -> 9; matrix products, arithmetic and copies ran while one was open for 0% -> 0% of each run, Pallas kernels for 3% -> 5%
where the time goes in v3:
time: 140 us; the launch traced here: 138 us
  starting transfers between devices  77.1 us (55%)
  waiting for transfers between devices  35.9 us (26%)
  Pallas kernels  17.3 us (12%)
  local copies, waits for them, and re-layouts  7.26 us (5%)
    ppermute x12, starting transfers between devices, shifted(): return lax.ppermute(piece, axes, pairs)  38 us
    all_to_all x2, waiting for transfers between devices, per_device(): sums = lax.all_to_all(sums, 'gx', 0, 0)  21.5 us
    all_to_all x2, starting transfers between devices, per_device(): sums = lax.all_to_all(sums, 'gx', 0, 0)  18 us
    pallas_call x15, Pallas kernels, call(): pl.pallas_call(kernel, out_shape=[jax.ShapeDtypeStruct(s, d) for s, d in...  17.3 us
    ppermute x2, starting transfers between devices, partner(): return lax.ppermute(piece, 'gc', [(0, 1), (1, 0)])  11 us
    all_to_all x1, starting transfers between devices, per_device(): sums = lax.all_to_all(sums, 'gz', 0, 0)  10.1 us
    ppermute x12, waiting for transfers between devices, shifted(): return lax.ppermute(piece, axes, pairs)  9.21 us
    unnamed x20, local copies, waits for them, and re-layouts  7.26 us
  transfers between devices with their start and end apart: 17, of which 9 were waited for; matrix products, arithmetic and copies ran while one was open for 0% of the time, Pallas kernels for 5%

profile of v3, /device:TPU:1, one launch (start us, length us, event | category | flops | bytes accessed | tf_op | source)
XLA Modules:
  0.0 138.5 jit_solution(16913546732257383560)
XLA Ops:
  0.6 0.9 copy-done.4
  1.5 0.9 copy-done.5
  2.4 0.4 shard_map.109
  2.9 4.0 %collective-permute-start = (bf16[12,32,128]{2,1,0:T(8,128)(2,1)S(1)}, bf16[12,32,128]{2,1,0:T(8,128)(2,1)S(1)}, u32[]{:S(2)}, u32[]{:S(2)}) collective-permute-start(bf16[12,32,128]{2,1,0:T(8,128)(2,1)S(1)} %get-tuple-element.59), channel_id=1, source_target_pairs={{0,16},{16,32},{32,48},{48,64},{64,80},{80,96},{96,112},{112,128},... | collective-permute-start | bytes 294920 | tf_op jit(solution)/shard_map/ppermute | solution.py:19
  6.9 1.3 collective-permute-start.1
  8.2 5.0 %collective-permute-start.2 = (bf16[4,32,128]{2,1,0:T(8,128)(2,1)S(1)}, bf16[4,32,128]{2,1,0:T(8,128)(2,1)S(1)}, u32[]{:S(2)}, u32[]{:S(2)}) collective-permute-start(bf16[4,32,128]{2,1,0:T(8,128)(2,1)S(1)} %get-tuple-element.61), channel_id=1, source_target_pairs={{0,32},{16,48},{32,64},{48,80},{64,96},{80,112},{96,128},{112,144}... | collective-permute-start | bytes 98312 | tf_op jit(solution)/shard_map/ppermute | solution.py:19
  13.2 1.3 collective-permute-start.3
  14.6 1.0 copy-done.6
  15.6 1.0 copy-done.7
  16.6 1.0 copy-done.8
  17.6 0.9 copy-done.9
  18.5 1.3 shard_map.110
  19.8 1.4 %collective-permute-done.3.xhi2 = bf16[4,32,128]{2,1,0:T(8,128)(2,1)S(1)} collective-permute-done((bf16[4,32,128]{2,1,0:T(8,128)(2,1)S(1)}, bf16[4,32,128]{2,1,0:T(8,128)(2,1)S(1)}, u32[]{:S(2)}, u32[]{:S(2)}) %collective-permute-start.3) | collective-permute-done | bytes 32800 | tf_op jit(solution)/shard_map/ppermute | solution.py:19
  21.2 1.0 shard_map.111
  22.3 6.3 %collective-permute-start.4 = (bf16[6,5,32,128]{3,2,1,0:T(8,128)(2,1)}, bf16[6,5,32,128]{3,2,1,0:T(8,128)(2,1)S(1)}, u32[]{:S(2)}, u32[]{:S(2)}) collective-permute-start(bf16[6,5,32,128]{3,2,1,0:T(8,128)(2,1)} %get-tuple-element.64), channel_id=1, source_target_pairs={{0,1},{1,2},{2,3},{3,4},{4,5},{5,6},{6,7},{7,8},{8,9},{9,10},{10,1... | collective-permute-start | bytes 737288 | tf_op jit(solution)/shard_map/ppermute | solution.py:19
  28.5 1.9 %collective-permute-start.5 = (bf16[6,5,32,128]{3,2,1,0:T(8,128)(2,1)}, bf16[6,5,32,128]{3,2,1,0:T(8,128)(2,1)S(1)}, u32[]{:S(2)}, u32[]{:S(2)}) collective-permute-start(bf16[6,5,32,128]{3,2,1,0:T(8,128)(2,1)} %get-tuple-element.65), channel_id=1, source_target_pairs={{1,0},{2,1},{3,2},{4,3},{5,4},{6,5},{7,6},{8,7},{9,8},{10,9},{11,1... | collective-permute-start | bytes 737288 | tf_op jit(solution)/shard_map/ppermute | solution.py:19
  30.5 1.4 %collective-permute-done.4.ylo.refs_0_ = bf16[6,5,32,128]{3,2,1,0:T(8,128)(2,1)S(1)} collective-permute-done((bf16[6,5,32,128]{3,2,1,0:T(8,128)(2,1)}, bf16[6,5,32,128]{3,2,1,0:T(8,128)(2,1)S(1)}, u32[]{:S(2)}, u32[]{:S(2)}) %collective-permute-start.4) | collective-permute-done | bytes 245792 | tf_op jit(solution)/shard_map/ppermute | solution.py:19
  32.0 4.3 %collective-permute-done.5.yhi.refs_1_ = bf16[6,5,32,128]{3,2,1,0:T(8,128)(2,1)S(1)} collective-permute-done((bf16[6,5,32,128]{3,2,1,0:T(8,128)(2,1)}, bf16[6,5,32,128]{3,2,1,0:T(8,128)(2,1)S(1)}, u32[]{:S(2)}, u32[]{:S(2)}) %collective-permute-start.5) | collective-permute-done | bytes 245792 | tf_op jit(solution)/shard_map/ppermute | solution.py:19
  36.3 0.8 copy-done.1
  37.0 0.8 copy-done.3
  37.8 2.5 %shard_map.112 = (bf16[8,18,32,64]{3,2,1,0:T(8,128)(2,1)S(1)}, bf16[2,10,32,64]{3,2,1,0:T(8,128)(2,1)S(1)}, f32[512,64]{1,0:T(8,128)S(1)}, bf16[3,8,16,64]{3,2,1,0:T(8,128)(2,1)S(1)}) custom-call(bf16[2,8,32,64]{3,2,1,0:T(8,128)(2,1)S(1)} %get-tuple-element.57.f_ref, bf16[6,5,32,128]{3,2,1,0:T(8,128)(2,1)S(1)} %collective-permute-done.4.ylo.refs_0_, ...), custom_call_target="tpu_custom_call" | custom-call | flops 1000000 | bytes 10000 | tf_op jit(solution)/shard_map/pallas_call | solution.py:31
  40.3 1.4 shard_map.113
  41.7 0.8 shard_map.114
  42.5 1.3 collective-permute-start.7
  43.8 4.0 %collective-permute-start.6 = (bf16[96,128]{1,0:T(8,128)(2,1)S(1)}, bf16[96,128]{1,0:T(8,128)(2,1)S(1)}, u32[]{:S(2)}, u32[]{:S(2)}) collective-permute-start(bf16[96,128]{1,0:T(8,128)(2,1)S(1)} %get-tuple-element.71.lg_ref), channel_id=1, source_target_pairs={{0,16},{16,32},{32,48},{48,64},{64,80},{80,96},{96,112},{112,128},... | collective-permute-start | bytes 73736 | tf_op jit(solution)/shard_map/ppermute | solution.py:19
  47.8 1.3 shard_map.115
  49.2 1.1 shard_map.116
  50.3 1.9 %collective-permute-start.8 = (bf16[32,80,128]{2,1,0:T(8,128)(2,1)S(1)}, bf16[32,80,128]{2,1,0:T(8,128)(2,1)S(1)}, u32[]{:S(2)}, u32[]{:S(2)}) collective-permute-start(bf16[32,80,128]{2,1,0:T(8,128)(2,1)S(1)} %get-tuple-element.83), channel_id=1, source_target_pairs={{0,1},{1,0},{2,3},{3,2},{4,5},{5,4},{6,7},{7,6},{8,9},{9,8},{10,11... | collective-permute-start | bytes 1966088 | tf_op jit(solution)/shard_map/ppermute | solution.py:27
  52.3 2.1 %collective-permute-done.8.b_ref = bf16[32,80,128]{2,1,0:T(8,128)(2,1)S(1)} collective-permute-done((bf16[32,80,128]{2,1,0:T(8,128)(2,1)S(1)}, bf16[32,80,128]{2,1,0:T(8,128)(2,1)S(1)}, u32[]{:S(2)}, u32[]{:S(2)}) %collective-permute-start.8) | collective-permute-done | bytes 655392 | tf_op jit(solution)/shard_map/ppermute | solution.py:27
  54.3 1.0 shard_map.117
  55.3 11.8 %all-to-all-start = ((bf16[32,80,128]{2,1,0:T(8,128)(2,1)}), bf16[32,80,128]{2,1,0:T(8,128)(2,1)S(1)}, u32[]{:S(2)}, u32[]{:S(2)}) async-start(bf16[32,80,128]{2,1,0:T(8,128)(2,1)} %shard_map.117), calls=%async_computation | async-start | bytes 1310720 | tf_op jit(solution)/shard_map/all_to_all | solution.py:490
  67.2 4.3 %collective-permute-start.9 = (bf16[32,128]{1,0:T(8,128)(2,1)S(1)}, bf16[32,128]{1,0:T(8,128)(2,1)S(1)}, u32[]{:S(2)}, u32[]{:S(2)}) collective-permute-start(bf16[32,128]{1,0:T(8,128)(2,1)S(1)} %get-tuple-element.87), channel_id=1, source_target_pairs={{0,1},{1,2},{2,3},{3,4},{4,5},{5,6},{6,7},{7,8},{8,9},{9,10},{10,1... | collective-permute-start | bytes 24584 | tf_op jit(solution)/shard_map/ppermute | solution.py:19
  71.5 1.9 %collective-permute-start.10 = (bf16[32,128]{1,0:T(8,128)(2,1)S(1)}, bf16[32,128]{1,0:T(8,128)(2,1)S(1)}, u32[]{:S(2)}, u32[]{:S(2)}) collective-permute-start(bf16[32,128]{1,0:T(8,128)(2,1)S(1)} %get-tuple-element.88), channel_id=1, source_target_pairs={{1,0},{2,1},{3,2},{4,3},{5,4},{6,5},{7,6},{8,7},{9,8},{10,9},{11,1... | collective-permute-start | bytes 24584 | tf_op jit(solution)/shard_map/ppermute | solution.py:19
  73.4 10.5 %all-to-all-done.parts_ref = bf16[32,80,128]{2,1,0:T(8,128)(2,1)S(1)} async-done(((bf16[32,80,128]{2,1,0:T(8,128)(2,1)}), bf16[32,80,128]{2,1,0:T(8,128)(2,1)S(1)}, u32[]{:S(2)}, u32[]{:S(2)}) %all-to-all-start) | async-done | bytes 655392 | tf_op jit(solution)/shard_map/all_to_all | solution.py:490
  83.9 0.8 shard_map.118
  84.7 10.1 %all-to-all-start.1 = ((bf16[8,80,128]{2,1,0:T(8,128)(2,1)}), bf16[8,80,128]{2,1,0:T(8,128)(2,1)S(1)}, u32[]{:S(2)}, u32[]{:S(2)}) async-start(bf16[8,80,128]{2,1,0:T(8,128)(2,1)} %shard_map.118), calls=%async_computation.1 | async-start | bytes 327680 | tf_op jit(solution)/shard_map/all_to_all | solution.py:494
  94.9 5.4 %collective-permute-start.11 = (bf16[416,128]{1,0:T(8,128)(2,1)S(1)}, bf16[416,128]{1,0:T(8,128)(2,1)S(1)}, u32[]{:S(2)}, u32[]{:S(2)}) collective-permute-start(bf16[416,128]{1,0:T(8,128)(2,1)S(1)} %get-tuple-element.93), channel_id=1, source_target_pairs={{0,16},{16,32},{32,48},{48,64},{64,80},{80,96},{96,112},{112,128},... | collective-permute-start | bytes 319496 | tf_op jit(solution)/shard_map/ppermute | solution.py:19
  100.3 1.3 collective-permute-start.12
  101.6 1.4 %all-to-all-done.1.parts_ref = bf16[8,80,128]{2,1,0:T(8,128)(2,1)S(1)} async-done(((bf16[8,80,128]{2,1,0:T(8,128)(2,1)}), bf16[8,80,128]{2,1,0:T(8,128)(2,1)S(1)}, u32[]{:S(2)}, u32[]{:S(2)}) %all-to-all-start.1) | async-done | bytes 163872 | tf_op jit(solution)/shard_map/all_to_all | solution.py:494
  103.1 0.9 shard_map.119
  104.0 2.1 %collective-permute-done.12.xhi = bf16[416,128]{1,0:T(8,128)(2,1)S(1)} collective-permute-done((bf16[416,128]{1,0:T(8,128)(2,1)S(1)}, bf16[416,128]{1,0:T(8,128)(2,1)S(1)}, u32[]{:S(2)}, u32[]{:S(2)}) %collective-permute-start.12) | collective-permute-done | bytes 106528 | tf_op jit(solution)/shard_map/ppermute | solution.py:19
  106.1 6.1 %all-to-all-start.2 = ((bf16[32,80,128]{2,1,0:T(8,128)(2,1)}), bf16[32,80,128]{2,1,0:T(8,128)(2,1)S(1)}, u32[]{:S(2)}, u32[]{:S(2)}) async-start(bf16[32,80,128]{2,1,0:T(8,128)(2,1)} %shard_map.119), calls=%async_computation.2 | async-start | bytes 1310720 | tf_op jit(solution)/shard_map/all_to_all | solution.py:501
  112.2 1.3 shard_map.122
  113.5 1.5 %shard_map.121 = bf16[2,8,32,64]{3,2,1,0:T(8,128)(2,1)} custom-call(bf16[2,10,32,64]{3,2,1,0:T(8,128)(2,1)S(1)} %get-tuple-element.79.enc_ref, bf16[2,10,32,64]{3,2,1,0:T(8,128)(2,1)S(1)} %get-tuple-element.96.lifted_ref, bf16[416,128]{1,0:T(8,128)(2,1)S(1)} %collective-permute-done.11.xlo, bf16[416,128]{1,0:T(8,128)(2,1)S(1)} %collective-permute-done.12.xhi, ...), custom_call_target="tpu_custom_call" | custom-call | flops 1000000 | bytes 10000 | tf_op jit(solution)/shard_map/pallas_call | solution.py:31
  114.9 11.0 %all-to-all-done.2.own_ref = bf16[32,80,128]{2,1,0:T(8,128)(2,1)S(1)} async-done(((bf16[32,80,128]{2,1,0:T(8,128)(2,1)}), bf16[32,80,128]{2,1,0:T(8,128)(2,1)S(1)}, u32[]{:S(2)}, u32[]{:S(2)}) %all-to-all-start.2) | async-done | bytes 655392 | tf_op jit(solution)/shard_map/all_to_all | solution.py:501
  125.9 9.1 %collective-permute-start.13 = (bf16[32,80,128]{2,1,0:T(8,128)(2,1)S(1)}, bf16[32,80,128]{2,1,0:T(8,128)(2,1)S(1)}, u32[]{:S(2)}, u32[]{:S(2)}) collective-permute-start(bf16[32,80,128]{2,1,0:T(8,128)(2,1)S(1)} %all-to-all-done.2.own_ref), channel_id=1, source_target_pairs={{0,1},{1,0},{2,3},{3,2},{4,5},{5,4},{6,7},{7,6},{8,9},{9,8},{10,11... | collective-permute-start | bytes 1966088 | tf_op jit(solution)/shard_map/ppermute | solution.py:27
  135.0 1.7 %collective-permute-done.13.other_ref = bf16[32,80,128]{2,1,0:T(8,128)(2,1)S(1)} collective-permute-done((bf16[32,80,128]{2,1,0:T(8,128)(2,1)S(1)}, bf16[32,80,128]{2,1,0:T(8,128)(2,1)S(1)}, u32[]{:S(2)}, u32[]{:S(2)}) %collective-permute-start.13) | collective-permute-done | bytes 655392 | tf_op jit(solution)/shard_map/ppermute | solution.py:27
  136.7 1.8 %shard_map.123 = (f32[27,64,64]{2,1,0:T(8,128)}, f32[27,64,128]{2,1,0:T(8,128)}, f32[27,64,128]{2,1,0:T(8,128)}, f32[8,64,128]{2,1,0:T(8,128)}) custom-call(s32[1]{0:T(128)} %bitcast.7.core, bf16[32,80,128]{2,1,0:T(8,128)(2,1)S(1)} %all-to-all-done.2.own_ref, bf16[32,80,128]{2,1,0:T(8,128)(2,1)S(1)} %collective-permute-done.13.other_ref), custom_call_target="tpu_custom_call" | custom-call | flops 1000000 | bytes 10000 | tf_op jit(solution)/shard_map/pallas_call | solution.py:31
  (22 shorter events, 0.3 us)
Async XLA Ops:
  0.6 0.9 copy-start.4
  1.5 0.9 copy-start.5
  2.9 11.7 %collective-permute-start = (bf16[12,32,128]{2,1,0:T(8,128)(2,1)S(1)}, bf16[12,32,128]{2,1,0:T(8,128)(2,1)S(1)}, u32[]{:S(2)}, u32[]{:S(2)}) collective-permute-start(bf16[12,32,128]{2,1,0:T(8,128)(2,1)S(1)} %get-tuple-element.59), channel_id=1, source_target_pairs={{0,16},{16,32},{32,48},{48,64},{64,80},{80,96},{96,112},{112,128},... | collective-permute-start | bytes 294920 | tf_op jit(solution)/shard_map/ppermute | solution.py:19
  6.9 7.6 %collective-permute-start.1 = (bf16[12,32,128]{2,1,0:T(8,128)(2,1)S(1)}, bf16[12,32,128]{2,1,0:T(8,128)(2,1)S(1)}, u32[]{:S(2)}, u32[]{:S(2)}) collective-permute-start(bf16[12,32,128]{2,1,0:T(8,128)(2,1)S(1)} %get-tuple-element.60), channel_id=1, source_target_pairs={{16,0},{32,16},{48,32},{64,48},{80,64},{96,80},{112,96},{128,112},... | collective-permute-start | bytes 294920 | tf_op jit(solution)/shard_map/ppermute | solution.py:19
  8.2 11.6 %collective-permute-start.2 = (bf16[4,32,128]{2,1,0:T(8,128)(2,1)S(1)}, bf16[4,32,128]{2,1,0:T(8,128)(2,1)S(1)}, u32[]{:S(2)}, u32[]{:S(2)}) collective-permute-start(bf16[4,32,128]{2,1,0:T(8,128)(2,1)S(1)} %get-tuple-element.61), channel_id=1, source_target_pairs={{0,32},{16,48},{32,64},{48,80},{64,96},{80,112},{96,128},{112,144}... | collective-permute-start | bytes 98312 | tf_op jit(solution)/shard_map/ppermute | solution.py:19
  13.2 8.0 %collective-permute-start.3 = (bf16[4,32,128]{2,1,0:T(8,128)(2,1)S(1)}, bf16[4,32,128]{2,1,0:T(8,128)(2,1)S(1)}, u32[]{:S(2)}, u32[]{:S(2)}) collective-permute-start(bf16[4,32,128]{2,1,0:T(8,128)(2,1)S(1)} %get-tuple-element.62), channel_id=1, source_target_pairs={{32,0},{48,16},{64,32},{80,48},{96,64},{112,80},{128,96},{144,112}... | collective-permute-start | bytes 98312 | tf_op jit(solution)/shard_map/ppermute | solution.py:19
  14.6 1.0 copy-start.6
  15.6 1.0 copy-start.7
  16.6 1.0 copy-start.8
  17.6 0.9 copy-start.9
  19.8 12.2 %copy-start = (bf16[4,32,128]{2,1,0:T(8,128)(2,1)}, bf16[4,32,128]{2,1,0:T(8,128)(2,1)S(1)}, u32[]{:S(2)}) copy-start(bf16[4,32,128]{2,1,0:T(8,128)(2,1)S(1)} %collective-permute-done.2.xlo2) | copy-start | bytes 98308
  21.2 10.8 %copy-start.2 = (bf16[4,32,128]{2,1,0:T(8,128)(2,1)}, bf16[4,32,128]{2,1,0:T(8,128)(2,1)S(1)}, u32[]{:S(2)}) copy-start(bf16[4,32,128]{2,1,0:T(8,128)(2,1)S(1)} %collective-permute-done.3.xhi2) | copy-start | bytes 98308
  22.3 9.7 %collective-permute-start.4 = (bf16[6,5,32,128]{3,2,1,0:T(8,128)(2,1)}, bf16[6,5,32,128]{3,2,1,0:T(8,128)(2,1)S(1)}, u32[]{:S(2)}, u32[]{:S(2)}) collective-permute-start(bf16[6,5,32,128]{3,2,1,0:T(8,128)(2,1)} %get-tuple-element.64), channel_id=1, source_target_pairs={{0,1},{1,2},{2,3},{3,4},{4,5},{5,6},{6,7},{7,8},{8,9},{9,10},{10,1... | collective-permute-start | bytes 737288 | tf_op jit(solution)/shard_map/ppermute | solution.py:19
  28.5 7.7 %collective-permute-start.5 = (bf16[6,5,32,128]{3,2,1,0:T(8,128)(2,1)}, bf16[6,5,32,128]{3,2,1,0:T(8,128)(2,1)S(1)}, u32[]{:S(2)}, u32[]{:S(2)}) collective-permute-start(bf16[6,5,32,128]{3,2,1,0:T(8,128)(2,1)} %get-tuple-element.65), channel_id=1, source_target_pairs={{1,0},{2,1},{3,2},{4,3},{5,4},{6,5},{7,6},{8,7},{9,8},{10,9},{11,1... | collective-permute-start | bytes 737288 | tf_op jit(solution)/shard_map/ppermute | solution.py:19
  36.3 0.8 copy-start.1
  37.0 0.8 copy-start.3
  42.5 6.7 %collective-permute-start.7 = (bf16[96,128]{1,0:T(8,128)(2,1)S(1)}, bf16[96,128]{1,0:T(8,128)(2,1)S(1)}, u32[]{:S(2)}, u32[]{:S(2)}) collective-permute-start(bf16[96,128]{1,0:T(8,128)(2,1)S(1)} %get-tuple-element.71.lg_ref), channel_id=1, source_target_pairs={{16,0},{32,16},{48,32},{64,48},{80,64},{96,80},{112,96},{128,112},... | collective-permute-start | bytes 73736 | tf_op jit(solution)/shard_map/ppermute | solution.py:19
  43.8 5.4 %collective-permute-start.6 = (bf16[96,128]{1,0:T(8,128)(2,1)S(1)}, bf16[96,128]{1,0:T(8,128)(2,1)S(1)}, u32[]{:S(2)}, u32[]{:S(2)}) collective-permute-start(bf16[96,128]{1,0:T(8,128)(2,1)S(1)} %get-tuple-element.71.lg_ref), channel_id=1, source_target_pairs={{0,16},{16,32},{32,48},{48,64},{64,80},{80,96},{96,112},{112,128},... | collective-permute-start | bytes 73736 | tf_op jit(solution)/shard_map/ppermute | solution.py:19
  50.3 4.0 %collective-permute-start.8 = (bf16[32,80,128]{2,1,0:T(8,128)(2,1)S(1)}, bf16[32,80,128]{2,1,0:T(8,128)(2,1)S(1)}, u32[]{:S(2)}, u32[]{:S(2)}) collective-permute-start(bf16[32,80,128]{2,1,0:T(8,128)(2,1)S(1)} %get-tuple-element.83), channel_id=1, source_target_pairs={{0,1},{1,0},{2,3},{3,2},{4,5},{5,4},{6,7},{7,6},{8,9},{9,8},{10,11... | collective-permute-start | bytes 1966088 | tf_op jit(solution)/shard_map/ppermute | solution.py:27
  55.3 28.6 %all-to-all-start = ((bf16[32,80,128]{2,1,0:T(8,128)(2,1)}), bf16[32,80,128]{2,1,0:T(8,128)(2,1)S(1)}, u32[]{:S(2)}, u32[]{:S(2)}) async-start(bf16[32,80,128]{2,1,0:T(8,128)(2,1)} %shard_map.117), calls=%async_computation | async-start | bytes 1310720 | tf_op jit(solution)/shard_map/all_to_all | solution.py:490
  67.2 17.5 %collective-permute-start.9 = (bf16[32,128]{1,0:T(8,128)(2,1)S(1)}, bf16[32,128]{1,0:T(8,128)(2,1)S(1)}, u32[]{:S(2)}, u32[]{:S(2)}) collective-permute-start(bf16[32,128]{1,0:T(8,128)(2,1)S(1)} %get-tuple-element.87), channel_id=1, source_target_pairs={{0,1},{1,2},{2,3},{3,4},{4,5},{5,6},{6,7},{7,8},{8,9},{9,10},{10,1... | collective-permute-start | bytes 24584 | tf_op jit(solution)/shard_map/ppermute | solution.py:19
  71.5 13.2 %collective-permute-start.10 = (bf16[32,128]{1,0:T(8,128)(2,1)S(1)}, bf16[32,128]{1,0:T(8,128)(2,1)S(1)}, u32[]{:S(2)}, u32[]{:S(2)}) collective-permute-start(bf16[32,128]{1,0:T(8,128)(2,1)S(1)} %get-tuple-element.88), channel_id=1, source_target_pairs={{1,0},{2,1},{3,2},{4,3},{5,4},{6,5},{7,6},{8,7},{9,8},{10,9},{11,1... | collective-permute-start | bytes 24584 | tf_op jit(solution)/shard_map/ppermute | solution.py:19
  84.7 18.4 %all-to-all-start.1 = ((bf16[8,80,128]{2,1,0:T(8,128)(2,1)}), bf16[8,80,128]{2,1,0:T(8,128)(2,1)S(1)}, u32[]{:S(2)}, u32[]{:S(2)}) async-start(bf16[8,80,128]{2,1,0:T(8,128)(2,1)} %shard_map.118), calls=%async_computation.1 | async-start | bytes 327680 | tf_op jit(solution)/shard_map/all_to_all | solution.py:494
  94.9 9.0 %collective-permute-start.11 = (bf16[416,128]{1,0:T(8,128)(2,1)S(1)}, bf16[416,128]{1,0:T(8,128)(2,1)S(1)}, u32[]{:S(2)}, u32[]{:S(2)}) collective-permute-start(bf16[416,128]{1,0:T(8,128)(2,1)S(1)} %get-tuple-element.93), channel_id=1, source_target_pairs={{0,16},{16,32},{32,48},{48,64},{64,80},{80,96},{96,112},{112,128},... | collective-permute-start | bytes 319496 | tf_op jit(solution)/shard_map/ppermute | solution.py:19
  100.3 5.7 %collective-permute-start.12 = (bf16[416,128]{1,0:T(8,128)(2,1)S(1)}, bf16[416,128]{1,0:T(8,128)(2,1)S(1)}, u32[]{:S(2)}, u32[]{:S(2)}) collective-permute-start(bf16[416,128]{1,0:T(8,128)(2,1)S(1)} %get-tuple-element.94), channel_id=1, source_target_pairs={{16,0},{32,16},{48,32},{64,48},{80,64},{96,80},{112,96},{128,112},... | collective-permute-start | bytes 319496 | tf_op jit(solution)/shard_map/ppermute | solution.py:19
  106.1 19.9 %all-to-all-start.2 = ((bf16[32,80,128]{2,1,0:T(8,128)(2,1)}), bf16[32,80,128]{2,1,0:T(8,128)(2,1)S(1)}, u32[]{:S(2)}, u32[]{:S(2)}) async-start(bf16[32,80,128]{2,1,0:T(8,128)(2,1)} %shard_map.119), calls=%async_computation.2 | async-start | bytes 1310720 | tf_op jit(solution)/shard_map/all_to_all | solution.py:501
  125.9 10.8 %collective-permute-start.13 = (bf16[32,80,128]{2,1,0:T(8,128)(2,1)S(1)}, bf16[32,80,128]{2,1,0:T(8,128)(2,1)S(1)}, u32[]{:S(2)}, u32[]{:S(2)}) collective-permute-start(bf16[32,80,128]{2,1,0:T(8,128)(2,1)S(1)} %all-to-all-done.2.own_ref), channel_id=1, source_target_pairs={{0,1},{1,0},{2,3},{3,2},{4,5},{5,4},{6,7},{7,6},{8,9},{9,8},{10,11... | collective-permute-start | bytes 1966088 | tf_op jit(solution)/shard_map/ppermute | solution.py:27

commit v4 on v3

--- a/solution.py
+++ b/solution.py
@@ -119,7 +119,7 @@
         copy.wait()
 
 
-def stack_kernel(first_ref, second_ref, enc_ref, low_ref, dec_ref, lift_ref, *refs):
+def stack_kernel(first_ref, enc_ref, low_ref, dec_ref, lift_ref, *refs):
     outs, lift_out, (enc, low, dec, sems) = refs[:6], refs[6], refs[7:]
     fetched(sems, (enc_ref, enc), (low_ref, low), (dec_ref, dec), (lift_ref, lift_out))
     for ref, forward, backward in (
@@ -141,7 +141,7 @@
         out2[...] = paired[x]
 
 
-def pack_y_kernel(f_ref, c_ref, xlo, xhi, xlo2, xhi2, after_ref, lo_ref, hi_ref):
+def pack_y_kernel(f_ref, c_ref, xlo, xhi, xlo2, xhi2, lo_ref, hi_ref):
     for first, out in ((0, lo_ref), (3, hi_ref)):
         at = slice(first, first + 5)
         out[0] = xlo[at]
@@ -409,6 +409,13 @@
     )
     x_halo = swapped(lo, hi, GX)
     far_halo = [shifted(hi2, GX, 2), shifted(lo2, GX, -2)]
+    edges = call(
+        pack_y_kernel,
+        [((6, 5, 32, 128), BF16)] * 2,
+        [],
+        [f, c, *x_halo, *far_halo],
+    )
+    y_halo = swapped(*edges, GY)
     enc_fwd, enc_bwd, low_fwd, low_bwd, dec_fwd, dec_bwd, lift = call(
         stack_kernel,
         [
@@ -426,18 +433,10 @@
             ((27, 64, 128), BF16),
             (pltpu.SemaphoreType.DMA((4,)), None),
         ],
-        [*x_halo, encoder_weight, lower_t, decoder_weight, lift_weight],
-        spaces={k: pltpu.HBM for k in range(6)},
+        [edges[0], encoder_weight, lower_t, decoder_weight, lift_weight],
+        spaces={k: pltpu.HBM for k in range(5)},
         flops=2 * 10**9,
     )
-    edges = call(
-        pack_y_kernel,
-        [((6, 5, 32, 128), BF16)] * 2,
-        [],
-        [f, c, *x_halo, *far_halo, enc_fwd],
-        spaces={6: pltpu.HBM},
-    )
-    y_halo = swapped(*edges, GY)
     fx, encoded, slope, pooled = call(
         encode_kernel,
         [((8, 18, 32, 64), BF16), (tall, BF16), ((512, 64), F32), ((3, 8, 16, 64), BF16)],

time: 140 us -> 137 us (0.979)
  local copies, waits for them, and re-layouts: 7.26 us -> 5.74 us
    all_to_all x1, starting transfers between devices: 10.1 us -> 11.9 us  [per_device(): sums = lax.all_to_all(sums, 'gz', 0, 0)]
    all_to_all x2, starting transfers between devices: 18 us -> 16.4 us  [per_device(): sums = lax.all_to_all(sums, 'gx', 0, 0)]
    unnamed x20 -> x12, local copies, waits for them, and re-layouts: 7.26 us -> 5.74 us
  transfers between devices with their start and end apart: 17 -> 17, of which waited for: 9 -> 8; matrix products, arithmetic and copies ran while one was open for 0% -> 0% of each run, Pallas kernels for 5% -> 5%
where the time goes in v4:
time: 137 us; the launch traced here: 136 us
  starting transfers between devices  78.1 us (57%)
  waiting for transfers between devices  34.9 us (25%)
  Pallas kernels  16.5 us (12%)
  local copies, waits for them, and re-layouts  5.74 us (4%)
    ppermute x12, starting transfers between devices, shifted(): return lax.ppermute(piece, axes, pairs)  38.7 us
    all_to_all x2, waiting for transfers between devices, per_device(): sums = lax.all_to_all(sums, 'gx', 0, 0)  20.7 us
    pallas_call x15, Pallas kernels, call(): pl.pallas_call(kernel, out_shape=[jax.ShapeDtypeStruct(s, d) for s, d in...  16.5 us
    all_to_all x2, starting transfers between devices, per_device(): sums = lax.all_to_all(sums, 'gx', 0, 0)  16.4 us
    all_to_all x1, starting transfers between devices, per_device(): sums = lax.all_to_all(sums, 'gz', 0, 0)  11.9 us
    ppermute x2, starting transfers between devices, partner(): return lax.ppermute(piece, 'gc', [(0, 1), (1, 0)])  11 us
    ppermute x12, waiting for transfers between devices, shifted(): return lax.ppermute(piece, axes, pairs)  8.97 us
    unnamed x12, local copies, waits for them, and re-layouts  5.74 us
  transfers between devices with their start and end apart: 17, of which 8 were waited for; matrix products, arithmetic and copies ran while one was open for 0% of the time, Pallas kernels for 5%

profile of v4, /device:TPU:1, one launch (start us, length us, event | category | flops | bytes accessed | tf_op | source)
XLA Modules:
  0.0 136.3 jit_solution(14978057113235268705)
XLA Ops:
  0.6 0.9 copy-done
  1.5 0.9 copy-done.1
  2.4 0.4 shard_map.109
  2.9 4.0 %collective-permute-start = (bf16[12,32,128]{2,1,0:T(8,128)(2,1)S(1)}, bf16[12,32,128]{2,1,0:T(8,128)(2,1)S(1)}, u32[]{:S(2)}, u32[]{:S(2)}) collective-permute-start(bf16[12,32,128]{2,1,0:T(8,128)(2,1)S(1)} %get-tuple-element.59), channel_id=1, source_target_pairs={{0,16},{16,32},{32,48},{48,64},{64,80},{80,96},{96,112},{112,128},... | collective-permute-start | bytes 294920 | tf_op jit(solution)/shard_map/ppermute | solution.py:19
  6.9 1.3 collective-permute-start.1
  8.2 5.0 %collective-permute-start.2 = (bf16[4,32,128]{2,1,0:T(8,128)(2,1)S(1)}, bf16[4,32,128]{2,1,0:T(8,128)(2,1)S(1)}, u32[]{:S(2)}, u32[]{:S(2)}) collective-permute-start(bf16[4,32,128]{2,1,0:T(8,128)(2,1)S(1)} %get-tuple-element.61), channel_id=1, source_target_pairs={{0,32},{16,48},{32,64},{48,80},{64,96},{80,112},{96,128},{112,144}... | collective-permute-start | bytes 98312 | tf_op jit(solution)/shard_map/ppermute | solution.py:19
  13.2 1.3 collective-permute-start.3
  14.6 6.6 %collective-permute-done.3.xhi2 = bf16[4,32,128]{2,1,0:T(8,128)(2,1)S(1)} collective-permute-done((bf16[4,32,128]{2,1,0:T(8,128)(2,1)S(1)}, bf16[4,32,128]{2,1,0:T(8,128)(2,1)S(1)}, u32[]{:S(2)}, u32[]{:S(2)}) %collective-permute-start.3) | collective-permute-done | bytes 32800 | tf_op jit(solution)/shard_map/ppermute | solution.py:19
  21.2 0.0 collective-permute-done.xlo.refs_2_
  21.2 0.3 shard_map.110
  21.5 6.3 %collective-permute-start.4 = (bf16[6,5,32,128]{3,2,1,0:T(8,128)(2,1)S(1)}, bf16[6,5,32,128]{3,2,1,0:T(8,128)(2,1)S(1)}, u32[]{:S(2)}, u32[]{:S(2)}) collective-permute-start(bf16[6,5,32,128]{3,2,1,0:T(8,128)(2,1)S(1)} %get-tuple-element.63), channel_id=1, source_target_pairs={{0,1},{1,2},{2,3},{3,4},{4,5},{5,6},{6,7},{7,8},{8,9},{9,10},{10,1... | collective-permute-start | bytes 737288 | tf_op jit(solution)/shard_map/ppermute | solution.py:19
  27.8 1.9 %collective-permute-start.5 = (bf16[6,5,32,128]{3,2,1,0:T(8,128)(2,1)S(1)}, bf16[6,5,32,128]{3,2,1,0:T(8,128)(2,1)S(1)}, u32[]{:S(2)}, u32[]{:S(2)}) collective-permute-start(bf16[6,5,32,128]{3,2,1,0:T(8,128)(2,1)S(1)} %get-tuple-element.64.first_ref), channel_id=1, source_target_pairs={{1,0},{2,1},{3,2},{4,3},{5,4},{6,5},{7,6},{8,7},{9,8},{10,9},{11,1... | collective-permute-start | bytes 737288 | tf_op jit(solution)/shard_map/ppermute | solution.py:19
  29.7 0.1 add_convert_fusion.inside
  29.8 1.0 copy-done.2
  30.8 1.0 copy-done.3
  31.9 1.0 copy-done.4
  32.9 0.9 copy-done.5
  33.8 1.3 shard_map.111
  35.1 0.3 collective-permute-done.5.yhi.refs_1_
  35.3 1.4 shard_map.113
  36.7 2.5 %shard_map.112 = (bf16[8,18,32,64]{3,2,1,0:T(8,128)(2,1)S(1)}, bf16[2,10,32,64]{3,2,1,0:T(8,128)(2,1)S(1)}, f32[512,64]{1,0:T(8,128)S(1)}, bf16[3,8,16,64]{3,2,1,0:T(8,128)(2,1)S(1)}) custom-call(bf16[2,8,32,64]{3,2,1,0:T(8,128)(2,1)S(1)} %get-tuple-element.57.f_ref, bf16[6,5,32,128]{3,2,1,0:T(8,128)(2,1)S(1)} %collective-permute-done.4.ylo.refs_0_, ...), custom_call_target="tpu_custom_call" | custom-call | flops 1000000 | bytes 10000 | tf_op jit(solution)/shard_map/pallas_call | solution.py:31
  39.2 0.8 shard_map.114
  40.1 1.3 collective-permute-start.7
  41.4 4.0 %collective-permute-start.6 = (bf16[96,128]{1,0:T(8,128)(2,1)S(1)}, bf16[96,128]{1,0:T(8,128)(2,1)S(1)}, u32[]{:S(2)}, u32[]{:S(2)}) collective-permute-start(bf16[96,128]{1,0:T(8,128)(2,1)S(1)} %get-tuple-element.71.lg_ref), channel_id=1, source_target_pairs={{0,16},{16,32},{32,48},{48,64},{64,80},{80,96},{96,112},{112,128},... | collective-permute-start | bytes 73736 | tf_op jit(solution)/shard_map/ppermute | solution.py:19
  45.4 1.3 shard_map.115
  46.7 1.1 shard_map.116
  47.9 1.9 %collective-permute-start.8 = (bf16[32,80,128]{2,1,0:T(8,128)(2,1)S(1)}, bf16[32,80,128]{2,1,0:T(8,128)(2,1)S(1)}, u32[]{:S(2)}, u32[]{:S(2)}) collective-permute-start(bf16[32,80,128]{2,1,0:T(8,128)(2,1)S(1)} %get-tuple-element.83), channel_id=1, source_target_pairs={{0,1},{1,0},{2,3},{3,2},{4,5},{5,4},{6,7},{7,6},{8,9},{9,8},{10,11... | collective-permute-start | bytes 1966088 | tf_op jit(solution)/shard_map/ppermute | solution.py:27
  49.8 2.1 %collective-permute-done.8.b_ref = bf16[32,80,128]{2,1,0:T(8,128)(2,1)S(1)} collective-permute-done((bf16[32,80,128]{2,1,0:T(8,128)(2,1)S(1)}, bf16[32,80,128]{2,1,0:T(8,128)(2,1)S(1)}, u32[]{:S(2)}, u32[]{:S(2)}) %collective-permute-start.8) | collective-permute-done | bytes 655392 | tf_op jit(solution)/shard_map/ppermute | solution.py:27
  51.9 1.0 shard_map.117
  52.9 10.2 %all-to-all-start = ((bf16[32,80,128]{2,1,0:T(8,128)(2,1)}), bf16[32,80,128]{2,1,0:T(8,128)(2,1)S(1)}, u32[]{:S(2)}, u32[]{:S(2)}) async-start(bf16[32,80,128]{2,1,0:T(8,128)(2,1)} %shard_map.117), calls=%async_computation | async-start | bytes 1310720 | tf_op jit(solution)/shard_map/all_to_all | solution.py:489
  63.1 5.1 %collective-permute-start.9 = (bf16[32,128]{1,0:T(8,128)(2,1)S(1)}, bf16[32,128]{1,0:T(8,128)(2,1)S(1)}, u32[]{:S(2)}, u32[]{:S(2)}) collective-permute-start(bf16[32,128]{1,0:T(8,128)(2,1)S(1)} %get-tuple-element.87), channel_id=1, source_target_pairs={{0,1},{1,2},{2,3},{3,4},{4,5},{5,6},{6,7},{7,8},{8,9},{9,10},{10,1... | collective-permute-start | bytes 24584 | tf_op jit(solution)/shard_map/ppermute | solution.py:19
  68.3 1.9 %collective-permute-start.10 = (bf16[32,128]{1,0:T(8,128)(2,1)S(1)}, bf16[32,128]{1,0:T(8,128)(2,1)S(1)}, u32[]{:S(2)}, u32[]{:S(2)}) collective-permute-start(bf16[32,128]{1,0:T(8,128)(2,1)S(1)} %get-tuple-element.88), channel_id=1, source_target_pairs={{1,0},{2,1},{3,2},{4,3},{5,4},{6,5},{7,6},{8,7},{9,8},{10,9},{11,1... | collective-permute-start | bytes 24584 | tf_op jit(solution)/shard_map/ppermute | solution.py:19
  70.2 9.7 %all-to-all-done.parts_ref = bf16[32,80,128]{2,1,0:T(8,128)(2,1)S(1)} async-done(((bf16[32,80,128]{2,1,0:T(8,128)(2,1)}), bf16[32,80,128]{2,1,0:T(8,128)(2,1)S(1)}, u32[]{:S(2)}, u32[]{:S(2)}) %all-to-all-start) | async-done | bytes 655392 | tf_op jit(solution)/shard_map/all_to_all | solution.py:489
  79.9 0.8 shard_map.118
  80.7 11.9 %all-to-all-start.1 = ((bf16[8,80,128]{2,1,0:T(8,128)(2,1)}), bf16[8,80,128]{2,1,0:T(8,128)(2,1)S(1)}, u32[]{:S(2)}, u32[]{:S(2)}) async-start(bf16[8,80,128]{2,1,0:T(8,128)(2,1)} %shard_map.118), calls=%async_computation.1 | async-start | bytes 327680 | tf_op jit(solution)/shard_map/all_to_all | solution.py:493
  92.6 0.1 shard_map.120
  92.7 5.3 %collective-permute-start.11 = (bf16[416,128]{1,0:T(8,128)(2,1)S(1)}, bf16[416,128]{1,0:T(8,128)(2,1)S(1)}, u32[]{:S(2)}, u32[]{:S(2)}) collective-permute-start(bf16[416,128]{1,0:T(8,128)(2,1)S(1)} %get-tuple-element.93), channel_id=1, source_target_pairs={{0,16},{16,32},{32,48},{48,64},{64,80},{80,96},{96,112},{112,128},... | collective-permute-start | bytes 319496 | tf_op jit(solution)/shard_map/ppermute | solution.py:19
  98.0 1.3 collective-permute-start.12
  99.3 1.5 %all-to-all-done.1.parts_ref = bf16[8,80,128]{2,1,0:T(8,128)(2,1)S(1)} async-done(((bf16[8,80,128]{2,1,0:T(8,128)(2,1)}), bf16[8,80,128]{2,1,0:T(8,128)(2,1)S(1)}, u32[]{:S(2)}, u32[]{:S(2)}) %all-to-all-start.1) | async-done | bytes 163872 | tf_op jit(solution)/shard_map/all_to_all | solution.py:493
  100.8 0.9 shard_map.119
  101.7 2.0 %collective-permute-done.12.xhi = bf16[416,128]{1,0:T(8,128)(2,1)S(1)} collective-permute-done((bf16[416,128]{1,0:T(8,128)(2,1)S(1)}, bf16[416,128]{1,0:T(8,128)(2,1)S(1)}, u32[]{:S(2)}, u32[]{:S(2)}) %collective-permute-start.12) | collective-permute-done | bytes 106528 | tf_op jit(solution)/shard_map/ppermute | solution.py:19
  103.8 6.2 %all-to-all-start.2 = ((bf16[32,80,128]{2,1,0:T(8,128)(2,1)}), bf16[32,80,128]{2,1,0:T(8,128)(2,1)S(1)}, u32[]{:S(2)}, u32[]{:S(2)}) async-start(bf16[32,80,128]{2,1,0:T(8,128)(2,1)} %shard_map.119), calls=%async_computation.2 | async-start | bytes 1310720 | tf_op jit(solution)/shard_map/all_to_all | solution.py:500
  110.0 1.3 shard_map.122
  111.3 1.5 %shard_map.121 = bf16[2,8,32,64]{3,2,1,0:T(8,128)(2,1)} custom-call(bf16[2,10,32,64]{3,2,1,0:T(8,128)(2,1)S(1)} %get-tuple-element.79.enc_ref, bf16[2,10,32,64]{3,2,1,0:T(8,128)(2,1)S(1)} %get-tuple-element.96.lifted_ref, bf16[416,128]{1,0:T(8,128)(2,1)S(1)} %collective-permute-done.11.xlo, bf16[416,128]{1,0:T(8,128)(2,1)S(1)} %collective-permute-done.12.xhi, ...), custom_call_target="tpu_custom_call" | custom-call | flops 1000000 | bytes 10000 | tf_op jit(solution)/shard_map/pallas_call | solution.py:31
  112.7 11.0 %all-to-all-done.2.own_ref = bf16[32,80,128]{2,1,0:T(8,128)(2,1)S(1)} async-done(((bf16[32,80,128]{2,1,0:T(8,128)(2,1)}), bf16[32,80,128]{2,1,0:T(8,128)(2,1)S(1)}, u32[]{:S(2)}, u32[]{:S(2)}) %all-to-all-start.2) | async-done | bytes 655392 | tf_op jit(solution)/shard_map/all_to_all | solution.py:500
  123.7 9.1 %collective-permute-start.13 = (bf16[32,80,128]{2,1,0:T(8,128)(2,1)S(1)}, bf16[32,80,128]{2,1,0:T(8,128)(2,1)S(1)}, u32[]{:S(2)}, u32[]{:S(2)}) collective-permute-start(bf16[32,80,128]{2,1,0:T(8,128)(2,1)S(1)} %all-to-all-done.2.own_ref), channel_id=1, source_target_pairs={{0,1},{1,0},{2,3},{3,2},{4,5},{5,4},{6,7},{7,6},{8,9},{9,8},{10,11... | collective-permute-start | bytes 1966088 | tf_op jit(solution)/shard_map/ppermute | solution.py:27
  132.8 1.7 %collective-permute-done.13.other_ref = bf16[32,80,128]{2,1,0:T(8,128)(2,1)S(1)} collective-permute-done((bf16[32,80,128]{2,1,0:T(8,128)(2,1)S(1)}, bf16[32,80,128]{2,1,0:T(8,128)(2,1)S(1)}, u32[]{:S(2)}, u32[]{:S(2)}) %collective-permute-start.13) | collective-permute-done | bytes 655392 | tf_op jit(solution)/shard_map/ppermute | solution.py:27
  134.5 1.8 %shard_map.123 = (f32[27,64,64]{2,1,0:T(8,128)}, f32[27,64,128]{2,1,0:T(8,128)}, f32[27,64,128]{2,1,0:T(8,128)}, f32[8,64,128]{2,1,0:T(8,128)}) custom-call(s32[1]{0:T(128)} %bitcast.7.core, bf16[32,80,128]{2,1,0:T(8,128)(2,1)S(1)} %all-to-all-done.2.own_ref, bf16[32,80,128]{2,1,0:T(8,128)(2,1)S(1)} %collective-permute-done.13.other_ref), custom_call_target="tpu_custom_call" | custom-call | flops 1000000 | bytes 10000 | tf_op jit(solution)/shard_map/pallas_call | solution.py:31
  (14 shorter events, 0.0 us)
Async XLA Ops:
  0.6 0.9 copy-start
  1.5 0.9 copy-start.1
  2.9 18.3 %collective-permute-start = (bf16[12,32,128]{2,1,0:T(8,128)(2,1)S(1)}, bf16[12,32,128]{2,1,0:T(8,128)(2,1)S(1)}, u32[]{:S(2)}, u32[]{:S(2)}) collective-permute-start(bf16[12,32,128]{2,1,0:T(8,128)(2,1)S(1)} %get-tuple-element.59), channel_id=1, source_target_pairs={{0,16},{16,32},{32,48},{48,64},{64,80},{80,96},{96,112},{112,128},... | collective-permute-start | bytes 294920 | tf_op jit(solution)/shard_map/ppermute | solution.py:19
  6.9 14.3 %collective-permute-start.1 = (bf16[12,32,128]{2,1,0:T(8,128)(2,1)S(1)}, bf16[12,32,128]{2,1,0:T(8,128)(2,1)S(1)}, u32[]{:S(2)}, u32[]{:S(2)}) collective-permute-start(bf16[12,32,128]{2,1,0:T(8,128)(2,1)S(1)} %get-tuple-element.60), channel_id=1, source_target_pairs={{16,0},{32,16},{48,32},{64,48},{80,64},{96,80},{112,96},{128,112},... | collective-permute-start | bytes 294920 | tf_op jit(solution)/shard_map/ppermute | solution.py:19
  8.2 6.3 %collective-permute-start.2 = (bf16[4,32,128]{2,1,0:T(8,128)(2,1)S(1)}, bf16[4,32,128]{2,1,0:T(8,128)(2,1)S(1)}, u32[]{:S(2)}, u32[]{:S(2)}) collective-permute-start(bf16[4,32,128]{2,1,0:T(8,128)(2,1)S(1)} %get-tuple-element.61), channel_id=1, source_target_pairs={{0,32},{16,48},{32,64},{48,80},{64,96},{80,112},{96,128},{112,144}... | collective-permute-start | bytes 98312 | tf_op jit(solution)/shard_map/ppermute | solution.py:19
  13.2 8.0 %collective-permute-start.3 = (bf16[4,32,128]{2,1,0:T(8,128)(2,1)S(1)}, bf16[4,32,128]{2,1,0:T(8,128)(2,1)S(1)}, u32[]{:S(2)}, u32[]{:S(2)}) collective-permute-start(bf16[4,32,128]{2,1,0:T(8,128)(2,1)S(1)} %get-tuple-element.62), channel_id=1, source_target_pairs={{32,0},{48,16},{64,32},{80,48},{96,64},{112,80},{128,96},{144,112}... | collective-permute-start | bytes 98312 | tf_op jit(solution)/shard_map/ppermute | solution.py:19
  21.5 13.5 %collective-permute-start.4 = (bf16[6,5,32,128]{3,2,1,0:T(8,128)(2,1)S(1)}, bf16[6,5,32,128]{3,2,1,0:T(8,128)(2,1)S(1)}, u32[]{:S(2)}, u32[]{:S(2)}) collective-permute-start(bf16[6,5,32,128]{3,2,1,0:T(8,128)(2,1)S(1)} %get-tuple-element.63), channel_id=1, source_target_pairs={{0,1},{1,2},{2,3},{3,4},{4,5},{5,6},{6,7},{7,8},{8,9},{9,10},{10,1... | collective-permute-start | bytes 737288 | tf_op jit(solution)/shard_map/ppermute | solution.py:19
  27.8 7.5 %collective-permute-start.5 = (bf16[6,5,32,128]{3,2,1,0:T(8,128)(2,1)S(1)}, bf16[6,5,32,128]{3,2,1,0:T(8,128)(2,1)S(1)}, u32[]{:S(2)}, u32[]{:S(2)}) collective-permute-start(bf16[6,5,32,128]{3,2,1,0:T(8,128)(2,1)S(1)} %get-tuple-element.64.first_ref), channel_id=1, source_target_pairs={{1,0},{2,1},{3,2},{4,3},{5,4},{6,5},{7,6},{8,7},{9,8},{10,9},{11,1... | collective-permute-start | bytes 737288 | tf_op jit(solution)/shard_map/ppermute | solution.py:19
  29.8 1.0 copy-start.2
  30.8 1.0 copy-start.3
  31.9 1.0 copy-start.4
  32.9 0.9 copy-start.5
  40.1 6.6 %collective-permute-start.7 = (bf16[96,128]{1,0:T(8,128)(2,1)S(1)}, bf16[96,128]{1,0:T(8,128)(2,1)S(1)}, u32[]{:S(2)}, u32[]{:S(2)}) collective-permute-start(bf16[96,128]{1,0:T(8,128)(2,1)S(1)} %get-tuple-element.71.lg_ref), channel_id=1, source_target_pairs={{16,0},{32,16},{48,32},{64,48},{80,64},{96,80},{112,96},{128,112},... | collective-permute-start | bytes 73736 | tf_op jit(solution)/shard_map/ppermute | solution.py:19
  41.4 5.4 %collective-permute-start.6 = (bf16[96,128]{1,0:T(8,128)(2,1)S(1)}, bf16[96,128]{1,0:T(8,128)(2,1)S(1)}, u32[]{:S(2)}, u32[]{:S(2)}) collective-permute-start(bf16[96,128]{1,0:T(8,128)(2,1)S(1)} %get-tuple-element.71.lg_ref), channel_id=1, source_target_pairs={{0,16},{16,32},{32,48},{48,64},{64,80},{80,96},{96,112},{112,128},... | collective-permute-start | bytes 73736 | tf_op jit(solution)/shard_map/ppermute | solution.py:19
  47.9 4.0 %collective-permute-start.8 = (bf16[32,80,128]{2,1,0:T(8,128)(2,1)S(1)}, bf16[32,80,128]{2,1,0:T(8,128)(2,1)S(1)}, u32[]{:S(2)}, u32[]{:S(2)}) collective-permute-start(bf16[32,80,128]{2,1,0:T(8,128)(2,1)S(1)} %get-tuple-element.83), channel_id=1, source_target_pairs={{0,1},{1,0},{2,3},{3,2},{4,5},{5,4},{6,7},{7,6},{8,9},{9,8},{10,11... | collective-permute-start | bytes 1966088 | tf_op jit(solution)/shard_map/ppermute | solution.py:27
  52.9 27.0 %all-to-all-start = ((bf16[32,80,128]{2,1,0:T(8,128)(2,1)}), bf16[32,80,128]{2,1,0:T(8,128)(2,1)S(1)}, u32[]{:S(2)}, u32[]{:S(2)}) async-start(bf16[32,80,128]{2,1,0:T(8,128)(2,1)} %shard_map.117), calls=%async_computation | async-start | bytes 1310720 | tf_op jit(solution)/shard_map/all_to_all | solution.py:489
  63.1 17.5 %collective-permute-start.9 = (bf16[32,128]{1,0:T(8,128)(2,1)S(1)}, bf16[32,128]{1,0:T(8,128)(2,1)S(1)}, u32[]{:S(2)}, u32[]{:S(2)}) collective-permute-start(bf16[32,128]{1,0:T(8,128)(2,1)S(1)} %get-tuple-element.87), channel_id=1, source_target_pairs={{0,1},{1,2},{2,3},{3,4},{4,5},{5,6},{6,7},{7,8},{8,9},{9,10},{10,1... | collective-permute-start | bytes 24584 | tf_op jit(solution)/shard_map/ppermute | solution.py:19
  68.3 12.4 %collective-permute-start.10 = (bf16[32,128]{1,0:T(8,128)(2,1)S(1)}, bf16[32,128]{1,0:T(8,128)(2,1)S(1)}, u32[]{:S(2)}, u32[]{:S(2)}) collective-permute-start(bf16[32,128]{1,0:T(8,128)(2,1)S(1)} %get-tuple-element.88), channel_id=1, source_target_pairs={{1,0},{2,1},{3,2},{4,3},{5,4},{6,5},{7,6},{8,7},{9,8},{10,9},{11,1... | collective-permute-start | bytes 24584 | tf_op jit(solution)/shard_map/ppermute | solution.py:19
  80.7 20.2 %all-to-all-start.1 = ((bf16[8,80,128]{2,1,0:T(8,128)(2,1)}), bf16[8,80,128]{2,1,0:T(8,128)(2,1)S(1)}, u32[]{:S(2)}, u32[]{:S(2)}) async-start(bf16[8,80,128]{2,1,0:T(8,128)(2,1)} %shard_map.118), calls=%async_computation.1 | async-start | bytes 327680 | tf_op jit(solution)/shard_map/all_to_all | solution.py:493
  92.7 9.0 %collective-permute-start.11 = (bf16[416,128]{1,0:T(8,128)(2,1)S(1)}, bf16[416,128]{1,0:T(8,128)(2,1)S(1)}, u32[]{:S(2)}, u32[]{:S(2)}) collective-permute-start(bf16[416,128]{1,0:T(8,128)(2,1)S(1)} %get-tuple-element.93), channel_id=1, source_target_pairs={{0,16},{16,32},{32,48},{48,64},{64,80},{80,96},{96,112},{112,128},... | collective-permute-start | bytes 319496 | tf_op jit(solution)/shard_map/ppermute | solution.py:19
  98.0 5.7 %collective-permute-start.12 = (bf16[416,128]{1,0:T(8,128)(2,1)S(1)}, bf16[416,128]{1,0:T(8,128)(2,1)S(1)}, u32[]{:S(2)}, u32[]{:S(2)}) collective-permute-start(bf16[416,128]{1,0:T(8,128)(2,1)S(1)} %get-tuple-element.94), channel_id=1, source_target_pairs={{16,0},{32,16},{48,32},{64,48},{80,64},{96,80},{112,96},{128,112},... | collective-permute-start | bytes 319496 | tf_op jit(solution)/shard_map/ppermute | solution.py:19
  103.8 19.9 %all-to-all-start.2 = ((bf16[32,80,128]{2,1,0:T(8,128)(2,1)}), bf16[32,80,128]{2,1,0:T(8,128)(2,1)S(1)}, u32[]{:S(2)}, u32[]{:S(2)}) async-start(bf16[32,80,128]{2,1,0:T(8,128)(2,1)} %shard_map.119), calls=%async_computation.2 | async-start | bytes 1310720 | tf_op jit(solution)/shard_map/all_to_all | solution.py:500
  123.7 10.8 %collective-permute-start.13 = (bf16[32,80,128]{2,1,0:T(8,128)(2,1)S(1)}, bf16[32,80,128]{2,1,0:T(8,128)(2,1)S(1)}, u32[]{:S(2)}, u32[]{:S(2)}) collective-permute-start(bf16[32,80,128]{2,1,0:T(8,128)(2,1)S(1)} %all-to-all-done.2.own_ref), channel_id=1, source_target_pairs={{0,1},{1,0},{2,3},{3,2},{4,5},{5,4},{6,7},{7,6},{8,9},{9,8},{10,11... | collective-permute-start | bytes 1966088 | tf_op jit(solution)/shard_map/ppermute | solution.py:27

commit v5 on v4

--- a/solution.py
+++ b/solution.py
@@ -27,7 +27,7 @@
     return lax.ppermute(piece, "gc", [(0, 1), (1, 0)])
 
 
-def call(kernel, outs, scratch, operands, spaces=(), flops=10**6, aliases=()):
+def call(kernel, outs, scratch, operands, spaces=(), flops=10**6):
     return pl.pallas_call(
         kernel,
         out_shape=[jax.ShapeDtypeStruct(s, d) for s, d in outs],
@@ -36,7 +36,6 @@
         ],
         out_specs=[pl.BlockSpec(memory_space=pltpu.VMEM)] * len(outs),
         scratch_shapes=[s if d is None else pltpu.VMEM(s, d) for s, d in scratch],
-        input_output_aliases=dict(aliases),
         compiler_params=pltpu.CompilerParams(vmem_limit_bytes=40 * 2**20),
         cost_estimate=pl.CostEstimate(flops=flops, bytes_accessed=10**4, transcendentals=0),
     )(*operands)
@@ -173,9 +172,9 @@
         pre = combined(nt(stacked(fx_ref, x, 1, 16, False), weight), 32, False)
         sigma = jax.nn.sigmoid(pre)
         enc = (pre * sigma).astype(BF16)
+        slope = sigma[128:384] * (1.0 + pre[128:384] * (1.0 - sigma[128:384]))
+        slope_ref[x] = slope if x in (2, 3) else slope * inside[0 if x < 2 else 1]
         if x in (2, 3):
-            slope = sigma * (1.0 + pre * (1.0 - sigma))
-            slope_ref[pl.ds((x - 2) * 256, 256), :] = slope[128:384]
             enc_ref[x - 2, 1:9] = enc[128:384].reshape(8, 32, 64)
             enc_ref[x - 2, 0] = (enc[96:128].astype(F32) * inside[2]).astype(BF16)
             enc_ref[x - 2, 9] = (enc[384:416].astype(F32) * inside[3]).astype(BF16)
@@ -229,20 +228,35 @@
     return put
 
 
-def lower_kernel(px, inside, w_ref, adj_ref, la_ref, lg_ref):
+def lower_kernel(px, inside, w_ref, adj_ref, enc_ref, la_ref, lg_ref, lo_ref, hi_ref):
     def masked(value):
         first, last = value[0:16] * inside[2], value[80:96] * inside[3]
         return jnp.concatenate([first, value[16:80], last], 0).astype(BF16)
 
     pre = combined(nn(stacked(px, 0, 1, 6, False), w_ref[...]), 16, False)
     sigma = jax.nn.sigmoid(pre)
-    la_ref[...] = masked(pre * sigma)
-    lg_ref[...] = masked(adj_ref[...] * (sigma * (1.0 + pre * (1.0 - sigma))))
+    la = masked(pre * sigma)
+    lg = masked(adj_ref[...] * (sigma * (1.0 + pre * (1.0 - sigma))))
+    la_ref[...] = la
+    lg_ref[...] = lg
+    for x, msg in ((0, lo_ref), (1, hi_ref)):
+        msg[0:96] = la
+        msg[96:192] = lg
+        enc = enc_ref[x].reshape(320, 64)
+        msg[192:352] = jnp.concatenate([enc[:160], enc[160:]], -1)
+
+
+def doubled(coarse, tmp):
+    tmp[pl.ds(0, 64, stride=2), :] = coarse
+    tmp[pl.ds(1, 64, stride=2), :] = coarse
+    wide = tmp[...].reshape(4, 1, 32, 64)
+    return jnp.broadcast_to(wide, (4, 2, 32, 64)).reshape(256, 64)
 
 
 def grads_kernel(px, la_ref, lg_ref, core, lift_ref, kids_ref, cx_ref, enc_ref, *refs):
-    lifted_ref, keep_ref, send_ref, tmp, halves = refs
-    put = halver(halves)
+    (w_ref, slope_ref, jg_ref, fx_ref), refs = refs[:4], refs[4:]
+    lifted_ref, keep_ref, send_ref, tmp, halves, enc_halves, wide = refs
+    put, put_enc = halver(halves), halver(enc_halves)
     la, lg = la_ref[...], lg_ref[...]
     fine = nt(la, lift_ref[...].reshape(512, 128)).astype(BF16).astype(F32)
     for p in range(2):
@@ -275,9 +289,31 @@
         put(3456 + 64 * k, lift[64 * k : 64 * k + 64])
     for row in (3968, 4032):
         put(row, jnp.zeros((64, 128), F32))
+    lg = lg_ref[...].reshape(6, 16, 128)
+    source = jnp.concatenate([lg[2 - b : 6 - b].reshape(64, 128) for b in range(3)], -1)
+    grad = jnp.zeros((192, 576), F32)
+    for a in range(3):
+        pg = combined(nt(source, w_ref[:, 384 * a : 384 * a + 384]), 16, True)
+        fine = doubled(pg * 0.125, wide)
+        parts = []
+        for x in (2 * a, 2 * a + 1):
+            own = fine if a != 1 else fine + jg_ref[256 * x - 512 : 256 * x - 256].astype(F32)
+            parts.append(own * slope_ref[x])
+        eg = ztaps(jnp.concatenate(parts, 0), 32, True)
+        grad = grad + tn(eg, stacked(fx_ref, 2 * a, 2, 8, False, 4))
+    for ab in range(9):
+        for c in range(3):
+            block = grad[64 * c : 64 * c + 64, 64 * ab : 64 * ab + 64]
+            block = jnp.concatenate([block[:32], block[32:]], -1)
+            put_enc((3 * ab + c) * 32, block[:16])
+            put_enc((3 * ab + c) * 32 + 16, block[16:])
+    for row in range(864, 1024, 16):
+        put_enc(row, jnp.zeros((16, 128), F32))
     mine, chunk = core[0], halves.shape[2]
     keep_ref[:, :chunk, :] = halves[mine]
     send_ref[:, :chunk, :] = halves[1 - mine]
+    keep_ref[:, chunk:, :] = enc_halves[mine]
+    send_ref[:, chunk:, :] = enc_halves[1 - mine]
 
 
 def add_kernel(a_ref, b_ref, out_ref):
@@ -289,16 +325,13 @@
     hi_ref[...] = jnp.concatenate([eg_ref[0, 7], eg_ref[1, 7]], -1)
 
 
-def edge_x_kernel(eg_ref, enc_ref, la_ref, ylo_ref, yhi_ref, lo_ref, hi_ref):
+def edge_x_kernel(eg_ref, ylo_ref, yhi_ref, lo_ref, hi_ref):
     for x, out in ((0, lo_ref), (1, hi_ref)):
         cols = slice(64 * x, 64 * x + 64)
         eg = eg_ref[x].reshape(256, 64)
         first = jnp.concatenate([ylo_ref[:, cols], eg[:128]], 0)
         second = jnp.concatenate([eg[128:], yhi_ref[:, cols]], 0)
-        out[0:160] = jnp.concatenate([first, second], -1)
-        enc = enc_ref[x].reshape(320, 64)
-        out[160:320] = jnp.concatenate([enc[:160], enc[160:]], -1)
-        out[320:416] = la_ref[...]
+        out[...] = jnp.concatenate([first, second], -1)
 
 
 def column(rows):
@@ -309,33 +342,18 @@
     return jnp.concatenate([rows[:, :64], rows[:, 64:]], 0).reshape(1, 10, 32, 64)
 
 
-def encoder_grad_kernel(lg_ref, xlo, xhi, core, w_ref, slope_ref, jg_ref, fx_ref, *refs):
-    eg_ref, keep_ref, send_ref, lo_ref, hi_ref, lx, tmp, halves = refs[2:]
-    put = halver(halves)
-    lx[0] = xlo[...].reshape(6, 16, 128)
+def encoder_grad_kernel(
+    lg_ref, xlo, xhi, w_ref, slope_ref, jg_ref, eg_ref, lo_ref, hi_ref, lx, tmp
+):
+    lx[0] = xlo[96:192].reshape(6, 16, 128)
     lx[1] = lg_ref[...].reshape(6, 16, 128)
-    lx[2] = xhi[...].reshape(6, 16, 128)
+    lx[2] = xhi[96:192].reshape(6, 16, 128)
     pg = combined(nt(stacked(lx, 0, 1, 4, True), w_ref[...]), 16, True)
-    pg = pg.astype(BF16).astype(F32) * 0.125
-    tmp[pl.ds(0, 64, stride=2), :] = pg
-    tmp[pl.ds(1, 64, stride=2), :] = pg
-    wide = tmp[...].reshape(1, 4, 1, 32, 64)
-    wide = jnp.broadcast_to(wide, (2, 4, 2, 32, 64)).reshape(512, 64)
-    eg = ((jg_ref[...].astype(F32) + wide) * slope_ref[...]).astype(BF16)
-    eg_ref[...] = eg.reshape(2, 8, 32, 64)
+    fine = doubled(pg.astype(BF16).astype(F32) * 0.125, tmp)
+    for x in range(2):
+        total = jg_ref[256 * x : 256 * x + 256].astype(F32) + fine
+        eg_ref[x] = (total * slope_ref[2 + x]).astype(BF16).reshape(8, 32, 64)
     edge_y_kernel(eg_ref, lo_ref, hi_ref)
-    grad = tn(ztaps(eg.astype(F32), 32, True), stacked(fx_ref, 2, 2, 8, False, 4))
-    for ab in range(9):
-        for c in range(3):
-            block = grad[64 * c : 64 * c + 64, 64 * ab : 64 * ab + 64]
-            block = jnp.concatenate([block[:32], block[32:]], -1)
-            put((3 * ab + c) * 32, block[:16])
-            put((3 * ab + c) * 32 + 16, block[16:])
-    for row in range(864, 1024, 16):
-        put(row, jnp.zeros((16, 128), F32))
-    mine, chunk = core[0], keep_ref.shape[1] - halves.shape[2]
-    keep_ref[:, chunk:, :] = halves[mine]
-    send_ref[:, chunk:, :] = halves[1 - mine]
 
 
 def decode_kernel(enc_ref, lifted_ref, xlo, xhi, lift_ref, w_ref, out_ref, jx, tx):
@@ -343,14 +361,14 @@
     for p, h in ((1, xlo), (0, xhi)):
         for q in range(2):
             for r in range(2):
-                fine = nt(h[320:416], lift_ref[4 * p + 2 * q + r]).astype(BF16).astype(F32)
+                fine = nt(h[0:96], lift_ref[4 * p + 2 * q + r]).astype(BF16).astype(F32)
                 for j in range(6):
                     y = 2 * j + q - 1
                     if 0 <= y < 10:
                         tx[pl.ds(32 * y + r, 16, stride=2), :] = fine[16 * j : 16 * j + 16]
         lifted = tx[...].astype(BF16).reshape(1, 10, 32, 64)
         x = 0 if p == 1 else 3
-        jx[x : x + 1] = jnp.concatenate([plane(h[160:320]), lifted], -1)
+        jx[x : x + 1] = jnp.concatenate([plane(h[192:352]), lifted], -1)
     weight = w_ref[...]
     for x in range(2):
         out = combined(nt(stacked(jx, x, 1, 8, False), weight), 32, False)
@@ -358,7 +376,7 @@
 
 
 def input_grad_kernel(eg_ref, ylo, yhi, xlo, xhi, w_ref, out_ref, ex):
-    sides = [column(ylo[...]), column(yhi[...]), plane(xlo[0:160]), plane(xhi[0:160])]
+    sides = [column(ylo[...]), column(yhi[...]), plane(xlo[...]), plane(xhi[...])]
     assemble(ex, eg_ref[...], *sides)
     weight = w_ref[...]
     for x in range(2):
@@ -439,7 +457,7 @@
     )
     fx, encoded, slope, pooled = call(
         encode_kernel,
-        [((8, 18, 32, 64), BF16), (tall, BF16), ((512, 64), F32), ((3, 8, 16, 64), BF16)],
+        [((8, 18, 32, 64), BF16), (tall, BF16), ((6, 256, 64), F32), ((3, 8, 16, 64), BF16)],
         [((256, 64), F32)],
         [f, *y_halo, *x_halo, *far_halo, inside, enc_fwd],
         spaces={7: pltpu.SMEM},
@@ -456,61 +474,58 @@
         [c, *y_halo, *x_halo, dec_bwd, lift],
     )
     half = (size_x, 2560 // size_x, 128)
-    la, lg = call(
+    la, lg, *edges = call(
         lower_kernel,
-        [((96, 128), BF16)] * 2,
+        [((96, 128), BF16)] * 2 + [((352, 128), BF16)] * 2,
         [],
-        [pooled, inside, low_fwd, adj],
+        [pooled, inside, low_fwd, adj, encoded],
         spaces={1: pltpu.SMEM},
     )
-    halo = swapped(lg, lg, GX)
     lifted, keep, send = call(
         grads_kernel,
         [(tall, BF16), (half, LINK), (half, LINK)],
-        [((640, 64), F32), ((2, size_x, 2048 // size_x, 128), LINK)],
-        [pooled, la, lg, core, lift, kids, cx, encoded],
+        [
+            ((640, 64), F32),
+            ((2, size_x, 2048 // size_x, 128), LINK),
+            ((2, size_x, 512 // size_x, 128), LINK),
+            ((128, 64), F32),
+        ],
+        [pooled, la, lg, core, lift, kids, cx, encoded, low_bwd, slope, jg, fx],
         spaces={3: pltpu.SMEM},
-        flops=2 * 10**9,
-    )
-    eg, keep, send, *edges = call(
-        encoder_grad_kernel,
-        [(brick, BF16), (half, LINK), (half, LINK)] + [((32, 128), BF16)] * 2,
-        [
-            ((3, 6, 16, 128), BF16),
-            ((128, 64), F32),
-            ((2, size_x, 512 // size_x, 128), LINK),
-        ],
-        [lg, *halo, core, low_bwd, slope, jg, fx, keep, send],
-        spaces={3: pltpu.SMEM},
-        aliases={8: 1, 9: 2},
     )
     (sums,) = call(add_kernel, [(half, LINK)], [], [keep, partner(send)])
     sums, edges = lax.optimization_barrier((sums, edges))
     sums = lax.all_to_all(sums, "gx", 0, 0)
+    halo = swapped(*edges, GX)
+    (sums,) = call(sum_kernel, [((size_z,) + half[1:], LINK)], [], [sums])
+    sums, halo = lax.optimization_barrier((sums, halo))
+    sums = lax.all_to_all(sums, "gz", 0, 0)
+    eg, *edges = call(
+        encoder_grad_kernel,
+        [(brick, BF16)] + [((32, 128), BF16)] * 2,
+        [((3, 6, 16, 128), BF16), ((128, 64), F32)],
+        [lg, *halo, low_bwd, slope, jg],
+    )
     y_halo = swapped(*edges, GY)
-    (sums,) = call(sum_kernel, [((size_z,) + half[1:], LINK)], [], [sums])
+    (sums,) = call(sum_kernel, [(half, LINK)], [], [sums])
     sums, y_halo = lax.optimization_barrier((sums, y_halo))
-    sums = lax.all_to_all(sums, "gz", 0, 0)
-    edges = call(
-        edge_x_kernel, [((416, 128), BF16)] * 2, [], [eg, encoded, la, *y_halo]
-    )
-    halo = swapped(*edges, GX)
-    (sums,) = call(sum_kernel, [(half, LINK)], [], [sums])
-    sums, halo = lax.optimization_barrier((sums, halo))
     sums = lax.all_to_all(sums, "gx", 0, 0)
+    edges = call(edge_x_kernel, [((160, 128), BF16)] * 2, [], [eg, *y_halo])
+    x_halo = swapped(*edges, GX)
     (decoded,) = call(
         decode_kernel,
         [(brick, BF16)],
         [((4, 10, 32, 128), BF16), ((320, 64), F32)],
         [encoded, lifted, *halo, lift, dec_fwd],
     )
+    sums, x_halo, decoded = lax.optimization_barrier((sums, x_halo, decoded))
     (input_grad,) = call(
         input_grad_kernel,
         [(brick, BF16)],
         [((4, 10, 32, 64), BF16)],
-        [eg, *y_halo, *halo, enc_bwd],
-    )
-    sums, decoded, input_grad = lax.optimization_barrier((sums, decoded, input_grad))
+        [eg, *y_halo, *x_halo, enc_bwd],
+        flops=2 * 10**9,
+    )
     encoder_gradient, decoder_gradient, lower_gradient, lift_gradient = call(
         widen_kernel,
         [((27, 64, 64), F32), ((27, 64, 128), F32), ((27, 64, 128), F32), ((8, 64, 128), F32)],

time: 137 us -> 131 us (0.956)
  starting transfers between devices: 78.1 us -> 72.1 us
    ppermute x12, waiting for transfers between devices: 8.97 us -> 18.5 us  [shifted(): return lax.ppermute(piece, axes, pairs)]
    all_to_all x2, waiting for transfers between devices: 20.7 us -> 13 us  [per_device(): sums = lax.all_to_all(sums, 'gx', 0, 0)]
    all_to_all x2, starting transfers between devices: 16.4 us -> 12.2 us  [per_device(): sums = lax.all_to_all(sums, 'gx', 0, 0)]
    ppermute x2, starting transfers between devices: 11 us -> 9.32 us  [partner(): return lax.ppermute(piece, 'gc', [(0, 1), (1, 0)])]
    all_to_all x1, starting transfers between devices: 11.9 us -> 10.3 us  [per_device(): sums = lax.all_to_all(sums, 'gz', 0, 0)]
    ppermute x12, starting transfers between devices: 38.7 us -> 40.3 us  [shifted(): return lax.ppermute(piece, axes, pairs)]
    all_to_all x1, waiting for transfers between devices: 1.5 us -> 0.01 us  [per_device(): sums = lax.all_to_all(sums, 'gz', 0, 0)]
    unnamed x12 -> x16, local copies, waits for them, and re-layouts: 5.74 us -> 5.75 us
  transfers between devices with their start and end apart: 17 -> 17, of which waited for: 8 -> 10; matrix products, arithmetic and copies ran while one was open for 0% -> 0% of each run, Pallas kernels for 5% -> 5%
where the time goes in v5:
time: 131 us; the launch traced here: 130 us
  starting transfers between devices  72.1 us (55%)
  waiting for transfers between devices  34 us (26%)
  Pallas kernels  17.4 us (13%)
  local copies, waits for them, and re-layouts  5.75 us (4%)
    ppermute x12, starting transfers between devices, shifted(): return lax.ppermute(piece, axes, pairs)  40.3 us
    ppermute x12, waiting for transfers between devices, shifted(): return lax.ppermute(piece, axes, pairs)  18.5 us
    pallas_call x15, Pallas kernels, call(): pl.pallas_call(kernel, out_shape=[jax.ShapeDtypeStruct(s, d) for s, d in...  17.4 us
    all_to_all x2, waiting for transfers between devices, per_device(): sums = lax.all_to_all(sums, 'gx', 0, 0)  13 us
    all_to_all x2, starting transfers between devices, per_device(): sums = lax.all_to_all(sums, 'gx', 0, 0)  12.2 us
    all_to_all x1, starting transfers between devices, per_device(): sums = lax.all_to_all(sums, 'gz', 0, 0)  10.3 us
    ppermute x2, starting transfers between devices, partner(): return lax.ppermute(piece, 'gc', [(0, 1), (1, 0)])  9.32 us
    unnamed x16, local copies, waits for them, and re-layouts  5.75 us
  transfers between devices with their start and end apart: 17, of which 10 were waited for; matrix products, arithmetic and copies ran while one was open for 0% of the time, Pallas kernels for 5%

profile of v5, /device:TPU:1, one launch (start us, length us, event | category | flops | bytes accessed | tf_op | source)
XLA Modules:
  0.0 130.2 jit_solution(3523440180958544607)
XLA Ops:
  0.6 0.9 copy-done
  1.5 0.9 copy-done.1
  2.4 0.4 shard_map.109
  2.9 4.0 %collective-permute-start = (bf16[12,32,128]{2,1,0:T(8,128)(2,1)S(1)}, bf16[12,32,128]{2,1,0:T(8,128)(2,1)S(1)}, u32[]{:S(2)}, u32[]{:S(2)}) collective-permute-start(bf16[12,32,128]{2,1,0:T(8,128)(2,1)S(1)} %get-tuple-element.60), channel_id=1, source_target_pairs={{0,16},{16,32},{32,48},{48,64},{64,80},{80,96},{96,112},{112,128},... | collective-permute-start | bytes 294920 | tf_op jit(solution)/shard_map/ppermute | solution.py:19
  6.9 1.3 collective-permute-start.1
  8.2 5.0 %collective-permute-start.2 = (bf16[4,32,128]{2,1,0:T(8,128)(2,1)S(1)}, bf16[4,32,128]{2,1,0:T(8,128)(2,1)S(1)}, u32[]{:S(2)}, u32[]{:S(2)}) collective-permute-start(bf16[4,32,128]{2,1,0:T(8,128)(2,1)S(1)} %get-tuple-element.62), channel_id=1, source_target_pairs={{0,32},{16,48},{32,64},{48,80},{64,96},{80,112},{96,128},{112,144}... | collective-permute-start | bytes 98312 | tf_op jit(solution)/shard_map/ppermute | solution.py:19
  13.2 1.3 collective-permute-start.3
  14.6 6.6 %collective-permute-done.3.xhi2 = bf16[4,32,128]{2,1,0:T(8,128)(2,1)S(1)} collective-permute-done((bf16[4,32,128]{2,1,0:T(8,128)(2,1)S(1)}, bf16[4,32,128]{2,1,0:T(8,128)(2,1)S(1)}, u32[]{:S(2)}, u32[]{:S(2)}) %collective-permute-start.3) | collective-permute-done | bytes 32800 | tf_op jit(solution)/shard_map/ppermute | solution.py:19
  21.2 0.3 shard_map.110
  21.5 6.3 %collective-permute-start.4 = (bf16[6,5,32,128]{3,2,1,0:T(8,128)(2,1)S(1)}, bf16[6,5,32,128]{3,2,1,0:T(8,128)(2,1)S(1)}, u32[]{:S(2)}, u32[]{:S(2)}) collective-permute-start(bf16[6,5,32,128]{3,2,1,0:T(8,128)(2,1)S(1)} %get-tuple-element.64), channel_id=1, source_target_pairs={{0,1},{1,2},{2,3},{3,4},{4,5},{5,6},{6,7},{7,8},{8,9},{9,10},{10,1... | collective-permute-start | bytes 737288 | tf_op jit(solution)/shard_map/ppermute | solution.py:19
  27.8 1.9 %collective-permute-start.5 = (bf16[6,5,32,128]{3,2,1,0:T(8,128)(2,1)S(1)}, bf16[6,5,32,128]{3,2,1,0:T(8,128)(2,1)S(1)}, u32[]{:S(2)}, u32[]{:S(2)}) collective-permute-start(bf16[6,5,32,128]{3,2,1,0:T(8,128)(2,1)S(1)} %get-tuple-element.65.first_ref), channel_id=1, source_target_pairs={{1,0},{2,1},{3,2},{4,3},{5,4},{6,5},{7,6},{8,7},{9,8},{10,9},{11,1... | collective-permute-start | bytes 737288 | tf_op jit(solution)/shard_map/ppermute | solution.py:19
  29.8 1.0 copy-done.2
  30.8 1.0 copy-done.3
  31.9 1.0 copy-done.4
  32.9 0.9 copy-done.5
  33.8 1.3 shard_map.111
  35.1 0.2 collective-permute-done.5.yhi.refs_1_
  35.3 1.4 %shard_map.113 = (bf16[4,14,32,64]{3,2,1,0:T(8,128)(2,1)S(1)}, bf16[512,64]{1,0:T(8,128)(2,1)S(1)}, bf16[64,512]{1,0:T(8,128)(2,1)S(1)}, f32[96,128]{1,0:T(8,128)S(1)}) custom-call(bf16[2,8,32,64]{3,2,1,0:T(8,128)(2,1)S(1)} %get-tuple-element.59.c_ref, bf16[6,5,32,128]{3,2,1,0:T(8,128)(2,1)S(1)} %collective-permute-done.4.ylo.refs_0_, ...), custom_call_target="tpu_custom_call" | custom-call | flops 1000000 | bytes 10000 | tf_op jit(solution)/shard_map/pallas_call | solution.py:31
  36.7 2.6 %shard_map.112 = (bf16[8,18,32,64]{3,2,1,0:T(8,128)(2,1)S(1)}, bf16[2,10,32,64]{3,2,1,0:T(8,128)(2,1)S(1)}, f32[6,256,64]{2,1,0:T(8,128)S(1)}, bf16[3,8,16,64]{3,2,1,0:T(8,128)(2,1)S(1)}) custom-call(bf16[2,8,32,64]{3,2,1,0:T(8,128)(2,1)S(1)} %get-tuple-element.58.f_ref, bf16[6,5,32,128]{3,2,1,0:T(8,128)(2,1)S(1)} %collective-permute-done.4.ylo.refs_0_, ...), custom_call_target="tpu_custom_call" | custom-call | flops 1000000 | bytes 10000 | tf_op jit(solution)/shard_map/pallas_call | solution.py:31
  39.3 0.8 shard_map.114
  40.1 2.8 %shard_map.115 = (bf16[2,10,32,64]{3,2,1,0:T(8,128)(2,1)S(1)}, bf16[32,80,128]{2,1,0:T(8,128)(2,1)S(1)}, bf16[32,80,128]{2,1,0:T(8,128)(2,1)S(1)}) custom-call(bf16[3,8,16,64]{3,2,1,0:T(8,128)(2,1)S(1)} %get-tuple-element.67.px, bf16[96,128]{1,0:T(8,128)(2,1)S(1)} %get-tuple-element.73.la_ref, bf16[96,128]{1,0:T(8,128)(2,1)S(1)} %get-tuple-element.74.lg_ref, ...), custom_call_target="tpu_custom_call" | custom-call | flops 1000000 | bytes 10000 | tf_op jit(solution)/shard_map/pallas_call | solution.py:31
  42.9 1.9 %collective-permute-start.6 = (bf16[32,80,128]{2,1,0:T(8,128)(2,1)S(1)}, bf16[32,80,128]{2,1,0:T(8,128)(2,1)S(1)}, u32[]{:S(2)}, u32[]{:S(2)}) collective-permute-start(bf16[32,80,128]{2,1,0:T(8,128)(2,1)S(1)} %get-tuple-element.82), channel_id=1, source_target_pairs={{0,1},{1,0},{2,3},{3,2},{4,5},{5,4},{6,7},{7,6},{8,9},{9,8},{10,11... | collective-permute-start | bytes 1966088 | tf_op jit(solution)/shard_map/ppermute | solution.py:27
  44.8 2.1 %collective-permute-done.6.b_ref = bf16[32,80,128]{2,1,0:T(8,128)(2,1)S(1)} collective-permute-done((bf16[32,80,128]{2,1,0:T(8,128)(2,1)S(1)}, bf16[32,80,128]{2,1,0:T(8,128)(2,1)S(1)}, u32[]{:S(2)}, u32[]{:S(2)}) %collective-permute-start.6) | collective-permute-done | bytes 655392 | tf_op jit(solution)/shard_map/ppermute | solution.py:27
  46.9 1.0 shard_map.116
  47.9 8.1 %all-to-all-start = ((bf16[32,80,128]{2,1,0:T(8,128)(2,1)}), bf16[32,80,128]{2,1,0:T(8,128)(2,1)S(1)}, u32[]{:S(2)}, u32[]{:S(2)}) async-start(bf16[32,80,128]{2,1,0:T(8,128)(2,1)} %shard_map.116), calls=%async_computation | async-start | bytes 1310720 | tf_op jit(solution)/shard_map/all_to_all | solution.py:498
  56.0 3.1 %collective-permute-start.7 = (bf16[352,128]{1,0:T(8,128)(2,1)S(1)}, bf16[352,128]{1,0:T(8,128)(2,1)S(1)}, u32[]{:S(2)}, u32[]{:S(2)}) collective-permute-start(bf16[352,128]{1,0:T(8,128)(2,1)S(1)} %get-tuple-element.86), channel_id=1, source_target_pairs={{0,16},{16,32},{32,48},{48,64},{64,80},{80,96},{96,112},{112,128},... | collective-permute-start | bytes 270344 | tf_op jit(solution)/shard_map/ppermute | solution.py:19
  59.2 1.3 collective-permute-start.8
  60.5 12.3 %all-to-all-done.parts_ref = bf16[32,80,128]{2,1,0:T(8,128)(2,1)S(1)} async-done(((bf16[32,80,128]{2,1,0:T(8,128)(2,1)}), bf16[32,80,128]{2,1,0:T(8,128)(2,1)S(1)}, u32[]{:S(2)}, u32[]{:S(2)}) %all-to-all-start) | async-done | bytes 655392 | tf_op jit(solution)/shard_map/all_to_all | solution.py:498
  72.8 0.8 shard_map.117
  73.5 0.1 collective-permute-done.8.xhi
  73.7 10.3 %all-to-all-start.1 = ((bf16[8,80,128]{2,1,0:T(8,128)(2,1)}), bf16[8,80,128]{2,1,0:T(8,128)(2,1)S(1)}, u32[]{:S(2)}, u32[]{:S(2)}) async-start(bf16[8,80,128]{2,1,0:T(8,128)(2,1)} %shard_map.117), calls=%async_computation.1 | async-start | bytes 327680 | tf_op jit(solution)/shard_map/all_to_all | solution.py:502
  84.0 0.5 shard_map.119
  84.5 9.7 %collective-permute-start.9 = (bf16[32,128]{1,0:T(8,128)(2,1)S(1)}, bf16[32,128]{1,0:T(8,128)(2,1)S(1)}, u32[]{:S(2)}, u32[]{:S(2)}) collective-permute-start(bf16[32,128]{1,0:T(8,128)(2,1)S(1)} %get-tuple-element.91), channel_id=1, source_target_pairs={{0,1},{1,2},{2,3},{3,4},{4,5},{5,6},{6,7},{7,8},{8,9},{9,10},{10,1... | collective-permute-start | bytes 24584 | tf_op jit(solution)/shard_map/ppermute | solution.py:19
  94.2 1.9 %collective-permute-start.10 = (bf16[32,128]{1,0:T(8,128)(2,1)S(1)}, bf16[32,128]{1,0:T(8,128)(2,1)S(1)}, u32[]{:S(2)}, u32[]{:S(2)}) collective-permute-start(bf16[32,128]{1,0:T(8,128)(2,1)S(1)} %get-tuple-element.92), channel_id=1, source_target_pairs={{1,0},{2,1},{3,2},{4,3},{5,4},{6,5},{7,6},{8,7},{9,8},{10,9},{11,1... | collective-permute-start | bytes 24584 | tf_op jit(solution)/shard_map/ppermute | solution.py:19
  96.2 0.9 shard_map.118
  97.0 2.2 %collective-permute-done.10.yhi_ref.yhi = bf16[32,128]{1,0:T(8,128)(2,1)S(1)} collective-permute-done((bf16[32,128]{1,0:T(8,128)(2,1)S(1)}, bf16[32,128]{1,0:T(8,128)(2,1)S(1)}, u32[]{:S(2)}, u32[]{:S(2)}) %collective-permute-start.10) | collective-permute-done | bytes 8224 | tf_op jit(solution)/shard_map/ppermute | solution.py:19
  99.2 4.1 %all-to-all-start.2 = ((bf16[32,80,128]{2,1,0:T(8,128)(2,1)}), bf16[32,80,128]{2,1,0:T(8,128)(2,1)S(1)}, u32[]{:S(2)}, u32[]{:S(2)}) async-start(bf16[32,80,128]{2,1,0:T(8,128)(2,1)} %shard_map.118), calls=%async_computation.2 | async-start | bytes 1310720 | tf_op jit(solution)/shard_map/all_to_all | solution.py:512
  103.3 0.1 shard_map.120
  103.5 3.1 %collective-permute-start.11 = (bf16[160,128]{1,0:T(8,128)(2,1)S(1)}, bf16[160,128]{1,0:T(8,128)(2,1)S(1)}, u32[]{:S(2)}, u32[]{:S(2)}) collective-permute-start(bf16[160,128]{1,0:T(8,128)(2,1)S(1)} %get-tuple-element.97), channel_id=1, source_target_pairs={{0,16},{16,32},{32,48},{48,64},{64,80},{80,96},{96,112},{112,128},... | collective-permute-start | bytes 122888 | tf_op jit(solution)/shard_map/ppermute | solution.py:19
  106.6 1.3 collective-permute-start.12
  107.9 1.5 %shard_map.121 = bf16[2,8,32,64]{3,2,1,0:T(8,128)(2,1)} custom-call(bf16[2,10,32,64]{3,2,1,0:T(8,128)(2,1)S(1)} %get-tuple-element.72.enc_ref, bf16[2,10,32,64]{3,2,1,0:T(8,128)(2,1)S(1)} %get-tuple-element.99.lifted_ref, bf16[352,128]{1,0:T(8,128)(2,1)S(1)} %collective-permute-done.7.xlo, bf16[352,128]{1,0:T(8,128)(2,1)S(1)} %collective-permute-done.8.xhi, ...), custom_call_target="tpu_custom_call" | custom-call | flops 1000000 | bytes 10000 | tf_op jit(solution)/shard_map/pallas_call | solution.py:31
  109.4 4.3 %collective-permute-done.11.xlo = bf16[160,128]{1,0:T(8,128)(2,1)S(1)} collective-permute-done((bf16[160,128]{1,0:T(8,128)(2,1)S(1)}, bf16[160,128]{1,0:T(8,128)(2,1)S(1)}, u32[]{:S(2)}, u32[]{:S(2)}) %collective-permute-start.11) | collective-permute-done | bytes 40992 | tf_op jit(solution)/shard_map/ppermute | solution.py:19
  113.7 5.0 %collective-permute-done.12.xhi = bf16[160,128]{1,0:T(8,128)(2,1)S(1)} collective-permute-done((bf16[160,128]{1,0:T(8,128)(2,1)S(1)}, bf16[160,128]{1,0:T(8,128)(2,1)S(1)}, u32[]{:S(2)}, u32[]{:S(2)}) %collective-permute-start.12) | collective-permute-done | bytes 40992 | tf_op jit(solution)/shard_map/ppermute | solution.py:19
  118.7 0.7 all-to-all-done.2.own_ref
  119.4 7.4 %collective-permute-start.13 = (bf16[32,80,128]{2,1,0:T(8,128)(2,1)S(1)}, bf16[32,80,128]{2,1,0:T(8,128)(2,1)S(1)}, u32[]{:S(2)}, u32[]{:S(2)}) collective-permute-start(bf16[32,80,128]{2,1,0:T(8,128)(2,1)S(1)} %all-to-all-done.2.own_ref), channel_id=1, source_target_pairs={{0,1},{1,0},{2,3},{3,2},{4,5},{5,4},{6,7},{7,6},{8,9},{9,8},{10,11... | collective-permute-start | bytes 1966088 | tf_op jit(solution)/shard_map/ppermute | solution.py:27
  126.8 1.3 shard_map.122
  128.1 0.4 collective-permute-done.13.other_ref
  128.5 1.8 %shard_map.123 = (f32[27,64,64]{2,1,0:T(8,128)}, f32[27,64,128]{2,1,0:T(8,128)}, f32[27,64,128]{2,1,0:T(8,128)}, f32[8,64,128]{2,1,0:T(8,128)}) custom-call(s32[1]{0:T(128)} %bitcast.7.core, bf16[32,80,128]{2,1,0:T(8,128)(2,1)S(1)} %all-to-all-done.2.own_ref, bf16[32,80,128]{2,1,0:T(8,128)(2,1)S(1)} %collective-permute-done.13.other_ref), custom_call_target="tpu_custom_call" | custom-call | flops 1000000 | bytes 10000 | tf_op jit(solution)/shard_map/pallas_call | solution.py:31
  (18 shorter events, 0.1 us)
Async XLA Ops:
  0.6 0.9 copy-start
  1.5 0.9 copy-start.1
  2.9 18.3 %collective-permute-start = (bf16[12,32,128]{2,1,0:T(8,128)(2,1)S(1)}, bf16[12,32,128]{2,1,0:T(8,128)(2,1)S(1)}, u32[]{:S(2)}, u32[]{:S(2)}) collective-permute-start(bf16[12,32,128]{2,1,0:T(8,128)(2,1)S(1)} %get-tuple-element.60), channel_id=1, source_target_pairs={{0,16},{16,32},{32,48},{48,64},{64,80},{80,96},{96,112},{112,128},... | collective-permute-start | bytes 294920 | tf_op jit(solution)/shard_map/ppermute | solution.py:19
  6.9 14.3 %collective-permute-start.1 = (bf16[12,32,128]{2,1,0:T(8,128)(2,1)S(1)}, bf16[12,32,128]{2,1,0:T(8,128)(2,1)S(1)}, u32[]{:S(2)}, u32[]{:S(2)}) collective-permute-start(bf16[12,32,128]{2,1,0:T(8,128)(2,1)S(1)} %get-tuple-element.61), channel_id=1, source_target_pairs={{16,0},{32,16},{48,32},{64,48},{80,64},{96,80},{112,96},{128,112},... | collective-permute-start | bytes 294920 | tf_op jit(solution)/shard_map/ppermute | solution.py:19
  8.2 6.3 %collective-permute-start.2 = (bf16[4,32,128]{2,1,0:T(8,128)(2,1)S(1)}, bf16[4,32,128]{2,1,0:T(8,128)(2,1)S(1)}, u32[]{:S(2)}, u32[]{:S(2)}) collective-permute-start(bf16[4,32,128]{2,1,0:T(8,128)(2,1)S(1)} %get-tuple-element.62), channel_id=1, source_target_pairs={{0,32},{16,48},{32,64},{48,80},{64,96},{80,112},{96,128},{112,144}... | collective-permute-start | bytes 98312 | tf_op jit(solution)/shard_map/ppermute | solution.py:19
  13.2 8.0 %collective-permute-start.3 = (bf16[4,32,128]{2,1,0:T(8,128)(2,1)S(1)}, bf16[4,32,128]{2,1,0:T(8,128)(2,1)S(1)}, u32[]{:S(2)}, u32[]{:S(2)}) collective-permute-start(bf16[4,32,128]{2,1,0:T(8,128)(2,1)S(1)} %get-tuple-element.63), channel_id=1, source_target_pairs={{32,0},{48,16},{64,32},{80,48},{96,64},{112,80},{128,96},{144,112}... | collective-permute-start | bytes 98312 | tf_op jit(solution)/shard_map/ppermute | solution.py:19
  21.5 13.5 %collective-permute-start.4 = (bf16[6,5,32,128]{3,2,1,0:T(8,128)(2,1)S(1)}, bf16[6,5,32,128]{3,2,1,0:T(8,128)(2,1)S(1)}, u32[]{:S(2)}, u32[]{:S(2)}) collective-permute-start(bf16[6,5,32,128]{3,2,1,0:T(8,128)(2,1)S(1)} %get-tuple-element.64), channel_id=1, source_target_pairs={{0,1},{1,2},{2,3},{3,4},{4,5},{5,6},{6,7},{7,8},{8,9},{9,10},{10,1... | collective-permute-start | bytes 737288 | tf_op jit(solution)/shard_map/ppermute | solution.py:19
  27.8 7.5 %collective-permute-start.5 = (bf16[6,5,32,128]{3,2,1,0:T(8,128)(2,1)S(1)}, bf16[6,5,32,128]{3,2,1,0:T(8,128)(2,1)S(1)}, u32[]{:S(2)}, u32[]{:S(2)}) collective-permute-start(bf16[6,5,32,128]{3,2,1,0:T(8,128)(2,1)S(1)} %get-tuple-element.65.first_ref), channel_id=1, source_target_pairs={{1,0},{2,1},{3,2},{4,3},{5,4},{6,5},{7,6},{8,7},{9,8},{10,9},{11,1... | collective-permute-start | bytes 737288 | tf_op jit(solution)/shard_map/ppermute | solution.py:19
  29.8 1.0 copy-start.2
  30.8 1.0 copy-start.3
  31.9 1.0 copy-start.4
  32.9 0.9 copy-start.5
  35.1 1.6 %copy-start.6 = (bf16[576,192]{1,0:T(8,128)(2,1)}, bf16[576,192]{1,0:T(8,128)(2,1)S(1)}, u32[]{:S(2)}) copy-start(bf16[576,192]{1,0:T(8,128)(2,1)S(1)} %get-tuple-element.104.w_ref) | copy-start | bytes 663556
  42.9 4.0 %collective-permute-start.6 = (bf16[32,80,128]{2,1,0:T(8,128)(2,1)S(1)}, bf16[32,80,128]{2,1,0:T(8,128)(2,1)S(1)}, u32[]{:S(2)}, u32[]{:S(2)}) collective-permute-start(bf16[32,80,128]{2,1,0:T(8,128)(2,1)S(1)} %get-tuple-element.82), channel_id=1, source_target_pairs={{0,1},{1,0},{2,3},{3,2},{4,5},{5,4},{6,7},{7,6},{8,9},{9,8},{10,11... | collective-permute-start | bytes 1966088 | tf_op jit(solution)/shard_map/ppermute | solution.py:27
  47.9 24.9 %all-to-all-start = ((bf16[32,80,128]{2,1,0:T(8,128)(2,1)}), bf16[32,80,128]{2,1,0:T(8,128)(2,1)S(1)}, u32[]{:S(2)}, u32[]{:S(2)}) async-start(bf16[32,80,128]{2,1,0:T(8,128)(2,1)} %shard_map.116), calls=%async_computation | async-start | bytes 1310720 | tf_op jit(solution)/shard_map/all_to_all | solution.py:498
  56.0 17.5 %collective-permute-start.7 = (bf16[352,128]{1,0:T(8,128)(2,1)S(1)}, bf16[352,128]{1,0:T(8,128)(2,1)S(1)}, u32[]{:S(2)}, u32[]{:S(2)}) collective-permute-start(bf16[352,128]{1,0:T(8,128)(2,1)S(1)} %get-tuple-element.86), channel_id=1, source_target_pairs={{0,16},{16,32},{32,48},{48,64},{64,80},{80,96},{96,112},{112,128},... | collective-permute-start | bytes 270344 | tf_op jit(solution)/shard_map/ppermute | solution.py:19
  59.2 14.5 %collective-permute-start.8 = (bf16[352,128]{1,0:T(8,128)(2,1)S(1)}, bf16[352,128]{1,0:T(8,128)(2,1)S(1)}, u32[]{:S(2)}, u32[]{:S(2)}) collective-permute-start(bf16[352,128]{1,0:T(8,128)(2,1)S(1)} %get-tuple-element.87), channel_id=1, source_target_pairs={{16,0},{32,16},{48,32},{64,48},{80,64},{96,80},{112,96},{128,112},... | collective-permute-start | bytes 270344 | tf_op jit(solution)/shard_map/ppermute | solution.py:19
  73.7 22.5 %all-to-all-start.1 = ((bf16[8,80,128]{2,1,0:T(8,128)(2,1)}), bf16[8,80,128]{2,1,0:T(8,128)(2,1)S(1)}, u32[]{:S(2)}, u32[]{:S(2)}) async-start(bf16[8,80,128]{2,1,0:T(8,128)(2,1)} %shard_map.117), calls=%async_computation.1 | async-start | bytes 327680 | tf_op jit(solution)/shard_map/all_to_all | solution.py:502
  84.5 12.5 %collective-permute-start.9 = (bf16[32,128]{1,0:T(8,128)(2,1)S(1)}, bf16[32,128]{1,0:T(8,128)(2,1)S(1)}, u32[]{:S(2)}, u32[]{:S(2)}) collective-permute-start(bf16[32,128]{1,0:T(8,128)(2,1)S(1)} %get-tuple-element.91), channel_id=1, source_target_pairs={{0,1},{1,2},{2,3},{3,4},{4,5},{5,6},{6,7},{7,8},{8,9},{9,10},{10,1... | collective-permute-start | bytes 24584 | tf_op jit(solution)/shard_map/ppermute | solution.py:19
  94.2 5.0 %collective-permute-start.10 = (bf16[32,128]{1,0:T(8,128)(2,1)S(1)}, bf16[32,128]{1,0:T(8,128)(2,1)S(1)}, u32[]{:S(2)}, u32[]{:S(2)}) collective-permute-start(bf16[32,128]{1,0:T(8,128)(2,1)S(1)} %get-tuple-element.92), channel_id=1, source_target_pairs={{1,0},{2,1},{3,2},{4,3},{5,4},{6,5},{7,6},{8,7},{9,8},{10,9},{11,1... | collective-permute-start | bytes 24584 | tf_op jit(solution)/shard_map/ppermute | solution.py:19
  97.0 29.7 %copy-start.7 = (bf16[576,192]{1,0:T(8,128)(2,1)S(1)}, bf16[576,192]{1,0:T(8,128)(2,1)}, u32[]{:S(2)}) copy-start(bf16[576,192]{1,0:T(8,128)(2,1)} %copy-done.6) | copy-start | bytes 663556
  99.2 20.1 %all-to-all-start.2 = ((bf16[32,80,128]{2,1,0:T(8,128)(2,1)}), bf16[32,80,128]{2,1,0:T(8,128)(2,1)S(1)}, u32[]{:S(2)}, u32[]{:S(2)}) async-start(bf16[32,80,128]{2,1,0:T(8,128)(2,1)} %shard_map.118), calls=%async_computation.2 | async-start | bytes 1310720 | tf_op jit(solution)/shard_map/all_to_all | solution.py:512
  103.5 10.2 %collective-permute-start.11 = (bf16[160,128]{1,0:T(8,128)(2,1)S(1)}, bf16[160,128]{1,0:T(8,128)(2,1)S(1)}, u32[]{:S(2)}, u32[]{:S(2)}) collective-permute-start(bf16[160,128]{1,0:T(8,128)(2,1)S(1)} %get-tuple-element.97), channel_id=1, source_target_pairs={{0,16},{16,32},{32,48},{48,64},{64,80},{80,96},{96,112},{112,128},... | collective-permute-start | bytes 122888 | tf_op jit(solution)/shard_map/ppermute | solution.py:19
  106.6 12.1 %collective-permute-start.12 = (bf16[160,128]{1,0:T(8,128)(2,1)S(1)}, bf16[160,128]{1,0:T(8,128)(2,1)S(1)}, u32[]{:S(2)}, u32[]{:S(2)}) collective-permute-start(bf16[160,128]{1,0:T(8,128)(2,1)S(1)} %get-tuple-element.98), channel_id=1, source_target_pairs={{16,0},{32,16},{48,32},{64,48},{80,64},{96,80},{112,96},{128,112},... | collective-permute-start | bytes 122888 | tf_op jit(solution)/shard_map/ppermute | solution.py:19
  119.4 9.1 %collective-permute-start.13 = (bf16[32,80,128]{2,1,0:T(8,128)(2,1)S(1)}, bf16[32,80,128]{2,1,0:T(8,128)(2,1)S(1)}, u32[]{:S(2)}, u32[]{:S(2)}) collective-permute-start(bf16[32,80,128]{2,1,0:T(8,128)(2,1)S(1)} %all-to-all-done.2.own_ref), channel_id=1, source_target_pairs={{0,1},{1,0},{2,3},{3,2},{4,5},{5,4},{6,7},{7,6},{8,9},{9,8},{10,11... | collective-permute-start | bytes 1966088 | tf_op jit(solution)/shard_map/ppermute | solution.py:27

commit v6 on v5

--- a/solution.py
+++ b/solution.py
@@ -101,48 +101,31 @@
     )
 
 
-def assemble(ext, own, ylo, yhi, xlo, xhi):
-    size_x, size_y = own.shape[:2]
-    ext[1 : 1 + size_x, 1 : 1 + size_y] = own
-    ext[1 : 1 + size_x, 0:1] = ylo
-    ext[1 : 1 + size_x, 1 + size_y : 2 + size_y] = yhi
-    ext[0:1] = xlo
-    ext[1 + size_x : 2 + size_x] = xhi
-
-
-def fetched(sems, *pairs):
-    copies = [pltpu.make_async_copy(a, b, sems.at[k]) for k, (a, b) in enumerate(pairs)]
-    for copy in copies:
-        copy.start()
-    for copy in copies:
-        copy.wait()
-
-
-def stack_kernel(first_ref, enc_ref, low_ref, dec_ref, lift_ref, *refs):
-    outs, lift_out, (enc, low, dec, sems) = refs[:6], refs[6], refs[7:]
-    fetched(sems, (enc_ref, enc), (low_ref, low), (dec_ref, dec), (lift_ref, lift_out))
+def stack_kernel(first_ref, enc_ref, low_ref, dec_ref, lift_ref, *outs):
     for ref, forward, backward in (
-        (enc, nt_weight, nn_weight),
-        (low, nn_weight, nt_weight),
-        (dec, nt_weight, nn_weight),
+        (enc_ref, nt_weight, nn_weight),
+        (low_ref, nn_weight, nt_weight),
+        (dec_ref, nt_weight, nn_weight),
     ):
         outs[0][...] = forward(ref)
         outs[1][...] = backward(ref)
         outs = outs[2:]
-
-
-def pack_x_kernel(f_any, c_any, f_ref, c_ref, lo_ref, hi_ref, lo2_ref, hi2_ref, sems):
-    fetched(sems, (f_any, f_ref), (c_any, c_ref))
-    paired = [jnp.concatenate([f_ref[x, 0:4], f_ref[x, 4:8]], -1) for x in range(2)]
+    outs[0][...] = lift_ref[...]
+
+
+def pack_x_kernel(f_in, c_in, f_ref, c_ref, lo_ref, hi_ref, lo2_ref, hi2_ref):
+    f_ref[...] = f_in[...]
+    c_ref[...] = c_in[...]
+    paired = [jnp.concatenate([f_in[x, 0:4], f_in[x, 4:8]], -1) for x in range(2)]
     for x, out, out2 in ((0, lo_ref, lo2_ref), (1, hi_ref, hi2_ref)):
-        out[0:8] = jnp.concatenate([f_ref[x], c_ref[x]], -1)
+        out[0:8] = jnp.concatenate([f_in[x], c_in[x]], -1)
         out[8:12] = paired[1 - x]
         out2[...] = paired[x]
 
 
 def pack_y_kernel(f_ref, c_ref, xlo, xhi, xlo2, xhi2, lo_ref, hi_ref):
-    for first, out in ((0, lo_ref), (3, hi_ref)):
-        at = slice(first, first + 5)
+    for first, out in ((0, lo_ref), (1, hi_ref)):
+        at = slice(first, first + 7)
         out[0] = xlo[at]
         for x in range(2):
             out[1 + x] = jnp.concatenate([f_ref[x, at], c_ref[x, at]], -1)
@@ -155,66 +138,72 @@
 def encode_kernel(
     f_ref, ylo, yhi, xlo, xhi, xlo2, xhi2, inside, w_ref, fx_ref, enc_ref, slope_ref, pool_ref, tmp
 ):
-    fx_ref[3:5, 5:13] = f_ref[...]
-    fx_ref[2, 5:13] = xlo[0:8, :, :64]
-    fx_ref[5, 5:13] = xhi[0:8, :, :64]
+    fx_ref[3:5, 7:15] = f_ref[...]
+    fx_ref[2, 7:15] = xlo[0:8, :, :64]
+    fx_ref[5, 7:15] = xhi[0:8, :, :64]
     for x, ref, first in ((1, xlo, 8), (6, xhi, 8), (0, xlo2, 0), (7, xhi2, 0)):
-        fx_ref[x, 5:9] = ref[first : first + 4, :, :64]
-        fx_ref[x, 9:13] = ref[first : first + 4, :, 64:]
-    for y, ref in ((0, ylo), (13, yhi)):
-        at = slice(y, y + 5)
+        fx_ref[x, 7:11] = ref[first : first + 4, :, :64]
+        fx_ref[x, 11:15] = ref[first : first + 4, :, 64:]
+    for y, ref in ((0, ylo), (15, yhi)):
+        at = slice(y, y + 7)
         fx_ref[2:6, at] = ref[0:4, :, :, :64]
         for x, k in ((0, 4), (6, 5)):
             fx_ref[x, at] = ref[k, :, :, :64]
             fx_ref[x + 1, at] = ref[k, :, :, 64:]
     weight = w_ref[...]
+
+    def edged(value, x):
+        if x < 2 or x > 3:
+            value = value * inside[0 if x < 2 else 1]
+        return jnp.concatenate(
+            [value[0:32] * inside[2], value[32:288], value[288:320] * inside[3]], 0
+        )
+
     for x in range(6):
-        pre = combined(nt(stacked(fx_ref, x, 1, 16, False), weight), 32, False)
+        pre = combined(nt(stacked(fx_ref, x, 1, 20, False), weight), 32, False)
         sigma = jax.nn.sigmoid(pre)
-        enc = (pre * sigma).astype(BF16)
-        slope = sigma[128:384] * (1.0 + pre[128:384] * (1.0 - sigma[128:384]))
-        slope_ref[x] = slope if x in (2, 3) else slope * inside[0 if x < 2 else 1]
-        if x in (2, 3):
-            enc_ref[x - 2, 1:9] = enc[128:384].reshape(8, 32, 64)
-            enc_ref[x - 2, 0] = (enc[96:128].astype(F32) * inside[2]).astype(BF16)
-            enc_ref[x - 2, 9] = (enc[384:416].astype(F32) * inside[3]).astype(BF16)
-        wide = enc.astype(F32).reshape(8, 2, 32, 64)
+        enc = (pre * sigma).astype(BF16).astype(F32)
+        near, slope = pre[160:480], sigma[160:480]
+        slope_ref[x] = edged(slope * (1.0 + near * (1.0 - slope)), x)
+        if 0 < x < 5:
+            enc_ref[x - 1] = edged(enc[160:480], x).astype(BF16).reshape(10, 32, 64)
+        wide = enc.reshape(10, 2, 32, 64)
         part = wide[:, 0] + wide[:, 1]
         if x % 2 == 0:
             held = part
             continue
-        tmp[...] = (held + part).reshape(256, 64)
-        pooled = tmp[pl.ds(0, 128, stride=2), :] + tmp[pl.ds(1, 128, stride=2), :]
+        tmp[...] = (held + part).reshape(320, 64)
+        pooled = tmp[pl.ds(0, 160, stride=2), :] + tmp[pl.ds(1, 160, stride=2), :]
         pooled = pooled * (0.125 if x == 3 else 0.125 * inside[0 if x == 1 else 1])
-        pool_ref[x // 2, 2:6] = pooled[32:96].astype(BF16).reshape(4, 16, 64)
-        pool_ref[x // 2, 0:2] = (pooled[0:32] * inside[2]).astype(BF16).reshape(2, 16, 64)
-        pool_ref[x // 2, 6:8] = (pooled[96:128] * inside[3]).astype(BF16).reshape(2, 16, 64)
+        pool_ref[x // 2, 3:7] = pooled[48:112].astype(BF16).reshape(4, 16, 64)
+        pool_ref[x // 2, 0:3] = (pooled[0:48] * inside[2]).astype(BF16).reshape(3, 16, 64)
+        pool_ref[x // 2, 7:10] = (pooled[112:160] * inside[3]).astype(BF16).reshape(3, 16, 64)
 
 
 def joined_grad_kernel(c_ref, *refs):
     (ylo, yhi, xlo, xhi), (w_ref, lift_ref) = refs[:4], refs[4:6]
     cx_ref, jg_ref, kids_ref, adj_ref, tmp = refs[6:]
-    cx_ref[1:3, 3:11] = c_ref[...]
-    cx_ref[0, 3:11] = xlo[0:8, :, 64:]
-    cx_ref[3, 3:11] = xhi[0:8, :, 64:]
-    cx_ref[:, 0:3] = ylo[0:4, 2:5, :, 64:]
-    cx_ref[:, 11:14] = yhi[0:4, 0:3, :, 64:]
+    cx_ref[1:3, 5:13] = c_ref[...]
+    cx_ref[0, 5:13] = xlo[0:8, :, 64:]
+    cx_ref[3, 5:13] = xhi[0:8, :, 64:]
+    cx_ref[:, 0:5] = ylo[0:4, 2:7, :, 64:]
+    cx_ref[:, 13:18] = yhi[0:4, 0:5, :, 64:]
     weight = w_ref[...]
     for x in range(2):
-        grad = combined(nn(stacked(cx_ref, x, 1, 12, True), weight), 32, True)
+        grad = combined(nn(stacked(cx_ref, x, 1, 16, True), weight), 32, True)
         grad = grad.astype(BF16)
-        jg_ref[pl.ds(x * 256, 256), :] = grad[64:320, :64]
-        tmp[pl.ds(x * 384, 384), :] = grad.astype(F32)
+        jg_ref[x] = grad[96:416, :64]
+        tmp[pl.ds(x * 512, 512), :] = grad.astype(F32)
     kids = []
     for p in range(2):
         for q in range(2):
             for r in range(2):
                 rows = [
-                    tmp[pl.ds(p * 384 + (2 * j + q) * 32 + r, 16, stride=2), :] for j in range(6)
+                    tmp[pl.ds(p * 512 + (2 * j + q) * 32 + r, 16, stride=2), :] for j in range(8)
                 ]
                 kids.append(jnp.concatenate(rows, 0)[:, 64:])
     kids = jnp.concatenate(kids, -1).astype(BF16)
-    kids_ref[...] = kids[16:80]
+    kids_ref[...] = kids[32:96]
     adj_ref[...] = nn(kids, lift_ref[...].reshape(512, 128))
 
 
@@ -228,29 +217,27 @@
     return put
 
 
-def lower_kernel(px, inside, w_ref, adj_ref, enc_ref, la_ref, lg_ref, lo_ref, hi_ref):
+def lower_kernel(px, inside, w_ref, adj_ref, la_ref, lg_ref, msg_ref):
     def masked(value):
-        first, last = value[0:16] * inside[2], value[80:96] * inside[3]
-        return jnp.concatenate([first, value[16:80], last], 0).astype(BF16)
-
-    pre = combined(nn(stacked(px, 0, 1, 6, False), w_ref[...]), 16, False)
+        first, last = value[0:32] * inside[2], value[96:128] * inside[3]
+        return jnp.concatenate([first, value[32:96], last], 0).astype(BF16)
+
+    pre = combined(nn(stacked(px, 0, 1, 8, False), w_ref[...]), 16, False)
     sigma = jax.nn.sigmoid(pre)
     la = masked(pre * sigma)
     lg = masked(adj_ref[...] * (sigma * (1.0 + pre * (1.0 - sigma))))
-    la_ref[...] = la
+    la_ref[...] = la[16:112]
     lg_ref[...] = lg
-    for x, msg in ((0, lo_ref), (1, hi_ref)):
-        msg[0:96] = la
-        msg[96:192] = lg
-        enc = enc_ref[x].reshape(320, 64)
-        msg[192:352] = jnp.concatenate([enc[:160], enc[160:]], -1)
+    msg_ref[0:96] = la[16:112]
+    msg_ref[96:224] = lg
 
 
 def doubled(coarse, tmp):
-    tmp[pl.ds(0, 64, stride=2), :] = coarse
-    tmp[pl.ds(1, 64, stride=2), :] = coarse
-    wide = tmp[...].reshape(4, 1, 32, 64)
-    return jnp.broadcast_to(wide, (4, 2, 32, 64)).reshape(256, 64)
+    rows = coarse.shape[0]
+    tmp[pl.ds(0, rows, stride=2), :] = coarse
+    tmp[pl.ds(1, rows, stride=2), :] = coarse
+    wide = tmp[...].reshape(rows // 16, 1, 32, 64)
+    return jnp.broadcast_to(wide, (rows // 16, 2, 32, 64)).reshape(4 * rows, 64)
 
 
 def grads_kernel(px, la_ref, lg_ref, core, lift_ref, kids_ref, cx_ref, enc_ref, *refs):
@@ -271,15 +258,15 @@
                         ]
     lifted_ref[...] = tmp[...].astype(BF16).reshape(2, 10, 32, 64)
     lifted = jnp.concatenate([tmp[32:288], tmp[352:608]], 0)
-    la, lg = la[16:80], lg[16:80]
-    enc = enc_ref[:, 1:9].reshape(512, 64).astype(F32)
+    la, lg = la[16:80], lg[32:96]
+    enc = enc_ref[1:3, 1:9].reshape(512, 64).astype(F32)
     joined = ztaps(jnp.concatenate([enc, lifted], -1), 32, False)
-    dec = tn(stacked(cx_ref, 0, 2, 8, True, 2), joined)
+    dec = tn(stacked(cx_ref, 0, 2, 8, True, 4), joined)
     for ab in range(9):
         for c in range(3):
             block = dec[64 * ab : 64 * ab + 64, 128 * c : 128 * c + 128]
             put((3 * ab + c) * 64, block)
-    low = tn(stacked(px, 0, 1, 4, False, 1), ztaps(lg.astype(F32), 16, True))
+    low = tn(stacked(px, 0, 1, 4, False, 2), ztaps(lg.astype(F32), 16, True))
     for ab in range(9):
         for c in range(3):
             block = low[64 * ab : 64 * ab + 64, 128 * c : 128 * c + 128]
@@ -289,18 +276,18 @@
         put(3456 + 64 * k, lift[64 * k : 64 * k + 64])
     for row in (3968, 4032):
         put(row, jnp.zeros((64, 128), F32))
-    lg = lg_ref[...].reshape(6, 16, 128)
-    source = jnp.concatenate([lg[2 - b : 6 - b].reshape(64, 128) for b in range(3)], -1)
+    lg = lg_ref[...].reshape(8, 16, 128)
+    source = jnp.concatenate([lg[3 - b : 7 - b].reshape(64, 128) for b in range(3)], -1)
     grad = jnp.zeros((192, 576), F32)
     for a in range(3):
         pg = combined(nt(source, w_ref[:, 384 * a : 384 * a + 384]), 16, True)
         fine = doubled(pg * 0.125, wide)
         parts = []
         for x in (2 * a, 2 * a + 1):
-            own = fine if a != 1 else fine + jg_ref[256 * x - 512 : 256 * x - 256].astype(F32)
-            parts.append(own * slope_ref[x])
+            own = fine if a != 1 else fine + jg_ref[x - 2, 32:288].astype(F32)
+            parts.append(own * slope_ref[x, 32:288])
         eg = ztaps(jnp.concatenate(parts, 0), 32, True)
-        grad = grad + tn(eg, stacked(fx_ref, 2 * a, 2, 8, False, 4))
+        grad = grad + tn(eg, stacked(fx_ref, 2 * a, 2, 8, False, 6))
     for ab in range(9):
         for c in range(3):
             block = grad[64 * c : 64 * c + 64, 64 * ab : 64 * ab + 64]
@@ -320,24 +307,6 @@
     out_ref[...] = (a_ref[...].astype(F32) + b_ref[...].astype(F32)).astype(LINK)
 
 
-def edge_y_kernel(eg_ref, lo_ref, hi_ref):
-    lo_ref[...] = jnp.concatenate([eg_ref[0, 0], eg_ref[1, 0]], -1)
-    hi_ref[...] = jnp.concatenate([eg_ref[0, 7], eg_ref[1, 7]], -1)
-
-
-def edge_x_kernel(eg_ref, ylo_ref, yhi_ref, lo_ref, hi_ref):
-    for x, out in ((0, lo_ref), (1, hi_ref)):
-        cols = slice(64 * x, 64 * x + 64)
-        eg = eg_ref[x].reshape(256, 64)
-        first = jnp.concatenate([ylo_ref[:, cols], eg[:128]], 0)
-        second = jnp.concatenate([eg[128:], yhi_ref[:, cols]], 0)
-        out[...] = jnp.concatenate([first, second], -1)
-
-
-def column(rows):
-    return jnp.stack([rows[:, :64], rows[:, 64:]], 0).reshape(2, 1, 32, 64)
-
-
 def plane(rows):
     return jnp.concatenate([rows[:, :64], rows[:, 64:]], 0).reshape(1, 10, 32, 64)
 
@@ -345,19 +314,19 @@
 def encoder_grad_kernel(
     lg_ref, xlo, xhi, w_ref, slope_ref, jg_ref, eg_ref, lo_ref, hi_ref, lx, tmp
 ):
-    lx[0] = xlo[96:192].reshape(6, 16, 128)
-    lx[1] = lg_ref[...].reshape(6, 16, 128)
-    lx[2] = xhi[96:192].reshape(6, 16, 128)
-    pg = combined(nt(stacked(lx, 0, 1, 4, True), w_ref[...]), 16, True)
-    fine = doubled(pg.astype(BF16).astype(F32) * 0.125, tmp)
-    for x in range(2):
-        total = jg_ref[256 * x : 256 * x + 256].astype(F32) + fine
-        eg_ref[x] = (total * slope_ref[2 + x]).astype(BF16).reshape(8, 32, 64)
-    edge_y_kernel(eg_ref, lo_ref, hi_ref)
+    lx[0] = xlo[96:224].reshape(8, 16, 128)
+    lx[1] = lg_ref[...].reshape(8, 16, 128)
+    lx[2] = xhi[96:224].reshape(8, 16, 128)
+    pg = combined(nt(stacked(lx, 0, 1, 6, True), w_ref[...]), 16, True)
+    fine = doubled(pg.astype(BF16).astype(F32) * 0.125, tmp)[32:352]
+    for x, msg in ((0, lo_ref), (1, hi_ref)):
+        eg = ((jg_ref[x].astype(F32) + fine) * slope_ref[2 + x]).astype(BF16)
+        eg_ref[x] = eg.reshape(10, 32, 64)
+        msg[...] = jnp.concatenate([eg[:160], eg[160:]], -1)
 
 
 def decode_kernel(enc_ref, lifted_ref, xlo, xhi, lift_ref, w_ref, out_ref, jx, tx):
-    jx[1:3] = jnp.concatenate([enc_ref[...], lifted_ref[...]], -1)
+    jx[1:3] = jnp.concatenate([enc_ref[1:3], lifted_ref[...]], -1)
     for p, h in ((1, xlo), (0, xhi)):
         for q in range(2):
             for r in range(2):
@@ -368,16 +337,17 @@
                         tx[pl.ds(32 * y + r, 16, stride=2), :] = fine[16 * j : 16 * j + 16]
         lifted = tx[...].astype(BF16).reshape(1, 10, 32, 64)
         x = 0 if p == 1 else 3
-        jx[x : x + 1] = jnp.concatenate([plane(h[192:352]), lifted], -1)
+        jx[x : x + 1] = jnp.concatenate([enc_ref[x : x + 1], lifted], -1)
     weight = w_ref[...]
     for x in range(2):
         out = combined(nt(stacked(jx, x, 1, 8, False), weight), 32, False)
         out_ref[x] = out.astype(BF16).reshape(8, 32, 64)
 
 
-def input_grad_kernel(eg_ref, ylo, yhi, xlo, xhi, w_ref, out_ref, ex):
-    sides = [column(ylo[...]), column(yhi[...]), plane(xlo[...]), plane(xhi[...])]
-    assemble(ex, eg_ref[...], *sides)
+def input_grad_kernel(eg_ref, xlo, xhi, w_ref, out_ref, ex):
+    ex[0:1] = plane(xlo[...])
+    ex[1:3] = eg_ref[...]
+    ex[3:4] = plane(xhi[...])
     weight = w_ref[...]
     for x in range(2):
         out = combined(nn(stacked(ex, x, 1, 8, True), weight), 32, True)
@@ -421,15 +391,14 @@
     f, c, lo, hi, lo2, hi2 = call(
         pack_x_kernel,
         [(brick, BF16)] * 2 + [((12, 32, 128), BF16)] * 2 + [((4, 32, 128), BF16)] * 2,
-        [(pltpu.SemaphoreType.DMA((2,)), None)],
+        [],
         [f, c],
-        spaces={0: pltpu.HBM, 1: pltpu.HBM},
     )
     x_halo = swapped(lo, hi, GX)
     far_halo = [shifted(hi2, GX, 2), shifted(lo2, GX, -2)]
     edges = call(
         pack_y_kernel,
-        [((6, 5, 32, 128), BF16)] * 2,
+        [((6, 7, 32, 128), BF16)] * 2,
         [],
         [f, c, *x_halo, *far_halo],
     )
@@ -445,40 +414,36 @@
             ((576, 384), BF16),
             ((8, 64, 128), BF16),
         ],
-        [
-            ((27, 64, 64), BF16),
-            ((27, 64, 128), BF16),
-            ((27, 64, 128), BF16),
-            (pltpu.SemaphoreType.DMA((4,)), None),
-        ],
+        [],
         [edges[0], encoder_weight, lower_t, decoder_weight, lift_weight],
-        spaces={k: pltpu.HBM for k in range(5)},
+        spaces={0: pltpu.HBM},
         flops=2 * 10**9,
     )
     fx, encoded, slope, pooled = call(
         encode_kernel,
-        [((8, 18, 32, 64), BF16), (tall, BF16), ((6, 256, 64), F32), ((3, 8, 16, 64), BF16)],
-        [((256, 64), F32)],
+        [((8, 22, 32, 64), BF16), ((4, 10, 32, 64), BF16)]
+        + [((6, 320, 64), F32), ((3, 10, 16, 64), BF16)],
+        [((320, 64), F32)],
         [f, *y_halo, *x_halo, *far_halo, inside, enc_fwd],
         spaces={7: pltpu.SMEM},
     )
     cx, jg, kids, adj = call(
         joined_grad_kernel,
         [
-            ((4, 14, 32, 64), BF16),
-            ((512, 64), BF16),
+            ((4, 18, 32, 64), BF16),
+            ((2, 320, 64), BF16),
             ((64, 512), BF16),
-            ((96, 128), F32),
+            ((128, 128), F32),
         ],
-        [((768, 128), F32)],
+        [((1024, 128), F32)],
         [c, *y_halo, *x_halo, dec_bwd, lift],
     )
     half = (size_x, 2560 // size_x, 128)
-    la, lg, *edges = call(
+    la, lg, edge = call(
         lower_kernel,
-        [((96, 128), BF16)] * 2 + [((352, 128), BF16)] * 2,
+        [((96, 128), BF16), ((128, 128), BF16), ((224, 128), BF16)],
         [],
-        [pooled, inside, low_fwd, adj, encoded],
+        [pooled, inside, low_fwd, adj],
         spaces={1: pltpu.SMEM},
     )
     lifted, keep, send = call(
@@ -494,38 +459,35 @@
         spaces={3: pltpu.SMEM},
     )
     (sums,) = call(add_kernel, [(half, LINK)], [], [keep, partner(send)])
-    sums, edges = lax.optimization_barrier((sums, edges))
+    sums, edge = lax.optimization_barrier((sums, edge))
     sums = lax.all_to_all(sums, "gx", 0, 0)
-    halo = swapped(*edges, GX)
+    halo = swapped(edge, edge, GX)
     (sums,) = call(sum_kernel, [((size_z,) + half[1:], LINK)], [], [sums])
     sums, halo = lax.optimization_barrier((sums, halo))
     sums = lax.all_to_all(sums, "gz", 0, 0)
     eg, *edges = call(
         encoder_grad_kernel,
-        [(brick, BF16)] + [((32, 128), BF16)] * 2,
-        [((3, 6, 16, 128), BF16), ((128, 64), F32)],
+        [(tall, BF16)] + [((160, 128), BF16)] * 2,
+        [((3, 8, 16, 128), BF16), ((192, 64), F32)],
         [lg, *halo, low_bwd, slope, jg],
     )
-    y_halo = swapped(*edges, GY)
+    eg_halo = swapped(*edges, GX)
     (sums,) = call(sum_kernel, [(half, LINK)], [], [sums])
-    sums, y_halo = lax.optimization_barrier((sums, y_halo))
+    sums, eg_halo = lax.optimization_barrier((sums, eg_halo))
     sums = lax.all_to_all(sums, "gx", 0, 0)
-    edges = call(edge_x_kernel, [((160, 128), BF16)] * 2, [], [eg, *y_halo])
-    x_halo = swapped(*edges, GX)
     (decoded,) = call(
         decode_kernel,
         [(brick, BF16)],
         [((4, 10, 32, 128), BF16), ((320, 64), F32)],
         [encoded, lifted, *halo, lift, dec_fwd],
     )
-    sums, x_halo, decoded = lax.optimization_barrier((sums, x_halo, decoded))
     (input_grad,) = call(
         input_grad_kernel,
         [(brick, BF16)],
         [((4, 10, 32, 64), BF16)],
-        [eg, *y_halo, *x_halo, enc_bwd],
-        flops=2 * 10**9,
-    )
+        [eg, *eg_halo, enc_bwd],
+    )
+    sums, decoded, input_grad = lax.optimization_barrier((sums, decoded, input_grad))
     encoder_gradient, decoder_gradient, lower_gradient, lift_gradient = call(
         widen_kernel,
         [((27, 64, 64), F32), ((27, 64, 128), F32), ((27, 64, 128), F32), ((8, 64, 128), F32)],

time: 131 us -> 129 us (0.985)
  starting transfers between devices: 72.1 us -> 66.7 us
  waiting for transfers between devices: 34 us -> 38.1 us
    all_to_all x2, waiting for transfers between devices: 13 us -> 22.6 us  [per_device(): sums = lax.all_to_all(sums, 'gx', 0, 0)]
    ppermute x12 -> x10, starting transfers between devices: 40.3 us -> 32.6 us  [shifted(): return lax.ppermute(piece, axes, pairs)]
    ppermute x12 -> x10, waiting for transfers between devices: 18.5 us -> 11.5 us  [shifted(): return lax.ppermute(piece, axes, pairs)]
    all_to_all x2, starting transfers between devices: 12.2 us -> 13.8 us  [per_device(): sums = lax.all_to_all(sums, 'gx', 0, 0)]
    ppermute x2, starting transfers between devices: 9.32 us -> 10.9 us  [partner(): return lax.ppermute(piece, 'gc', [(0, 1), (1, 0)])]
    pallas_call x15 -> x14, Pallas kernels: 17.4 us -> 16.9 us  [call(): pl.pallas_call(kernel, out_shape=[jax.ShapeDtypeStruct(s, d) for s, d in...]
  transfers between devices with their start and end apart: 17 -> 15, of which waited for: 10 -> 8; matrix products, arithmetic and copies ran while one was open for 0% -> 0% of each run, Pallas kernels for 5% -> 4%
where the time goes in v6:
time: 129 us; the launch traced here: 128 us
  starting transfers between devices  66.7 us (52%)
  waiting for transfers between devices  38.1 us (30%)
  Pallas kernels  16.9 us (13%)
  local copies, waits for them, and re-layouts  5.76 us (4%)
    ppermute x10, starting transfers between devices, shifted(): return lax.ppermute(piece, axes, pairs)  32.6 us
    all_to_all x2, waiting for transfers between devices, per_device(): sums = lax.all_to_all(sums, 'gx', 0, 0)  22.6 us
    pallas_call x14, Pallas kernels, call(): pl.pallas_call(kernel, out_shape=[jax.ShapeDtypeStruct(s, d) for s, d in...  16.9 us
    all_to_all x2, starting transfers between devices, per_device(): sums = lax.all_to_all(sums, 'gx', 0, 0)  13.8 us
    ppermute x10, waiting for transfers between devices, shifted(): return lax.ppermute(piece, axes, pairs)  11.5 us
    ppermute x2, starting transfers between devices, partner(): return lax.ppermute(piece, 'gc', [(0, 1), (1, 0)])  10.9 us
    all_to_all x1, starting transfers between devices, per_device(): sums = lax.all_to_all(sums, 'gz', 0, 0)  9.41 us
    unnamed x16, local copies, waits for them, and re-layouts  5.76 us
  transfers between devices with their start and end apart: 15, of which 8 were waited for; matrix products, arithmetic and copies ran while one was open for 0% of the time, Pallas kernels for 4%

profile of v6, /device:TPU:1, one launch (start us, length us, event | category | flops | bytes accessed | tf_op | source)
XLA Modules:
  0.0 128.4 jit_solution(6833307244858937614)
XLA Ops:
  0.6 0.9 copy-done.2
  1.5 0.9 copy-done.3
  2.4 0.1 shard_map.109
  2.6 4.0 %collective-permute-start = (bf16[12,32,128]{2,1,0:T(8,128)(2,1)S(1)}, bf16[12,32,128]{2,1,0:T(8,128)(2,1)S(1)}, u32[]{:S(2)}, u32[]{:S(2)}) collective-permute-start(bf16[12,32,128]{2,1,0:T(8,128)(2,1)S(1)} %get-tuple-element.55), channel_id=1, source_target_pairs={{0,16},{16,32},{32,48},{48,64},{64,80},{80,96},{96,112},{112,128},... | collective-permute-start | bytes 294920 | tf_op jit(solution)/shard_map/ppermute | solution.py:19
  6.6 1.3 %collective-permute-start.1 = (bf16[12,32,128]{2,1,0:T(8,128)(2,1)S(1)}, bf16[12,32,128]{2,1,0:T(8,128)(2,1)S(1)}, u32[]{:S(2)}, u32[]{:S(2)}) collective-permute-start(bf16[12,32,128]{2,1,0:T(8,128)(2,1)S(1)} %get-tuple-element.56), channel_id=1, source_target_pairs={{16,0},{32,16},{48,32},{64,48},{80,64},{96,80},{112,96},{128,112},... | collective-permute-start | bytes 294920 | tf_op jit(solution)/shard_map/ppermute | solution.py:19
  7.9 5.0 %collective-permute-start.2 = (bf16[4,32,128]{2,1,0:T(8,128)(2,1)S(1)}, bf16[4,32,128]{2,1,0:T(8,128)(2,1)S(1)}, u32[]{:S(2)}, u32[]{:S(2)}) collective-permute-start(bf16[4,32,128]{2,1,0:T(8,128)(2,1)S(1)} %get-tuple-element.57), channel_id=1, source_target_pairs={{0,32},{16,48},{32,64},{48,80},{64,96},{80,112},{96,128},{112,144}... | collective-permute-start | bytes 98312 | tf_op jit(solution)/shard_map/ppermute | solution.py:19
  12.9 1.3 %collective-permute-start.3 = (bf16[4,32,128]{2,1,0:T(8,128)(2,1)S(1)}, bf16[4,32,128]{2,1,0:T(8,128)(2,1)S(1)}, u32[]{:S(2)}, u32[]{:S(2)}) collective-permute-start(bf16[4,32,128]{2,1,0:T(8,128)(2,1)S(1)} %get-tuple-element.58), channel_id=1, source_target_pairs={{32,0},{48,16},{64,32},{80,48},{96,64},{112,80},{128,96},{144,112}... | collective-permute-start | bytes 98312 | tf_op jit(solution)/shard_map/ppermute | solution.py:19
  14.2 6.7 %collective-permute-done.3.xhi2 = bf16[4,32,128]{2,1,0:T(8,128)(2,1)S(1)} collective-permute-done((bf16[4,32,128]{2,1,0:T(8,128)(2,1)S(1)}, bf16[4,32,128]{2,1,0:T(8,128)(2,1)S(1)}, u32[]{:S(2)}, u32[]{:S(2)}) %collective-permute-start.3) | collective-permute-done | bytes 32800 | tf_op jit(solution)/shard_map/ppermute | solution.py:19
  20.9 0.4 shard_map.110
  21.3 6.3 %collective-permute-start.4 = (bf16[6,7,32,128]{3,2,1,0:T(8,128)(2,1)S(1)}, bf16[6,7,32,128]{3,2,1,0:T(8,128)(2,1)S(1)}, u32[]{:S(2)}, u32[]{:S(2)}) collective-permute-start(bf16[6,7,32,128]{3,2,1,0:T(8,128)(2,1)S(1)} %get-tuple-element.59), channel_id=1, source_target_pairs={{0,1},{1,2},{2,3},{3,4},{4,5},{5,6},{6,7},{7,8},{8,9},{9,10},{10,1... | collective-permute-start | bytes 1032200 | tf_op jit(solution)/shard_map/ppermute | solution.py:19
  27.6 1.9 %collective-permute-start.5 = (bf16[6,7,32,128]{3,2,1,0:T(8,128)(2,1)S(1)}, bf16[6,7,32,128]{3,2,1,0:T(8,128)(2,1)S(1)}, u32[]{:S(2)}, u32[]{:S(2)}) collective-permute-start(bf16[6,7,32,128]{3,2,1,0:T(8,128)(2,1)S(1)} %get-tuple-element.60.first_ref), channel_id=1, source_target_pairs={{1,0},{2,1},{3,2},{4,3},{5,4},{6,5},{7,6},{8,7},{9,8},{10,9},{11,1... | collective-permute-start | bytes 1032200 | tf_op jit(solution)/shard_map/ppermute | solution.py:19
  29.6 0.1 add_convert_fusion.inside
  29.6 1.0 copy-done.4
  30.7 1.0 copy-done.5
  31.7 1.0 copy-done.6
  32.7 0.9 copy-done.7
  33.6 0.3 shard_map.111
  33.9 0.0 copy-start
  33.9 0.0 collective-permute-done.4.ylo.refs_0_
  33.9 2.3 %collective-permute-done.5.yhi.refs_1_ = bf16[6,7,32,128]{3,2,1,0:T(8,128)(2,1)S(1)} collective-permute-done((bf16[6,7,32,128]{3,2,1,0:T(8,128)(2,1)S(1)}, bf16[6,7,32,128]{3,2,1,0:T(8,128)(2,1)S(1)}, u32[]{:S(2)}, u32[]{:S(2)}) %collective-permute-start.5) | collective-permute-done | bytes 344096 | tf_op jit(solution)/shard_map/ppermute | solution.py:19
  36.2 1.6 %shard_map.113 = (bf16[4,18,32,64]{3,2,1,0:T(8,128)(2,1)S(1)}, bf16[2,320,64]{2,1,0:T(8,128)(2,1)S(1)}, bf16[64,512]{1,0:T(8,128)(2,1)S(1)}, f32[128,128]{1,0:T(8,128)S(1)}) custom-call(bf16[2,8,32,64]{3,2,1,0:T(8,128)(2,1)S(1)} %get-tuple-element.54.c_ref, bf16[6,7,32,128]{3,2,1,0:T(8,128)(2,1)S(1)} %collective-permute-done.4.ylo.refs_0_, ...), custom_call_target="tpu_custom_call" | custom-call | flops 1000000 | bytes 10000 | tf_op jit(solution)/shard_map/pallas_call | solution.py:31
  37.8 3.2 %shard_map.112 = (bf16[8,22,32,64]{3,2,1,0:T(8,128)(2,1)S(1)}, bf16[4,10,32,64]{3,2,1,0:T(8,128)(2,1)S(1)}, f32[6,320,64]{2,1,0:T(8,128)S(1)}, bf16[3,10,16,64]{3,2,1,0:T(8,128)(2,1)S(1)}) custom-call(bf16[2,8,32,64]{3,2,1,0:T(8,128)(2,1)S(1)} %get-tuple-element.53.f_ref, bf16[6,7,32,128]{3,2,1,0:T(8,128)(2,1)S(1)} %collective-permute-done.4.ylo.refs_0_, ...), custom_call_target="tpu_custom_call" | custom-call | flops 1000000 | bytes 10000 | tf_op jit(solution)/shard_map/pallas_call | solution.py:31
  41.0 0.9 shard_map.114
  41.8 2.8 %shard_map.115 = (bf16[2,10,32,64]{3,2,1,0:T(8,128)(2,1)S(1)}, bf16[32,80,128]{2,1,0:T(8,128)(2,1)S(1)}, bf16[32,80,128]{2,1,0:T(8,128)(2,1)S(1)}) custom-call(bf16[3,10,16,64]{3,2,1,0:T(8,128)(2,1)S(1)} %get-tuple-element.62.px, bf16[96,128]{1,0:T(8,128)(2,1)S(1)} %get-tuple-element.67.la_ref, bf16[128,128]{1,0:T(8,128)(2,1)S(1)} %get-tuple-element.68.lg_ref, ...), custom_call_target="tpu_custom_call" | custom-call | flops 1000000 | bytes 10000 | tf_op jit(solution)/shard_map/pallas_call | solution.py:31
  44.6 1.9 %collective-permute-start.6 = (bf16[32,80,128]{2,1,0:T(8,128)(2,1)S(1)}, bf16[32,80,128]{2,1,0:T(8,128)(2,1)S(1)}, u32[]{:S(2)}, u32[]{:S(2)}) collective-permute-start(bf16[32,80,128]{2,1,0:T(8,128)(2,1)S(1)} %get-tuple-element.77), channel_id=1, source_target_pairs={{0,1},{1,0},{2,3},{3,2},{4,5},{5,4},{6,7},{7,6},{8,9},{9,8},{10,11... | collective-permute-start | bytes 1966088 | tf_op jit(solution)/shard_map/ppermute | solution.py:27
  46.6 2.1 %collective-permute-done.6.b_ref = bf16[32,80,128]{2,1,0:T(8,128)(2,1)S(1)} collective-permute-done((bf16[32,80,128]{2,1,0:T(8,128)(2,1)S(1)}, bf16[32,80,128]{2,1,0:T(8,128)(2,1)S(1)}, u32[]{:S(2)}, u32[]{:S(2)}) %collective-permute-start.6) | collective-permute-done | bytes 655392 | tf_op jit(solution)/shard_map/ppermute | solution.py:27
  48.6 1.0 shard_map.116
  49.6 8.1 %all-to-all-start = ((bf16[32,80,128]{2,1,0:T(8,128)(2,1)}), bf16[32,80,128]{2,1,0:T(8,128)(2,1)S(1)}, u32[]{:S(2)}, u32[]{:S(2)}) async-start(bf16[32,80,128]{2,1,0:T(8,128)(2,1)} %shard_map.116), calls=%async_computation | async-start | bytes 1310720 | tf_op jit(solution)/shard_map/all_to_all | solution.py:463
  57.7 1.3 %collective-permute-start.8 = (bf16[224,128]{1,0:T(8,128)(2,1)S(1)}, bf16[224,128]{1,0:T(8,128)(2,1)S(1)}, u32[]{:S(2)}, u32[]{:S(2)}) collective-permute-start(bf16[224,128]{1,0:T(8,128)(2,1)S(1)} %get-tuple-element.80), channel_id=1, source_target_pairs={{16,0},{32,16},{48,32},{64,48},{80,64},{96,80},{112,96},{128,112},... | collective-permute-start | bytes 172040 | tf_op jit(solution)/shard_map/ppermute | solution.py:19
  59.0 4.0 %collective-permute-start.7 = (bf16[224,128]{1,0:T(8,128)(2,1)S(1)}, bf16[224,128]{1,0:T(8,128)(2,1)S(1)}, u32[]{:S(2)}, u32[]{:S(2)}) collective-permute-start(bf16[224,128]{1,0:T(8,128)(2,1)S(1)} %get-tuple-element.80), channel_id=1, source_target_pairs={{0,16},{16,32},{32,48},{48,64},{64,80},{80,96},{96,112},{112,128},... | collective-permute-start | bytes 172040 | tf_op jit(solution)/shard_map/ppermute | solution.py:19
  63.0 11.5 %all-to-all-done.parts_ref = bf16[32,80,128]{2,1,0:T(8,128)(2,1)S(1)} async-done(((bf16[32,80,128]{2,1,0:T(8,128)(2,1)}), bf16[32,80,128]{2,1,0:T(8,128)(2,1)S(1)}, u32[]{:S(2)}, u32[]{:S(2)}) %all-to-all-start) | async-done | bytes 655392 | tf_op jit(solution)/shard_map/all_to_all | solution.py:463
  74.5 0.8 shard_map.117
  75.3 9.4 %all-to-all-start.1 = ((bf16[8,80,128]{2,1,0:T(8,128)(2,1)}), bf16[8,80,128]{2,1,0:T(8,128)(2,1)S(1)}, u32[]{:S(2)}, u32[]{:S(2)}) async-start(bf16[8,80,128]{2,1,0:T(8,128)(2,1)} %shard_map.117), calls=%async_computation.1 | async-start | bytes 327680 | tf_op jit(solution)/shard_map/all_to_all | solution.py:467
  84.7 0.5 shard_map.119
  85.1 0.0 copy-start.1
  85.2 6.2 %collective-permute-start.9 = (bf16[160,128]{1,0:T(8,128)(2,1)S(1)}, bf16[160,128]{1,0:T(8,128)(2,1)S(1)}, u32[]{:S(2)}, u32[]{:S(2)}) collective-permute-start(bf16[160,128]{1,0:T(8,128)(2,1)S(1)} %get-tuple-element.84), channel_id=1, source_target_pairs={{0,16},{16,32},{32,48},{48,64},{64,80},{80,96},{96,112},{112,128},... | collective-permute-start | bytes 122888 | tf_op jit(solution)/shard_map/ppermute | solution.py:19
  91.3 1.3 %collective-permute-start.10 = (bf16[160,128]{1,0:T(8,128)(2,1)S(1)}, bf16[160,128]{1,0:T(8,128)(2,1)S(1)}, u32[]{:S(2)}, u32[]{:S(2)}) collective-permute-start(bf16[160,128]{1,0:T(8,128)(2,1)S(1)} %get-tuple-element.85), channel_id=1, source_target_pairs={{16,0},{32,16},{48,32},{64,48},{80,64},{96,80},{112,96},{128,112},... | collective-permute-start | bytes 122888 | tf_op jit(solution)/shard_map/ppermute | solution.py:19
  92.6 0.3 all-to-all-done.1.parts_ref
  92.9 0.9 shard_map.118
  93.8 0.0 collective-permute-done.9.xlo
  93.8 2.5 %collective-permute-done.10.xhi = bf16[160,128]{1,0:T(8,128)(2,1)S(1)} collective-permute-done((bf16[160,128]{1,0:T(8,128)(2,1)S(1)}, bf16[160,128]{1,0:T(8,128)(2,1)S(1)}, u32[]{:S(2)}, u32[]{:S(2)}) %collective-permute-start.10) | collective-permute-done | bytes 40992 | tf_op jit(solution)/shard_map/ppermute | solution.py:19
  96.4 5.7 %all-to-all-start.2 = ((bf16[32,80,128]{2,1,0:T(8,128)(2,1)}), bf16[32,80,128]{2,1,0:T(8,128)(2,1)S(1)}, u32[]{:S(2)}, u32[]{:S(2)}) async-start(bf16[32,80,128]{2,1,0:T(8,128)(2,1)} %shard_map.118), calls=%async_computation.2 | async-start | bytes 1310720 | tf_op jit(solution)/shard_map/all_to_all | solution.py:477
  102.1 1.5 %shard_map.120 = bf16[2,8,32,64]{3,2,1,0:T(8,128)(2,1)} custom-call(bf16[4,10,32,64]{3,2,1,0:T(8,128)(2,1)S(1)} %get-tuple-element.71.enc_ref, bf16[2,10,32,64]{3,2,1,0:T(8,128)(2,1)S(1)} %get-tuple-element.87.lifted_ref, bf16[224,128]{1,0:T(8,128)(2,1)S(1)} %collective-permute-done.7.xlo, bf16[224,128]{1,0:T(8,128)(2,1)S(1)} %collective-permute-done.8.xhi, ...), custom_call_target="tpu_custom_call" | custom-call | flops 1000000 | bytes 10000 | tf_op jit(solution)/shard_map/pallas_call | solution.py:31
  103.6 1.3 shard_map.121
  104.9 11.1 %all-to-all-done.2.own_ref = bf16[32,80,128]{2,1,0:T(8,128)(2,1)S(1)} async-done(((bf16[32,80,128]{2,1,0:T(8,128)(2,1)}), bf16[32,80,128]{2,1,0:T(8,128)(2,1)S(1)}, u32[]{:S(2)}, u32[]{:S(2)}) %all-to-all-start.2) | async-done | bytes 655392 | tf_op jit(solution)/shard_map/all_to_all | solution.py:477
  116.0 9.0 %collective-permute-start.11 = (bf16[32,80,128]{2,1,0:T(8,128)(2,1)S(1)}, bf16[32,80,128]{2,1,0:T(8,128)(2,1)S(1)}, u32[]{:S(2)}, u32[]{:S(2)}) collective-permute-start(bf16[32,80,128]{2,1,0:T(8,128)(2,1)S(1)} %all-to-all-done.2.own_ref), channel_id=1, source_target_pairs={{0,1},{1,0},{2,3},{3,2},{4,5},{5,4},{6,7},{7,6},{8,9},{9,8},{10,11... | collective-permute-start | bytes 1966088 | tf_op jit(solution)/shard_map/ppermute | solution.py:27
  124.9 1.7 %collective-permute-done.11.other_ref = bf16[32,80,128]{2,1,0:T(8,128)(2,1)S(1)} collective-permute-done((bf16[32,80,128]{2,1,0:T(8,128)(2,1)S(1)}, bf16[32,80,128]{2,1,0:T(8,128)(2,1)S(1)}, u32[]{:S(2)}, u32[]{:S(2)}) %collective-permute-start.11) | collective-permute-done | bytes 655392 | tf_op jit(solution)/shard_map/ppermute | solution.py:27
  126.6 1.8 %shard_map.122 = (f32[27,64,64]{2,1,0:T(8,128)}, f32[27,64,128]{2,1,0:T(8,128)}, f32[27,64,128]{2,1,0:T(8,128)}, f32[8,64,128]{2,1,0:T(8,128)}) custom-call(s32[1]{0:T(128)} %bitcast.7.core, bf16[32,80,128]{2,1,0:T(8,128)(2,1)S(1)} %all-to-all-done.2.own_ref, bf16[32,80,128]{2,1,0:T(8,128)(2,1)S(1)} %collective-permute-done.11.other_ref), custom_call_target="tpu_custom_call" | custom-call | flops 1000000 | bytes 10000 | tf_op jit(solution)/shard_map/pallas_call | solution.py:31
  (13 shorter events, 0.0 us)
Async XLA Ops:
  0.6 0.9 copy-start.2
  1.5 0.9 copy-start.3
  2.6 18.3 %collective-permute-start = (bf16[12,32,128]{2,1,0:T(8,128)(2,1)S(1)}, bf16[12,32,128]{2,1,0:T(8,128)(2,1)S(1)}, u32[]{:S(2)}, u32[]{:S(2)}) collective-permute-start(bf16[12,32,128]{2,1,0:T(8,128)(2,1)S(1)} %get-tuple-element.55), channel_id=1, source_target_pairs={{0,16},{16,32},{32,48},{48,64},{64,80},{80,96},{96,112},{112,128},... | collective-permute-start | bytes 294920 | tf_op jit(solution)/shard_map/ppermute | solution.py:19
  6.6 14.3 %collective-permute-start.1 = (bf16[12,32,128]{2,1,0:T(8,128)(2,1)S(1)}, bf16[12,32,128]{2,1,0:T(8,128)(2,1)S(1)}, u32[]{:S(2)}, u32[]{:S(2)}) collective-permute-start(bf16[12,32,128]{2,1,0:T(8,128)(2,1)S(1)} %get-tuple-element.56), channel_id=1, source_target_pairs={{16,0},{32,16},{48,32},{64,48},{80,64},{96,80},{112,96},{128,112},... | collective-permute-start | bytes 294920 | tf_op jit(solution)/shard_map/ppermute | solution.py:19
  7.9 6.3 %collective-permute-start.2 = (bf16[4,32,128]{2,1,0:T(8,128)(2,1)S(1)}, bf16[4,32,128]{2,1,0:T(8,128)(2,1)S(1)}, u32[]{:S(2)}, u32[]{:S(2)}) collective-permute-start(bf16[4,32,128]{2,1,0:T(8,128)(2,1)S(1)} %get-tuple-element.57), channel_id=1, source_target_pairs={{0,32},{16,48},{32,64},{48,80},{64,96},{80,112},{96,128},{112,144}... | collective-permute-start | bytes 98312 | tf_op jit(solution)/shard_map/ppermute | solution.py:19
  12.9 8.0 %collective-permute-start.3 = (bf16[4,32,128]{2,1,0:T(8,128)(2,1)S(1)}, bf16[4,32,128]{2,1,0:T(8,128)(2,1)S(1)}, u32[]{:S(2)}, u32[]{:S(2)}) collective-permute-start(bf16[4,32,128]{2,1,0:T(8,128)(2,1)S(1)} %get-tuple-element.58), channel_id=1, source_target_pairs={{32,0},{48,16},{64,32},{80,48},{96,64},{112,80},{128,96},{144,112}... | collective-permute-start | bytes 98312 | tf_op jit(solution)/shard_map/ppermute | solution.py:19
  21.3 12.6 %collective-permute-start.4 = (bf16[6,7,32,128]{3,2,1,0:T(8,128)(2,1)S(1)}, bf16[6,7,32,128]{3,2,1,0:T(8,128)(2,1)S(1)}, u32[]{:S(2)}, u32[]{:S(2)}) collective-permute-start(bf16[6,7,32,128]{3,2,1,0:T(8,128)(2,1)S(1)} %get-tuple-element.59), channel_id=1, source_target_pairs={{0,1},{1,2},{2,3},{3,4},{4,5},{5,6},{6,7},{7,8},{8,9},{9,10},{10,1... | collective-permute-start | bytes 1032200 | tf_op jit(solution)/shard_map/ppermute | solution.py:19
  27.6 8.6 %collective-permute-start.5 = (bf16[6,7,32,128]{3,2,1,0:T(8,128)(2,1)S(1)}, bf16[6,7,32,128]{3,2,1,0:T(8,128)(2,1)S(1)}, u32[]{:S(2)}, u32[]{:S(2)}) collective-permute-start(bf16[6,7,32,128]{3,2,1,0:T(8,128)(2,1)S(1)} %get-tuple-element.60.first_ref), channel_id=1, source_target_pairs={{1,0},{2,1},{3,2},{4,3},{5,4},{6,5},{7,6},{8,7},{9,8},{10,9},{11,1... | collective-permute-start | bytes 1032200 | tf_op jit(solution)/shard_map/ppermute | solution.py:19
  29.6 1.0 copy-start.4
  30.7 1.0 copy-start.5
  31.7 1.0 copy-start.6
  32.7 0.9 copy-start.7
  33.9 7.1 %copy-start = (bf16[192,1152]{1,0:T(8,128)(2,1)}, bf16[192,1152]{1,0:T(8,128)(2,1)S(1)}, u32[]{:S(2)}) copy-start(bf16[192,1152]{1,0:T(8,128)(2,1)S(1)} %get-tuple-element.88.w_ref) | copy-start | bytes 1327108
  44.6 4.0 %collective-permute-start.6 = (bf16[32,80,128]{2,1,0:T(8,128)(2,1)S(1)}, bf16[32,80,128]{2,1,0:T(8,128)(2,1)S(1)}, u32[]{:S(2)}, u32[]{:S(2)}) collective-permute-start(bf16[32,80,128]{2,1,0:T(8,128)(2,1)S(1)} %get-tuple-element.77), channel_id=1, source_target_pairs={{0,1},{1,0},{2,3},{3,2},{4,5},{5,4},{6,7},{7,6},{8,9},{9,8},{10,11... | collective-permute-start | bytes 1966088 | tf_op jit(solution)/shard_map/ppermute | solution.py:27
  49.6 24.9 %all-to-all-start = ((bf16[32,80,128]{2,1,0:T(8,128)(2,1)}), bf16[32,80,128]{2,1,0:T(8,128)(2,1)S(1)}, u32[]{:S(2)}, u32[]{:S(2)}) async-start(bf16[32,80,128]{2,1,0:T(8,128)(2,1)} %shard_map.116), calls=%async_computation | async-start | bytes 1310720 | tf_op jit(solution)/shard_map/all_to_all | solution.py:463
  57.7 17.5 %collective-permute-start.8 = (bf16[224,128]{1,0:T(8,128)(2,1)S(1)}, bf16[224,128]{1,0:T(8,128)(2,1)S(1)}, u32[]{:S(2)}, u32[]{:S(2)}) collective-permute-start(bf16[224,128]{1,0:T(8,128)(2,1)S(1)} %get-tuple-element.80), channel_id=1, source_target_pairs={{16,0},{32,16},{48,32},{64,48},{80,64},{96,80},{112,96},{128,112},... | collective-permute-start | bytes 172040 | tf_op jit(solution)/shard_map/ppermute | solution.py:19
  59.0 16.2 %collective-permute-start.7 = (bf16[224,128]{1,0:T(8,128)(2,1)S(1)}, bf16[224,128]{1,0:T(8,128)(2,1)S(1)}, u32[]{:S(2)}, u32[]{:S(2)}) collective-permute-start(bf16[224,128]{1,0:T(8,128)(2,1)S(1)} %get-tuple-element.80), channel_id=1, source_target_pairs={{0,16},{16,32},{32,48},{48,64},{64,80},{80,96},{96,112},{112,128},... | collective-permute-start | bytes 172040 | tf_op jit(solution)/shard_map/ppermute | solution.py:19
  75.3 17.7 %all-to-all-start.1 = ((bf16[8,80,128]{2,1,0:T(8,128)(2,1)}), bf16[8,80,128]{2,1,0:T(8,128)(2,1)S(1)}, u32[]{:S(2)}, u32[]{:S(2)}) async-start(bf16[8,80,128]{2,1,0:T(8,128)(2,1)} %shard_map.117), calls=%async_computation.1 | async-start | bytes 327680 | tf_op jit(solution)/shard_map/all_to_all | solution.py:467
  85.1 17.0 %copy-start.1 = (bf16[192,1152]{1,0:T(8,128)(2,1)S(1)}, bf16[192,1152]{1,0:T(8,128)(2,1)}, u32[]{:S(2)}) copy-start(bf16[192,1152]{1,0:T(8,128)(2,1)} %copy-done) | copy-start | bytes 1327108
  85.2 8.7 %collective-permute-start.9 = (bf16[160,128]{1,0:T(8,128)(2,1)S(1)}, bf16[160,128]{1,0:T(8,128)(2,1)S(1)}, u32[]{:S(2)}, u32[]{:S(2)}) collective-permute-start(bf16[160,128]{1,0:T(8,128)(2,1)S(1)} %get-tuple-element.84), channel_id=1, source_target_pairs={{0,16},{16,32},{32,48},{48,64},{64,80},{80,96},{96,112},{112,128},... | collective-permute-start | bytes 122888 | tf_op jit(solution)/shard_map/ppermute | solution.py:19
  91.3 5.0 %collective-permute-start.10 = (bf16[160,128]{1,0:T(8,128)(2,1)S(1)}, bf16[160,128]{1,0:T(8,128)(2,1)S(1)}, u32[]{:S(2)}, u32[]{:S(2)}) collective-permute-start(bf16[160,128]{1,0:T(8,128)(2,1)S(1)} %get-tuple-element.85), channel_id=1, source_target_pairs={{16,0},{32,16},{48,32},{64,48},{80,64},{96,80},{112,96},{128,112},... | collective-permute-start | bytes 122888 | tf_op jit(solution)/shard_map/ppermute | solution.py:19
  96.4 19.6 %all-to-all-start.2 = ((bf16[32,80,128]{2,1,0:T(8,128)(2,1)}), bf16[32,80,128]{2,1,0:T(8,128)(2,1)S(1)}, u32[]{:S(2)}, u32[]{:S(2)}) async-start(bf16[32,80,128]{2,1,0:T(8,128)(2,1)} %shard_map.118), calls=%async_computation.2 | async-start | bytes 1310720 | tf_op jit(solution)/shard_map/all_to_all | solution.py:477
  116.0 10.7 %collective-permute-start.11 = (bf16[32,80,128]{2,1,0:T(8,128)(2,1)S(1)}, bf16[32,80,128]{2,1,0:T(8,128)(2,1)S(1)}, u32[]{:S(2)}, u32[]{:S(2)}) collective-permute-start(bf16[32,80,128]{2,1,0:T(8,128)(2,1)S(1)} %all-to-all-done.2.own_ref), channel_id=1, source_target_pairs={{0,1},{1,0},{2,3},{3,2},{4,5},{5,4},{6,7},{7,6},{8,9},{9,8},{10,11... | collective-permute-start | bytes 1966088 | tf_op jit(solution)/shard_map/ppermute | solution.py:27

commit v7 on v6

--- a/solution.py
+++ b/solution.py
@@ -27,14 +27,14 @@
     return lax.ppermute(piece, "gc", [(0, 1), (1, 0)])
 
 
-def call(kernel, outs, scratch, operands, spaces=(), flops=10**6):
+def call(kernel, outs, scratch, operands, spaces=(), flops=10**6, out_space=pltpu.VMEM):
     return pl.pallas_call(
         kernel,
         out_shape=[jax.ShapeDtypeStruct(s, d) for s, d in outs],
         in_specs=[
             pl.BlockSpec(memory_space=dict(spaces).get(i, pltpu.VMEM)) for i in range(len(operands))
         ],
-        out_specs=[pl.BlockSpec(memory_space=pltpu.VMEM)] * len(outs),
+        out_specs=[pl.BlockSpec(memory_space=out_space)] * len(outs),
         scratch_shapes=[s if d is None else pltpu.VMEM(s, d) for s, d in scratch],
         compiler_params=pltpu.CompilerParams(vmem_limit_bytes=40 * 2**20),
         cost_estimate=pl.CostEstimate(flops=flops, bytes_accessed=10**4, transcendentals=0),
@@ -363,18 +363,29 @@
         out_ref[k] = total
 
 
-def widen_kernel(core, own_ref, other_ref, encoder_ref, decoder_ref, lower_ref, lift_ref):
+def widen_kernel(core, own_ref, other_ref, *refs):
+    outs, (encoder, decoder, lower, lift), sems = refs[:4], refs[4:8], refs[8]
     own, other = own_ref[...].astype(F32), other_ref[...].astype(F32)
     first = core[0] == 0
     both = jnp.stack([jnp.where(first, own, other), jnp.where(first, other, own)], 1)
     chunk = own.shape[1] // 5 * 4
     sums = both[:, :, :chunk].reshape(4096, 128)
-    decoder_ref[...] = sums[0:1728].reshape(27, 64, 128)
-    lower_ref[...] = sums[1728:3456].reshape(27, 64, 128)
-    lift_ref[...] = sums[3456:3968].reshape(8, 64, 128)
     wide = both[:, :, chunk:].reshape(1024, 128)[:864].reshape(27, 32, 128)
-    encoder_ref[:, 0:32, :] = wide[..., :64]
-    encoder_ref[:, 32:64, :] = wide[..., 64:]
+    copies = [
+        pltpu.make_async_copy(a, b, sems.at[k])
+        for k, (a, b) in enumerate(zip((encoder, decoder, lower, lift), outs))
+    ]
+    decoder[...] = sums[0:1728].reshape(27, 64, 128)
+    copies[1].start()
+    lower[...] = sums[1728:3456].reshape(27, 64, 128)
+    copies[2].start()
+    lift[...] = sums[3456:3968].reshape(8, 64, 128)
+    copies[3].start()
+    encoder[:, 0:32, :] = wide[..., :64]
+    encoder[:, 32:64, :] = wide[..., 64:]
+    copies[0].start()
+    for copy in copies:
+        copy.wait()
 
 
 def per_device(features, encoder_weight, lower_weight, lift_weight, decoder_weight, cotangent):
@@ -470,30 +481,34 @@
         [(tall, BF16)] + [((160, 128), BF16)] * 2,
         [((3, 8, 16, 128), BF16), ((192, 64), F32)],
         [lg, *halo, low_bwd, slope, jg],
-    )
+        flops=2 * 10**9,
+    )
+    (sums,) = call(sum_kernel, [(half, LINK)], [], [sums])
+    sums, edges = lax.optimization_barrier((sums, edges))
+    sums = lax.all_to_all(sums, "gx", 0, 0)
     eg_halo = swapped(*edges, GX)
-    (sums,) = call(sum_kernel, [(half, LINK)], [], [sums])
-    sums, eg_halo = lax.optimization_barrier((sums, eg_halo))
-    sums = lax.all_to_all(sums, "gx", 0, 0)
     (decoded,) = call(
         decode_kernel,
         [(brick, BF16)],
         [((4, 10, 32, 128), BF16), ((320, 64), F32)],
         [encoded, lifted, *halo, lift, dec_fwd],
     )
+    sums, eg_halo, decoded = lax.optimization_barrier((sums, eg_halo, decoded))
     (input_grad,) = call(
         input_grad_kernel,
         [(brick, BF16)],
         [((4, 10, 32, 64), BF16)],
         [eg, *eg_halo, enc_bwd],
-    )
-    sums, decoded, input_grad = lax.optimization_barrier((sums, decoded, input_grad))
+        flops=2 * 10**9,
+    )
+    shapes = [((27, 64, 64), F32), ((27, 64, 128), F32), ((27, 64, 128), F32), ((8, 64, 128), F32)]
     encoder_gradient, decoder_gradient, lower_gradient, lift_gradient = call(
         widen_kernel,
-        [((27, 64, 64), F32), ((27, 64, 128), F32), ((27, 64, 128), F32), ((8, 64, 128), F32)],
-        [],
+        shapes,
+        shapes + [(pltpu.SemaphoreType.DMA((4,)), None)],
         [core, sums, partner(sums)],
         spaces={0: pltpu.SMEM},
+        out_space=pltpu.HBM,
     )
     return (
         jnp.transpose(decoded, (3, 0, 1, 2)),

time: 129 us -> 131 us (1.016)
    all_to_all x2, waiting for transfers between devices: 22.6 us -> 11.7 us  [per_device(): sums = lax.all_to_all(sums, 'gx', 0, 0)]
    all_to_all x1, waiting for transfers between devices: 0.3 us -> 7.79 us  [per_device(): sums = lax.all_to_all(sums, 'gz', 0, 0)]
    ppermute x10, waiting for transfers between devices: 11.5 us -> 16.9 us  [shifted(): return lax.ppermute(piece, axes, pairs)]
    ppermute x10, starting transfers between devices: 32.6 us -> 29.5 us  [shifted(): return lax.ppermute(piece, axes, pairs)]
    all_to_all x2, starting transfers between devices: 13.8 us -> 16.5 us  [per_device(): sums = lax.all_to_all(sums, 'gx', 0, 0)]
    ppermute x2, waiting for transfers between devices: 3.77 us -> 2.07 us  [partner(): return lax.ppermute(piece, 'gc', [(0, 1), (1, 0)])]
    unnamed x16 -> x24, local copies, waits for them, and re-layouts: 5.76 us -> 6.68 us
  transfers between devices with their start and end apart: 15 -> 15, of which waited for: 8 -> 8; matrix products, arithmetic and copies ran while one was open for 0% -> 0% of each run, Pallas kernels for 4% -> 3%
where the time goes in v7:
time: 131 us; the launch traced here: 130 us
  starting transfers between devices  66.7 us (51%)
  waiting for transfers between devices  38.5 us (29%)
  Pallas kernels  17.5 us (13%)
  local copies, waits for them, and re-layouts  6.68 us (5%)
    ppermute x10, starting transfers between devices, shifted(): return lax.ppermute(piece, axes, pairs)  29.5 us
    pallas_call x14, Pallas kernels, call(): pl.pallas_call(kernel, out_shape=[jax.ShapeDtypeStruct(s, d) for s, d in...  17.5 us
    ppermute x10, waiting for transfers between devices, shifted(): return lax.ppermute(piece, axes, pairs)  16.9 us
    all_to_all x2, starting transfers between devices, per_device(): sums = lax.all_to_all(sums, 'gx', 0, 0)  16.5 us
    all_to_all x2, waiting for transfers between devices, per_device(): sums = lax.all_to_all(sums, 'gx', 0, 0)  11.7 us
    ppermute x2, starting transfers between devices, partner(): return lax.ppermute(piece, 'gc', [(0, 1), (1, 0)])  11.3 us
    all_to_all x1, starting transfers between devices, per_device(): sums = lax.all_to_all(sums, 'gz', 0, 0)  9.41 us
    all_to_all x1, waiting for transfers between devices, per_device(): sums = lax.all_to_all(sums, 'gz', 0, 0)  7.79 us
  transfers between devices with their start and end apart: 15, of which 8 were waited for; matrix products, arithmetic and copies ran while one was open for 0% of the time, Pallas kernels for 3%

profile of v7, /device:TPU:1, one launch (start us, length us, event | category | flops | bytes accessed | tf_op | source)
XLA Modules:
  0.0 130.4 jit_solution(12982835768668061069)
XLA Ops:
  0.6 0.9 copy-done.2
  1.5 0.9 copy-done.3
  2.4 0.1 shard_map.109
  2.6 4.0 %collective-permute-start = (bf16[12,32,128]{2,1,0:T(8,128)(2,1)S(1)}, bf16[12,32,128]{2,1,0:T(8,128)(2,1)S(1)}, u32[]{:S(2)}, u32[]{:S(2)}) collective-permute-start(bf16[12,32,128]{2,1,0:T(8,128)(2,1)S(1)} %get-tuple-element.56), channel_id=1, source_target_pairs={{0,16},{16,32},{32,48},{48,64},{64,80},{80,96},{96,112},{112,128},... | collective-permute-start | bytes 294920 | tf_op jit(solution)/shard_map/ppermute | solution.py:19
  6.6 1.3 collective-permute-start.1
  7.9 5.0 %collective-permute-start.2 = (bf16[4,32,128]{2,1,0:T(8,128)(2,1)S(1)}, bf16[4,32,128]{2,1,0:T(8,128)(2,1)S(1)}, u32[]{:S(2)}, u32[]{:S(2)}) collective-permute-start(bf16[4,32,128]{2,1,0:T(8,128)(2,1)S(1)} %get-tuple-element.58), channel_id=1, source_target_pairs={{0,32},{16,48},{32,64},{48,80},{64,96},{80,112},{96,128},{112,144}... | collective-permute-start | bytes 98312 | tf_op jit(solution)/shard_map/ppermute | solution.py:19
  12.9 1.3 collective-permute-start.3
  14.2 6.7 %collective-permute-done.3.xhi2 = bf16[4,32,128]{2,1,0:T(8,128)(2,1)S(1)} collective-permute-done((bf16[4,32,128]{2,1,0:T(8,128)(2,1)S(1)}, bf16[4,32,128]{2,1,0:T(8,128)(2,1)S(1)}, u32[]{:S(2)}, u32[]{:S(2)}) %collective-permute-start.3) | collective-permute-done | bytes 32800 | tf_op jit(solution)/shard_map/ppermute | solution.py:19
  20.9 0.4 shard_map.110
  21.3 6.3 %collective-permute-start.4 = (bf16[6,7,32,128]{3,2,1,0:T(8,128)(2,1)S(1)}, bf16[6,7,32,128]{3,2,1,0:T(8,128)(2,1)S(1)}, u32[]{:S(2)}, u32[]{:S(2)}) collective-permute-start(bf16[6,7,32,128]{3,2,1,0:T(8,128)(2,1)S(1)} %get-tuple-element.60), channel_id=1, source_target_pairs={{0,1},{1,2},{2,3},{3,4},{4,5},{5,6},{6,7},{7,8},{8,9},{9,10},{10,1... | collective-permute-start | bytes 1032200 | tf_op jit(solution)/shard_map/ppermute | solution.py:19
  27.6 1.9 %collective-permute-start.5 = (bf16[6,7,32,128]{3,2,1,0:T(8,128)(2,1)S(1)}, bf16[6,7,32,128]{3,2,1,0:T(8,128)(2,1)S(1)}, u32[]{:S(2)}, u32[]{:S(2)}) collective-permute-start(bf16[6,7,32,128]{3,2,1,0:T(8,128)(2,1)S(1)} %get-tuple-element.61.first_ref), channel_id=1, source_target_pairs={{1,0},{2,1},{3,2},{4,3},{5,4},{6,5},{7,6},{8,7},{9,8},{10,9},{11,1... | collective-permute-start | bytes 1032200 | tf_op jit(solution)/shard_map/ppermute | solution.py:19
  29.6 0.1 add_convert_fusion.inside
  29.7 1.0 copy-done.4
  30.7 1.0 copy-done.5
  31.7 1.0 copy-done.6
  32.7 0.9 copy-done.7
  33.6 0.3 shard_map.111
  33.9 0.0 copy-start.8
  33.9 0.0 copy-start.1
  33.9 2.3 %collective-permute-done.5.yhi.refs_1_ = bf16[6,7,32,128]{3,2,1,0:T(8,128)(2,1)S(1)} collective-permute-done((bf16[6,7,32,128]{3,2,1,0:T(8,128)(2,1)S(1)}, bf16[6,7,32,128]{3,2,1,0:T(8,128)(2,1)S(1)}, u32[]{:S(2)}, u32[]{:S(2)}) %collective-permute-start.5) | collective-permute-done | bytes 344096 | tf_op jit(solution)/shard_map/ppermute | solution.py:19
  36.2 1.6 %shard_map.113 = (bf16[4,18,32,64]{3,2,1,0:T(8,128)(2,1)S(1)}, bf16[2,320,64]{2,1,0:T(8,128)(2,1)S(1)}, bf16[64,512]{1,0:T(8,128)(2,1)S(1)}, f32[128,128]{1,0:T(8,128)S(1)}) custom-call(bf16[2,8,32,64]{3,2,1,0:T(8,128)(2,1)S(1)} %get-tuple-element.55.c_ref, bf16[6,7,32,128]{3,2,1,0:T(8,128)(2,1)S(1)} %collective-permute-done.4.ylo.refs_0_, ...), custom_call_target="tpu_custom_call" | custom-call | flops 1000000 | bytes 10000 | tf_op jit(solution)/shard_map/pallas_call | solution.py:31
  37.9 3.1 %shard_map.112 = (bf16[8,22,32,64]{3,2,1,0:T(8,128)(2,1)S(1)}, bf16[4,10,32,64]{3,2,1,0:T(8,128)(2,1)S(1)}, f32[6,320,64]{2,1,0:T(8,128)S(1)}, bf16[3,10,16,64]{3,2,1,0:T(8,128)(2,1)S(1)}) custom-call(bf16[2,8,32,64]{3,2,1,0:T(8,128)(2,1)S(1)} %get-tuple-element.54.f_ref, bf16[6,7,32,128]{3,2,1,0:T(8,128)(2,1)S(1)} %collective-permute-done.4.ylo.refs_0_, ...), custom_call_target="tpu_custom_call" | custom-call | flops 1000000 | bytes 10000 | tf_op jit(solution)/shard_map/pallas_call | solution.py:31
  41.0 1.5 %shard_map.114 = (bf16[96,128]{1,0:T(8,128)(2,1)S(1)}, bf16[128,128]{1,0:T(8,128)(2,1)S(1)}, bf16[224,128]{1,0:T(8,128)(2,1)}) custom-call(bf16[3,10,16,64]{3,2,1,0:T(8,128)(2,1)S(1)} %get-tuple-element.63.px, f32[4]{0:T(128)S(1)} %add_convert_fusion.inside, bf16[576,384]{1,0:T(8,128)(2,1)S(1)} %get-tuple-element.64.w_ref, ...), custom_call_target="tpu_custom_call" | custom-call | flops 1000000 | bytes 10000 | tf_op jit(solution)/shard_map/pallas_call | solution.py:31
  42.5 2.8 %shard_map.115 = (bf16[2,10,32,64]{3,2,1,0:T(8,128)(2,1)S(1)}, bf16[32,80,128]{2,1,0:T(8,128)(2,1)S(1)}, bf16[32,80,128]{2,1,0:T(8,128)(2,1)S(1)}) custom-call(bf16[3,10,16,64]{3,2,1,0:T(8,128)(2,1)S(1)} %get-tuple-element.63.px, bf16[96,128]{1,0:T(8,128)(2,1)S(1)} %get-tuple-element.68.la_ref, bf16[128,128]{1,0:T(8,128)(2,1)S(1)} %get-tuple-element.69.lg_ref, ...), custom_call_target="tpu_custom_call" | custom-call | flops 1000000 | bytes 10000 | tf_op jit(solution)/shard_map/pallas_call | solution.py:31
  45.3 1.9 %collective-permute-start.6 = (bf16[32,80,128]{2,1,0:T(8,128)(2,1)S(1)}, bf16[32,80,128]{2,1,0:T(8,128)(2,1)S(1)}, u32[]{:S(2)}, u32[]{:S(2)}) collective-permute-start(bf16[32,80,128]{2,1,0:T(8,128)(2,1)S(1)} %get-tuple-element.78), channel_id=1, source_target_pairs={{0,1},{1,0},{2,3},{3,2},{4,5},{5,4},{6,7},{7,6},{8,9},{9,8},{10,11... | collective-permute-start | bytes 1966088 | tf_op jit(solution)/shard_map/ppermute | solution.py:27
  47.2 2.1 %collective-permute-done.6.b_ref = bf16[32,80,128]{2,1,0:T(8,128)(2,1)S(1)} collective-permute-done((bf16[32,80,128]{2,1,0:T(8,128)(2,1)S(1)}, bf16[32,80,128]{2,1,0:T(8,128)(2,1)S(1)}, u32[]{:S(2)}, u32[]{:S(2)}) %collective-permute-start.6) | collective-permute-done | bytes 655392 | tf_op jit(solution)/shard_map/ppermute | solution.py:27
  49.3 1.0 shard_map.116
  50.2 8.1 %all-to-all-start = ((bf16[32,80,128]{2,1,0:T(8,128)(2,1)}), bf16[32,80,128]{2,1,0:T(8,128)(2,1)S(1)}, u32[]{:S(2)}, u32[]{:S(2)}) async-start(bf16[32,80,128]{2,1,0:T(8,128)(2,1)} %shard_map.116), calls=%async_computation | async-start | bytes 1310720 | tf_op jit(solution)/shard_map/all_to_all | solution.py:474
  58.4 1.3 collective-permute-start.8
  59.7 4.0 %collective-permute-start.7 = (bf16[224,128]{1,0:T(8,128)(2,1)}, bf16[224,128]{1,0:T(8,128)(2,1)S(1)}, u32[]{:S(2)}, u32[]{:S(2)}) collective-permute-start(bf16[224,128]{1,0:T(8,128)(2,1)} %get-tuple-element.81), channel_id=1, source_target_pairs={{0,16},{16,32},{32,48},{48,64},{64,80},{80,96},{96,112},{112,128},... | collective-permute-start | bytes 172040 | tf_op jit(solution)/shard_map/ppermute | solution.py:19
  63.7 11.5 %all-to-all-done.parts_ref = bf16[32,80,128]{2,1,0:T(8,128)(2,1)S(1)} async-done(((bf16[32,80,128]{2,1,0:T(8,128)(2,1)}), bf16[32,80,128]{2,1,0:T(8,128)(2,1)S(1)}, u32[]{:S(2)}, u32[]{:S(2)}) %all-to-all-start) | async-done | bytes 655392 | tf_op jit(solution)/shard_map/all_to_all | solution.py:474
  75.1 0.8 shard_map.117
  75.9 9.4 %all-to-all-start.1 = ((bf16[8,80,128]{2,1,0:T(8,128)(2,1)}), bf16[8,80,128]{2,1,0:T(8,128)(2,1)S(1)}, u32[]{:S(2)}, u32[]{:S(2)}) async-start(bf16[8,80,128]{2,1,0:T(8,128)(2,1)} %shard_map.117), calls=%async_computation.1 | async-start | bytes 327680 | tf_op jit(solution)/shard_map/all_to_all | solution.py:478
  85.3 0.5 shard_map.119
  85.8 0.0 copy-start.10
  85.8 7.8 %all-to-all-done.1.parts_ref = bf16[8,80,128]{2,1,0:T(8,128)(2,1)S(1)} async-done(((bf16[8,80,128]{2,1,0:T(8,128)(2,1)}), bf16[8,80,128]{2,1,0:T(8,128)(2,1)S(1)}, u32[]{:S(2)}, u32[]{:S(2)}) %all-to-all-start.1) | async-done | bytes 163872 | tf_op jit(solution)/shard_map/all_to_all | solution.py:478
  93.6 0.9 shard_map.118
  94.5 8.4 %all-to-all-start.2 = ((bf16[32,80,128]{2,1,0:T(8,128)(2,1)}), bf16[32,80,128]{2,1,0:T(8,128)(2,1)S(1)}, u32[]{:S(2)}, u32[]{:S(2)}) async-start(bf16[32,80,128]{2,1,0:T(8,128)(2,1)} %shard_map.118), calls=%async_computation.2 | async-start | bytes 1310720 | tf_op jit(solution)/shard_map/all_to_all | solution.py:488
  102.9 3.1 %collective-permute-start.9 = (bf16[160,128]{1,0:T(8,128)(2,1)S(1)}, bf16[160,128]{1,0:T(8,128)(2,1)S(1)}, u32[]{:S(2)}, u32[]{:S(2)}) collective-permute-start(bf16[160,128]{1,0:T(8,128)(2,1)S(1)} %get-tuple-element.88), channel_id=1, source_target_pairs={{0,16},{16,32},{32,48},{48,64},{64,80},{80,96},{96,112},{112,128},... | collective-permute-start | bytes 122888 | tf_op jit(solution)/shard_map/ppermute | solution.py:19
  106.0 1.3 collective-permute-start.10
  107.3 1.5 %shard_map.120 = bf16[2,8,32,64]{3,2,1,0:T(8,128)(2,1)} custom-call(bf16[4,10,32,64]{3,2,1,0:T(8,128)(2,1)S(1)} %get-tuple-element.72.enc_ref, bf16[2,10,32,64]{3,2,1,0:T(8,128)(2,1)S(1)} %get-tuple-element.90.lifted_ref, bf16[224,128]{1,0:T(8,128)(2,1)S(1)} %collective-permute-done.7.xlo, bf16[224,128]{1,0:T(8,128)(2,1)S(1)} %collective-permute-done.8.xhi, ...), custom_call_target="tpu_custom_call" | custom-call | flops 1000000 | bytes 10000 | tf_op jit(solution)/shard_map/pallas_call | solution.py:31
  108.8 3.6 %collective-permute-done.9.xlo = bf16[160,128]{1,0:T(8,128)(2,1)S(1)} collective-permute-done((bf16[160,128]{1,0:T(8,128)(2,1)S(1)}, bf16[160,128]{1,0:T(8,128)(2,1)S(1)}, u32[]{:S(2)}, u32[]{:S(2)}) %collective-permute-start.9) | collective-permute-done | bytes 40992 | tf_op jit(solution)/shard_map/ppermute | solution.py:19
  112.4 4.4 %collective-permute-done.10.xhi = bf16[160,128]{1,0:T(8,128)(2,1)S(1)} collective-permute-done((bf16[160,128]{1,0:T(8,128)(2,1)S(1)}, bf16[160,128]{1,0:T(8,128)(2,1)S(1)}, u32[]{:S(2)}, u32[]{:S(2)}) %collective-permute-start.10) | collective-permute-done | bytes 40992 | tf_op jit(solution)/shard_map/ppermute | solution.py:19
  116.8 0.3 all-to-all-done.2.own_ref
  117.0 9.4 %collective-permute-start.11 = (bf16[32,80,128]{2,1,0:T(8,128)(2,1)S(1)}, bf16[32,80,128]{2,1,0:T(8,128)(2,1)S(1)}, u32[]{:S(2)}, u32[]{:S(2)}) collective-permute-start(bf16[32,80,128]{2,1,0:T(8,128)(2,1)S(1)} %all-to-all-done.2.own_ref), channel_id=1, source_target_pairs={{0,1},{1,0},{2,3},{3,2},{4,5},{5,4},{6,7},{7,6},{8,9},{9,8},{10,11... | collective-permute-start | bytes 1966088 | tf_op jit(solution)/shard_map/ppermute | solution.py:27
  126.4 0.9 copy-done.11
  127.3 1.3 shard_map.121
  128.6 1.8 %shard_map.122 = (f32[27,64,64]{2,1,0:T(8,128)}, f32[27,64,128]{2,1,0:T(8,128)}, f32[27,64,128]{2,1,0:T(8,128)}, f32[8,64,128]{2,1,0:T(8,128)}) custom-call(s32[1]{0:T(128)} %bitcast.7.core, bf16[32,80,128]{2,1,0:T(8,128)(2,1)S(1)} %all-to-all-done.2.own_ref, bf16[32,80,128]{2,1,0:T(8,128)(2,1)S(1)} %collective-permute-done.11.other_ref), custom_call_target="tpu_custom_call" | custom-call | flops 1000000 | bytes 10000 | tf_op jit(solution)/shard_map/pallas_call | solution.py:31
  (21 shorter events, 0.0 us)
Async XLA Ops:
  0.6 0.9 copy-start.2
  1.5 0.9 copy-start.3
  2.6 18.3 %collective-permute-start = (bf16[12,32,128]{2,1,0:T(8,128)(2,1)S(1)}, bf16[12,32,128]{2,1,0:T(8,128)(2,1)S(1)}, u32[]{:S(2)}, u32[]{:S(2)}) collective-permute-start(bf16[12,32,128]{2,1,0:T(8,128)(2,1)S(1)} %get-tuple-element.56), channel_id=1, source_target_pairs={{0,16},{16,32},{32,48},{48,64},{64,80},{80,96},{96,112},{112,128},... | collective-permute-start | bytes 294920 | tf_op jit(solution)/shard_map/ppermute | solution.py:19
  6.6 14.3 %collective-permute-start.1 = (bf16[12,32,128]{2,1,0:T(8,128)(2,1)S(1)}, bf16[12,32,128]{2,1,0:T(8,128)(2,1)S(1)}, u32[]{:S(2)}, u32[]{:S(2)}) collective-permute-start(bf16[12,32,128]{2,1,0:T(8,128)(2,1)S(1)} %get-tuple-element.57), channel_id=1, source_target_pairs={{16,0},{32,16},{48,32},{64,48},{80,64},{96,80},{112,96},{128,112},... | collective-permute-start | bytes 294920 | tf_op jit(solution)/shard_map/ppermute | solution.py:19
  7.9 6.3 %collective-permute-start.2 = (bf16[4,32,128]{2,1,0:T(8,128)(2,1)S(1)}, bf16[4,32,128]{2,1,0:T(8,128)(2,1)S(1)}, u32[]{:S(2)}, u32[]{:S(2)}) collective-permute-start(bf16[4,32,128]{2,1,0:T(8,128)(2,1)S(1)} %get-tuple-element.58), channel_id=1, source_target_pairs={{0,32},{16,48},{32,64},{48,80},{64,96},{80,112},{96,128},{112,144}... | collective-permute-start | bytes 98312 | tf_op jit(solution)/shard_map/ppermute | solution.py:19
  12.9 8.0 %collective-permute-start.3 = (bf16[4,32,128]{2,1,0:T(8,128)(2,1)S(1)}, bf16[4,32,128]{2,1,0:T(8,128)(2,1)S(1)}, u32[]{:S(2)}, u32[]{:S(2)}) collective-permute-start(bf16[4,32,128]{2,1,0:T(8,128)(2,1)S(1)} %get-tuple-element.59), channel_id=1, source_target_pairs={{32,0},{48,16},{64,32},{80,48},{96,64},{112,80},{128,96},{144,112}... | collective-permute-start | bytes 98312 | tf_op jit(solution)/shard_map/ppermute | solution.py:19
  20.9 6.7 %copy-start = (bf16[4,32,128]{2,1,0:T(8,128)(2,1)}, bf16[4,32,128]{2,1,0:T(8,128)(2,1)S(1)}, u32[]{:S(2)}) copy-start(bf16[4,32,128]{2,1,0:T(8,128)(2,1)S(1)} %collective-permute-done.3.xhi2) | copy-start | bytes 98308
  21.3 12.6 %collective-permute-start.4 = (bf16[6,7,32,128]{3,2,1,0:T(8,128)(2,1)S(1)}, bf16[6,7,32,128]{3,2,1,0:T(8,128)(2,1)S(1)}, u32[]{:S(2)}, u32[]{:S(2)}) collective-permute-start(bf16[6,7,32,128]{3,2,1,0:T(8,128)(2,1)S(1)} %get-tuple-element.60), channel_id=1, source_target_pairs={{0,1},{1,2},{2,3},{3,4},{4,5},{5,6},{6,7},{7,8},{8,9},{9,10},{10,1... | collective-permute-start | bytes 1032200 | tf_op jit(solution)/shard_map/ppermute | solution.py:19
  27.6 8.6 %collective-permute-start.5 = (bf16[6,7,32,128]{3,2,1,0:T(8,128)(2,1)S(1)}, bf16[6,7,32,128]{3,2,1,0:T(8,128)(2,1)S(1)}, u32[]{:S(2)}, u32[]{:S(2)}) collective-permute-start(bf16[6,7,32,128]{3,2,1,0:T(8,128)(2,1)S(1)} %get-tuple-element.61.first_ref), channel_id=1, source_target_pairs={{1,0},{2,1},{3,2},{4,3},{5,4},{6,5},{7,6},{8,7},{9,8},{10,9},{11,1... | collective-permute-start | bytes 1032200 | tf_op jit(solution)/shard_map/ppermute | solution.py:19
  29.7 1.0 copy-start.4
  30.7 1.0 copy-start.5
  31.7 1.0 copy-start.6
  32.7 0.9 copy-start.7
  33.9 3.9 %copy-start.8 = (bf16[576,192]{1,0:T(8,128)(2,1)}, bf16[576,192]{1,0:T(8,128)(2,1)S(1)}, u32[]{:S(2)}) copy-start(bf16[576,192]{1,0:T(8,128)(2,1)S(1)} %get-tuple-element.96.w_ref) | copy-start | bytes 663556
  33.9 3.9 %copy-start.1 = (bf16[4,32,128]{2,1,0:T(8,128)(2,1)S(1)}, bf16[4,32,128]{2,1,0:T(8,128)(2,1)}, u32[]{:S(2)}) copy-start(bf16[4,32,128]{2,1,0:T(8,128)(2,1)} %copy-done) | copy-start | bytes 98308
  45.3 4.0 %collective-permute-start.6 = (bf16[32,80,128]{2,1,0:T(8,128)(2,1)S(1)}, bf16[32,80,128]{2,1,0:T(8,128)(2,1)S(1)}, u32[]{:S(2)}, u32[]{:S(2)}) collective-permute-start(bf16[32,80,128]{2,1,0:T(8,128)(2,1)S(1)} %get-tuple-element.78), channel_id=1, source_target_pairs={{0,1},{1,0},{2,3},{3,2},{4,5},{5,4},{6,7},{7,6},{8,9},{9,8},{10,11... | collective-permute-start | bytes 1966088 | tf_op jit(solution)/shard_map/ppermute | solution.py:27
  50.2 24.9 %all-to-all-start = ((bf16[32,80,128]{2,1,0:T(8,128)(2,1)}), bf16[32,80,128]{2,1,0:T(8,128)(2,1)S(1)}, u32[]{:S(2)}, u32[]{:S(2)}) async-start(bf16[32,80,128]{2,1,0:T(8,128)(2,1)} %shard_map.116), calls=%async_computation | async-start | bytes 1310720 | tf_op jit(solution)/shard_map/all_to_all | solution.py:474
  58.4 17.5 %collective-permute-start.8 = (bf16[224,128]{1,0:T(8,128)(2,1)}, bf16[224,128]{1,0:T(8,128)(2,1)S(1)}, u32[]{:S(2)}, u32[]{:S(2)}) collective-permute-start(bf16[224,128]{1,0:T(8,128)(2,1)} %get-tuple-element.81), channel_id=1, source_target_pairs={{16,0},{32,16},{48,32},{64,48},{80,64},{96,80},{112,96},{128,112},... | collective-permute-start | bytes 172040 | tf_op jit(solution)/shard_map/ppermute | solution.py:19
  59.7 16.2 %collective-permute-start.7 = (bf16[224,128]{1,0:T(8,128)(2,1)}, bf16[224,128]{1,0:T(8,128)(2,1)S(1)}, u32[]{:S(2)}, u32[]{:S(2)}) collective-permute-start(bf16[224,128]{1,0:T(8,128)(2,1)} %get-tuple-element.81), channel_id=1, source_target_pairs={{0,16},{16,32},{32,48},{48,64},{64,80},{80,96},{96,112},{112,128},... | collective-permute-start | bytes 172040 | tf_op jit(solution)/shard_map/ppermute | solution.py:19
  75.9 17.7 %all-to-all-start.1 = ((bf16[8,80,128]{2,1,0:T(8,128)(2,1)}), bf16[8,80,128]{2,1,0:T(8,128)(2,1)S(1)}, u32[]{:S(2)}, u32[]{:S(2)}) async-start(bf16[8,80,128]{2,1,0:T(8,128)(2,1)} %shard_map.117), calls=%async_computation.1 | async-start | bytes 327680 | tf_op jit(solution)/shard_map/all_to_all | solution.py:478
  85.8 8.7 %copy-start.10 = (bf16[2,10,32,64]{3,2,1,0:T(8,128)(2,1)}, bf16[2,10,32,64]{3,2,1,0:T(8,128)(2,1)S(1)}, u32[]{:S(2)}) copy-start(bf16[2,10,32,64]{3,2,1,0:T(8,128)(2,1)S(1)} %get-tuple-element.93.eg_ref) | copy-start | bytes 245764
  94.5 32.0 %copy-start.9 = (bf16[576,192]{1,0:T(8,128)(2,1)S(1)}, bf16[576,192]{1,0:T(8,128)(2,1)}, u32[]{:S(2)}) copy-start(bf16[576,192]{1,0:T(8,128)(2,1)} %copy-done.8) | copy-start | bytes 663556
  94.5 22.6 %all-to-all-start.2 = ((bf16[32,80,128]{2,1,0:T(8,128)(2,1)}), bf16[32,80,128]{2,1,0:T(8,128)(2,1)S(1)}, u32[]{:S(2)}, u32[]{:S(2)}) async-start(bf16[32,80,128]{2,1,0:T(8,128)(2,1)} %shard_map.118), calls=%async_computation.2 | async-start | bytes 1310720 | tf_op jit(solution)/shard_map/all_to_all | solution.py:488
  102.9 9.5 %collective-permute-start.9 = (bf16[160,128]{1,0:T(8,128)(2,1)S(1)}, bf16[160,128]{1,0:T(8,128)(2,1)S(1)}, u32[]{:S(2)}, u32[]{:S(2)}) collective-permute-start(bf16[160,128]{1,0:T(8,128)(2,1)S(1)} %get-tuple-element.88), channel_id=1, source_target_pairs={{0,16},{16,32},{32,48},{48,64},{64,80},{80,96},{96,112},{112,128},... | collective-permute-start | bytes 122888 | tf_op jit(solution)/shard_map/ppermute | solution.py:19
  106.0 10.7 %collective-permute-start.10 = (bf16[160,128]{1,0:T(8,128)(2,1)S(1)}, bf16[160,128]{1,0:T(8,128)(2,1)S(1)}, u32[]{:S(2)}, u32[]{:S(2)}) collective-permute-start(bf16[160,128]{1,0:T(8,128)(2,1)S(1)} %get-tuple-element.89), channel_id=1, source_target_pairs={{16,0},{32,16},{48,32},{64,48},{80,64},{96,80},{112,96},{128,112},... | collective-permute-start | bytes 122888 | tf_op jit(solution)/shard_map/ppermute | solution.py:19
  117.0 11.6 %collective-permute-start.11 = (bf16[32,80,128]{2,1,0:T(8,128)(2,1)S(1)}, bf16[32,80,128]{2,1,0:T(8,128)(2,1)S(1)}, u32[]{:S(2)}, u32[]{:S(2)}) collective-permute-start(bf16[32,80,128]{2,1,0:T(8,128)(2,1)S(1)} %all-to-all-done.2.own_ref), channel_id=1, source_target_pairs={{0,1},{1,0},{2,3},{3,2},{4,5},{5,4},{6,7},{7,6},{8,9},{9,8},{10,11... | collective-permute-start | bytes 1966088 | tf_op jit(solution)/shard_map/ppermute | solution.py:27
  126.4 0.9 copy-start.11

commit v8 on v6

--- a/solution.py
+++ b/solution.py
@@ -180,9 +180,9 @@
         pool_ref[x // 2, 7:10] = (pooled[112:160] * inside[3]).astype(BF16).reshape(3, 16, 64)
 
 
-def joined_grad_kernel(c_ref, *refs):
-    (ylo, yhi, xlo, xhi), (w_ref, lift_ref) = refs[:4], refs[4:6]
-    cx_ref, jg_ref, kids_ref, adj_ref, tmp = refs[6:]
+def joined_grad_kernel(
+    c_ref, ylo, yhi, xlo, xhi, w_ref, lift_ref, cx_ref, jg_ref, kids_ref, adj_ref, tmp
+):
     cx_ref[1:3, 5:13] = c_ref[...]
     cx_ref[0, 5:13] = xlo[0:8, :, 64:]
     cx_ref[3, 5:13] = xhi[0:8, :, 64:]
@@ -303,6 +303,22 @@
     send_ref[:, chunk:, :] = enc_halves[1 - mine]
 
 
+def middle_kernel(f_ref, c_ref, *refs):
+    (ylo, yhi, xlo, xhi, xlo2, xhi2, inside, core), refs = refs[:8], refs[8:]
+    (enc_w, dec_w, low_w, low_wt, lift), refs = refs[:5], refs[5:]
+    (enc, slope, jg, lg, msg, lifted, keep, send), refs = refs[:8], refs[8:]
+    (fx, cx, pool, kids, adj, la, tmp, kid_tmp, lift_tmp, halves, enc_halves, wide) = refs
+    joined_grad_kernel(c_ref, ylo, yhi, xlo, xhi, dec_w, lift, cx, jg, kids, adj, kid_tmp)
+    encode_kernel(
+        f_ref, ylo, yhi, xlo, xhi, xlo2, xhi2, inside, enc_w, fx, enc, slope, pool, tmp
+    )
+    lower_kernel(pool, inside, low_w, adj, la, lg, msg)
+    grads_kernel(
+        *(pool, la, lg, core, lift, kids, cx, enc, low_wt, slope, jg, fx),
+        *(lifted, keep, send, lift_tmp, halves, enc_halves, wide),
+    )
+
+
 def add_kernel(a_ref, b_ref, out_ref):
     out_ref[...] = (a_ref[...].astype(F32) + b_ref[...].astype(F32)).astype(LINK)
 
@@ -419,52 +435,38 @@
         spaces={0: pltpu.HBM},
         flops=2 * 10**9,
     )
-    fx, encoded, slope, pooled = call(
-        encode_kernel,
-        [((8, 22, 32, 64), BF16), ((4, 10, 32, 64), BF16)]
-        + [((6, 320, 64), F32), ((3, 10, 16, 64), BF16)],
-        [((320, 64), F32)],
-        [f, *y_halo, *x_halo, *far_halo, inside, enc_fwd],
-        spaces={7: pltpu.SMEM},
-    )
-    cx, jg, kids, adj = call(
-        joined_grad_kernel,
+    half = (size_x, 2560 // size_x, 128)
+    encoded, slope, jg, lg, edge, lifted, keep, send = call(
+        middle_kernel,
+        [((4, 10, 32, 64), BF16), ((6, 320, 64), F32), ((2, 320, 64), BF16)]
+        + [((128, 128), BF16), ((224, 128), BF16), (tall, BF16), (half, LINK), (half, LINK)],
         [
+            ((8, 22, 32, 64), BF16),
             ((4, 18, 32, 64), BF16),
-            ((2, 320, 64), BF16),
+            ((3, 10, 16, 64), BF16),
             ((64, 512), BF16),
             ((128, 128), F32),
-        ],
-        [((1024, 128), F32)],
-        [c, *y_halo, *x_halo, dec_bwd, lift],
-    )
-    half = (size_x, 2560 // size_x, 128)
-    la, lg, edge = call(
-        lower_kernel,
-        [((96, 128), BF16), ((128, 128), BF16), ((224, 128), BF16)],
-        [],
-        [pooled, inside, low_fwd, adj],
-        spaces={1: pltpu.SMEM},
-    )
-    lifted, keep, send = call(
-        grads_kernel,
-        [(tall, BF16), (half, LINK), (half, LINK)],
-        [
+            ((96, 128), BF16),
+            ((320, 64), F32),
+            ((1024, 128), F32),
             ((640, 64), F32),
             ((2, size_x, 2048 // size_x, 128), LINK),
             ((2, size_x, 512 // size_x, 128), LINK),
             ((128, 64), F32),
         ],
-        [pooled, la, lg, core, lift, kids, cx, encoded, low_bwd, slope, jg, fx],
-        spaces={3: pltpu.SMEM},
+        [f, c, *y_halo, *x_halo, *far_halo, inside, core]
+        + [enc_fwd, dec_bwd, low_fwd, low_bwd, lift],
+        spaces={8: pltpu.SMEM, 9: pltpu.SMEM},
     )
     (sums,) = call(add_kernel, [(half, LINK)], [], [keep, partner(send)])
+    sums = lax.all_to_all(sums, "gx", 0, 0)
+    (sums,) = call(sum_kernel, [((size_z,) + half[1:], LINK)], [], [sums])
     sums, edge = lax.optimization_barrier((sums, edge))
+    sums = lax.all_to_all(sums, "gz", 0, 0)
+    halo = swapped(edge, edge, GX)
+    (sums,) = call(sum_kernel, [(half, LINK)], [], [sums])
+    sums, halo = lax.optimization_barrier((sums, halo))
     sums = lax.all_to_all(sums, "gx", 0, 0)
-    halo = swapped(edge, edge, GX)
-    (sums,) = call(sum_kernel, [((size_z,) + half[1:], LINK)], [], [sums])
-    sums, halo = lax.optimization_barrier((sums, halo))
-    sums = lax.all_to_all(sums, "gz", 0, 0)
     eg, *edges = call(
         encoder_grad_kernel,
         [(tall, BF16)] + [((160, 128), BF16)] * 2,
@@ -472,22 +474,20 @@
         [lg, *halo, low_bwd, slope, jg],
     )
     eg_halo = swapped(*edges, GX)
-    (sums,) = call(sum_kernel, [(half, LINK)], [], [sums])
-    sums, eg_halo = lax.optimization_barrier((sums, eg_halo))
-    sums = lax.all_to_all(sums, "gx", 0, 0)
     (decoded,) = call(
         decode_kernel,
         [(brick, BF16)],
         [((4, 10, 32, 128), BF16), ((320, 64), F32)],
         [encoded, lifted, *halo, lift, dec_fwd],
     )
+    sums, eg_halo, decoded = lax.optimization_barrier((sums, eg_halo, decoded))
     (input_grad,) = call(
         input_grad_kernel,
         [(brick, BF16)],
         [((4, 10, 32, 64), BF16)],
         [eg, *eg_halo, enc_bwd],
-    )
-    sums, decoded, input_grad = lax.optimization_barrier((sums, decoded, input_grad))
+        flops=2 * 10**9,
+    )
     encoder_gradient, decoder_gradient, lower_gradient, lift_gradient = call(
         widen_kernel,
         [((27, 64, 64), F32), ((27, 64, 128), F32), ((27, 64, 128), F32), ((8, 64, 128), F32)],

time: 129 us -> 130 us (level)
  blocking collectives: 0 us -> 24.7 us
  waiting for transfers between devices: 38.1 us -> 21.9 us
  starting transfers between devices: 66.7 us -> 61.8 us
  local copies, waits for them, and re-layouts: 5.76 us -> 3.87 us
    all_to_all x0 -> x1, blocking collectives: none -> 24.7 us  [per_device(): sums = lax.all_to_all(sums, 'gx', 0, 0)]
    all_to_all x2 -> x1, waiting for transfers between devices: 22.6 us -> 0.5 us  [per_device(): sums = lax.all_to_all(sums, 'gx', 0, 0)]
    ppermute x10, waiting for transfers between devices: 11.5 us -> 18.6 us  [shifted(): return lax.ppermute(piece, axes, pairs)]
    all_to_all x2 -> x1, starting transfers between devices: 13.8 us -> 9.25 us  [per_device(): sums = lax.all_to_all(sums, 'gx', 0, 0)]
    unnamed x16 -> x24, local copies, waits for them, and re-layouts: 5.76 us -> 3.87 us
    pallas_call x14 -> x11, Pallas kernels: 16.9 us -> 16.2 us  [call(): pl.pallas_call(kernel, out_shape=[jax.ShapeDtypeStruct(s, d) for s, d in...]
  transfers between devices with their start and end apart: 15 -> 14, of which waited for: 8 -> 9; matrix products, arithmetic and copies ran while one was open for 0% -> 0% of each run, Pallas kernels for 4% -> 3%
where the time goes in v8:
time: 130 us; the launch traced here: 129 us
  starting transfers between devices  61.8 us (48%)
  blocking collectives  24.7 us (19%)
  waiting for transfers between devices  21.9 us (17%)
  Pallas kernels  16.2 us (12%)
  local copies, waits for them, and re-layouts  3.87 us (3%)
    ppermute x10, starting transfers between devices, shifted(): return lax.ppermute(piece, axes, pairs)  32.2 us
    all_to_all x1, blocking collectives, per_device(): sums = lax.all_to_all(sums, 'gx', 0, 0)  24.7 us
    ppermute x10, waiting for transfers between devices, shifted(): return lax.ppermute(piece, axes, pairs)  18.6 us
    pallas_call x11, Pallas kernels, call(): pl.pallas_call(kernel, out_shape=[jax.ShapeDtypeStruct(s, d) for s, d in...  16.2 us
    ppermute x2, starting transfers between devices, partner(): return lax.ppermute(piece, 'gc', [(0, 1), (1, 0)])  11 us
    all_to_all x1, starting transfers between devices, per_device(): sums = lax.all_to_all(sums, 'gz', 0, 0)  9.41 us
    all_to_all x1, starting transfers between devices, per_device(): sums = lax.all_to_all(sums, 'gx', 0, 0)  9.25 us
    unnamed x24, local copies, waits for them, and re-layouts  3.87 us
  transfers between devices with their start and end apart: 14, of which 9 were waited for; matrix products, arithmetic and copies ran while one was open for 0% of the time, Pallas kernels for 3%

profile of v8, /device:TPU:1, one launch (start us, length us, event | category | flops | bytes accessed | tf_op | source)
XLA Modules:
  0.0 129.4 jit_solution(4956093717819289820)
XLA Ops:
  0.6 0.9 copy-done.4
  1.5 0.9 copy-done.5
  2.4 0.1 shard_map.109
  2.6 4.0 %collective-permute-start = (bf16[12,32,128]{2,1,0:T(8,128)(2,1)S(1)}, bf16[12,32,128]{2,1,0:T(8,128)(2,1)S(1)}, u32[]{:S(2)}, u32[]{:S(2)}) collective-permute-start(bf16[12,32,128]{2,1,0:T(8,128)(2,1)S(1)} %get-tuple-element.47), channel_id=1, source_target_pairs={{0,16},{16,32},{32,48},{48,64},{64,80},{80,96},{96,112},{112,128},... | collective-permute-start | bytes 294920 | tf_op jit(solution)/shard_map/ppermute | solution.py:19
  6.6 1.3 collective-permute-start.1
  7.9 5.0 %collective-permute-start.2 = (bf16[4,32,128]{2,1,0:T(8,128)(2,1)S(1)}, bf16[4,32,128]{2,1,0:T(8,128)(2,1)S(1)}, u32[]{:S(2)}, u32[]{:S(2)}) collective-permute-start(bf16[4,32,128]{2,1,0:T(8,128)(2,1)S(1)} %get-tuple-element.49), channel_id=1, source_target_pairs={{0,32},{16,48},{32,64},{48,80},{64,96},{80,112},{96,128},{112,144}... | collective-permute-start | bytes 98312 | tf_op jit(solution)/shard_map/ppermute | solution.py:19
  12.9 1.3 collective-permute-start.3
  14.2 0.0 collective-permute-done.2.xlo2.refs_4_
  14.2 6.7 %collective-permute-done.3.xhi2.refs_5_ = bf16[4,32,128]{2,1,0:T(8,128)(2,1)S(1)} collective-permute-done((bf16[4,32,128]{2,1,0:T(8,128)(2,1)S(1)}, bf16[4,32,128]{2,1,0:T(8,128)(2,1)S(1)}, u32[]{:S(2)}, u32[]{:S(2)}) %collective-permute-start.3) | collective-permute-done | bytes 32800 | tf_op jit(solution)/shard_map/ppermute | solution.py:19
  20.9 0.0 collective-permute-done.xlo.refs_2_
  20.9 1.2 shard_map.110
  22.1 6.3 %collective-permute-start.4 = (bf16[6,7,32,128]{3,2,1,0:T(8,128)(2,1)}, bf16[6,7,32,128]{3,2,1,0:T(8,128)(2,1)S(1)}, u32[]{:S(2)}, u32[]{:S(2)}) collective-permute-start(bf16[6,7,32,128]{3,2,1,0:T(8,128)(2,1)} %get-tuple-element.51), channel_id=1, source_target_pairs={{0,1},{1,2},{2,3},{3,4},{4,5},{5,6},{6,7},{7,8},{8,9},{9,10},{10,1... | collective-permute-start | bytes 1032200 | tf_op jit(solution)/shard_map/ppermute | solution.py:19
  28.4 1.9 %collective-permute-start.5 = (bf16[6,7,32,128]{3,2,1,0:T(8,128)(2,1)}, bf16[6,7,32,128]{3,2,1,0:T(8,128)(2,1)S(1)}, u32[]{:S(2)}, u32[]{:S(2)}) collective-permute-start(bf16[6,7,32,128]{3,2,1,0:T(8,128)(2,1)} %get-tuple-element.52.first_ref), channel_id=1, source_target_pairs={{1,0},{2,1},{3,2},{4,3},{5,4},{6,5},{7,6},{8,7},{9,8},{10,9},{11,1... | collective-permute-start | bytes 1032200 | tf_op jit(solution)/shard_map/ppermute | solution.py:19
  30.3 0.1 add_convert_fusion.refs_6_
  30.4 1.0 copy-done.7
  31.4 1.0 copy-done.8
  32.5 0.3 shard_map.111
  32.8 0.0 copy-start.10
  32.8 0.1 collective-permute-done.4.refs_0_
  32.9 4.3 %collective-permute-done.5.refs_1_ = bf16[6,7,32,128]{3,2,1,0:T(8,128)(2,1)S(1)} collective-permute-done((bf16[6,7,32,128]{3,2,1,0:T(8,128)(2,1)}, bf16[6,7,32,128]{3,2,1,0:T(8,128)(2,1)S(1)}, u32[]{:S(2)}, u32[]{:S(2)}) %collective-permute-start.5) | collective-permute-done | bytes 344096 | tf_op jit(solution)/shard_map/ppermute | solution.py:19
  37.2 7.8 %shard_map.112 = (bf16[4,10,32,64]{3,2,1,0:T(8,128)(2,1)S(1)}, f32[6,320,64]{2,1,0:T(8,128)S(1)}, bf16[2,320,64]{2,1,0:T(8,128)(2,1)S(1)}, bf16[128,128]{1,0:T(8...) custom-call(bf16[2,8,32,64]{3,2,1,0:T(8,128)(2,1)S(1)} %get-tuple-el, ...), custom_call_target="tpu_custom_call" | custom-call | flops 1000000 | bytes 10000 | tf_op jit(solution)/shard_map/pallas_call | solution.py:31
  45.0 0.0 copy-start
  45.0 0.0 copy-start.2
  45.0 1.9 %collective-permute-start.6 = (bf16[32,80,128]{2,1,0:T(8,128)(2,1)S(1)}, bf16[32,80,128]{2,1,0:T(8,128)(2,1)S(1)}, u32[]{:S(2)}, u32[]{:S(2)}) collective-permute-start(bf16[32,80,128]{2,1,0:T(8,128)(2,1)S(1)} %get-tuple-element.59), channel_id=1, source_target_pairs={{0,1},{1,0},{2,3},{3,2},{4,5},{5,4},{6,7},{7,6},{8,9},{9,8},{10,11... | collective-permute-start | bytes 1966088 | tf_op jit(solution)/shard_map/ppermute | solution.py:27
  46.9 2.1 %collective-permute-done.6.b_ref = bf16[32,80,128]{2,1,0:T(8,128)(2,1)S(1)} collective-permute-done((bf16[32,80,128]{2,1,0:T(8,128)(2,1)S(1)}, bf16[32,80,128]{2,1,0:T(8,128)(2,1)S(1)}, u32[]{:S(2)}, u32[]{:S(2)}) %collective-permute-start.6) | collective-permute-done | bytes 655392 | tf_op jit(solution)/shard_map/ppermute | solution.py:27
  49.0 0.2 shard_map.113
  49.2 24.7 %all_to_all.15.parts_ref = bf16[32,80,128]{2,1,0:T(8,128)(2,1)S(1)} all-to-all(bf16[32,80,128]{2,1,0:T(8,128)(2,1)S(1)} %shard_map.113), channel_id=1, replica_groups=mesh['gx'=32,'gz'=8,'gc'=2] {'gx'}, dimensions={0} | all-to-all | bytes 1310720 | tf_op jit(solution)/shard_map/all_to_all | solution.py:462
  73.8 0.8 shard_map.114
  74.6 9.4 %all-to-all-start.1 = ((bf16[8,80,128]{2,1,0:T(8,128)(2,1)}), bf16[8,80,128]{2,1,0:T(8,128)(2,1)S(1)}, u32[]{:S(2)}, u32[]{:S(2)}) async-start(bf16[8,80,128]{2,1,0:T(8,128)(2,1)} %shard_map.114), calls=%async_computation.1 | async-start | bytes 327680 | tf_op jit(solution)/shard_map/all_to_all | solution.py:465
  84.0 1.3 collective-permute-start.8
  85.3 6.7 %collective-permute-start.7 = (bf16[224,128]{1,0:T(8,128)(2,1)S(1)}, bf16[224,128]{1,0:T(8,128)(2,1)S(1)}, u32[]{:S(2)}, u32[]{:S(2)}) collective-permute-start(bf16[224,128]{1,0:T(8,128)(2,1)S(1)} %get-tuple-element.62), channel_id=1, source_target_pairs={{0,16},{16,32},{32,48},{48,64},{64,80},{80,96},{96,112},{112,128},... | collective-permute-start | bytes 172040 | tf_op jit(solution)/shard_map/ppermute | solution.py:19
  92.0 0.3 all-to-all-done.1.parts_ref
  92.3 0.9 shard_map.115
  93.2 0.0 collective-permute-done.7.xlo
  93.2 9.3 %all-to-all-start.2 = ((bf16[32,80,128]{2,1,0:T(8,128)(2,1)}), bf16[32,80,128]{2,1,0:T(8,128)(2,1)S(1)}, u32[]{:S(2)}, u32[]{:S(2)}) async-start(bf16[32,80,128]{2,1,0:T(8,128)(2,1)} %shard_map.115), calls=%async_computation.2 | async-start | bytes 1310720 | tf_op jit(solution)/shard_map/all_to_all | solution.py:469
  102.5 0.0 copy-start.1
  102.5 0.5 shard_map.116
  103.0 3.1 %collective-permute-start.9 = (bf16[160,128]{1,0:T(8,128)(2,1)S(1)}, bf16[160,128]{1,0:T(8,128)(2,1)S(1)}, u32[]{:S(2)}, u32[]{:S(2)}) collective-permute-start(bf16[160,128]{1,0:T(8,128)(2,1)S(1)} %get-tuple-element.69), channel_id=1, source_target_pairs={{0,16},{16,32},{32,48},{48,64},{64,80},{80,96},{96,112},{112,128},... | collective-permute-start | bytes 122888 | tf_op jit(solution)/shard_map/ppermute | solution.py:19
  106.1 1.3 collective-permute-start.10
  107.4 0.0 copy-start.11
  107.4 1.5 %shard_map.117 = bf16[2,8,32,64]{3,2,1,0:T(8,128)(2,1)} custom-call(bf16[4,10,32,64]{3,2,1,0:T(8,128)(2,1)S(1)} %copy-done.1, bf16[2,10,32,64]{3,2,1,0:T(8,128)(2,1)S(1)} %get-tuple-element.72.lifted_ref, bf16[224,128]{1,0:T(8,128)(2,1)S(1)} %collective-permute-done.7.xlo, bf16[224,128]{1,0:T(8,128)(2,1)S(1)} %collective-permute-done.8.xhi, ...), custom_call_target="tpu_custom_call" | custom-call | flops 1000000 | bytes 10000 | tf_op jit(solution)/shard_map/pallas_call | solution.py:31
  108.9 3.0 %collective-permute-done.9.xlo = bf16[160,128]{1,0:T(8,128)(2,1)S(1)} collective-permute-done((bf16[160,128]{1,0:T(8,128)(2,1)S(1)}, bf16[160,128]{1,0:T(8,128)(2,1)S(1)}, u32[]{:S(2)}, u32[]{:S(2)}) %collective-permute-start.9) | collective-permute-done | bytes 40992 | tf_op jit(solution)/shard_map/ppermute | solution.py:19
  111.9 4.5 %collective-permute-done.10.xhi = bf16[160,128]{1,0:T(8,128)(2,1)S(1)} collective-permute-done((bf16[160,128]{1,0:T(8,128)(2,1)S(1)}, bf16[160,128]{1,0:T(8,128)(2,1)S(1)}, u32[]{:S(2)}, u32[]{:S(2)}) %collective-permute-start.10) | collective-permute-done | bytes 40992 | tf_op jit(solution)/shard_map/ppermute | solution.py:19
  116.4 0.5 all-to-all-done.2.own_ref
  116.9 9.1 %collective-permute-start.11 = (bf16[32,80,128]{2,1,0:T(8,128)(2,1)S(1)}, bf16[32,80,128]{2,1,0:T(8,128)(2,1)S(1)}, u32[]{:S(2)}, u32[]{:S(2)}) collective-permute-start(bf16[32,80,128]{2,1,0:T(8,128)(2,1)S(1)} %all-to-all-done.2.own_ref), channel_id=1, source_target_pairs={{0,1},{1,0},{2,3},{3,2},{4,5},{5,4},{6,7},{7,6},{8,9},{9,8},{10,11... | collective-permute-start | bytes 1966088 | tf_op jit(solution)/shard_map/ppermute | solution.py:27
  125.9 1.3 shard_map.118
  127.2 0.4 collective-permute-done.11.other_ref
  127.6 1.8 %shard_map.119 = (f32[27,64,64]{2,1,0:T(8,128)}, f32[27,64,128]{2,1,0:T(8,128)}, f32[27,64,128]{2,1,0:T(8,128)}, f32[8,64,128]{2,1,0:T(8,128)}) custom-call(s32[1]{0:T(128)} %bitcast.6.refs_7_.core, bf16[32,80,128]{2,1,0:T(8,128)(2,1)S(1)} %all-to-all-done.2.own_ref, bf16[32,80,128]{2,1,0:T(8,128)(2,1)S(1)} %collective-permute-done.11.other_ref), custom_call_target="tpu_custom_call" | custom-call | flops 1000000 | bytes 10000 | tf_op jit(solution)/shard_map/pallas_call | solution.py:31
  (17 shorter events, 0.0 us)
Async XLA Ops:
  0.6 0.9 copy-start.4
  1.5 0.9 copy-start.5
  2.4 28.0 %copy-start.6 = (bf16[27,64,64]{2,1,0:T(8,128)(2,1)S(1)}, bf16[27,64,64]{2,1,0:T(8,128)(2,1)}, u32[]{:S(2)}) copy-start(bf16[27,64,64]{2,1,0:T(8,128)(2,1)} %enc_ref.1) | copy-start | bytes 663556
  2.6 18.3 %collective-permute-start = (bf16[12,32,128]{2,1,0:T(8,128)(2,1)S(1)}, bf16[12,32,128]{2,1,0:T(8,128)(2,1)S(1)}, u32[]{:S(2)}, u32[]{:S(2)}) collective-permute-start(bf16[12,32,128]{2,1,0:T(8,128)(2,1)S(1)} %get-tuple-element.47), channel_id=1, source_target_pairs={{0,16},{16,32},{32,48},{48,64},{64,80},{80,96},{96,112},{112,128},... | collective-permute-start | bytes 294920 | tf_op jit(solution)/shard_map/ppermute | solution.py:19
  6.6 14.3 %collective-permute-start.1 = (bf16[12,32,128]{2,1,0:T(8,128)(2,1)S(1)}, bf16[12,32,128]{2,1,0:T(8,128)(2,1)S(1)}, u32[]{:S(2)}, u32[]{:S(2)}) collective-permute-start(bf16[12,32,128]{2,1,0:T(8,128)(2,1)S(1)} %get-tuple-element.48), channel_id=1, source_target_pairs={{16,0},{32,16},{48,32},{64,48},{80,64},{96,80},{112,96},{128,112},... | collective-permute-start | bytes 294920 | tf_op jit(solution)/shard_map/ppermute | solution.py:19
  7.9 6.3 %collective-permute-start.2 = (bf16[4,32,128]{2,1,0:T(8,128)(2,1)S(1)}, bf16[4,32,128]{2,1,0:T(8,128)(2,1)S(1)}, u32[]{:S(2)}, u32[]{:S(2)}) collective-permute-start(bf16[4,32,128]{2,1,0:T(8,128)(2,1)S(1)} %get-tuple-element.49), channel_id=1, source_target_pairs={{0,32},{16,48},{32,64},{48,80},{64,96},{80,112},{96,128},{112,144}... | collective-permute-start | bytes 98312 | tf_op jit(solution)/shard_map/ppermute | solution.py:19
  12.9 8.0 %collective-permute-start.3 = (bf16[4,32,128]{2,1,0:T(8,128)(2,1)S(1)}, bf16[4,32,128]{2,1,0:T(8,128)(2,1)S(1)}, u32[]{:S(2)}, u32[]{:S(2)}) collective-permute-start(bf16[4,32,128]{2,1,0:T(8,128)(2,1)S(1)} %get-tuple-element.50), channel_id=1, source_target_pairs={{32,0},{48,16},{64,32},{80,48},{96,64},{112,80},{128,96},{144,112}... | collective-permute-start | bytes 98312 | tf_op jit(solution)/shard_map/ppermute | solution.py:19
  20.9 9.5 %copy-start.9 = (bf16[8,64,128]{2,1,0:T(8,128)(2,1)S(1)}, bf16[8,64,128]{2,1,0:T(8,128)(2,1)}, u32[]{:S(2)}) copy-start(bf16[8,64,128]{2,1,0:T(8,128)(2,1)} %lift_ref.1) | copy-start | bytes 393220
  22.1 10.8 %collective-permute-start.4 = (bf16[6,7,32,128]{3,2,1,0:T(8,128)(2,1)}, bf16[6,7,32,128]{3,2,1,0:T(8,128)(2,1)S(1)}, u32[]{:S(2)}, u32[]{:S(2)}) collective-permute-start(bf16[6,7,32,128]{3,2,1,0:T(8,128)(2,1)} %get-tuple-element.51), channel_id=1, source_target_pairs={{0,1},{1,2},{2,3},{3,4},{4,5},{5,6},{6,7},{7,8},{8,9},{9,10},{10,1... | collective-permute-start | bytes 1032200 | tf_op jit(solution)/shard_map/ppermute | solution.py:19
  28.4 8.8 %collective-permute-start.5 = (bf16[6,7,32,128]{3,2,1,0:T(8,128)(2,1)}, bf16[6,7,32,128]{3,2,1,0:T(8,128)(2,1)S(1)}, u32[]{:S(2)}, u32[]{:S(2)}) collective-permute-start(bf16[6,7,32,128]{3,2,1,0:T(8,128)(2,1)} %get-tuple-element.52.first_ref), channel_id=1, source_target_pairs={{1,0},{2,1},{3,2},{4,3},{5,4},{6,5},{7,6},{8,7},{9,8},{10,9},{11,1... | collective-permute-start | bytes 1032200 | tf_op jit(solution)/shard_map/ppermute | solution.py:19
  30.4 1.0 copy-start.7
  31.4 1.0 copy-start.8
  32.8 12.2 %copy-start.10 = (bf16[576,192]{1,0:T(8,128)(2,1)}, bf16[576,192]{1,0:T(8,128)(2,1)S(1)}, u32[]{:S(2)}) copy-start(bf16[576,192]{1,0:T(8,128)(2,1)S(1)} %get-tuple-element.78.w_ref) | copy-start | bytes 663556
  45.0 4.2 %copy-start = (bf16[4,10,32,64]{3,2,1,0:T(8,128)(2,1)}, bf16[4,10,32,64]{3,2,1,0:T(8,128)(2,1)S(1)}, u32[]{:S(2)}) copy-start(bf16[4,10,32,64]{3,2,1,0:T(8,128)(2,1)S(1)} %get-tuple-element.71.enc_ref) | copy-start | bytes 491524
  45.0 4.2 %copy-start.2 = (bf16[2,320,64]{2,1,0:T(8,128)(2,1)}, bf16[2,320,64]{2,1,0:T(8,128)(2,1)S(1)}, u32[]{:S(2)}) copy-start(bf16[2,320,64]{2,1,0:T(8,128)(2,1)S(1)} %get-tuple-element.68.jg_ref) | copy-start | bytes 245764
  45.0 4.0 %collective-permute-start.6 = (bf16[32,80,128]{2,1,0:T(8,128)(2,1)S(1)}, bf16[32,80,128]{2,1,0:T(8,128)(2,1)S(1)}, u32[]{:S(2)}, u32[]{:S(2)}) collective-permute-start(bf16[32,80,128]{2,1,0:T(8,128)(2,1)S(1)} %get-tuple-element.59), channel_id=1, source_target_pairs={{0,1},{1,0},{2,3},{3,2},{4,5},{5,4},{6,7},{7,6},{8,9},{9,8},{10,11... | collective-permute-start | bytes 1966088 | tf_op jit(solution)/shard_map/ppermute | solution.py:27
  74.6 17.7 %all-to-all-start.1 = ((bf16[8,80,128]{2,1,0:T(8,128)(2,1)}), bf16[8,80,128]{2,1,0:T(8,128)(2,1)S(1)}, u32[]{:S(2)}, u32[]{:S(2)}) async-start(bf16[8,80,128]{2,1,0:T(8,128)(2,1)} %shard_map.114), calls=%async_computation.1 | async-start | bytes 327680 | tf_op jit(solution)/shard_map/all_to_all | solution.py:465
  84.0 9.2 %collective-permute-start.8 = (bf16[224,128]{1,0:T(8,128)(2,1)S(1)}, bf16[224,128]{1,0:T(8,128)(2,1)S(1)}, u32[]{:S(2)}, u32[]{:S(2)}) collective-permute-start(bf16[224,128]{1,0:T(8,128)(2,1)S(1)} %get-tuple-element.62), channel_id=1, source_target_pairs={{16,0},{32,16},{48,32},{64,48},{80,64},{96,80},{112,96},{128,112},... | collective-permute-start | bytes 172040 | tf_op jit(solution)/shard_map/ppermute | solution.py:19
  85.3 7.9 %collective-permute-start.7 = (bf16[224,128]{1,0:T(8,128)(2,1)S(1)}, bf16[224,128]{1,0:T(8,128)(2,1)S(1)}, u32[]{:S(2)}, u32[]{:S(2)}) collective-permute-start(bf16[224,128]{1,0:T(8,128)(2,1)S(1)} %get-tuple-element.62), channel_id=1, source_target_pairs={{0,16},{16,32},{32,48},{48,64},{64,80},{80,96},{96,112},{112,128},... | collective-permute-start | bytes 172040 | tf_op jit(solution)/shard_map/ppermute | solution.py:19
  93.2 9.3 %copy-start.3 = (bf16[2,320,64]{2,1,0:T(8,128)(2,1)S(1)}, bf16[2,320,64]{2,1,0:T(8,128)(2,1)}, u32[]{:S(2)}) copy-start(bf16[2,320,64]{2,1,0:T(8,128)(2,1)} %copy-done.2) | copy-start | bytes 245764
  93.2 23.7 %all-to-all-start.2 = ((bf16[32,80,128]{2,1,0:T(8,128)(2,1)}), bf16[32,80,128]{2,1,0:T(8,128)(2,1)S(1)}, u32[]{:S(2)}, u32[]{:S(2)}) async-start(bf16[32,80,128]{2,1,0:T(8,128)(2,1)} %shard_map.115), calls=%async_computation.2 | async-start | bytes 1310720 | tf_op jit(solution)/shard_map/all_to_all | solution.py:469
  102.5 4.9 %copy-start.1 = (bf16[4,10,32,64]{3,2,1,0:T(8,128)(2,1)S(1)}, bf16[4,10,32,64]{3,2,1,0:T(8,128)(2,1)}, u32[]{:S(2)}) copy-start(bf16[4,10,32,64]{3,2,1,0:T(8,128)(2,1)} %copy-done) | copy-start | bytes 491524
  103.0 8.9 %collective-permute-start.9 = (bf16[160,128]{1,0:T(8,128)(2,1)S(1)}, bf16[160,128]{1,0:T(8,128)(2,1)S(1)}, u32[]{:S(2)}, u32[]{:S(2)}) collective-permute-start(bf16[160,128]{1,0:T(8,128)(2,1)S(1)} %get-tuple-element.69), channel_id=1, source_target_pairs={{0,16},{16,32},{32,48},{48,64},{64,80},{80,96},{96,112},{112,128},... | collective-permute-start | bytes 122888 | tf_op jit(solution)/shard_map/ppermute | solution.py:19
  106.1 10.2 %collective-permute-start.10 = (bf16[160,128]{1,0:T(8,128)(2,1)S(1)}, bf16[160,128]{1,0:T(8,128)(2,1)S(1)}, u32[]{:S(2)}, u32[]{:S(2)}) collective-permute-start(bf16[160,128]{1,0:T(8,128)(2,1)S(1)} %get-tuple-element.70), channel_id=1, source_target_pairs={{16,0},{32,16},{48,32},{64,48},{80,64},{96,80},{112,96},{128,112},... | collective-permute-start | bytes 122888 | tf_op jit(solution)/shard_map/ppermute | solution.py:19
  107.4 18.5 %copy-start.11 = (bf16[576,192]{1,0:T(8,128)(2,1)S(1)}, bf16[576,192]{1,0:T(8,128)(2,1)}, u32[]{:S(2)}) copy-start(bf16[576,192]{1,0:T(8,128)(2,1)} %copy-done.10) | copy-start | bytes 663556
  116.9 10.8 %collective-permute-start.11 = (bf16[32,80,128]{2,1,0:T(8,128)(2,1)S(1)}, bf16[32,80,128]{2,1,0:T(8,128)(2,1)S(1)}, u32[]{:S(2)}, u32[]{:S(2)}) collective-permute-start(bf16[32,80,128]{2,1,0:T(8,128)(2,1)S(1)} %all-to-all-done.2.own_ref), channel_id=1, source_target_pairs={{0,1},{1,0},{2,3},{3,2},{4,5},{5,4},{6,7},{7,6},{8,9},{9,8},{10,11... | collective-permute-start | bytes 1966088 | tf_op jit(solution)/shard_map/ppermute | solution.py:27

commit v9 on v8

--- a/solution.py
+++ b/solution.py
@@ -25,6 +25,24 @@
 
 def partner(piece):
     return lax.ppermute(piece, "gc", [(0, 1), (1, 0)])
+
+
+def exchanged(blocks, wide):
+    size_x, size_z = lax.axis_size("gx"), lax.axis_size("gz")
+    size_y = size_z
+    assert size_x % size_y == 0
+
+    def place(x, y, z, core):
+        return ((x * size_y + y) * size_z + z) * 2 + core
+
+    xs, ys, zs = range(size_x // size_y), range(size_y), range(size_z)
+    if wide:
+        groups = [[place(x, y, z, 0) for x in xs for y in ys] for z in zs]
+        groups += [[place(x, y, z, 1) for x in xs for z in zs] for y in ys]
+    else:
+        groups = [[place(x, y, z, 0) for z in zs] for x in xs for y in ys]
+        groups += [[place(x, y, z, 1) for y in ys] for x in xs for z in zs]
+    return lax.all_to_all(blocks, ("gx", "gz", "gc"), 0, 0, axis_index_groups=groups)
 
 
 def call(kernel, outs, scratch, operands, spaces=(), flops=10**6):
@@ -432,7 +450,6 @@
         ],
         [],
         [edges[0], encoder_weight, lower_t, decoder_weight, lift_weight],
-        spaces={0: pltpu.HBM},
         flops=2 * 10**9,
     )
     half = (size_x, 2560 // size_x, 128)
@@ -459,14 +476,12 @@
         spaces={8: pltpu.SMEM, 9: pltpu.SMEM},
     )
     (sums,) = call(add_kernel, [(half, LINK)], [], [keep, partner(send)])
-    sums = lax.all_to_all(sums, "gx", 0, 0)
+    sums, edge = lax.optimization_barrier((sums, edge))
+    sums = exchanged(sums, True)
+    halo = swapped(edge, edge, GX)
     (sums,) = call(sum_kernel, [((size_z,) + half[1:], LINK)], [], [sums])
-    sums, edge = lax.optimization_barrier((sums, edge))
-    sums = lax.all_to_all(sums, "gz", 0, 0)
-    halo = swapped(edge, edge, GX)
-    (sums,) = call(sum_kernel, [(half, LINK)], [], [sums])
     sums, halo = lax.optimization_barrier((sums, halo))
-    sums = lax.all_to_all(sums, "gx", 0, 0)
+    sums = exchanged(sums, False)
     eg, *edges = call(
         encoder_grad_kernel,
         [(tall, BF16)] + [((160, 128), BF16)] * 2,
@@ -474,20 +489,22 @@
         [lg, *halo, low_bwd, slope, jg],
     )
     eg_halo = swapped(*edges, GX)
+    (sums,) = call(sum_kernel, [(half, LINK)], [], [sums])
+    sums, eg_halo = lax.optimization_barrier((sums, eg_halo))
+    sums = exchanged(sums, True)
     (decoded,) = call(
         decode_kernel,
         [(brick, BF16)],
         [((4, 10, 32, 128), BF16), ((320, 64), F32)],
         [encoded, lifted, *halo, lift, dec_fwd],
     )
-    sums, eg_halo, decoded = lax.optimization_barrier((sums, eg_halo, decoded))
     (input_grad,) = call(
         input_grad_kernel,
         [(brick, BF16)],
         [((4, 10, 32, 64), BF16)],
         [eg, *eg_halo, enc_bwd],
-        flops=2 * 10**9,
-    )
+    )
+    sums, decoded, input_grad = lax.optimization_barrier((sums, decoded, input_grad))
     encoder_gradient, decoder_gradient, lower_gradient, lift_gradient = call(
         widen_kernel,
         [((27, 64, 64), F32), ((27, 64, 128), F32), ((27, 64, 128), F32), ((8, 64, 128), F32)],

time: 130 us -> 122 us (0.938)
  blocking collectives: 24.7 us -> 0 us
  waiting for transfers between devices: 21.9 us -> 34.8 us
  Pallas kernels: 16.2 us -> 18 us
    all_to_all x1 -> x0, blocking collectives: 24.7 us -> none  [per_device(): sums = lax.all_to_all(sums, 'gx', 0, 0)]
    all_to_all x2 -> x3, waiting for transfers between devices: 0.82 us -> 21.7 us  [exchanged(): lax.all_to_all(blocks, ('gx', 'gz', 'gc'), 0, 0, axis_index_groups=groups)]
    ppermute x10, waiting for transfers between devices: 18.6 us -> 9.37 us  [shifted(): return lax.ppermute(piece, axes, pairs)]
    all_to_all x2 -> x3, starting transfers between devices: 18.7 us -> 23.4 us  [exchanged(): lax.all_to_all(blocks, ('gx', 'gz', 'gc'), 0, 0, axis_index_groups=groups)]
    ppermute x10, starting transfers between devices: 32.2 us -> 29.7 us  [shifted(): return lax.ppermute(piece, axes, pairs)]
    pallas_call x11, Pallas kernels: 16.2 us -> 18 us  [call(): pl.pallas_call(kernel, out_shape=[jax.ShapeDtypeStruct(s, d) for s, d in...]
    ppermute x2, starting transfers between devices: 11 us -> 9.45 us  [partner(): return lax.ppermute(piece, 'gc', [(0, 1), (1, 0)])]
    unnamed x24 -> x28, local copies, waits for them, and re-layouts: 3.87 us -> 4.58 us
  transfers between devices with their start and end apart: 14 -> 15, of which waited for: 9 -> 7; matrix products, arithmetic and copies ran while one was open for 0% -> 0% of each run, Pallas kernels for 3% -> 5%
where the time goes in v9:
time: 122 us; the launch traced here: 121 us
  starting transfers between devices  62.6 us (51%)
  waiting for transfers between devices  34.8 us (29%)
  Pallas kernels  18 us (15%)
  local copies, waits for them, and re-layouts  4.58 us (4%)
    ppermute x10, starting transfers between devices, shifted(): return lax.ppermute(piece, axes, pairs)  29.7 us
    all_to_all x3, starting transfers between devices, exchanged(): lax.all_to_all(blocks, ('gx', 'gz', 'gc'), 0, 0, axis_index_groups=groups)  23.4 us
    all_to_all x3, waiting for transfers between devices, exchanged(): lax.all_to_all(blocks, ('gx', 'gz', 'gc'), 0, 0, axis_index_groups=groups)  21.7 us
    pallas_call x11, Pallas kernels, call(): pl.pallas_call(kernel, out_shape=[jax.ShapeDtypeStruct(s, d) for s, d in...  18 us
    ppermute x2, starting transfers between devices, partner(): return lax.ppermute(piece, 'gc', [(0, 1), (1, 0)])  9.45 us
    ppermute x10, waiting for transfers between devices, shifted(): return lax.ppermute(piece, axes, pairs)  9.37 us
    unnamed x28, local copies, waits for them, and re-layouts  4.58 us
    ppermute x2, waiting for transfers between devices, partner(): return lax.ppermute(piece, 'gc', [(0, 1), (1, 0)])  3.77 us
  transfers between devices with their start and end apart: 15, of which 7 were waited for; matrix products, arithmetic and copies ran while one was open for 0% of the time, Pallas kernels for 5%

profile of v9, /device:TPU:1, one launch (start us, length us, event | category | flops | bytes accessed | tf_op | source)
XLA Modules:
  0.0 120.9 jit_solution(9182048078941703438)
XLA Ops:
  0.6 0.9 copy-done.6
  1.5 0.9 copy-done.7
  2.4 0.1 shard_map.109
  2.6 4.0 %collective-permute-start = (bf16[12,32,128]{2,1,0:T(8,128)(2,1)S(1)}, bf16[12,32,128]{2,1,0:T(8,128)(2,1)S(1)}, u32[]{:S(2)}, u32[]{:S(2)}) collective-permute-start(bf16[12,32,128]{2,1,0:T(8,128)(2,1)S(1)} %get-tuple-element.49), channel_id=1, source_target_pairs={{0,16},{16,32},{32,48},{48,64},{64,80},{80,96},{96,112},{112,128},... | collective-permute-start | bytes 294920 | tf_op jit(solution)/shard_map/ppermute | solution.py:19
  6.6 1.3 %collective-permute-start.1 = (bf16[12,32,128]{2,1,0:T(8,128)(2,1)S(1)}, bf16[12,32,128]{2,1,0:T(8,128)(2,1)S(1)}, u32[]{:S(2)}, u32[]{:S(2)}) collective-permute-start(bf16[12,32,128]{2,1,0:T(8,128)(2,1)S(1)} %get-tuple-element.50), channel_id=1, source_target_pairs={{16,0},{32,16},{48,32},{64,48},{80,64},{96,80},{112,96},{128,112},... | collective-permute-start | bytes 294920 | tf_op jit(solution)/shard_map/ppermute | solution.py:19
  7.9 5.0 %collective-permute-start.2 = (bf16[4,32,128]{2,1,0:T(8,128)(2,1)S(1)}, bf16[4,32,128]{2,1,0:T(8,128)(2,1)S(1)}, u32[]{:S(2)}, u32[]{:S(2)}) collective-permute-start(bf16[4,32,128]{2,1,0:T(8,128)(2,1)S(1)} %get-tuple-element.51), channel_id=1, source_target_pairs={{0,32},{16,48},{32,64},{48,80},{64,96},{80,112},{96,128},{112,144}... | collective-permute-start | bytes 98312 | tf_op jit(solution)/shard_map/ppermute | solution.py:19
  12.9 1.3 %collective-permute-start.3 = (bf16[4,32,128]{2,1,0:T(8,128)(2,1)S(1)}, bf16[4,32,128]{2,1,0:T(8,128)(2,1)S(1)}, u32[]{:S(2)}, u32[]{:S(2)}) collective-permute-start(bf16[4,32,128]{2,1,0:T(8,128)(2,1)S(1)} %get-tuple-element.52), channel_id=1, source_target_pairs={{32,0},{48,16},{64,32},{80,48},{96,64},{112,80},{128,96},{144,112}... | collective-permute-start | bytes 98312 | tf_op jit(solution)/shard_map/ppermute | solution.py:19
  14.2 0.0 collective-permute-done.2.xlo2.refs_4_
  14.2 6.7 %collective-permute-done.3.xhi2.refs_5_ = bf16[4,32,128]{2,1,0:T(8,128)(2,1)S(1)} collective-permute-done((bf16[4,32,128]{2,1,0:T(8,128)(2,1)S(1)}, bf16[4,32,128]{2,1,0:T(8,128)(2,1)S(1)}, u32[]{:S(2)}, u32[]{:S(2)}) %collective-permute-start.3) | collective-permute-done | bytes 32800 | tf_op jit(solution)/shard_map/ppermute | solution.py:19
  20.9 0.0 collective-permute-done.xlo.refs_2_
  20.9 0.0 collective-permute-done.1.xhi.refs_3_
  20.9 1.2 %shard_map.110 = (bf16[6,7,32,128]{3,2,1,0:T(8,128)(2,1)}, bf16[6,7,32,128]{3,2,1,0:T(8,128)(2,1)}) custom-call(bf16[2,8,32,64]{3,2,1,0:T(8,128)(2,1)S(1)} %get-tuple-element.47.f_ref, bf16[2,8,32,64]{3,2,1,0:T(8,128)(2,1)S(1)} %get-tuple-element.48.c_ref, bf16[12,32,128]{2,1,0:T(8,128)(2,1)S(1)} %collective-permute-done.xlo.refs_2_, ...), custom_call_target="tpu_custom_call" | custom-call | flops 1000000 | bytes 10000 | tf_op jit(solution)/shard_map/pallas_call | solution.py:49
  22.1 6.3 %collective-permute-start.4 = (bf16[6,7,32,128]{3,2,1,0:T(8,128)(2,1)}, bf16[6,7,32,128]{3,2,1,0:T(8,128)(2,1)S(1)}, u32[]{:S(2)}, u32[]{:S(2)}) collective-permute-start(bf16[6,7,32,128]{3,2,1,0:T(8,128)(2,1)} %get-tuple-element.53), channel_id=1, source_target_pairs={{0,1},{1,2},{2,3},{3,4},{4,5},{5,6},{6,7},{7,8},{8,9},{9,10},{10,1... | collective-permute-start | bytes 1032200 | tf_op jit(solution)/shard_map/ppermute | solution.py:19
  28.4 1.9 %collective-permute-start.5 = (bf16[6,7,32,128]{3,2,1,0:T(8,128)(2,1)}, bf16[6,7,32,128]{3,2,1,0:T(8,128)(2,1)S(1)}, u32[]{:S(2)}, u32[]{:S(2)}) collective-permute-start(bf16[6,7,32,128]{3,2,1,0:T(8,128)(2,1)} %get-tuple-element.54.first_ref), channel_id=1, source_target_pairs={{1,0},{2,1},{3,2},{4,3},{5,4},{6,5},{7,6},{8,7},{9,8},{10,9},{11,1... | collective-permute-start | bytes 1032200 | tf_op jit(solution)/shard_map/ppermute | solution.py:19
  30.3 0.1 add_convert_fusion.refs_6_
  30.4 1.0 copy-done.9
  31.4 1.0 copy-done.10
  32.5 1.3 %shard_map.111 = (bf16[192,576]{1,0:T(8,128)(2,1)S(1)}, bf16[576,192]{1,0:T(8,128)(2,1)S(1)}, bf16[576,384]{1,0:T(8,128)(2,1)S(1)}, bf16[192,1152]{1,0:T(8,128)(...) custom-call(bf16[6,7,32,128]{3,2,1,0:T(8,128)(2,1)} %get-tuple-element.54.fir, ...), custom_call_target="tpu_custom_call" | custom-call | flops 2000000000 | bytes 10000 | tf_op jit(solution)/shard_map/pallas_call | solution.py:49
  33.8 0.0 copy-start.2
  33.8 0.7 copy-done.2
  34.5 0.0 collective-permute-done.4.refs_0_
  34.5 2.7 %collective-permute-done.5.refs_1_ = bf16[6,7,32,128]{3,2,1,0:T(8,128)(2,1)S(1)} collective-permute-done((bf16[6,7,32,128]{3,2,1,0:T(8,128)(2,1)}, bf16[6,7,32,128]{3,2,1,0:T(8,128)(2,1)S(1)}, u32[]{:S(2)}, u32[]{:S(2)}) %collective-permute-start.5) | collective-permute-done | bytes 344096 | tf_op jit(solution)/shard_map/ppermute | solution.py:19
  37.2 7.8 %shard_map.112 = (bf16[4,10,32,64]{3,2,1,0:T(8,128)(2,1)S(1)}, f32[6,320,64]{2,1,0:T(8,128)S(1)}, bf16[2,320,64]{2,1,0:T(8,128)(2,1)S(1)}, bf16[128,128]{1,0:T(8...) custom-call(bf16[2,8,32,64]{3,2,1,0:T(8,128)(2,1)S(1)} %get-tuple-el, ...), custom_call_target="tpu_custom_call" | custom-call | flops 1000000 | bytes 10000 | tf_op jit(solution)/shard_map/pallas_call | solution.py:49
  45.0 0.0 copy-start
  45.0 0.0 copy-start.4
  45.0 0.0 copy-start.12
  45.0 1.9 %collective-permute-start.6 = (bf16[32,80,128]{2,1,0:T(8,128)(2,1)S(1)}, bf16[32,80,128]{2,1,0:T(8,128)(2,1)S(1)}, u32[]{:S(2)}, u32[]{:S(2)}) collective-permute-start(bf16[32,80,128]{2,1,0:T(8,128)(2,1)S(1)} %get-tuple-element.61), channel_id=1, source_target_pairs={{0,1},{1,0},{2,3},{3,2},{4,5},{5,4},{6,7},{7,6},{8,9},{9,8},{10,11... | collective-permute-start | bytes 1966088 | tf_op jit(solution)/shard_map/ppermute | solution.py:27
  46.9 2.1 %collective-permute-done.6.b_ref = bf16[32,80,128]{2,1,0:T(8,128)(2,1)S(1)} collective-permute-done((bf16[32,80,128]{2,1,0:T(8,128)(2,1)S(1)}, bf16[32,80,128]{2,1,0:T(8,128)(2,1)S(1)}, u32[]{:S(2)}, u32[]{:S(2)}) %collective-permute-start.6) | collective-permute-done | bytes 655392 | tf_op jit(solution)/shard_map/ppermute | solution.py:27
  49.0 1.0 shard_map.113
  50.0 12.4 %all-to-all-start = ((bf16[32,80,128]{2,1,0:T(8,128)(2,1)}), bf16[32,80,128]{2,1,0:T(8,128)(2,1)S(1)}, u32[]{:S(2)}, u32[]{:S(2)}) async-start(bf16[32,80,128]{2,1,0:T(8,128)(2,1)} %shard_map.113), calls=%async_computation | async-start | bytes 1310720 | tf_op jit(solution)/shard_map/all_to_all | solution.py:45
  62.4 1.3 %collective-permute-start.8 = (bf16[224,128]{1,0:T(8,128)(2,1)S(1)}, bf16[224,128]{1,0:T(8,128)(2,1)S(1)}, u32[]{:S(2)}, u32[]{:S(2)}) collective-permute-start(bf16[224,128]{1,0:T(8,128)(2,1)S(1)} %copy-done.13), channel_id=1, source_target_pairs={{16,0},{32,16},{48,32},{64,48},{80,64},{96,80},{112,96},{128,112},... | collective-permute-start | bytes 172040 | tf_op jit(solution)/shard_map/ppermute | solution.py:19
  63.7 4.0 %collective-permute-start.7 = (bf16[224,128]{1,0:T(8,128)(2,1)S(1)}, bf16[224,128]{1,0:T(8,128)(2,1)S(1)}, u32[]{:S(2)}, u32[]{:S(2)}) collective-permute-start(bf16[224,128]{1,0:T(8,128)(2,1)S(1)} %copy-done.13), channel_id=1, source_target_pairs={{0,16},{16,32},{32,48},{48,64},{64,80},{80,96},{96,112},{112,128},... | collective-permute-start | bytes 172040 | tf_op jit(solution)/shard_map/ppermute | solution.py:19
  67.7 8.0 %all-to-all-done.parts_ref = bf16[32,80,128]{2,1,0:T(8,128)(2,1)S(1)} async-done(((bf16[32,80,128]{2,1,0:T(8,128)(2,1)}), bf16[32,80,128]{2,1,0:T(8,128)(2,1)S(1)}, u32[]{:S(2)}, u32[]{:S(2)}) %all-to-all-start) | async-done | bytes 655392 | tf_op jit(solution)/shard_map/all_to_all | solution.py:45
  75.7 0.8 shard_map.114
  76.5 5.4 %all-to-all-start.1 = ((bf16[8,80,128]{2,1,0:T(8,128)(2,1)}), bf16[8,80,128]{2,1,0:T(8,128)(2,1)S(1)}, u32[]{:S(2)}, u32[]{:S(2)}) async-start(bf16[8,80,128]{2,1,0:T(8,128)(2,1)} %shard_map.114), calls=%async_computation.1 | async-start | bytes 327680 | tf_op jit(solution)/shard_map/all_to_all | solution.py:45
  81.9 0.5 shard_map.116
  82.4 3.4 %collective-permute-start.9 = (bf16[160,128]{1,0:T(8,128)(2,1)S(1)}, bf16[160,128]{1,0:T(8,128)(2,1)S(1)}, u32[]{:S(2)}, u32[]{:S(2)}) collective-permute-start(bf16[160,128]{1,0:T(8,128)(2,1)S(1)} %get-tuple-element.71), channel_id=1, source_target_pairs={{0,16},{16,32},{32,48},{48,64},{64,80},{80,96},{96,112},{112,128},... | collective-permute-start | bytes 122888 | tf_op jit(solution)/shard_map/ppermute | solution.py:19
  85.7 1.3 %collective-permute-start.10 = (bf16[160,128]{1,0:T(8,128)(2,1)S(1)}, bf16[160,128]{1,0:T(8,128)(2,1)S(1)}, u32[]{:S(2)}, u32[]{:S(2)}) collective-permute-start(bf16[160,128]{1,0:T(8,128)(2,1)S(1)} %get-tuple-element.72), channel_id=1, source_target_pairs={{16,0},{32,16},{48,32},{64,48},{80,64},{96,80},{112,96},{128,112},... | collective-permute-start | bytes 122888 | tf_op jit(solution)/shard_map/ppermute | solution.py:19
  87.0 3.1 %all-to-all-done.1.parts_ref = bf16[8,80,128]{2,1,0:T(8,128)(2,1)S(1)} async-done(((bf16[8,80,128]{2,1,0:T(8,128)(2,1)}), bf16[8,80,128]{2,1,0:T(8,128)(2,1)S(1)}, u32[]{:S(2)}, u32[]{:S(2)}) %all-to-all-start.1) | async-done | bytes 163872 | tf_op jit(solution)/shard_map/all_to_all | solution.py:45
  90.2 0.9 shard_map.115
  91.1 5.6 %all-to-all-start.2 = ((bf16[32,80,128]{2,1,0:T(8,128)(2,1)}), bf16[32,80,128]{2,1,0:T(8,128)(2,1)S(1)}, u32[]{:S(2)}, u32[]{:S(2)}) async-start(bf16[32,80,128]{2,1,0:T(8,128)(2,1)} %shard_map.115), calls=%async_computation.2 | async-start | bytes 1310720 | tf_op jit(solution)/shard_map/all_to_all | solution.py:45
  96.7 0.0 copy-start.3
  96.7 1.5 %shard_map.117 = bf16[2,8,32,64]{3,2,1,0:T(8,128)(2,1)} custom-call(bf16[4,10,32,64]{3,2,1,0:T(8,128)(2,1)S(1)} %copy-done.1, bf16[2,10,32,64]{3,2,1,0:T(8,128)(2,1)S(1)} %get-tuple-element.75.lifted_ref, bf16[224,128]{1,0:T(8,128)(2,1)S(1)} %collective-permute-done.7.xlo, bf16[224,128]{1,0:T(8,128)(2,1)S(1)} %collective-permute-done.8.xhi, ...), custom_call_target="tpu_custom_call" | custom-call | flops 1000000 | bytes 10000 | tf_op jit(solution)/shard_map/pallas_call | solution.py:49
  98.1 1.3 %shard_map.118 = bf16[2,8,32,64]{3,2,1,0:T(8,128)(2,1)} custom-call(bf16[2,10,32,64]{3,2,1,0:T(8,128)(2,1)S(1)} %get-tuple-element.77.eg_ref, bf16[160,128]{1,0:T(8,128)(2,1)S(1)} %collective-permute-done.9.xlo, bf16[160,128]{1,0:T(8,128)(2,1)S(1)} %collective-permute-done.10.xhi, bf16[576,192]{1,0:T(8,128)(2,1)S(1)} %copy-done.3), custom_call_target="tpu_custom_call" | custom-call | flops 1000000 | bytes 10000 | tf_op jit(solution)/shard_map/pallas_call | solution.py:49
  99.4 10.5 %all-to-all-done.2.own_ref = bf16[32,80,128]{2,1,0:T(8,128)(2,1)S(1)} async-done(((bf16[32,80,128]{2,1,0:T(8,128)(2,1)}), bf16[32,80,128]{2,1,0:T(8,128)(2,1)S(1)}, u32[]{:S(2)}, u32[]{:S(2)}) %all-to-all-start.2) | async-done | bytes 655392 | tf_op jit(solution)/shard_map/all_to_all | solution.py:45
  109.9 7.5 %collective-permute-start.11 = (bf16[32,80,128]{2,1,0:T(8,128)(2,1)S(1)}, bf16[32,80,128]{2,1,0:T(8,128)(2,1)S(1)}, u32[]{:S(2)}, u32[]{:S(2)}) collective-permute-start(bf16[32,80,128]{2,1,0:T(8,128)(2,1)S(1)} %all-to-all-done.2.own_ref), channel_id=1, source_target_pairs={{0,1},{1,0},{2,3},{3,2},{4,5},{5,4},{6,7},{7,6},{8,9},{9,8},{10,11... | collective-permute-start | bytes 1966088 | tf_op jit(solution)/shard_map/ppermute | solution.py:27
  117.5 1.7 %collective-permute-done.11.other_ref = bf16[32,80,128]{2,1,0:T(8,128)(2,1)S(1)} collective-permute-done((bf16[32,80,128]{2,1,0:T(8,128)(2,1)S(1)}, bf16[32,80,128]{2,1,0:T(8,128)(2,1)S(1)}, u32[]{:S(2)}, u32[]{:S(2)}) %collective-permute-start.11) | collective-permute-done | bytes 655392 | tf_op jit(solution)/shard_map/ppermute | solution.py:27
  119.2 1.8 %shard_map.119 = (f32[27,64,64]{2,1,0:T(8,128)}, f32[27,64,128]{2,1,0:T(8,128)}, f32[27,64,128]{2,1,0:T(8,128)}, f32[8,64,128]{2,1,0:T(8,128)}) custom-call(s32[1]{0:T(128)} %bitcast.6.refs_7_.core, bf16[32,80,128]{2,1,0:T(8,128)(2,1)S(1)} %all-to-all-done.2.own_ref, bf16[32,80,128]{2,1,0:T(8,128)(2,1)S(1)} %collective-permute-done.11.other_ref), custom_call_target="tpu_custom_call" | custom-call | flops 1000000 | bytes 10000 | tf_op jit(solution)/shard_map/pallas_call | solution.py:49
  (22 shorter events, 0.0 us)
Async XLA Ops:
  0.6 0.9 copy-start.6
  1.5 0.9 copy-start.7
  2.4 28.0 %copy-start.8 = (bf16[27,64,64]{2,1,0:T(8,128)(2,1)S(1)}, bf16[27,64,64]{2,1,0:T(8,128)(2,1)}, u32[]{:S(2)}) copy-start(bf16[27,64,64]{2,1,0:T(8,128)(2,1)} %enc_ref.1) | copy-start | bytes 663556
  2.6 18.3 %collective-permute-start = (bf16[12,32,128]{2,1,0:T(8,128)(2,1)S(1)}, bf16[12,32,128]{2,1,0:T(8,128)(2,1)S(1)}, u32[]{:S(2)}, u32[]{:S(2)}) collective-permute-start(bf16[12,32,128]{2,1,0:T(8,128)(2,1)S(1)} %get-tuple-element.49), channel_id=1, source_target_pairs={{0,16},{16,32},{32,48},{48,64},{64,80},{80,96},{96,112},{112,128},... | collective-permute-start | bytes 294920 | tf_op jit(solution)/shard_map/ppermute | solution.py:19
  6.6 14.3 %collective-permute-start.1 = (bf16[12,32,128]{2,1,0:T(8,128)(2,1)S(1)}, bf16[12,32,128]{2,1,0:T(8,128)(2,1)S(1)}, u32[]{:S(2)}, u32[]{:S(2)}) collective-permute-start(bf16[12,32,128]{2,1,0:T(8,128)(2,1)S(1)} %get-tuple-element.50), channel_id=1, source_target_pairs={{16,0},{32,16},{48,32},{64,48},{80,64},{96,80},{112,96},{128,112},... | collective-permute-start | bytes 294920 | tf_op jit(solution)/shard_map/ppermute | solution.py:19
  7.9 6.3 %collective-permute-start.2 = (bf16[4,32,128]{2,1,0:T(8,128)(2,1)S(1)}, bf16[4,32,128]{2,1,0:T(8,128)(2,1)S(1)}, u32[]{:S(2)}, u32[]{:S(2)}) collective-permute-start(bf16[4,32,128]{2,1,0:T(8,128)(2,1)S(1)} %get-tuple-element.51), channel_id=1, source_target_pairs={{0,32},{16,48},{32,64},{48,80},{64,96},{80,112},{96,128},{112,144}... | collective-permute-start | bytes 98312 | tf_op jit(solution)/shard_map/ppermute | solution.py:19
  12.9 8.0 %collective-permute-start.3 = (bf16[4,32,128]{2,1,0:T(8,128)(2,1)S(1)}, bf16[4,32,128]{2,1,0:T(8,128)(2,1)S(1)}, u32[]{:S(2)}, u32[]{:S(2)}) collective-permute-start(bf16[4,32,128]{2,1,0:T(8,128)(2,1)S(1)} %get-tuple-element.52), channel_id=1, source_target_pairs={{32,0},{48,16},{64,32},{80,48},{96,64},{112,80},{128,96},{144,112}... | collective-permute-start | bytes 98312 | tf_op jit(solution)/shard_map/ppermute | solution.py:19
  20.9 9.5 %copy-start.11 = (bf16[8,64,128]{2,1,0:T(8,128)(2,1)S(1)}, bf16[8,64,128]{2,1,0:T(8,128)(2,1)}, u32[]{:S(2)}) copy-start(bf16[8,64,128]{2,1,0:T(8,128)(2,1)} %lift_ref.1) | copy-start | bytes 393220
  22.1 12.4 %collective-permute-start.4 = (bf16[6,7,32,128]{3,2,1,0:T(8,128)(2,1)}, bf16[6,7,32,128]{3,2,1,0:T(8,128)(2,1)S(1)}, u32[]{:S(2)}, u32[]{:S(2)}) collective-permute-start(bf16[6,7,32,128]{3,2,1,0:T(8,128)(2,1)} %get-tuple-element.53), channel_id=1, source_target_pairs={{0,1},{1,2},{2,3},{3,4},{4,5},{5,6},{6,7},{7,8},{8,9},{9,10},{10,1... | collective-permute-start | bytes 1032200 | tf_op jit(solution)/shard_map/ppermute | solution.py:19
  28.4 8.8 %collective-permute-start.5 = (bf16[6,7,32,128]{3,2,1,0:T(8,128)(2,1)}, bf16[6,7,32,128]{3,2,1,0:T(8,128)(2,1)S(1)}, u32[]{:S(2)}, u32[]{:S(2)}) collective-permute-start(bf16[6,7,32,128]{3,2,1,0:T(8,128)(2,1)} %get-tuple-element.54.first_ref), channel_id=1, source_target_pairs={{1,0},{2,1},{3,2},{4,3},{5,4},{6,5},{7,6},{8,7},{9,8},{10,9},{11,1... | collective-permute-start | bytes 1032200 | tf_op jit(solution)/shard_map/ppermute | solution.py:19
  30.4 1.0 copy-start.9
  31.4 1.0 copy-start.10
  33.8 0.7 copy-start.2
  45.0 5.0 %copy-start = (bf16[4,10,32,64]{3,2,1,0:T(8,128)(2,1)}, bf16[4,10,32,64]{3,2,1,0:T(8,128)(2,1)S(1)}, u32[]{:S(2)}) copy-start(bf16[4,10,32,64]{3,2,1,0:T(8,128)(2,1)S(1)} %get-tuple-element.74.enc_ref) | copy-start | bytes 491524
  45.0 5.0 %copy-start.4 = (bf16[2,320,64]{2,1,0:T(8,128)(2,1)}, bf16[2,320,64]{2,1,0:T(8,128)(2,1)S(1)}, u32[]{:S(2)}) copy-start(bf16[2,320,64]{2,1,0:T(8,128)(2,1)S(1)} %get-tuple-element.70.jg_ref) | copy-start | bytes 245764
  45.0 5.0 %copy-start.12 = (bf16[224,128]{1,0:T(8,128)(2,1)}, bf16[224,128]{1,0:T(8,128)(2,1)S(1)}, u32[]{:S(2)}) copy-start(bf16[224,128]{1,0:T(8,128)(2,1)S(1)} %get-tuple-element.64) | copy-start | bytes 172036
  45.0 4.0 %collective-permute-start.6 = (bf16[32,80,128]{2,1,0:T(8,128)(2,1)S(1)}, bf16[32,80,128]{2,1,0:T(8,128)(2,1)S(1)}, u32[]{:S(2)}, u32[]{:S(2)}) collective-permute-start(bf16[32,80,128]{2,1,0:T(8,128)(2,1)S(1)} %get-tuple-element.61), channel_id=1, source_target_pairs={{0,1},{1,0},{2,3},{3,2},{4,5},{5,4},{6,7},{7,6},{8,9},{9,8},{10,11... | collective-permute-start | bytes 1966088 | tf_op jit(solution)/shard_map/ppermute | solution.py:27
  50.0 12.4 %copy-start.13 = (bf16[224,128]{1,0:T(8,128)(2,1)S(1)}, bf16[224,128]{1,0:T(8,128)(2,1)}, u32[]{:S(2)}) copy-start(bf16[224,128]{1,0:T(8,128)(2,1)} %copy-done.12) | copy-start | bytes 172036
  50.0 25.7 %all-to-all-start = ((bf16[32,80,128]{2,1,0:T(8,128)(2,1)}), bf16[32,80,128]{2,1,0:T(8,128)(2,1)S(1)}, u32[]{:S(2)}, u32[]{:S(2)}) async-start(bf16[32,80,128]{2,1,0:T(8,128)(2,1)} %shard_map.113), calls=%async_computation | async-start | bytes 1310720 | tf_op jit(solution)/shard_map/all_to_all | solution.py:45
  62.4 14.0 %collective-permute-start.8 = (bf16[224,128]{1,0:T(8,128)(2,1)S(1)}, bf16[224,128]{1,0:T(8,128)(2,1)S(1)}, u32[]{:S(2)}, u32[]{:S(2)}) collective-permute-start(bf16[224,128]{1,0:T(8,128)(2,1)S(1)} %copy-done.13), channel_id=1, source_target_pairs={{16,0},{32,16},{48,32},{64,48},{80,64},{96,80},{112,96},{128,112},... | collective-permute-start | bytes 172040 | tf_op jit(solution)/shard_map/ppermute | solution.py:19
  63.7 12.8 %collective-permute-start.7 = (bf16[224,128]{1,0:T(8,128)(2,1)S(1)}, bf16[224,128]{1,0:T(8,128)(2,1)S(1)}, u32[]{:S(2)}, u32[]{:S(2)}) collective-permute-start(bf16[224,128]{1,0:T(8,128)(2,1)S(1)} %copy-done.13), channel_id=1, source_target_pairs={{0,16},{16,32},{32,48},{48,64},{64,80},{80,96},{96,112},{112,128},... | collective-permute-start | bytes 172040 | tf_op jit(solution)/shard_map/ppermute | solution.py:19
  76.5 5.4 %copy-start.5 = (bf16[2,320,64]{2,1,0:T(8,128)(2,1)S(1)}, bf16[2,320,64]{2,1,0:T(8,128)(2,1)}, u32[]{:S(2)}) copy-start(bf16[2,320,64]{2,1,0:T(8,128)(2,1)} %copy-done.4) | copy-start | bytes 245764
  76.5 13.7 %all-to-all-start.1 = ((bf16[8,80,128]{2,1,0:T(8,128)(2,1)}), bf16[8,80,128]{2,1,0:T(8,128)(2,1)S(1)}, u32[]{:S(2)}, u32[]{:S(2)}) async-start(bf16[8,80,128]{2,1,0:T(8,128)(2,1)} %shard_map.114), calls=%async_computation.1 | async-start | bytes 327680 | tf_op jit(solution)/shard_map/all_to_all | solution.py:45
  82.4 8.7 %collective-permute-start.9 = (bf16[160,128]{1,0:T(8,128)(2,1)S(1)}, bf16[160,128]{1,0:T(8,128)(2,1)S(1)}, u32[]{:S(2)}, u32[]{:S(2)}) collective-permute-start(bf16[160,128]{1,0:T(8,128)(2,1)S(1)} %get-tuple-element.71), channel_id=1, source_target_pairs={{0,16},{16,32},{32,48},{48,64},{64,80},{80,96},{96,112},{112,128},... | collective-permute-start | bytes 122888 | tf_op jit(solution)/shard_map/ppermute | solution.py:19
  85.7 5.3 %collective-permute-start.10 = (bf16[160,128]{1,0:T(8,128)(2,1)S(1)}, bf16[160,128]{1,0:T(8,128)(2,1)S(1)}, u32[]{:S(2)}, u32[]{:S(2)}) collective-permute-start(bf16[160,128]{1,0:T(8,128)(2,1)S(1)} %get-tuple-element.72), channel_id=1, source_target_pairs={{16,0},{32,16},{48,32},{64,48},{80,64},{96,80},{112,96},{128,112},... | collective-permute-start | bytes 122888 | tf_op jit(solution)/shard_map/ppermute | solution.py:19
  91.1 5.6 %copy-start.1 = (bf16[4,10,32,64]{3,2,1,0:T(8,128)(2,1)S(1)}, bf16[4,10,32,64]{3,2,1,0:T(8,128)(2,1)}, u32[]{:S(2)}) copy-start(bf16[4,10,32,64]{3,2,1,0:T(8,128)(2,1)} %copy-done) | copy-start | bytes 491524
  91.1 18.9 %all-to-all-start.2 = ((bf16[32,80,128]{2,1,0:T(8,128)(2,1)}), bf16[32,80,128]{2,1,0:T(8,128)(2,1)S(1)}, u32[]{:S(2)}, u32[]{:S(2)}) async-start(bf16[32,80,128]{2,1,0:T(8,128)(2,1)} %shard_map.115), calls=%async_computation.2 | async-start | bytes 1310720 | tf_op jit(solution)/shard_map/all_to_all | solution.py:45
  96.7 1.5 %copy-start.3 = (bf16[576,192]{1,0:T(8,128)(2,1)S(1)}, bf16[576,192]{1,0:T(8,128)(2,1)}, u32[]{:S(2)}) copy-start(bf16[576,192]{1,0:T(8,128)(2,1)} %copy-done.2) | copy-start | bytes 663556
  109.9 9.2 %collective-permute-start.11 = (bf16[32,80,128]{2,1,0:T(8,128)(2,1)S(1)}, bf16[32,80,128]{2,1,0:T(8,128)(2,1)S(1)}, u32[]{:S(2)}, u32[]{:S(2)}) collective-permute-start(bf16[32,80,128]{2,1,0:T(8,128)(2,1)S(1)} %all-to-all-done.2.own_ref), channel_id=1, source_target_pairs={{0,1},{1,0},{2,3},{3,2},{4,5},{5,4},{6,7},{7,6},{8,9},{9,8},{10,11... | collective-permute-start | bytes 1966088 | tf_op jit(solution)/shard_map/ppermute | solution.py:27

commit v10 on v6

--- a/solution.py
+++ b/solution.py
@@ -25,6 +25,24 @@
 
 def partner(piece):
     return lax.ppermute(piece, "gc", [(0, 1), (1, 0)])
+
+
+def exchanged(blocks, wide):
+    size_x, size_z = lax.axis_size("gx"), lax.axis_size("gz")
+    size_y = size_z
+    assert size_x % size_y == 0
+
+    def place(x, y, z, core):
+        return ((x * size_y + y) * size_z + z) * 2 + core
+
+    xs, ys, zs = range(size_x // size_y), range(size_y), range(size_z)
+    if wide:
+        groups = [[place(x, y, z, 0) for x in xs for y in ys] for z in zs]
+        groups += [[place(x, y, z, 1) for x in xs for z in zs] for y in ys]
+    else:
+        groups = [[place(x, y, z, 0) for z in zs] for x in xs for y in ys]
+        groups += [[place(x, y, z, 1) for y in ys] for x in xs for z in zs]
+    return lax.all_to_all(blocks, ("gx", "gz", "gc"), 0, 0, axis_index_groups=groups)
 
 
 def call(kernel, outs, scratch, operands, spaces=(), flops=10**6):
@@ -460,11 +478,11 @@
     )
     (sums,) = call(add_kernel, [(half, LINK)], [], [keep, partner(send)])
     sums, edge = lax.optimization_barrier((sums, edge))
-    sums = lax.all_to_all(sums, "gx", 0, 0)
+    sums = exchanged(sums, True)
     halo = swapped(edge, edge, GX)
     (sums,) = call(sum_kernel, [((size_z,) + half[1:], LINK)], [], [sums])
     sums, halo = lax.optimization_barrier((sums, halo))
-    sums = lax.all_to_all(sums, "gz", 0, 0)
+    sums = exchanged(sums, False)
     eg, *edges = call(
         encoder_grad_kernel,
         [(tall, BF16)] + [((160, 128), BF16)] * 2,
@@ -474,7 +492,7 @@
     eg_halo = swapped(*edges, GX)
     (sums,) = call(sum_kernel, [(half, LINK)], [], [sums])
     sums, eg_halo = lax.optimization_barrier((sums, eg_halo))
-    sums = lax.all_to_all(sums, "gx", 0, 0)
+    sums = exchanged(sums, True)
     (decoded,) = call(
         decode_kernel,
         [(brick, BF16)],

time: 129 us -> 121 us (0.938)
  starting transfers between devices: 66.7 us -> 62.5 us
  waiting for transfers between devices: 38.1 us -> 34.3 us
    ppermute x10, starting transfers between devices: 32.6 us -> 29.9 us  [shifted(): return lax.ppermute(piece, axes, pairs)]
    ppermute x10, waiting for transfers between devices: 11.5 us -> 8.96 us  [shifted(): return lax.ppermute(piece, axes, pairs)]
    ppermute x2, starting transfers between devices: 10.9 us -> 9.51 us  [partner(): return lax.ppermute(piece, 'gc', [(0, 1), (1, 0)])]
  transfers between devices with their start and end apart: 15 -> 15, of which waited for: 8 -> 7; matrix products, arithmetic and copies ran while one was open for 0% -> 0% of each run, Pallas kernels for 4% -> 4%
where the time goes in v10:
time: 121 us; the launch traced here: 120 us
  starting transfers between devices  62.5 us (52%)
  waiting for transfers between devices  34.3 us (28%)
  Pallas kernels  16.9 us (14%)
  local copies, waits for them, and re-layouts  5.76 us (5%)
    ppermute x10, starting transfers between devices, shifted(): return lax.ppermute(piece, axes, pairs)  29.9 us
    all_to_all x3, starting transfers between devices, exchanged(): lax.all_to_all(blocks, ('gx', 'gz', 'gc'), 0, 0, axis_index_groups=groups)  23.1 us
    all_to_all x3, waiting for transfers between devices, exchanged(): lax.all_to_all(blocks, ('gx', 'gz', 'gc'), 0, 0, axis_index_groups=groups)  21.6 us
    pallas_call x14, Pallas kernels, call(): pl.pallas_call(kernel, out_shape=[jax.ShapeDtypeStruct(s, d) for s, d in...  16.9 us
    ppermute x2, starting transfers between devices, partner(): return lax.ppermute(piece, 'gc', [(0, 1), (1, 0)])  9.51 us
    ppermute x10, waiting for transfers between devices, shifted(): return lax.ppermute(piece, axes, pairs)  8.96 us
    unnamed x16, local copies, waits for them, and re-layouts  5.76 us
    ppermute x2, waiting for transfers between devices, partner(): return lax.ppermute(piece, 'gc', [(0, 1), (1, 0)])  3.77 us
  transfers between devices with their start and end apart: 15, of which 7 were waited for; matrix products, arithmetic and copies ran while one was open for 0% of the time, Pallas kernels for 4%

profile of v10, /device:TPU:1, one launch (start us, length us, event | category | flops | bytes accessed | tf_op | source)
XLA Modules:
  0.0 120.4 jit_solution(10878397612992987232)
XLA Ops:
  0.6 0.9 copy-done.2
  1.5 0.9 copy-done.3
  2.4 0.1 shard_map.109
  2.6 4.0 %collective-permute-start = (bf16[12,32,128]{2,1,0:T(8,128)(2,1)S(1)}, bf16[12,32,128]{2,1,0:T(8,128)(2,1)S(1)}, u32[]{:S(2)}, u32[]{:S(2)}) collective-permute-start(bf16[12,32,128]{2,1,0:T(8,128)(2,1)S(1)} %get-tuple-element.55), channel_id=1, source_target_pairs={{0,16},{16,32},{32,48},{48,64},{64,80},{80,96},{96,112},{112,128},... | collective-permute-start | bytes 294920 | tf_op jit(solution)/shard_map/ppermute | solution.py:19
  6.6 1.3 %collective-permute-start.1 = (bf16[12,32,128]{2,1,0:T(8,128)(2,1)S(1)}, bf16[12,32,128]{2,1,0:T(8,128)(2,1)S(1)}, u32[]{:S(2)}, u32[]{:S(2)}) collective-permute-start(bf16[12,32,128]{2,1,0:T(8,128)(2,1)S(1)} %get-tuple-element.56), channel_id=1, source_target_pairs={{16,0},{32,16},{48,32},{64,48},{80,64},{96,80},{112,96},{128,112},... | collective-permute-start | bytes 294920 | tf_op jit(solution)/shard_map/ppermute | solution.py:19
  7.9 5.0 %collective-permute-start.2 = (bf16[4,32,128]{2,1,0:T(8,128)(2,1)S(1)}, bf16[4,32,128]{2,1,0:T(8,128)(2,1)S(1)}, u32[]{:S(2)}, u32[]{:S(2)}) collective-permute-start(bf16[4,32,128]{2,1,0:T(8,128)(2,1)S(1)} %get-tuple-element.57), channel_id=1, source_target_pairs={{0,32},{16,48},{32,64},{48,80},{64,96},{80,112},{96,128},{112,144}... | collective-permute-start | bytes 98312 | tf_op jit(solution)/shard_map/ppermute | solution.py:19
  12.9 1.3 %collective-permute-start.3 = (bf16[4,32,128]{2,1,0:T(8,128)(2,1)S(1)}, bf16[4,32,128]{2,1,0:T(8,128)(2,1)S(1)}, u32[]{:S(2)}, u32[]{:S(2)}) collective-permute-start(bf16[4,32,128]{2,1,0:T(8,128)(2,1)S(1)} %get-tuple-element.58), channel_id=1, source_target_pairs={{32,0},{48,16},{64,32},{80,48},{96,64},{112,80},{128,96},{144,112}... | collective-permute-start | bytes 98312 | tf_op jit(solution)/shard_map/ppermute | solution.py:19
  14.2 6.7 %collective-permute-done.3.xhi2 = bf16[4,32,128]{2,1,0:T(8,128)(2,1)S(1)} collective-permute-done((bf16[4,32,128]{2,1,0:T(8,128)(2,1)S(1)}, bf16[4,32,128]{2,1,0:T(8,128)(2,1)S(1)}, u32[]{:S(2)}, u32[]{:S(2)}) %collective-permute-start.3) | collective-permute-done | bytes 32800 | tf_op jit(solution)/shard_map/ppermute | solution.py:19
  20.9 0.0 collective-permute-done.xlo.refs_2_
  20.9 0.4 shard_map.110
  21.3 6.3 %collective-permute-start.4 = (bf16[6,7,32,128]{3,2,1,0:T(8,128)(2,1)S(1)}, bf16[6,7,32,128]{3,2,1,0:T(8,128)(2,1)S(1)}, u32[]{:S(2)}, u32[]{:S(2)}) collective-permute-start(bf16[6,7,32,128]{3,2,1,0:T(8,128)(2,1)S(1)} %get-tuple-element.59), channel_id=1, source_target_pairs={{0,1},{1,2},{2,3},{3,4},{4,5},{5,6},{6,7},{7,8},{8,9},{9,10},{10,1... | collective-permute-start | bytes 1032200 | tf_op jit(solution)/shard_map/ppermute | solution.py:19
  27.6 1.9 %collective-permute-start.5 = (bf16[6,7,32,128]{3,2,1,0:T(8,128)(2,1)S(1)}, bf16[6,7,32,128]{3,2,1,0:T(8,128)(2,1)S(1)}, u32[]{:S(2)}, u32[]{:S(2)}) collective-permute-start(bf16[6,7,32,128]{3,2,1,0:T(8,128)(2,1)S(1)} %get-tuple-element.60.first_ref), channel_id=1, source_target_pairs={{1,0},{2,1},{3,2},{4,3},{5,4},{6,5},{7,6},{8,7},{9,8},{10,9},{11,1... | collective-permute-start | bytes 1032200 | tf_op jit(solution)/shard_map/ppermute | solution.py:19
  29.6 0.1 add_convert_fusion.inside
  29.6 1.0 copy-done.4
  30.7 1.0 copy-done.5
  31.7 1.0 copy-done.6
  32.7 0.9 copy-done.7
  33.6 0.3 shard_map.111
  33.9 0.0 copy-start
  33.9 0.0 collective-permute-done.4.ylo.refs_0_
  33.9 2.3 %collective-permute-done.5.yhi.refs_1_ = bf16[6,7,32,128]{3,2,1,0:T(8,128)(2,1)S(1)} collective-permute-done((bf16[6,7,32,128]{3,2,1,0:T(8,128)(2,1)S(1)}, bf16[6,7,32,128]{3,2,1,0:T(8,128)(2,1)S(1)}, u32[]{:S(2)}, u32[]{:S(2)}) %collective-permute-start.5) | collective-permute-done | bytes 344096 | tf_op jit(solution)/shard_map/ppermute | solution.py:19
  36.2 1.6 %shard_map.113 = (bf16[4,18,32,64]{3,2,1,0:T(8,128)(2,1)S(1)}, bf16[2,320,64]{2,1,0:T(8,128)(2,1)S(1)}, bf16[64,512]{1,0:T(8,128)(2,1)S(1)}, f32[128,128]{1,0:T(8,128)S(1)}) custom-call(bf16[2,8,32,64]{3,2,1,0:T(8,128)(2,1)S(1)} %get-tuple-element.54.c_ref, bf16[6,7,32,128]{3,2,1,0:T(8,128)(2,1)S(1)} %collective-permute-done.4.ylo.refs_0_, ...), custom_call_target="tpu_custom_call" | custom-call | flops 1000000 | bytes 10000 | tf_op jit(solution)/shard_map/pallas_call | solution.py:49
  37.8 3.2 %shard_map.112 = (bf16[8,22,32,64]{3,2,1,0:T(8,128)(2,1)S(1)}, bf16[4,10,32,64]{3,2,1,0:T(8,128)(2,1)S(1)}, f32[6,320,64]{2,1,0:T(8,128)S(1)}, bf16[3,10,16,64]{3,2,1,0:T(8,128)(2,1)S(1)}) custom-call(bf16[2,8,32,64]{3,2,1,0:T(8,128)(2,1)S(1)} %get-tuple-element.53.f_ref, bf16[6,7,32,128]{3,2,1,0:T(8,128)(2,1)S(1)} %collective-permute-done.4.ylo.refs_0_, ...), custom_call_target="tpu_custom_call" | custom-call | flops 1000000 | bytes 10000 | tf_op jit(solution)/shard_map/pallas_call | solution.py:49
  41.0 0.9 shard_map.114
  41.8 2.8 %shard_map.115 = (bf16[2,10,32,64]{3,2,1,0:T(8,128)(2,1)S(1)}, bf16[32,80,128]{2,1,0:T(8,128)(2,1)S(1)}, bf16[32,80,128]{2,1,0:T(8,128)(2,1)S(1)}) custom-call(bf16[3,10,16,64]{3,2,1,0:T(8,128)(2,1)S(1)} %get-tuple-element.62.px, bf16[96,128]{1,0:T(8,128)(2,1)S(1)} %get-tuple-element.67.la_ref, bf16[128,128]{1,0:T(8,128)(2,1)S(1)} %get-tuple-element.68.lg_ref, ...), custom_call_target="tpu_custom_call" | custom-call | flops 1000000 | bytes 10000 | tf_op jit(solution)/shard_map/pallas_call | solution.py:49
  44.6 1.9 %collective-permute-start.6 = (bf16[32,80,128]{2,1,0:T(8,128)(2,1)S(1)}, bf16[32,80,128]{2,1,0:T(8,128)(2,1)S(1)}, u32[]{:S(2)}, u32[]{:S(2)}) collective-permute-start(bf16[32,80,128]{2,1,0:T(8,128)(2,1)S(1)} %get-tuple-element.77), channel_id=1, source_target_pairs={{0,1},{1,0},{2,3},{3,2},{4,5},{5,4},{6,7},{7,6},{8,9},{9,8},{10,11... | collective-permute-start | bytes 1966088 | tf_op jit(solution)/shard_map/ppermute | solution.py:27
  46.6 2.1 %collective-permute-done.6.b_ref = bf16[32,80,128]{2,1,0:T(8,128)(2,1)S(1)} collective-permute-done((bf16[32,80,128]{2,1,0:T(8,128)(2,1)S(1)}, bf16[32,80,128]{2,1,0:T(8,128)(2,1)S(1)}, u32[]{:S(2)}, u32[]{:S(2)}) %collective-permute-start.6) | collective-permute-done | bytes 655392 | tf_op jit(solution)/shard_map/ppermute | solution.py:27
  48.6 1.0 shard_map.116
  49.6 12.3 %all-to-all-start = ((bf16[32,80,128]{2,1,0:T(8,128)(2,1)}), bf16[32,80,128]{2,1,0:T(8,128)(2,1)S(1)}, u32[]{:S(2)}, u32[]{:S(2)}) async-start(bf16[32,80,128]{2,1,0:T(8,128)(2,1)} %shard_map.116), calls=%async_computation | async-start | bytes 1310720 | tf_op jit(solution)/shard_map/all_to_all | solution.py:45
  61.9 1.3 %collective-permute-start.8 = (bf16[224,128]{1,0:T(8,128)(2,1)S(1)}, bf16[224,128]{1,0:T(8,128)(2,1)S(1)}, u32[]{:S(2)}, u32[]{:S(2)}) collective-permute-start(bf16[224,128]{1,0:T(8,128)(2,1)S(1)} %get-tuple-element.80), channel_id=1, source_target_pairs={{16,0},{32,16},{48,32},{64,48},{80,64},{96,80},{112,96},{128,112},... | collective-permute-start | bytes 172040 | tf_op jit(solution)/shard_map/ppermute | solution.py:19
  63.2 4.0 %collective-permute-start.7 = (bf16[224,128]{1,0:T(8,128)(2,1)S(1)}, bf16[224,128]{1,0:T(8,128)(2,1)S(1)}, u32[]{:S(2)}, u32[]{:S(2)}) collective-permute-start(bf16[224,128]{1,0:T(8,128)(2,1)S(1)} %get-tuple-element.80), channel_id=1, source_target_pairs={{0,16},{16,32},{32,48},{48,64},{64,80},{80,96},{96,112},{112,128},... | collective-permute-start | bytes 172040 | tf_op jit(solution)/shard_map/ppermute | solution.py:19
  67.2 8.0 %all-to-all-done.parts_ref = bf16[32,80,128]{2,1,0:T(8,128)(2,1)S(1)} async-done(((bf16[32,80,128]{2,1,0:T(8,128)(2,1)}), bf16[32,80,128]{2,1,0:T(8,128)(2,1)S(1)}, u32[]{:S(2)}, u32[]{:S(2)}) %all-to-all-start) | async-done | bytes 655392 | tf_op jit(solution)/shard_map/all_to_all | solution.py:45
  75.2 0.8 shard_map.117
  75.9 0.0 collective-permute-done.8.xhi
  75.9 5.3 %all-to-all-start.1 = ((bf16[8,80,128]{2,1,0:T(8,128)(2,1)}), bf16[8,80,128]{2,1,0:T(8,128)(2,1)S(1)}, u32[]{:S(2)}, u32[]{:S(2)}) async-start(bf16[8,80,128]{2,1,0:T(8,128)(2,1)} %shard_map.117), calls=%async_computation.1 | async-start | bytes 327680 | tf_op jit(solution)/shard_map/all_to_all | solution.py:45
  81.2 0.5 shard_map.119
  81.7 0.0 copy-start.1
  81.7 3.5 %collective-permute-start.9 = (bf16[160,128]{1,0:T(8,128)(2,1)S(1)}, bf16[160,128]{1,0:T(8,128)(2,1)S(1)}, u32[]{:S(2)}, u32[]{:S(2)}) collective-permute-start(bf16[160,128]{1,0:T(8,128)(2,1)S(1)} %get-tuple-element.84), channel_id=1, source_target_pairs={{0,16},{16,32},{32,48},{48,64},{64,80},{80,96},{96,112},{112,128},... | collective-permute-start | bytes 122888 | tf_op jit(solution)/shard_map/ppermute | solution.py:19
  85.2 1.3 %collective-permute-start.10 = (bf16[160,128]{1,0:T(8,128)(2,1)S(1)}, bf16[160,128]{1,0:T(8,128)(2,1)S(1)}, u32[]{:S(2)}, u32[]{:S(2)}) collective-permute-start(bf16[160,128]{1,0:T(8,128)(2,1)S(1)} %get-tuple-element.85), channel_id=1, source_target_pairs={{16,0},{32,16},{48,32},{64,48},{80,64},{96,80},{112,96},{128,112},... | collective-permute-start | bytes 122888 | tf_op jit(solution)/shard_map/ppermute | solution.py:19
  86.5 3.0 %all-to-all-done.1.parts_ref = bf16[8,80,128]{2,1,0:T(8,128)(2,1)S(1)} async-done(((bf16[8,80,128]{2,1,0:T(8,128)(2,1)}), bf16[8,80,128]{2,1,0:T(8,128)(2,1)S(1)}, u32[]{:S(2)}, u32[]{:S(2)}) %all-to-all-start.1) | async-done | bytes 163872 | tf_op jit(solution)/shard_map/all_to_all | solution.py:45
  89.5 0.9 shard_map.118
  90.4 5.6 %all-to-all-start.2 = ((bf16[32,80,128]{2,1,0:T(8,128)(2,1)}), bf16[32,80,128]{2,1,0:T(8,128)(2,1)S(1)}, u32[]{:S(2)}, u32[]{:S(2)}) async-start(bf16[32,80,128]{2,1,0:T(8,128)(2,1)} %shard_map.118), calls=%async_computation.2 | async-start | bytes 1310720 | tf_op jit(solution)/shard_map/all_to_all | solution.py:45
  96.0 1.5 %shard_map.120 = bf16[2,8,32,64]{3,2,1,0:T(8,128)(2,1)} custom-call(bf16[4,10,32,64]{3,2,1,0:T(8,128)(2,1)S(1)} %get-tuple-element.71.enc_ref, bf16[2,10,32,64]{3,2,1,0:T(8,128)(2,1)S(1)} %get-tuple-element.87.lifted_ref, bf16[224,128]{1,0:T(8,128)(2,1)S(1)} %collective-permute-done.7.xlo, bf16[224,128]{1,0:T(8,128)(2,1)S(1)} %collective-permute-done.8.xhi, ...), custom_call_target="tpu_custom_call" | custom-call | flops 1000000 | bytes 10000 | tf_op jit(solution)/shard_map/pallas_call | solution.py:49
  97.4 1.3 %shard_map.121 = bf16[2,8,32,64]{3,2,1,0:T(8,128)(2,1)} custom-call(bf16[2,10,32,64]{3,2,1,0:T(8,128)(2,1)S(1)} %get-tuple-element.89.eg_ref, bf16[160,128]{1,0:T(8,128)(2,1)S(1)} %collective-permute-done.9.xlo, bf16[160,128]{1,0:T(8,128)(2,1)S(1)} %collective-permute-done.10.xhi, bf16[576,192]{1,0:T(8,128)(2,1)S(1)} %get-tuple-element.92.w_ref), custom_call_target="tpu_custom_call" | custom-call | flops 1000000 | bytes 10000 | tf_op jit(solution)/shard_map/pallas_call | solution.py:49
  98.7 10.6 %all-to-all-done.2.own_ref = bf16[32,80,128]{2,1,0:T(8,128)(2,1)S(1)} async-done(((bf16[32,80,128]{2,1,0:T(8,128)(2,1)}), bf16[32,80,128]{2,1,0:T(8,128)(2,1)S(1)}, u32[]{:S(2)}, u32[]{:S(2)}) %all-to-all-start.2) | async-done | bytes 655392 | tf_op jit(solution)/shard_map/all_to_all | solution.py:45
  109.3 7.6 %collective-permute-start.11 = (bf16[32,80,128]{2,1,0:T(8,128)(2,1)S(1)}, bf16[32,80,128]{2,1,0:T(8,128)(2,1)S(1)}, u32[]{:S(2)}, u32[]{:S(2)}) collective-permute-start(bf16[32,80,128]{2,1,0:T(8,128)(2,1)S(1)} %all-to-all-done.2.own_ref), channel_id=1, source_target_pairs={{0,1},{1,0},{2,3},{3,2},{4,5},{5,4},{6,7},{7,6},{8,9},{9,8},{10,11... | collective-permute-start | bytes 1966088 | tf_op jit(solution)/shard_map/ppermute | solution.py:27
  116.9 1.7 %collective-permute-done.11.other_ref = bf16[32,80,128]{2,1,0:T(8,128)(2,1)S(1)} collective-permute-done((bf16[32,80,128]{2,1,0:T(8,128)(2,1)S(1)}, bf16[32,80,128]{2,1,0:T(8,128)(2,1)S(1)}, u32[]{:S(2)}, u32[]{:S(2)}) %collective-permute-start.11) | collective-permute-done | bytes 655392 | tf_op jit(solution)/shard_map/ppermute | solution.py:27
  118.6 1.8 %shard_map.122 = (f32[27,64,64]{2,1,0:T(8,128)}, f32[27,64,128]{2,1,0:T(8,128)}, f32[27,64,128]{2,1,0:T(8,128)}, f32[8,64,128]{2,1,0:T(8,128)}) custom-call(s32[1]{0:T(128)} %bitcast.7.core, bf16[32,80,128]{2,1,0:T(8,128)(2,1)S(1)} %all-to-all-done.2.own_ref, bf16[32,80,128]{2,1,0:T(8,128)(2,1)S(1)} %collective-permute-done.11.other_ref), custom_call_target="tpu_custom_call" | custom-call | flops 1000000 | bytes 10000 | tf_op jit(solution)/shard_map/pallas_call | solution.py:49
  (13 shorter events, 0.0 us)
Async XLA Ops:
  0.6 0.9 copy-start.2
  1.5 0.9 copy-start.3
  2.6 18.3 %collective-permute-start = (bf16[12,32,128]{2,1,0:T(8,128)(2,1)S(1)}, bf16[12,32,128]{2,1,0:T(8,128)(2,1)S(1)}, u32[]{:S(2)}, u32[]{:S(2)}) collective-permute-start(bf16[12,32,128]{2,1,0:T(8,128)(2,1)S(1)} %get-tuple-element.55), channel_id=1, source_target_pairs={{0,16},{16,32},{32,48},{48,64},{64,80},{80,96},{96,112},{112,128},... | collective-permute-start | bytes 294920 | tf_op jit(solution)/shard_map/ppermute | solution.py:19
  6.6 14.3 %collective-permute-start.1 = (bf16[12,32,128]{2,1,0:T(8,128)(2,1)S(1)}, bf16[12,32,128]{2,1,0:T(8,128)(2,1)S(1)}, u32[]{:S(2)}, u32[]{:S(2)}) collective-permute-start(bf16[12,32,128]{2,1,0:T(8,128)(2,1)S(1)} %get-tuple-element.56), channel_id=1, source_target_pairs={{16,0},{32,16},{48,32},{64,48},{80,64},{96,80},{112,96},{128,112},... | collective-permute-start | bytes 294920 | tf_op jit(solution)/shard_map/ppermute | solution.py:19
  7.9 6.3 %collective-permute-start.2 = (bf16[4,32,128]{2,1,0:T(8,128)(2,1)S(1)}, bf16[4,32,128]{2,1,0:T(8,128)(2,1)S(1)}, u32[]{:S(2)}, u32[]{:S(2)}) collective-permute-start(bf16[4,32,128]{2,1,0:T(8,128)(2,1)S(1)} %get-tuple-element.57), channel_id=1, source_target_pairs={{0,32},{16,48},{32,64},{48,80},{64,96},{80,112},{96,128},{112,144}... | collective-permute-start | bytes 98312 | tf_op jit(solution)/shard_map/ppermute | solution.py:19
  12.9 8.0 %collective-permute-start.3 = (bf16[4,32,128]{2,1,0:T(8,128)(2,1)S(1)}, bf16[4,32,128]{2,1,0:T(8,128)(2,1)S(1)}, u32[]{:S(2)}, u32[]{:S(2)}) collective-permute-start(bf16[4,32,128]{2,1,0:T(8,128)(2,1)S(1)} %get-tuple-element.58), channel_id=1, source_target_pairs={{32,0},{48,16},{64,32},{80,48},{96,64},{112,80},{128,96},{144,112}... | collective-permute-start | bytes 98312 | tf_op jit(solution)/shard_map/ppermute | solution.py:19
  21.3 12.6 %collective-permute-start.4 = (bf16[6,7,32,128]{3,2,1,0:T(8,128)(2,1)S(1)}, bf16[6,7,32,128]{3,2,1,0:T(8,128)(2,1)S(1)}, u32[]{:S(2)}, u32[]{:S(2)}) collective-permute-start(bf16[6,7,32,128]{3,2,1,0:T(8,128)(2,1)S(1)} %get-tuple-element.59), channel_id=1, source_target_pairs={{0,1},{1,2},{2,3},{3,4},{4,5},{5,6},{6,7},{7,8},{8,9},{9,10},{10,1... | collective-permute-start | bytes 1032200 | tf_op jit(solution)/shard_map/ppermute | solution.py:19
  27.6 8.6 %collective-permute-start.5 = (bf16[6,7,32,128]{3,2,1,0:T(8,128)(2,1)S(1)}, bf16[6,7,32,128]{3,2,1,0:T(8,128)(2,1)S(1)}, u32[]{:S(2)}, u32[]{:S(2)}) collective-permute-start(bf16[6,7,32,128]{3,2,1,0:T(8,128)(2,1)S(1)} %get-tuple-element.60.first_ref), channel_id=1, source_target_pairs={{1,0},{2,1},{3,2},{4,3},{5,4},{6,5},{7,6},{8,7},{9,8},{10,9},{11,1... | collective-permute-start | bytes 1032200 | tf_op jit(solution)/shard_map/ppermute | solution.py:19
  29.6 1.0 copy-start.4
  30.7 1.0 copy-start.5
  31.7 1.0 copy-start.6
  32.7 0.9 copy-start.7
  33.9 7.1 %copy-start = (bf16[192,1152]{1,0:T(8,128)(2,1)}, bf16[192,1152]{1,0:T(8,128)(2,1)S(1)}, u32[]{:S(2)}) copy-start(bf16[192,1152]{1,0:T(8,128)(2,1)S(1)} %get-tuple-element.88.w_ref) | copy-start | bytes 1327108
  44.6 4.0 %collective-permute-start.6 = (bf16[32,80,128]{2,1,0:T(8,128)(2,1)S(1)}, bf16[32,80,128]{2,1,0:T(8,128)(2,1)S(1)}, u32[]{:S(2)}, u32[]{:S(2)}) collective-permute-start(bf16[32,80,128]{2,1,0:T(8,128)(2,1)S(1)} %get-tuple-element.77), channel_id=1, source_target_pairs={{0,1},{1,0},{2,3},{3,2},{4,5},{5,4},{6,7},{7,6},{8,9},{9,8},{10,11... | collective-permute-start | bytes 1966088 | tf_op jit(solution)/shard_map/ppermute | solution.py:27
  49.6 25.6 %all-to-all-start = ((bf16[32,80,128]{2,1,0:T(8,128)(2,1)}), bf16[32,80,128]{2,1,0:T(8,128)(2,1)S(1)}, u32[]{:S(2)}, u32[]{:S(2)}) async-start(bf16[32,80,128]{2,1,0:T(8,128)(2,1)} %shard_map.116), calls=%async_computation | async-start | bytes 1310720 | tf_op jit(solution)/shard_map/all_to_all | solution.py:45
  61.9 14.1 %collective-permute-start.8 = (bf16[224,128]{1,0:T(8,128)(2,1)S(1)}, bf16[224,128]{1,0:T(8,128)(2,1)S(1)}, u32[]{:S(2)}, u32[]{:S(2)}) collective-permute-start(bf16[224,128]{1,0:T(8,128)(2,1)S(1)} %get-tuple-element.80), channel_id=1, source_target_pairs={{16,0},{32,16},{48,32},{64,48},{80,64},{96,80},{112,96},{128,112},... | collective-permute-start | bytes 172040 | tf_op jit(solution)/shard_map/ppermute | solution.py:19
  63.2 12.8 %collective-permute-start.7 = (bf16[224,128]{1,0:T(8,128)(2,1)S(1)}, bf16[224,128]{1,0:T(8,128)(2,1)S(1)}, u32[]{:S(2)}, u32[]{:S(2)}) collective-permute-start(bf16[224,128]{1,0:T(8,128)(2,1)S(1)} %get-tuple-element.80), channel_id=1, source_target_pairs={{0,16},{16,32},{32,48},{48,64},{64,80},{80,96},{96,112},{112,128},... | collective-permute-start | bytes 172040 | tf_op jit(solution)/shard_map/ppermute | solution.py:19
  75.9 13.6 %all-to-all-start.1 = ((bf16[8,80,128]{2,1,0:T(8,128)(2,1)}), bf16[8,80,128]{2,1,0:T(8,128)(2,1)S(1)}, u32[]{:S(2)}, u32[]{:S(2)}) async-start(bf16[8,80,128]{2,1,0:T(8,128)(2,1)} %shard_map.117), calls=%async_computation.1 | async-start | bytes 327680 | tf_op jit(solution)/shard_map/all_to_all | solution.py:45
  81.7 14.3 %copy-start.1 = (bf16[192,1152]{1,0:T(8,128)(2,1)S(1)}, bf16[192,1152]{1,0:T(8,128)(2,1)}, u32[]{:S(2)}) copy-start(bf16[192,1152]{1,0:T(8,128)(2,1)} %copy-done) | copy-start | bytes 1327108
  81.7 8.7 %collective-permute-start.9 = (bf16[160,128]{1,0:T(8,128)(2,1)S(1)}, bf16[160,128]{1,0:T(8,128)(2,1)S(1)}, u32[]{:S(2)}, u32[]{:S(2)}) collective-permute-start(bf16[160,128]{1,0:T(8,128)(2,1)S(1)} %get-tuple-element.84), channel_id=1, source_target_pairs={{0,16},{16,32},{32,48},{48,64},{64,80},{80,96},{96,112},{112,128},... | collective-permute-start | bytes 122888 | tf_op jit(solution)/shard_map/ppermute | solution.py:19
  85.2 5.2 %collective-permute-start.10 = (bf16[160,128]{1,0:T(8,128)(2,1)S(1)}, bf16[160,128]{1,0:T(8,128)(2,1)S(1)}, u32[]{:S(2)}, u32[]{:S(2)}) collective-permute-start(bf16[160,128]{1,0:T(8,128)(2,1)S(1)} %get-tuple-element.85), channel_id=1, source_target_pairs={{16,0},{32,16},{48,32},{64,48},{80,64},{96,80},{112,96},{128,112},... | collective-permute-start | bytes 122888 | tf_op jit(solution)/shard_map/ppermute | solution.py:19
  90.4 18.9 %all-to-all-start.2 = ((bf16[32,80,128]{2,1,0:T(8,128)(2,1)}), bf16[32,80,128]{2,1,0:T(8,128)(2,1)S(1)}, u32[]{:S(2)}, u32[]{:S(2)}) async-start(bf16[32,80,128]{2,1,0:T(8,128)(2,1)} %shard_map.118), calls=%async_computation.2 | async-start | bytes 1310720 | tf_op jit(solution)/shard_map/all_to_all | solution.py:45
  109.3 9.3 %collective-permute-start.11 = (bf16[32,80,128]{2,1,0:T(8,128)(2,1)S(1)}, bf16[32,80,128]{2,1,0:T(8,128)(2,1)S(1)}, u32[]{:S(2)}, u32[]{:S(2)}) collective-permute-start(bf16[32,80,128]{2,1,0:T(8,128)(2,1)S(1)} %all-to-all-done.2.own_ref), channel_id=1, source_target_pairs={{0,1},{1,0},{2,3},{3,2},{4,5},{5,4},{6,7},{7,6},{8,9},{9,8},{10,11... | collective-permute-start | bytes 1966088 | tf_op jit(solution)/shard_map/ppermute | solution.py:27
